TPU v7x, 32 devices: a whole 2x2x4 slice. The times are simulated.
32 devices in a mesh: dp: 8 (over y, x, core), tensor: 4 (over z).
Axes of the slice: x: 2, y: 2, z: 4, core: 2. Of those that a mesh axis runs over, the one named last changes fastest.
Arguments:
- tokens: bfloat16 [10240, 2048], P(('dp', 'tensor')), may hold values from -6 to 6
- cotangent: bfloat16 [10240, 2048], P(('dp', 'tensor')), may hold values from -6 to 6
- attention_gain: bfloat16 [2048], replicated, may hold values from 0.5 to 1.5
- feed_gain: bfloat16 [2048], replicated, may hold values from 0.5 to 1.5
- query_weight: bfloat16 [2048, 2048], P('dp', 'tensor'), may hold values from -0.125 to 0.125
- key_weight: bfloat16 [2048, 2048], P('dp', 'tensor'), may hold values from -0.125 to 0.125
- value_weight: bfloat16 [2048, 2048], P('dp', 'tensor'), may hold values from -0.125 to 0.125
- output_weight: bfloat16 [2048, 2048], P('dp', 'tensor'), may hold values from -0.75 to 0.75
- gate_weight: bfloat16 [2048, 8192], P('dp', 'tensor'), may hold values from -0.125 to 0.125
- up_weight: bfloat16 [2048, 8192], P('dp', 'tensor'), may hold values from -0.125 to 0.125
- down_weight: bfloat16 [2048, 8192], P('dp', 'tensor'), may hold values from -0.0625 to 0.0625
- entry_maps: bfloat16 [5, 8, 2048, 16], replicated, may hold values from -0.125 to 0.125
- head_exits: bfloat16 [3, 8, 16, 2048], P(None, None, None, 'tensor'), may hold values from -1.5 to 1.5
- unit_exits: bfloat16 [2, 8, 16, 8192], P(None, None, None, 'tensor'), may hold values from -1.5 to 1.5
- output_entry: bfloat16 [8, 2048, 16], P(None, 'tensor'), may hold values from -0.75 to 0.75
- down_entry: bfloat16 [8, 8192, 16], P(None, 'tensor'), may hold values from -0.0625 to 0.0625
- final_exits: bfloat16 [2, 8, 16, 2048], replicated, may hold values from -1.5 to 1.5
- parents: int32 [8, 20], P('dp'), may hold values from -1 to 11, as said below
- adapter_pick: int32 [8], P('dp'), may hold values from 0 to 7
Outputs:
- result: bfloat16 [10240, 2048], P(('dp', 'tensor'))
- grad_tokens: bfloat16 [10240, 2048], P(('dp', 'tensor'))
- grad_entries: float32 [5, 8, 2048, 16], replicated
- grad_heads: float32 [3, 8, 16, 2048], P(None, None, None, 'tensor')
- grad_units: float32 [2, 8, 16, 8192], P(None, None, None, 'tensor')
- grad_output: float32 [8, 2048, 16], P(None, 'tensor')
- grad_down: float32 [8, 8192, 16], P(None, 'tensor')
- grad_finals: float32 [2, 8, 16, 2048], replicated
Inputs may be any that keep to these rules, and one draw needn't show every extreme that they name: `parents`: in every tree, blocks 0 to 7 form the trunk, each the child of the block before it (block 0 has -1); blocks 8 to 11 are branches whose parent is block 7; blocks 12 to 19 are leaves whose parent is a branch block, each branch the parent of two leaves.
All inputs are finite; a program needn't handle non-finite values.
Results may differ from a plain program's by a relative error of at most 0.024.
Values may be sent and summed in bfloat16 or wider, within the bound.
A program may use at most 320 MiB of HBM per device.

v0:
```python
import jax
import jax.numpy as jnp
from jax import lax
from jax.sharding import PartitionSpec as P

HEAD_DIM = 64


eps = 1e-05
theta = 130000.0
highest = lax.Precision.HIGHEST


def exact(left, right):
    return jnp.dot(left, right, precision=highest, preferred_element_type=jnp.float32)


def matmul(left, right):
    return jnp.dot(left, right, preferred_element_type=jnp.float32)


def times_t(left, right):
    return lax.dot_general(
        left, right, (((1,), (1,)), ((), ())), preferred_element_type=jnp.float32
    )


def ancestry(parent_row):
    count = parent_row.shape[0]
    ids = jnp.arange(count, dtype=jnp.int32)
    step = (parent_row[:, None] == ids[None, :]).astype(jnp.float32)
    identity = jnp.eye(count, dtype=jnp.float32)

    def grow(index, reach):
        return jnp.minimum(identity + exact(step, reach), 1.0)

    return lax.fori_loop(0, count, grow, identity)


def tree_layout(parent_row, seg):
    reach = ancestry(parent_row)
    depth = jnp.sum(reach, axis=1) - 1.0
    total = reach.shape[0] * seg
    place = jnp.arange(total, dtype=jnp.int32)
    offset = (place % seg).astype(jnp.float32)
    position = jnp.repeat(depth, seg) * seg + offset
    allowed = jnp.repeat(jnp.repeat(reach, seg, axis=0), seg, axis=1) > 0.5
    allowed = allowed & (place[None, :] <= place[:, None])
    return (position, allowed)


def rotate(values, position, sign):
    half = values.shape[-1] // 2
    freq = theta ** (-jnp.arange(half, dtype=jnp.float32) / half)
    angle = position[:, None] * freq[None, :]
    cosine = jnp.cos(angle)[:, None, :]
    sine = sign * jnp.sin(angle)[:, None, :]
    first = values[..., :half]
    second = values[..., half:]
    return jnp.concatenate(
        [first * cosine - second * sine, second * cosine + first * sine], axis=-1
    )


def norm_forward(rows, gain):
    rms = lax.rsqrt(jnp.mean(rows * rows, axis=1, keepdims=True) + eps)
    return ((rows * rms * gain).astype(jnp.bfloat16), rms)


def norm_backward(rows, rms, gain, grad):
    scaled = grad * gain
    return rms * (scaled - rows * (rms * rms) * jnp.mean(scaled * rows, axis=1, keepdims=True))


def gather_rows(rows):
    return lax.all_gather(rows, "tensor", axis=0, tiled=True)


def sum_terms(term, total):
    return lax.psum_scatter(
        term(0, total).astype(jnp.bfloat16), "tensor", scatter_dimension=0, tiled=True
    ).astype(jnp.float32)


def head_forward(q_head, k_head, v_head, allowed, scale):
    scores = matmul(q_head, k_head.T) * scale
    scores = jnp.where(allowed, scores, -1e30)
    top = jnp.max(scores, axis=1, keepdims=True)
    weights = jnp.exp(scores - top)
    summed = jnp.sum(weights, axis=1, keepdims=True)
    probs = weights / summed
    output = matmul(probs.astype(jnp.bfloat16), v_head).astype(jnp.bfloat16)
    return (output, (top + jnp.log(summed))[:, 0])


def head_backward(q_head, k_head, v_head, log_total, grad_head, allowed, scale):
    scores = matmul(q_head, k_head.T) * scale
    probs = jnp.where(allowed, jnp.exp(scores - log_total[:, None]), 0.0)
    grad_probs = matmul(grad_head, v_head.T)
    delta = jnp.sum(grad_probs * probs, axis=1, keepdims=True)
    grad_scores = (probs * (grad_probs - delta)).astype(jnp.bfloat16)
    grad_q = matmul(grad_scores, k_head) * scale
    grad_k = matmul(grad_scores.T, q_head) * scale
    grad_v = matmul(probs.astype(jnp.bfloat16).T, grad_head)
    return (grad_q, grad_k, grad_v)


def spread(grad, chosen, axis):
    shape = [1] * (grad.ndim + 1)
    shape[axis] = chosen.shape[0]
    return jnp.expand_dims(grad, axis) * chosen.reshape(shape)


def local(
    tokens,
    cotangent,
    attention_gain,
    feed_gain,
    query_weight,
    key_weight,
    value_weight,
    output_weight,
    gate_weight,
    up_weight,
    down_weight,
    entry_maps,
    head_exits,
    unit_exits,
    output_entry,
    down_entry,
    final_exits,
    parents,
    adapter_pick,
):
    pick = adapter_pick[0]
    entries = entry_maps[:, pick]
    heads_exit = head_exits[:, pick]
    units_exit = unit_exits[:, pick]
    out_entry = output_entry[pick]
    fall_entry = down_entry[pick]
    finals = final_exits[:, pick]
    parent_row = parents[0]
    rows_here = tokens.astype(jnp.float32)
    local_rows = rows_here.shape[0]
    total = local_rows * lax.axis_size("tensor")
    position, allowed = tree_layout(parent_row, total // parent_row.shape[0])
    gain_one = attention_gain.astype(jnp.float32)
    gain_two = feed_gain.astype(jnp.float32)
    scale = HEAD_DIM ** (-0.5)
    final_one = finals[0].astype(jnp.float32)
    final_two = finals[1].astype(jnp.float32)
    w_query, w_key, w_value, w_output = (
        lax.all_gather(query_weight, "dp", axis=0, tiled=True),
        lax.all_gather(key_weight, "dp", axis=0, tiled=True),
        lax.all_gather(value_weight, "dp", axis=0, tiled=True),
        lax.all_gather(output_weight, "dp", axis=0, tiled=True),
    )
    normed_one, rms_one = norm_forward(rows_here, gain_one)
    full_one = gather_rows(normed_one)
    reduced_one = jnp.einsum(
        "td,kdr->ktr", full_one, entries[:3], preferred_element_type=jnp.float32
    )
    query_pre = matmul(full_one, w_query) + exact(reduced_one[0], heads_exit[0].astype(jnp.float32))
    key_pre = matmul(full_one, w_key) + exact(reduced_one[1], heads_exit[1].astype(jnp.float32))
    value_pre = matmul(full_one, w_value) + exact(reduced_one[2], heads_exit[2].astype(jnp.float32))
    query = (
        rotate(query_pre.reshape(total, -1, HEAD_DIM), position, 1.0)
        .astype(jnp.bfloat16)
        .transpose(1, 0, 2)
    )
    keys = (
        rotate(key_pre.reshape(total, -1, HEAD_DIM), position, 1.0)
        .astype(jnp.bfloat16)
        .transpose(1, 0, 2)
    )
    values = value_pre.astype(jnp.bfloat16).reshape(total, -1, HEAD_DIM).transpose(1, 0, 2)

    def attend_one(trio):
        return head_forward(trio[0], trio[1], trio[2], allowed, scale)

    per_head, log_totals = lax.map(attend_one, (query, keys, values))
    attended = per_head.transpose(1, 0, 2).reshape(total, -1)
    adapt_o = matmul(attended, out_entry)

    def term_one(start, count):
        return times_t(attended, w_output) + exact(adapt_o, final_one)

    middle = rows_here + sum_terms(term_one, total)
    w_gate, w_rise, w_fall = (
        lax.all_gather(gate_weight, "dp", axis=0, tiled=True),
        lax.all_gather(up_weight, "dp", axis=0, tiled=True),
        lax.all_gather(down_weight, "dp", axis=0, tiled=True),
    )
    normed_two, rms_two = norm_forward(middle, gain_two)
    full_two = gather_rows(normed_two)
    reduced_two = jnp.einsum(
        "td,kdr->ktr", full_two, entries[3:], preferred_element_type=jnp.float32
    )
    gate = matmul(full_two, w_gate) + exact(reduced_two[0], units_exit[0].astype(jnp.float32))
    rise = matmul(full_two, w_rise) + exact(reduced_two[1], units_exit[1].astype(jnp.float32))
    sigmoid_gate = jax.nn.sigmoid(gate)
    hidden = (gate * sigmoid_gate * rise).astype(jnp.bfloat16)
    adapt_d = matmul(hidden, fall_entry)

    def term_two(start, count):
        return times_t(hidden, w_fall) + exact(adapt_d, final_two)

    result = (middle + sum_terms(term_two, total)).astype(jnp.bfloat16)
    w_gate, w_rise, w_fall = (
        lax.all_gather(gate_weight, "dp", axis=0, tiled=True),
        lax.all_gather(up_weight, "dp", axis=0, tiled=True),
        lax.all_gather(down_weight, "dp", axis=0, tiled=True),
    )
    grad_out = gather_rows(cotangent)
    back_d = times_t(grad_out, finals[1]).astype(jnp.bfloat16)
    grad_hidden = matmul(grad_out, w_fall) + times_t(back_d, fall_entry)
    grad_fall_entry = matmul(hidden.T, back_d)
    grad_final_two = exact(adapt_d.T, grad_out.astype(jnp.float32))
    grad_gate = (grad_hidden * rise * sigmoid_gate * (1.0 + gate * (1.0 - sigmoid_gate))).astype(
        jnp.bfloat16
    )
    grad_rise = (grad_hidden * gate * sigmoid_gate).astype(jnp.bfloat16)
    unit_grads = jnp.stack([grad_gate, grad_rise])
    back_two = jnp.einsum(
        "ktf,krf->ktr", unit_grads, units_exit, preferred_element_type=jnp.float32
    )
    grad_units_here = jnp.einsum(
        "ktr,ktf->krf", reduced_two, unit_grads.astype(jnp.float32), precision=highest
    )
    grad_entries_two = jnp.einsum(
        "td,ktr->kdr", full_two.astype(jnp.float32), back_two, precision=highest
    )
    entries_two = entries[3:].astype(jnp.float32)

    def term_three(start, count):
        partial_value = times_t(grad_gate, w_gate) + times_t(grad_rise, w_rise)
        return partial_value + jnp.einsum("ktr,kdr->td", back_two, entries_two, precision=highest)

    grad_middle = cotangent.astype(jnp.float32) + norm_backward(
        middle, rms_two, gain_two, sum_terms(term_three, total)
    )
    w_query, w_key, w_value, w_output = (
        lax.all_gather(query_weight, "dp", axis=0, tiled=True),
        lax.all_gather(key_weight, "dp", axis=0, tiled=True),
        lax.all_gather(value_weight, "dp", axis=0, tiled=True),
        lax.all_gather(output_weight, "dp", axis=0, tiled=True),
    )
    grad_branch = gather_rows(grad_middle.astype(jnp.bfloat16))
    back_o = times_t(grad_branch, finals[0]).astype(jnp.bfloat16)
    grad_attended = (matmul(grad_branch, w_output) + times_t(back_o, out_entry)).astype(
        jnp.bfloat16
    )
    grad_out_entry = matmul(attended.T, back_o)
    grad_final_one = exact(adapt_o.T, grad_branch.astype(jnp.float32))
    grad_by_head = grad_attended.reshape(total, -1, HEAD_DIM).transpose(1, 0, 2)

    def back_one_head(items):
        return head_backward(items[0], items[1], items[2], items[3], items[4], allowed, scale)

    grad_q, grad_k, grad_v = lax.map(back_one_head, (query, keys, values, log_totals, grad_by_head))
    grad_query = (
        rotate(grad_q.transpose(1, 0, 2), position, -1.0).reshape(total, -1).astype(jnp.bfloat16)
    )
    grad_key = (
        rotate(grad_k.transpose(1, 0, 2), position, -1.0).reshape(total, -1).astype(jnp.bfloat16)
    )
    grad_value = grad_v.transpose(1, 0, 2).reshape(total, -1).astype(jnp.bfloat16)
    head_grads = jnp.stack([grad_query, grad_key, grad_value])
    back_one = jnp.einsum(
        "ktd,krd->ktr", head_grads, heads_exit, preferred_element_type=jnp.float32
    )
    grad_heads_here = jnp.einsum(
        "ktr,ktd->krd", reduced_one, head_grads.astype(jnp.float32), precision=highest
    )
    grad_entries_one = jnp.einsum(
        "td,ktr->kdr", full_one.astype(jnp.float32), back_one, precision=highest
    )
    entries_one = entries[:3].astype(jnp.float32)

    def term_four(start, count):
        partial_value = (
            times_t(grad_query, w_query) + times_t(grad_key, w_key) + times_t(grad_value, w_value)
        )
        return partial_value + jnp.einsum("ktr,kdr->td", back_one, entries_one, precision=highest)

    grad_tokens = (
        grad_middle + norm_backward(rows_here, rms_one, gain_one, sum_terms(term_four, total))
    ).astype(jnp.bfloat16)
    chosen = (jnp.arange(entry_maps.shape[1], dtype=jnp.int32) == pick).astype(jnp.float32)
    grad_entries = spread(jnp.concatenate([grad_entries_one, grad_entries_two], axis=0), chosen, 1)
    grad_finals = spread(jnp.stack([grad_final_one, grad_final_two]), chosen, 1)
    grad_heads = spread(grad_heads_here, chosen, 1)
    grad_units = spread(grad_units_here, chosen, 1)
    grad_output = spread(grad_out_entry, chosen, 0)
    grad_down = spread(grad_fall_entry, chosen, 0)
    grad_heads, grad_units, grad_output, grad_down = (
        lax.psum(grad_heads.astype(jnp.bfloat16), "dp").astype(jnp.float32),
        lax.psum(grad_units.astype(jnp.bfloat16), "dp").astype(jnp.float32),
        lax.psum(grad_output.astype(jnp.bfloat16), "dp").astype(jnp.float32),
        lax.psum(grad_down.astype(jnp.bfloat16), "dp").astype(jnp.float32),
    )
    grad_entries, grad_finals = lax.psum((grad_entries, grad_finals), ("dp", "tensor"))
    return (
        result,
        grad_tokens,
        grad_entries,
        grad_heads,
        grad_units,
        grad_output,
        grad_down,
        grad_finals,
    )


def solution(mesh):
    in_specs = (
        P(("dp", "tensor"), None),
        P(("dp", "tensor"), None),
        P(),
        P(),
        P("dp", "tensor"),
        P("dp", "tensor"),
        P("dp", "tensor"),
        P("dp", "tensor"),
        P("dp", "tensor"),
        P("dp", "tensor"),
        P("dp", "tensor"),
        P(),
        P(None, None, None, "tensor"),
        P(None, None, None, "tensor"),
        P(None, "tensor", None),
        P(None, "tensor", None),
        P(),
        P("dp", None),
        P("dp"),
    )
    out_specs = (
        P(("dp", "tensor"), None),
        P(("dp", "tensor"), None),
        P(),
        P(None, None, None, "tensor"),
        P(None, None, None, "tensor"),
        P(None, "tensor", None),
        P(None, "tensor", None),
        P(),
    )
    return jax.shard_map(local, mesh=mesh, in_specs=in_specs, out_specs=out_specs, check_vma=False)
```

profile of v0, /device:TPU:0, one launch (start us, length us, event | category | flops | bytes accessed | tf_op | source)
XLA Modules:
  0.0 1731.9 jit_solution(18252730930304002106)
XLA Ops:
  16.9 4.8 while.39
  23.7 17.1 all-gather.14.cloned.1.call-done
  40.9 100.2 %all-gather.12.cloned.1.call-done = bf16[1280,2048]{1,0:T(8,128)(2,1)} async-done(((bf16[320,2048]{1,0:T(8,128)(2,1)}), bf16[1280,2048]{1,0:T(8,128)(2,1)}) %all-gather.12.cloned.1.call-update) | async-done | bytes 5242896 | tf_op jit(solution)/shard_map/all_gather | solution.py:76
  141.1 6.4 fusion.142
  152.8 16.6 all-gather.16.cloned.1.call-done
  169.3 6.2 fusion.143
  187.9 11.1 all-gather.18.cloned.1.call-done
  199.0 6.2 fusion.144
  212.1 93.9 %while.40 = (s32[]{:T(128)}, bf16[8,1280,64]{1,2,0:T(8,128)(2,1)}, f32[8,1280]{1,0:T(8,128)}, bf16[8,1280,64]{2,1,0:T(8,128)(2,1)}, bf16[8,1280,64]{2,1,0:T(8,12...) while((s32[]{:T(128)}, bf16[8,1280,64]{1,2,0:T(8,128)(2,1)}, ...), condition=%wide.region_7.8_spmd.clone, body=%wide.region_4.7_spmd.clone.sunk | while | flops 435895040 | bytes 50388092 | solution.py:181
  219.1 4.8 fusion.234
  230.8 4.8 fusion.234
  242.6 4.8 fusion.234
  254.3 4.8 fusion.234
  266.1 4.8 fusion.234
  277.8 4.8 fusion.234
  289.5 4.8 fusion.234
  301.3 4.8 fusion.234
  307.7 5.0 fusion.145
  312.7 18.8 %add_convert_fusion.1 = bf16[1280,2048]{1,0:T(8,128)(2,1)} fusion(f32[1280,2048]{1,0:T(8,128)S(1)} %fusion.145, f32[1280,16]{0,1:T(8,128)S(1)} %fusion.105, bf16[2,8,16,2048]{3,2,1,0:T(8,128)(2,1)} %param.41, s32[]{:T(128)S(6)} %select_n.26), kind=kOutput, calls=%fused_computation.79 | convolution fusion | flops 508559360 | bytes 15876100 | tf_op jit(solution)/shard_map/dot_general | solution.py:15
  333.1 92.7 %reduce-scatter.5.cloned.1.call-done = bf16[320,2048]{1,0:T(8,128)(2,1)} async-done(((bf16[1280,2048]{1,0:T(8,128)(2,1)}), bf16[320,2048]{1,0:T(8,128)(2,1)}) %reduce-scatter.5.cloned.1.call-update) | async-done | bytes 1310736 | tf_op jit(solution)/shard_map/reduce_scatter | solution.py:80
  431.9 94.1 %all-gather.30.cloned.1.call-done = bf16[1280,2048]{1,0:T(8,128)(2,1)} async-done(((bf16[320,2048]{1,0:T(8,128)(2,1)}), bf16[1280,2048]{1,0:T(8,128)(2,1)}) %all-gather.30.cloned.1.call-update) | async-done | bytes 5242896 | tf_op jit(solution)/shard_map/all_gather | solution.py:76
  530.0 50.7 %all-gather.28.cloned.1.call-done = bf16[2048,2048]{1,0:T(8,128)(2,1)} async-done(((bf16[256,2048]{1,0:T(8,128)(2,1)}), bf16[2048,2048]{1,0:T(8,128)(2,1)}) %all-gather.28.cloned.1.call-update) | async-done | bytes 8388624 | tf_op jit(solution)/shard_map/all_gather | solution.py:192
  580.7 15.2 fusion.149
  595.9 6.4 convolution_add_fusion.3
  602.3 78.6 %all-gather.22.cloned.1.call-done = bf16[1280,2048]{1,0:T(8,128)(2,1)} async-done(((bf16[320,2048]{1,0:T(8,128)(2,1)}), bf16[1280,2048]{1,0:T(8,128)(2,1)}) %all-gather.22.cloned.1.call-update) | async-done | bytes 5242896 | tf_op jit(solution)/shard_map/all_gather | solution.py:76
  680.9 4.1 fusion.68
  685.1 50.4 %all-gather.26.cloned.1.call-done = bf16[2048,2048]{1,0:T(8,128)(2,1)} async-done(((bf16[256,2048]{1,0:T(8,128)(2,1)}), bf16[2048,2048]{1,0:T(8,128)(2,1)}) %all-gather.26.cloned.1.call-update) | async-done | bytes 8388624 | tf_op jit(solution)/shard_map/all_gather | solution.py:191
  735.5 15.2 fusion.147
  750.7 8.4 convolution_add_fusion.1
  759.1 32.7 %all-gather.24.cloned.1.call-done = bf16[2048,2048]{1,0:T(8,128)(2,1)} async-done(((bf16[256,2048]{1,0:T(8,128)(2,1)}), bf16[2048,2048]{1,0:T(8,128)(2,1)}) %all-gather.24.cloned.1.call-update) | async-done | bytes 8388624 | tf_op jit(solution)/shard_map/all_gather | solution.py:190
  791.8 17.2 fusion.146
  809.0 19.9 %multiply_convert_fusion.2 = (bf16[1280,2048]{1,0:T(8,128)(2,1)}, bf16[1280,2048]{1,0:T(8,128)(2,1)}, bf16[1280,2048]{1,0:T(8,128)(2,1)}) fusion(f32[1280,2048]{1,0:T(8,128)} %convolution_add_fusion.3, f32[1280,2048]{1,0:T(8,128)} %convolution_add_fusion.1, f32[1280,2048]{1,0:T(8,128)} %fusion.146, bf16[2,8,16,2048]{3,2,1,0:T(8,128)(2,1)} %param.38, ...), kind=kOutput, calls=%fused_computation.75 | convolution fusion | flops 547880960 | bytes 47333380 | tf_op jit(solution)/shard_map/dot_general | solution.py:15
  829.0 5.7 fusion.65
  834.7 7.4 fusion.96
  843.3 13.7 fusion.150
  857.0 21.3 %fusion.63 = bf16[1280,2048]{1,0:T(8,128)(2,1)} fusion(f32[1280,2048,1]{1,0,2:T(8,128)} %fusion.96, f32[1280,2048]{1,0:T(8,128)} %fusion.150, bf16[1280,2048]{1,0:T(8,128)(2,1)} %get-tuple-element.264, bf16[2048,2048]{1,0:T(8,128)(2,1)} %all-gather.26.cloned.1.call-done), kind=kOutput, calls=%fused_computation.73 | convolution fusion | flops 10745282560 | bytes 39845888 | tf_op jit(solution)/shard_map/dot_general | solution.py:23
  878.3 93.9 %reduce-scatter.9.cloned.1.call-done = bf16[320,2048]{1,0:T(8,128)(2,1)} async-done(((bf16[1280,2048]{1,0:T(8,128)(2,1)}), bf16[320,2048]{1,0:T(8,128)(2,1)}) %reduce-scatter.9.cloned.1.call-update) | async-done | bytes 1310736 | tf_op jit(solution)/shard_map/reduce_scatter | solution.py:80
  979.8 4.1 fusion.98
  987.5 5.7 convolution_bitcast_fusion
  994.2 4.9 fusion.64
  999.1 78.9 %all-gather.32.cloned.1.call-done = bf16[1280,2048]{1,0:T(8,128)(2,1)} async-done(((bf16[320,2048]{1,0:T(8,128)(2,1)}), bf16[1280,2048]{1,0:T(8,128)(2,1)}) %all-gather.32.cloned.1.call-update) | async-done | bytes 5242896 | tf_op jit(solution)/shard_map/all_gather | solution.py:76
  1093.4 164.4 %while.41 = (s32[]{:T(128)}, f32[8,1280,64]{1,2,0:T(8,128)}, f32[8,1280,64]{1,2,0:T(8,128)}, bf16[8,1280,64]{1,2,0:T(8,128)(2,1)}, bf16[8,1280,64]{2,1,0:T(8,128...) while((s32[]{:T(128)}, f32[8,1280,64]{1,2,0:T(8,128)}, ...), condition=%wide.region_15.16_spmd.clone, body=%wide.region_13.15_spmd.clone.sunk | while | flops 1066760960 | bytes 55762032 | solution.py:260
  1097.3 4.8 multiply_reduce_fusion.4
  1117.8 4.8 multiply_reduce_fusion.4
  1138.4 4.8 multiply_reduce_fusion.4
  1158.9 4.8 multiply_reduce_fusion.4
  1179.5 4.8 multiply_reduce_fusion.4
  1200.0 4.8 multiply_reduce_fusion.4
  1220.5 4.8 multiply_reduce_fusion.4
  1241.1 4.8 multiply_reduce_fusion.4
  1257.8 4.1 multiply_subtract_fusion.1
  1280.1 7.1 fusion.93
  1291.6 9.0 fusion.152
  1300.6 5.5 fusion.153
  1306.1 17.4 %fusion.62 = bf16[1280,2048]{1,0:T(8,128)(2,1)} fusion(f32[1280,2048,1]{1,0,2:T(8,128)} %fusion.93, f32[1280,2048]{1,0:T(8,128)} %fusion.152, f32[1280,2048]{1,0:T(8,128)} %fusion.153, bf16[1280,512]{0,1:T(8,128)(2,1)} %bitcast.42, bf16[2048,512]{1,0:T(8,128)(2,1)} %all-gather.18.cloned.1.call-done), kind=kOutput, calls=%fused_computation.71 | convolution fusion | flops 2694840320 | bytes 40108032 | tf_op jit(solution)/shard_map/dot_general | solution.py:23
  1323.5 15.7 fusion.148
  1339.2 7.6 add_convert_fusion
  1347.8 5.2 fusion.88
  1353.0 5.3 fusion.85
  1367.5 80.3 %reduce-scatter.11.cloned.1.call-done = bf16[320,2048]{1,0:T(8,128)(2,1)} async-done(((bf16[1280,2048]{1,0:T(8,128)(2,1)}), bf16[320,2048]{1,0:T(8,128)(2,1)}) %reduce-scatter.11.cloned.1.call-update) | async-done | bytes 1310736 | tf_op jit(solution)/shard_map/reduce_scatter | solution.py:80
  1450.1 94.2 %reduce-scatter.7.cloned.1.call-done = bf16[320,2048]{1,0:T(8,128)(2,1)} async-done(((bf16[1280,2048]{1,0:T(8,128)(2,1)}), bf16[320,2048]{1,0:T(8,128)(2,1)}) %reduce-scatter.7.cloned.1.call-update) | async-done | bytes 1310736 | tf_op jit(solution)/shard_map/reduce_scatter | solution.py:80
  1544.3 5.8 fusion.83
  1550.1 167.9 %all-reduce.5.cloned.1.call-done = (f32[5,8,2048,16]{2,3,1,0:T(8,128)}, f32[2,8,16,2048]{3,2,1,0:T(8,128)}) async-done(((f32[5,8,2048,16]{2,3,1,0:T(8,128)}, f32[2,8,16,2048]{3,2,1,0:T(8,128)}), (f32[5,8,2048,16]{2,3,1,0:T(8,128)}, f32[2,8,16,2048]{3,2,1,0:T(8,128)})) %all-reduce.5.cloned.1.call-update) | async-done | bytes 7340048 | tf_op jit(solution)/shard_map/psum | solution.py:302
  1717.9 5.6 copy.97
  (379 shorter events, 298.8 us)
Async XLA Ops:
  7.2 140.3 %copy-start = (bf16[5,8,2048,16]{2,3,1,0:T(8,128)(2,1)S(1)}, bf16[5,8,2048,16]{2,3,1,0:T(8,128)(2,1)}, u32[]{:S(2)}) copy-start(bf16[5,8,2048,16]{2,3,1,0:T(8,128)(2,1)} %param.36) | copy-start | bytes 7864324
  7.2 33.7 %all-gather.14.cloned.1.call-start = ((), (), s32[]{:S(2)}) async-start(), calls=%async_computation.5 | async-start | bytes 2359296 | tf_op jit(solution)/shard_map/all_gather | solution.py:153
  7.9 133.2 %all-gather.12.cloned.1.call-start = ((), (), s32[]{:S(2)}) async-start(), calls=%async_computation.4 | async-start | bytes 6553600 | tf_op jit(solution)/shard_map/all_gather | solution.py:76
  10.3 6.5 copy-start.49
  14.2 155.1 %all-gather.16.cloned.1.call-start = ((), (), s32[]{:S(2)}) async-start(), calls=%async_computation.6 | async-start | bytes 2359296 | tf_op jit(solution)/shard_map/all_gather | solution.py:154
  15.0 184.0 %all-gather.18.cloned.1.call-start = ((), (), s32[]{:S(2)}) async-start(), calls=%async_computation.7 | async-start | bytes 2359296 | tf_op jit(solution)/shard_map/all_gather | solution.py:155
  15.5 292.2 %all-gather.20.cloned.1.call-start = ((), (), s32[]{:S(2)}) async-start(), calls=%async_computation.8 | async-start | bytes 2359296 | tf_op jit(solution)/shard_map/all_gather | solution.py:156
  16.1 409.7 %reduce-scatter.5.cloned.1.call-start = ((), (), s32[]{:S(2)}) async-start(), calls=%async_computation.9 | async-start | bytes 6553600 | tf_op jit(solution)/shard_map/reduce_scatter | solution.py:80
  23.7 154.0 %copy-start.14 = (f32[1280,32]{0,1:T(8,128)}, f32[1280,32]{0,1:T(8,128)S(1)}, u32[]{:S(2)}) copy-start(f32[1280,32]{0,1:T(8,128)S(1)} %get-tuple-element.281) | copy-start | bytes 491524
  141.1 6.4 copy-start.4
  149.2 56.0 %copy-start.21 = (f32[3,16,1280]{2,1,0:T(8,128)}, f32[3,16,1280]{2,1,0:T(8,128)S(1)}, u32[]{:S(2)}) copy-start(f32[3,16,1280]{2,1,0:T(8,128)S(1)} %fusion.72) | copy-start | bytes 737284
  306.1 6.6 copy-start.11
  307.7 5.0 copy-start.25
  331.6 194.4 %all-gather.30.cloned.1.call-start = ((), (), s32[]{:S(2)}) async-start(), calls=%async_computation.15 | async-start | bytes 6553600 | tf_op jit(solution)/shard_map/all_gather | solution.py:76
  332.3 248.4 %all-gather.28.cloned.1.call-start = ((), (), s32[]{:S(2)}) async-start(), calls=%async_computation.13 | async-start | bytes 9437184 | tf_op jit(solution)/shard_map/all_gather | solution.py:192
  333.1 347.9 %all-gather.22.cloned.1.call-start = ((), (), s32[]{:S(2)}) async-start(), calls=%async_computation.10 | async-start | bytes 6553600 | tf_op jit(solution)/shard_map/all_gather | solution.py:76
  333.1 642.0 %copy-start.31 = (f32[2048]{0:T(1024)}, f32[2048]{0:T(1024)S(1)}, u32[]{:S(2)}) copy-start(f32[2048]{0:T(1024)S(1)} %convert_element_type.213) | copy-start | bytes 24580
  425.8 3.0 copy-start.2
  425.8 3.0 copy-start.5
  428.8 546.4 %copy-start.36 = (f32[320]{0:T(512)}, f32[320]{0:T(512)S(1)}, u32[]{:S(2)}) copy-start(f32[320]{0:T(512)S(1)} %get-tuple-element.285) | copy-start | bytes 3844
  430.5 305.0 %all-gather.26.cloned.1.call-start = ((), (), s32[]{:S(2)}) async-start(), calls=%async_computation.12 | async-start | bytes 9437184 | tf_op jit(solution)/shard_map/all_gather | solution.py:191
  431.1 360.7 %all-gather.24.cloned.1.call-start = ((), (), s32[]{:S(2)}) async-start(), calls=%async_computation.11 | async-start | bytes 9437184 | tf_op jit(solution)/shard_map/all_gather | solution.py:190
  431.8 540.3 %reduce-scatter.9.cloned.1.call-start = ((), (), s32[]{:S(2)}) async-start(), calls=%async_computation.16 | async-start | bytes 6553600 | tf_op jit(solution)/shard_map/reduce_scatter | solution.py:80
  834.7 7.5 copy-start.19
  834.7 7.5 copy-start.46
  834.7 8.6 copy-start.50
  878.3 97.4 %copy-start.38 = (f32[320]{0:T(512)S(1)}, f32[320]{0:T(512)}, u32[]{:S(2)}) copy-start(f32[320]{0:T(512)} %get-tuple-element.284) | copy-start | bytes 3844
  878.3 199.7 %all-gather.32.cloned.1.call-start = ((), (), s32[]{:S(2)}) async-start(), calls=%async_computation.17 | async-start | bytes 6553600 | tf_op jit(solution)/shard_map/all_gather | solution.py:76
  972.2 3.5 copy-start.3
  972.2 3.5 copy-start.6
  972.2 3.5 copy-start.8
  979.3 382.5 %all-reduce.7.cloned.1.call-start = ((), (), s32[]{:S(2)}) async-start(), calls=%async_computation.20 | async-start | bytes 4194304 | tf_op jit(solution)/shard_map/psum | solution.py:297
  979.8 14.3 slice-start.2
  979.8 14.3 slice-start.4
  983.9 3.6 copy-start.23
  983.9 10.2 slice-start.3
  983.9 10.2 slice-start.5
  1078.0 5.9 copy-start.7
  1078.0 5.9 copy-start.48
  1089.7 3.8 copy-start.12
  1093.4 164.4 %copy-start.15 = (f32[1280,32]{0,1:T(8,128)S(1)}, f32[1280,32]{0,1:T(8,128)}, u32[]{:S(2)}) copy-start(f32[1280,32]{0,1:T(8,128)} %copy-done.14) | copy-start | bytes 491524
  1267.8 4.9 copy-start.22
  1272.7 3.6 copy-start.16
  1272.7 3.6 copy-start.17
  1272.7 3.6 copy-start.18
  1276.3 10.9 slice-start
  1280.1 7.1 slice-start.1
  1280.1 7.1 copy-start.26
  1291.5 156.3 %reduce-scatter.11.cloned.1.call-start = ((), (), s32[]{:S(2)}) async-start(), calls=%async_computation.18 | async-start | bytes 6553600 | tf_op jit(solution)/shard_map/reduce_scatter | solution.py:80
  1291.6 9.0 copy-start.10
  1291.6 9.0 copy-start.47
  1323.5 15.8 copy-start.24
  1323.5 220.8 %reduce-scatter.7.cloned.1.call-start = ((), (), s32[]{:S(2)}) async-start(), calls=%async_computation.14 | async-start | bytes 6553600 | tf_op jit(solution)/shard_map/reduce_scatter | solution.py:80
  1346.9 371.1 %all-reduce.5.cloned.1.call-start = ((), (), s32[]{:S(2)}) async-start(), calls=%async_computation.19 | async-start | bytes 14680064 | tf_op jit(solution)/shard_map/psum | solution.py:302
  1361.8 4.0 copy-start.29
  1361.8 5.0 copy-start.33
  1361.8 86.0 %copy-start.35 = (f32[2048]{0:T(1024)S(1)}, f32[2048]{0:T(1024)}, u32[]{:S(2)}) copy-start(f32[2048]{0:T(1024)} %copy-done.34) | copy-start | bytes 24580
  1364.7 179.6 %copy-start.32 = (f32[2048]{0:T(1024)S(1)}, f32[2048]{0:T(1024)}, u32[]{:S(2)}) copy-start(f32[2048]{0:T(1024)} %copy-done.31) | copy-start | bytes 24580
  1364.7 179.6 %copy-start.37 = (f32[320]{0:T(512)S(1)}, f32[320]{0:T(512)}, u32[]{:S(2)}) copy-start(f32[320]{0:T(512)} %copy-done.36) | copy-start | bytes 3844
  1364.7 179.6 %copy-start.39 = (f32[320]{0:T(512)S(1)}, f32[320]{0:T(512)}, u32[]{:S(2)}) copy-start(f32[320]{0:T(512)} %get-tuple-element.284) | copy-start | bytes 3844
  1364.7 179.6 %copy-start.41 = (f32[320]{0:T(512)S(1)}, f32[320]{0:T(512)}, u32[]{:S(2)}) copy-start(f32[320]{0:T(512)} %copy-done.40) | copy-start | bytes 3844
  1364.7 179.6 %copy-start.43 = (f32[320]{0:T(512)S(1)}, f32[320]{0:T(512)}, u32[]{:S(2)}) copy-start(f32[320]{0:T(512)} %copy-done.42) | copy-start | bytes 3844
  1364.7 179.6 %copy-start.44 = (f32[320]{0:T(512)S(1)}, f32[320]{0:T(512)}, u32[]{:S(2)}) copy-start(f32[320]{0:T(512)} %get-tuple-element.282) | copy-start | bytes 3844
  1717.9 5.6 copy-start.13
  (17 other events, 36.7 us)
Sparse Core Ops, SparseCore 0:
  9.9 30.9 all-gather.13
  43.0 98.0 all-gather.11
  143.0 26.2 all-gather.15
  171.1 27.8 all-gather.17
  200.7 27.9 all-gather.19
  331.7 94.0 reduce-scatter.4
  427.4 98.5 all-gather.29
  527.9 52.7 all-gather.27
  582.8 98.0 all-gather.21
  682.7 52.7 all-gather.25
  737.4 54.3 all-gather.23
  878.4 93.7 reduce-scatter.8
  979.4 98.5 all-gather.31
  1291.7 60.2 all-reduce.6
  1354.7 93.0 reduce-scatter.10
  1450.0 94.2 reduce-scatter.6
  1550.5 167.4 all-reduce.4
where the time goes:
time: 1740 us; the launch traced here: 1730 us
  waiting for transfers between devices  1060 us (61%)
  matrix products  489 us (28%)
  other arithmetic  88.5 us (5%)
  local copies, waits for them, and re-layouts  71.7 us (4%)
    reduce_scatter x4, waiting for transfers between devices, sum_terms(): lax.psum_scatter(term(0, total).astype(jnp.bfloat16), 'tensor', scatter_d...  361 us
    all_gather x4, waiting for transfers between devices, gather_rows(): return lax.all_gather(rows, 'tensor', axis=0, tiled=True)  352 us
    dot_general x67, matrix products, matmul(): return jnp.dot(left, right, preferred_element_type=jnp.float32)  262 us
    psum x1, waiting for transfers between devices, local(): lax.psum((grad_entries, grad_finals), ('dp', 'tensor'))  168 us
    dot_general x11, matrix products, times_t(): lax.dot_general(left, right, (((1,), (1,)), ((), ())), preferred_element_...  104 us
    dot_general x29, matrix products, exact(): jnp.dot(left, right, precision=highest, preferred_element_type=jnp.float32)  75.6 us
    all_gather x1, waiting for transfers between devices, local(): lax.all_gather(down_weight, 'dp', axis=0, tiled=True)  50.7 us
    all_gather x1, waiting for transfers between devices, local(): lax.all_gather(up_weight, 'dp', axis=0, tiled=True)  50.4 us
  transfers between devices with their start and end apart: 17, of which 15 were waited for; matrix products, arithmetic and copies ran while one was open for 17% of the time, Pallas kernels for 0%

commit v1 on v0

v1 whole, which is shorter than its diff:
```python
import functools

import jax
import jax.numpy as jnp
import numpy as np
from jax import lax
from jax.experimental import pallas as pl
from jax.experimental.pallas import tpu as pltpu
from jax.sharding import PartitionSpec as P

HEAD_DIM = 64
TRUNK, BRANCHES = 8, 4
QT = 256
RANK_PAD = 128
VMEM_LIMIT = 60 * 1024 * 1024

eps = 1e-05
theta = 130000.0
bf16, f32 = jnp.bfloat16, jnp.float32


def nn(left, right):
    return jnp.dot(left, right, preferred_element_type=f32)


def nt(left, right):
    return lax.dot_general(left, right, (((1,), (1,)), ((), ())), preferred_element_type=f32)


def tn(left, right):
    return lax.dot_general(left, right, (((0,), (0,)), ((), ())), preferred_element_type=f32)


def permute(value, pairs):
    return lax.ppermute(value, "tensor", pairs)


def line_gather(value, edge):
    one = permute(value, [(0, 1), (1, 0), (2, 3), (3, 2)])
    mid = permute(value, [(1, 2), (2, 1)])
    two_edge = permute(mid, [(1, 0), (2, 3)])
    two_mid = permute(one, [(1, 2), (2, 1)])
    three_edge = permute(two_mid, [(1, 0), (2, 3)])
    two = jnp.where(edge, two_edge, two_mid)
    three = jnp.where(edge, three_edge, mid)
    return [value, one, two, three]


def add_rows(left, right):
    return (left.astype(f32) + right.astype(f32)).astype(bf16)


def line_scatter(parts, place):
    right = [(0, 1), (1, 2), (2, 3)]
    left = [(3, 2), (2, 1), (1, 0)]
    first = permute(parts[3], [(0, 1), (3, 2)])
    held = add_rows(parts[2], first)
    second_right = permute(held, right[:2])
    second_left = permute(held, left[:2])
    base_right = jnp.where(place == 1, parts[3], parts[1])
    base_left = jnp.where(place == 2, parts[3], parts[1])
    third_right = permute(add_rows(base_right, second_right), right)
    third_left = permute(add_rows(base_left, second_left), left)
    return parts[0].astype(f32) + third_right.astype(f32) + third_left.astype(f32)


def rope_tables(blocks, seg):
    depth = np.minimum(np.arange(blocks), TRUNK)
    depth[TRUNK + BRANCHES :] = TRUNK + 1
    position = (np.repeat(depth, seg) * seg + np.arange(blocks * seg) % seg).astype(np.float32)
    half = HEAD_DIM // 2
    freq = (np.float32(theta) ** (-np.arange(half, dtype=np.float32) / half)).astype(np.float32)
    angle = (position[:, None] * freq[None, :]).astype(np.float32)
    cosine = np.tile(np.cos(angle), (1, 4)).astype(np.float32)
    sine = np.sin(angle).astype(np.float32)
    sine = np.concatenate([-sine, sine, -sine, sine], axis=1)
    return jnp.asarray(cosine), jnp.asarray(sine)


def turn(values, cosine, sine):
    width = values.shape[1]
    reps = width // cosine.shape[1]
    if reps > 1:
        cosine = jnp.concatenate([cosine] * reps, axis=1)
        sine = jnp.concatenate([sine] * reps, axis=1)
    lane = lax.broadcasted_iota(jnp.int32, values.shape, 1)
    half = HEAD_DIM // 2
    other = jnp.where(
        lane % HEAD_DIM < half, pltpu.roll(values, width - half, 1), pltpu.roll(values, half, 1)
    )
    return values * cosine + other * sine


def project_body(rope, groups, *refs):
    if rope:
        slot_ref, x_ref, w_ref, e_ref, a_ref, cos_ref, sin_ref = refs[:7]
    else:
        slot_ref, x_ref, w_ref, e_ref, a_ref = refs[:5]
    y_ref, l_ref = refs[-2:]
    group = pl.program_id(0)

    @pl.when(group == 0)
    def _():
        l_ref[...] = nt(x_ref[...], e_ref[...]).astype(bf16)

    total = nn(x_ref[...], w_ref[...]) + nn(l_ref[...], a_ref[...])
    if rope:

        @pl.when(group < groups - 1)
        def _():
            y_ref[0] = turn(total, cos_ref[...], sin_ref[...]).astype(bf16)

        @pl.when(group == groups - 1)
        def _():
            y_ref[0] = total.astype(bf16)
    else:
        y_ref[0] = total.astype(bf16)


def project(slot, x, weight, entry, exits, groups, rows_total, tables, before):
    rows, features = x.shape
    width = weight.shape[1] // groups
    in_specs = [
        pl.BlockSpec((rows, features), lambda g, s: (0, 0)),
        pl.BlockSpec((features, width), lambda g, s: (0, g)),
        pl.BlockSpec((RANK_PAD, features), lambda g, s: (0, 0)),
        pl.BlockSpec((RANK_PAD, width), lambda g, s: (0, g)),
    ]
    operands = [x, weight, entry, exits]
    if tables is not None:
        in_specs += [pl.BlockSpec((rows, tables[0].shape[1]), lambda g, s: (s[0], 0))] * 2
        operands += list(tables)
    aliases = {}
    if before is not None:
        aliases = {len(operands) + 1: 0, len(operands) + 2: 1}
        in_specs += [pl.BlockSpec(memory_space=pl.ANY)] * 2
        operands += list(before)
    return pl.pallas_call(
        functools.partial(project_body, tables is not None, groups),
        grid_spec=pltpu.PrefetchScalarGridSpec(
            num_scalar_prefetch=1,
            grid=(groups,),
            in_specs=in_specs,
            out_specs=[
                pl.BlockSpec((1, rows, width), lambda g, s: (g, s[0], 0)),
                pl.BlockSpec((rows, RANK_PAD), lambda g, s: (s[0], 0)),
            ],
        ),
        out_shape=[
            jax.ShapeDtypeStruct((groups, rows_total, width), bf16),
            jax.ShapeDtypeStruct((rows_total, RANK_PAD), bf16),
        ],
        input_output_aliases=aliases,
        compiler_params=pltpu.CompilerParams(vmem_limit_bytes=VMEM_LIMIT),
        cost_estimate=pl.CostEstimate(
            flops=2 * rows * features * weight.shape[1],
            bytes_accessed=2 * weight.size + 4 * x.size,
            transcendentals=0,
        ),
    )(slot, *operands)


def collect_body(groups, slot_ref, d_ref, w_ref, a_ref, e_ref, y_ref, b_ref):
    tile = pl.program_id(0)
    width = d_ref.shape[2]

    @pl.when(tile == 0)
    def _():
        low = nt(d_ref[0], a_ref[:, :width])
        for g in range(1, groups):
            low += nt(d_ref[g], a_ref[:, g * width : (g + 1) * width])
        b_ref[...] = low.astype(bf16)

    total = nn(b_ref[...], e_ref[...])
    for g in range(groups):
        total += nt(d_ref[g], w_ref[:, g * width : (g + 1) * width])
    y_ref[...] = total.astype(bf16)


def collect(slot, d, weight, exits, entry, rows, tile=1024):
    groups, _, width = d.shape
    features = weight.shape[0]
    return pl.pallas_call(
        functools.partial(collect_body, groups),
        grid_spec=pltpu.PrefetchScalarGridSpec(
            num_scalar_prefetch=1,
            grid=(features // tile,),
            in_specs=[
                pl.BlockSpec((groups, rows, width), lambda i, s: (0, s[0], 0)),
                pl.BlockSpec((tile, groups * width), lambda i, s: (i, 0)),
                pl.BlockSpec((RANK_PAD, groups * width), lambda i, s: (0, 0)),
                pl.BlockSpec((RANK_PAD, tile), lambda i, s: (0, i)),
            ],
            out_specs=[
                pl.BlockSpec((rows, tile), lambda i, s: (0, i)),
                pl.BlockSpec((rows, RANK_PAD), lambda i, s: (0, 0)),
            ],
        ),
        out_shape=[
            jax.ShapeDtypeStruct((rows, features), bf16),
            jax.ShapeDtypeStruct((rows, RANK_PAD), bf16),
        ],
        compiler_params=pltpu.CompilerParams(vmem_limit_bytes=VMEM_LIMIT),
        cost_estimate=pl.CostEstimate(
            flops=2 * rows * weight.size, bytes_accessed=2 * weight.size + 4 * rows * features, transcendentals=0
        ),
    )(slot, d, weight, exits, entry)


def tree_tiles(seg, rows, parent_row):
    trunk = TRUNK * seg
    leaves = trunk + BRANCHES * seg
    key = lax.broadcasted_iota(jnp.int32, (QT, QT), 0)
    query = lax.broadcasted_iota(jnp.int32, (QT, QT), 1)
    causal = key <= query
    own = causal & (key // seg == query // seg)
    tiles = []
    for start in range(0, trunk, QT):
        pieces = [(0, start, None)] if start else []
        tiles.append((start, pieces + [(start, QT, causal)]))
    tiles.append((trunk, [(0, trunk, None), (trunk, QT, own)]))
    branch = lax.broadcasted_iota(jnp.int32, (BRANCHES * seg, QT), 0) // seg
    for start in range(leaves, rows, QT):
        mine = branch == parent_row[:, start - leaves : start - leaves + QT]
        tiles.append(
            (start, [(0, trunk, None), (trunk, BRANCHES * seg, mine), (start, QT, own)])
        )
    return tiles


def attend_body(seg, q_ref, k_ref, v_ref, p_ref, o_ref, lse_ref):
    rows = q_ref.shape[1]
    value_t = v_ref[0].T
    lane = lax.broadcasted_iota(jnp.int32, (QT, 2 * HEAD_DIM), 1)
    for start, pieces in tree_tiles(seg, rows, p_ref[...]):
        query = q_ref[0, start : start + QT] * bf16(HEAD_DIM**-0.5)
        outs = []
        for h in range(2):
            own_query = jnp.where(lane // HEAD_DIM == h, query, bf16(0))
            scores = []
            for k0, count, mask in pieces:
                s = nt(k_ref[0, k0 : k0 + count], own_query)
                scores.append(s if mask is None else jnp.where(mask, s, -1e30))
            top = functools.reduce(
                jnp.maximum, [jnp.max(s, axis=0, keepdims=True) for s in scores]
            )
            summed, out = 0.0, 0.0
            for (k0, count, _), s in zip(pieces, scores):
                weights = jnp.exp(s - top)
                summed += jnp.sum(weights, axis=0, keepdims=True)
                out += nn(
                    value_t[h * HEAD_DIM : (h + 1) * HEAD_DIM, k0 : k0 + count],
                    weights.astype(bf16),
                )
            outs.append(out / summed)
            lse_ref[0, h : h + 1, start : start + QT] = top + jnp.log(summed)
        o_ref[0, start : start + QT] = jnp.concatenate(outs, axis=0).T.astype(bf16)


def attend(qkv, leaf_parent, seg):
    _, rows, width = qkv.shape
    pairs = width // (2 * HEAD_DIM)
    return pl.pallas_call(
        functools.partial(attend_body, seg),
        grid=(pairs,),
        in_specs=[
            pl.BlockSpec((1, rows, 2 * HEAD_DIM), lambda j, g=g: (g, 0, j)) for g in range(3)
        ]
        + [pl.BlockSpec(leaf_parent.shape, lambda j: (0, 0))],
        out_specs=[
            pl.BlockSpec((1, rows, 2 * HEAD_DIM), lambda j: (0, 0, j)),
            pl.BlockSpec((1, 2, rows), lambda j: (j, 0, 0)),
        ],
        out_shape=[
            jax.ShapeDtypeStruct((1, rows, width), bf16),
            jax.ShapeDtypeStruct((pairs, 2, rows), f32),
        ],
        compiler_params=pltpu.CompilerParams(vmem_limit_bytes=VMEM_LIMIT),
        cost_estimate=pl.CostEstimate(
            flops=8 * rows * rows * width, bytes_accessed=8 * rows * width, transcendentals=0
        ),
    )(qkv, qkv, qkv, leaf_parent)


def attend_back_body(
    seg, q_ref, k_ref, v_ref, o_ref, g_ref, lse_ref, p_ref, cos_ref, sin_ref, d_ref, dq_t, dk, dv
):
    rows = q_ref.shape[1]
    scale = bf16(HEAD_DIM**-0.5)
    key_t = k_ref[0].T
    weighed_t = (g_ref[0].astype(f32) * o_ref[0].astype(f32)).T
    lane = lax.broadcasted_iota(jnp.int32, (QT, 2 * HEAD_DIM), 1)
    dk[...] = jnp.zeros_like(dk)
    dv[...] = jnp.zeros_like(dv)
    for start, pieces in tree_tiles(seg, rows, p_ref[...]):
        query = q_ref[0, start : start + QT] * scale
        grad = g_ref[0, start : start + QT]
        for h in range(2):
            mine = lane // HEAD_DIM == h
            own_query = jnp.where(mine, query, bf16(0))
            own_grad = jnp.where(mine, grad, bf16(0))
            band = slice(h * HEAD_DIM, (h + 1) * HEAD_DIM)
            delta = jnp.sum(weighed_t[band, start : start + QT], axis=0, keepdims=True)
            lse = lse_ref[0, h : h + 1, start : start + QT]
            grad_q = 0.0
            for k0, count, mask in pieces:
                probs = jnp.exp(nt(k_ref[0, k0 : k0 + count], own_query) - lse)
                if mask is not None:
                    probs = jnp.where(mask, probs, 0.0)
                grad_probs = nt(v_ref[0, k0 : k0 + count], own_grad)
                grad_scores = (probs * (grad_probs - delta)).astype(bf16)
                dk[k0 : k0 + count] += nn(grad_scores, own_query)
                dv[k0 : k0 + count] += nn(probs.astype(bf16), own_grad)
                grad_q += nn(key_t[band, k0 : k0 + count], grad_scores)
            dq_t[band, start : start + QT] = grad_q
    cosine, sine = cos_ref[...], -sin_ref[...]
    d_ref[0] = turn(dq_t[...].T * HEAD_DIM**-0.5, cosine, sine).astype(bf16)
    d_ref[1] = turn(dk[...], cosine, sine).astype(bf16)
    d_ref[2] = dv[...].astype(bf16)


def attend_back(qkv, attended, grad, lse, leaf_parent, tables, seg):
    _, rows, width = qkv.shape
    pairs = width // (2 * HEAD_DIM)
    pair = 2 * HEAD_DIM
    return pl.pallas_call(
        functools.partial(attend_back_body, seg),
        grid=(pairs,),
        in_specs=[pl.BlockSpec((1, rows, pair), lambda j, g=g: (g, 0, j)) for g in range(3)]
        + [
            pl.BlockSpec((1, rows, pair), lambda j: (0, 0, j)),
            pl.BlockSpec((1, rows, pair), lambda j: (0, 0, j)),
            pl.BlockSpec((1, 2, rows), lambda j: (j, 0, 0)),
            pl.BlockSpec(leaf_parent.shape, lambda j: (0, 0)),
            pl.BlockSpec((rows, pair), lambda j: (0, 0)),
            pl.BlockSpec((rows, pair), lambda j: (0, 0)),
        ],
        out_specs=pl.BlockSpec((3, rows, pair), lambda j: (0, 0, j)),
        out_shape=jax.ShapeDtypeStruct((3, rows, width), bf16),
        scratch_shapes=[
            pltpu.VMEM((pair, rows), f32),
            pltpu.VMEM((rows, pair), f32),
            pltpu.VMEM((rows, pair), f32),
        ],
        compiler_params=pltpu.CompilerParams(vmem_limit_bytes=VMEM_LIMIT),
        cost_estimate=pl.CostEstimate(
            flops=20 * rows * rows * width, bytes_accessed=16 * rows * width, transcendentals=0
        ),
    )(qkv, qkv, qkv, attended, grad, lse, leaf_parent, *tables)


def feed_body(
    rank, n_ref, c_ref, wg_ref, wu_ref, wd_ref, xg_ref, xu_ref, xd_ref, e_ref, f_ref,
    res_ref, back_ref, unit_ref, model_ref, low, low_t, acc_res, acc_back, acc_low,
):
    tile = pl.program_id(0)

    @pl.when(tile == 0)
    def _():
        first = nt(n_ref[...], e_ref[...]) + nt(c_ref[...], f_ref[...])
        low[...] = first.astype(bf16)
        low_t[...] = first.T.astype(bf16)
        acc_res[...] = jnp.zeros_like(acc_res)
        acc_back[...] = jnp.zeros_like(acc_back)
        acc_low[...] = jnp.zeros_like(acc_low)

    gate = nn(n_ref[...], wg_ref[...]) + nn(low[...], xg_ref[...])
    rise = nn(n_ref[...], wu_ref[...]) + nn(low[...], xu_ref[...])
    grad_hidden = nn(c_ref[...], wd_ref[...]) + nn(low[...], xd_ref[...])
    sigmoid = jax.nn.sigmoid(gate)
    silu = gate * sigmoid
    hidden = (silu * rise).astype(bf16)
    grad_gate = (grad_hidden * rise * sigmoid * (1.0 + gate * (1.0 - sigmoid))).astype(bf16)
    grad_rise = (grad_hidden * silu).astype(bf16)
    acc_back[...] += nt(grad_gate, wg_ref[...]) + nt(grad_rise, wu_ref[...])
    acc_res[...] += nt(hidden, wd_ref[...])
    acc_low[...] += (
        nt(grad_gate, xg_ref[...]) + nt(grad_rise, xu_ref[...]) + nt(hidden, xd_ref[...])
    )
    unit_ref[:rank] = nn(low_t[:rank], grad_gate)
    unit_ref[rank : 2 * rank] = nn(low_t[rank : 2 * rank], grad_rise)
    unit_ref[2 * rank :] = nn(low_t[2 * rank : 3 * rank], hidden)

    @pl.when(tile == pl.num_programs(0) - 1)
    def _():
        joined = acc_low[...].astype(bf16)
        joined_t = acc_low[...].T.astype(bf16)
        back_ref[...] = (acc_back[...] + nn(joined, e_ref[...])).astype(bf16)
        res_ref[...] = (acc_res[...] + nn(joined, f_ref[...])).astype(bf16)
        model_ref[: 2 * rank] = nn(joined_t[: 2 * rank], n_ref[...])
        model_ref[2 * rank :] = nn(joined_t[2 * rank : 3 * rank], c_ref[...])


def feed(normed, cot, w_gate, w_rise, w_fall, x_gate, x_rise, x_fall, entry, final, rank, tile=512):
    rows, features = normed.shape
    units = w_gate.shape[1]
    whole = pl.BlockSpec((rows, features), lambda i: (0, 0))
    weight = pl.BlockSpec((features, tile), lambda i: (0, i))
    exits = pl.BlockSpec((RANK_PAD, tile), lambda i: (0, i))
    entries = pl.BlockSpec((RANK_PAD, features), lambda i: (0, 0))
    return pl.pallas_call(
        functools.partial(feed_body, rank),
        grid=(units // tile,),
        in_specs=[whole, whole, weight, weight, weight, exits, exits, exits, entries, entries],
        out_specs=[
            whole,
            whole,
            pl.BlockSpec((3 * rank, tile), lambda i: (0, i)),
            pl.BlockSpec((3 * rank, features), lambda i: (0, 0)),
        ],
        out_shape=[
            jax.ShapeDtypeStruct((rows, features), bf16),
            jax.ShapeDtypeStruct((rows, features), bf16),
            jax.ShapeDtypeStruct((3 * rank, units), f32),
            jax.ShapeDtypeStruct((3 * rank, features), f32),
        ],
        scratch_shapes=[
            pltpu.VMEM((rows, RANK_PAD), bf16),
            pltpu.VMEM((RANK_PAD, rows), bf16),
            pltpu.VMEM((rows, features), f32),
            pltpu.VMEM((rows, features), f32),
            pltpu.VMEM((rows, RANK_PAD), f32),
        ],
        compiler_params=pltpu.CompilerParams(vmem_limit_bytes=VMEM_LIMIT),
        cost_estimate=pl.CostEstimate(
            flops=12 * rows * w_gate.size, bytes_accessed=6 * w_gate.size, transcendentals=0
        ),
    )(normed, cot, w_gate, w_rise, w_fall, x_gate, x_rise, x_fall, entry, final)


def norm_forward(rows, gain):
    rms = lax.rsqrt(jnp.mean(rows * rows, axis=1, keepdims=True) + eps)
    return (rows * rms * gain).astype(bf16), rms


def norm_backward(rows, rms, gain, grad):
    scaled = grad * gain
    return rms * (scaled - rows * (rms * rms) * jnp.mean(scaled * rows, axis=1, keepdims=True))


def stack_rows(blocks, rows=RANK_PAD):
    joined = jnp.concatenate(blocks, axis=0)
    return jnp.pad(joined, ((0, rows - joined.shape[0]), (0, 0)))


def place_rows(block, start):
    return jnp.pad(block, ((start, RANK_PAD - start - block.shape[0]), (0, 0)))


def per_tree(block):
    return lax.all_gather(block.astype(bf16), "dp", axis=0, tiled=False)


def by_adapter(gathered, picks, adapters):
    out = []
    for a in range(adapters):
        total = 0.0
        for tree in range(gathered.shape[0]):
            total += jnp.where(picks[tree] == a, gathered[tree].astype(f32), 0.0)
        out.append(total)
    return jnp.stack(out)


def local(
    tokens,
    cotangent,
    attention_gain,
    feed_gain,
    query_weight,
    key_weight,
    value_weight,
    output_weight,
    gate_weight,
    up_weight,
    down_weight,
    entry_maps,
    head_exits,
    unit_exits,
    output_entry,
    down_entry,
    final_exits,
    parents,
    adapter_pick,
):
    pick = adapter_pick[0]
    picks = lax.all_gather(adapter_pick, "dp", axis=0, tiled=True)
    adapters, rank = entry_maps.shape[1], entry_maps.shape[3]
    place = lax.axis_index("tensor")
    edge = (place == 0) | (place == 3)
    slots = [(place ^ s).reshape(1).astype(jnp.int32) for s in range(4)]
    rows_here = tokens.astype(f32)
    local_rows = rows_here.shape[0]
    total = local_rows * lax.axis_size("tensor")
    blocks = parents.shape[1]
    seg = total // blocks
    tables = rope_tables(blocks, seg)
    leaf_parent = (jnp.repeat(parents[0, TRUNK + BRANCHES :], seg) - TRUNK)[None, :]
    gain_one = attention_gain.astype(f32)
    gain_two = feed_gain.astype(f32)

    w_qkv = lax.all_gather(
        jnp.concatenate([query_weight, key_weight, value_weight], axis=1), "dp", axis=0, tiled=True
    )
    w_output = lax.all_gather(output_weight, "dp", axis=0, tiled=True)
    w_gate = lax.all_gather(gate_weight, "dp", axis=0, tiled=True)
    w_rise = lax.all_gather(up_weight, "dp", axis=0, tiled=True)
    w_fall = lax.all_gather(down_weight, "dp", axis=0, tiled=True)

    entries = jnp.swapaxes(entry_maps, 2, 3)[:, pick]
    heads_exit = head_exits[:, pick]
    units_exit = unit_exits[:, pick]
    out_entry = jnp.swapaxes(output_entry, 1, 2)[pick]
    fall_entry = jnp.swapaxes(down_entry, 1, 2)[pick]
    finals = final_exits[:, pick]
    width = heads_exit.shape[2]
    entry_one = stack_rows([entries[0], entries[1], entries[2]])
    exit_one = stack_rows(
        [
            jnp.pad(heads_exit[k], ((0, 0), (k * width, (2 - k) * width)))
            for k in range(3)
        ]
    )
    final_one = place_rows(finals[0], 0)
    exit_out = place_rows(out_entry, 0)
    entry_two = stack_rows([entries[3], entries[4]])
    final_two = place_rows(finals[1], 2 * rank)
    x_gate = place_rows(units_exit[0], 0)
    x_rise = place_rows(units_exit[1], rank)
    x_fall = place_rows(fall_entry, 2 * rank)

    normed_one, rms_one = norm_forward(rows_here, gain_one)
    full_one = line_gather(normed_one, edge)
    state = None
    for s in range(4):
        state = project(slots[s], full_one[s], w_qkv, entry_one, exit_one, 3, total, tables, state)
    qkv, low_one = state
    cot_start, _ = lax.optimization_barrier((cotangent, full_one[3]))
    full_cot = line_gather(cot_start, edge)
    attended, lse = attend(qkv, leaf_parent, seg)
    partial_one = [
        collect(slots[s], attended, w_output, exit_out, final_one, local_rows) for s in (3, 2, 1, 0)
    ][::-1]
    middle = rows_here + line_scatter([p[0] for p in partial_one], place)

    normed_two, rms_two = norm_forward(middle, gain_two)
    full_two = line_gather(normed_two, edge)
    fed = [
        feed(
            full_two[s], full_cot[s], w_gate, w_rise, w_fall, x_gate, x_rise, x_fall,
            entry_two, final_two, rank,
        )
        for s in range(4)
    ]
    grad_middle = cotangent.astype(f32) + norm_backward(
        middle, rms_two, gain_two, line_scatter([f[1] for f in fed], place)
    )
    result = (middle + line_scatter([f[0] for f in fed], place)).astype(bf16)
    unit_grads = functools.reduce(jnp.add, [f[2] for f in fed])
    model_grads = functools.reduce(jnp.add, [f[3] for f in fed])

    full_branch = line_gather(grad_middle.astype(bf16), edge)
    state = None
    for s in range(4):
        state = project(slots[s], full_branch[s], w_output, final_one, exit_out, 1, total, None, state)
    grad_attended, back_o = state
    head_grads = attend_back(qkv, attended, grad_attended, lse, leaf_parent, tables, seg)
    partial_four = [
        collect(slots[s], head_grads, w_qkv, exit_one, entry_one, local_rows) for s in (3, 2, 1, 0)
    ][::-1]
    grad_tokens = (
        grad_middle
        + norm_backward(rows_here, rms_one, gain_one, line_scatter([p[0] for p in partial_four], place))
    ).astype(bf16)

    out_grads = tn(back_o, attended[0])[:rank]
    final_one_grads = functools.reduce(
        jnp.add, [tn(partial_one[s][1], full_branch[s])[:rank] for s in range(4)]
    )
    entry_one_grads = functools.reduce(
        jnp.add, [tn(partial_four[s][1], full_one[s])[: 3 * rank] for s in range(4)]
    )
    head_parts = [
        tn(low_one[:, k * rank : (k + 1) * rank], head_grads[k]) for k in range(3)
    ]
    early = per_tree(
        lax.psum(jnp.concatenate([model_grads, final_one_grads]).astype(bf16), "tensor")
    )
    late = per_tree(lax.psum(entry_one_grads.astype(bf16), "tensor"))
    unit_all = per_tree(unit_grads)
    head_all = per_tree(jnp.concatenate(head_parts + [out_grads]))

    early = by_adapter(early, picks, adapters)
    late = by_adapter(late, picks, adapters)
    unit_all = by_adapter(unit_all, picks, adapters)
    head_all = by_adapter(head_all, picks, adapters)

    def cut(block, index):
        return block[:, index * rank : (index + 1) * rank]

    grad_entries = jnp.stack(
        [cut(late, 0), cut(late, 1), cut(late, 2), cut(early, 0), cut(early, 1)]
    ).swapaxes(2, 3)
    grad_finals = jnp.stack([cut(early, 3), cut(early, 2)])
    grad_heads = jnp.stack([cut(head_all, k) for k in range(3)])
    grad_output = cut(head_all, 3).swapaxes(1, 2)
    grad_units = jnp.stack([cut(unit_all, 0), cut(unit_all, 1)])
    grad_down = cut(unit_all, 2).swapaxes(1, 2)
    return (
        result,
        grad_tokens,
        grad_entries,
        grad_heads,
        grad_units,
        grad_output,
        grad_down,
        grad_finals,
    )


def solution(mesh):
    in_specs = (
        P(("dp", "tensor"), None),
        P(("dp", "tensor"), None),
        P(),
        P(),
        P("dp", "tensor"),
        P("dp", "tensor"),
        P("dp", "tensor"),
        P("dp", "tensor"),
        P("dp", "tensor"),
        P("dp", "tensor"),
        P("dp", "tensor"),
        P(),
        P(None, None, None, "tensor"),
        P(None, None, None, "tensor"),
        P(None, "tensor", None),
        P(None, "tensor", None),
        P(),
        P("dp", None),
        P("dp"),
    )
    out_specs = (
        P(("dp", "tensor"), None),
        P(("dp", "tensor"), None),
        P(),
        P(None, None, None, "tensor"),
        P(None, None, None, "tensor"),
        P(None, "tensor", None),
        P(None, "tensor", None),
        P(),
    )
    return jax.shard_map(local, mesh=mesh, in_specs=in_specs, out_specs=out_specs, check_vma=False)
```

time: 1740 us -> 1020 us (0.59)
  waiting for transfers between devices: 1060 us -> 438 us
  matrix products: 489 us -> 12.4 us
  Pallas kernels: 0 us -> 257 us
  starting transfers between devices: 1.08 us -> 112 us
  local copies, waits for them, and re-layouts: 71.7 us -> 18.9 us
  between operations: 15.8 us -> 55.5 us
  blocking collectives: 0 us -> 17.8 us
    all_gather x11 -> x8, waiting for transfers between devices: 530 us -> 0.11 us  [the longest x3 0.04 us: per_tree(): return lax.all_gather(block.astype(bf16), 'dp', axis=0, tiled=False)]
    dot_general x117 -> x12, matrix products: 489 us -> 12.4 us  [tn(): lax.dot_general(left, right, (((0,), (0,)), ((), ())), preferred_element_...]
    ppermute x0 -> x40, waiting for transfers between devices: none -> 400 us  [permute(): return lax.ppermute(value, 'tensor', pairs)]
    reduce_scatter x4 -> x0, waiting for transfers between devices: 361 us -> none  [sum_terms(): lax.psum_scatter(term(0, total).astype(jnp.bfloat16), 'tensor', scatter_d...]
    pallas_call x0 -> x22, Pallas kernels: none -> 257 us  [the longest x4 115 us: feed(): pl.pallas_call(functools.partial(feed_body, rank), grid=(units // tile,),...]
    psum x2 -> x1, waiting for transfers between devices: 168 us -> 35.1 us  [local(): late = per_tree(lax.psum(entry_one_grads.astype(bf16), 'tensor'))]
    ppermute x0 -> x40, starting transfers between devices: none -> 112 us  [permute(): return lax.ppermute(value, 'tensor', pairs)]
    convert_element_type x25 -> x14, other arithmetic: 53 us -> 41.1 us  [the longest x8 31.2 us: add_rows(): return (left.astype(f32) + right.astype(f32)).astype(bf16)]
  transfers between devices with their start and end apart: 17 -> 49, of which waited for: 15 -> 22; matrix products, arithmetic and copies ran while one was open for 17% -> 10% of each run, Pallas kernels for 0% -> 18%
where the time goes in v1:
time: 1020 us; the launch traced here: 1010 us
  waiting for transfers between devices  438 us (43%)
  Pallas kernels  257 us (25%)
  starting transfers between devices  112 us (11%)
  other arithmetic  96.4 us (9%)
  between operations  55.5 us (5%)
  local copies, waits for them, and re-layouts  18.9 us (2%)
  blocking collectives  17.8 us (2%)
  matrix products  12.4 us (1%)
    ppermute x40, waiting for transfers between devices, permute(): return lax.ppermute(value, 'tensor', pairs)  400 us
    pallas_call x4, Pallas kernels, feed(): pl.pallas_call(functools.partial(feed_body, rank), grid=(units // tile,),...  115 us
    ppermute x40, starting transfers between devices, permute(): return lax.ppermute(value, 'tensor', pairs)  112 us
    pallas_call x8, Pallas kernels, project(): pl.pallas_call(functools.partial(project_body, tables is not None, groups...  50.6 us
    pallas_call x8, Pallas kernels, collect(): pl.pallas_call(functools.partial(collect_body, groups), grid_spec=pltpu.P...  42.1 us
    psum x1, waiting for transfers between devices, local(): late = per_tree(lax.psum(entry_one_grads.astype(bf16), 'tensor'))  35.1 us
    convert_element_type x8, other arithmetic, add_rows(): return (left.astype(f32) + right.astype(f32)).astype(bf16)  31.2 us
    pallas_call x1, Pallas kernels, attend_back(): pl.pallas_call(functools.partial(attend_back_body, seg), grid=(pairs,), i...  29.3 us
  transfers between devices with their start and end apart: 49, of which 22 were waited for; matrix products, arithmetic and copies ran while one was open for 10% of the time, Pallas kernels for 18%

profile of v1, /device:TPU:0, one launch (start us, length us, event | category | flops | bytes accessed | tf_op | source)
XLA Modules:
  0.0 1008.1 jit_solution(15715205531087747784)
XLA Ops:
  16.0 3.0 collective-permute-start
  20.7 27.4 %collective-permute-done.refs_1_ = bf16[320,2048]{1,0:T(8,128)(2,1)} collective-permute-done((bf16[320,2048]{1,0:T(8,128)(2,1)}, bf16[320,2048]{1,0:T(8,128)(2,1)}, u32[]{:S(2)}, u32[]{:S(2)}) %collective-permute-start) | collective-permute-done | bytes 1310752 | tf_op jit(solution)/shard_map/ppermute | solution.py:35
  59.6 26.1 %collective-permute-done.4 = bf16[320,2048]{1,0:T(8,128)(2,1)} collective-permute-done((bf16[320,2048]{1,0:T(8,128)(2,1)}, bf16[320,2048]{1,0:T(8,128)(2,1)}, u32[]{:S(2)}, u32[]{:S(2)}) %collective-permute-start.4) | collective-permute-done | bytes 1310752 | tf_op jit(solution)/shard_map/ppermute | solution.py:35
  88.3 23.7 %collective-permute-done.2 = bf16[320,2048]{1,0:T(8,128)(2,1)S(1)} collective-permute-done((bf16[320,2048]{1,0:T(8,128)(2,1)}, bf16[320,2048]{1,0:T(8,128)(2,1)S(1)}, u32[]{:S(2)}, u32[]{:S(2)}) %collective-permute-start.2) | collective-permute-done | bytes 1310752 | tf_op jit(solution)/shard_map/ppermute | solution.py:35
  113.2 8.2 shard_map.260
  121.4 7.6 shard_map.261
  128.9 7.6 shard_map.262
  136.6 7.6 shard_map.263
  144.2 19.4 %shard_map.264 = (bf16[1,1280,512]{2,1,0:T(8,128)(2,1)}, f32[4,2,1280]{2,1,0:T(2,128)}) custom-call(bf16[3,1280,512]{2,1,0:T(8,128)(2,1)} %get-tuple-element.65.q_ref.k_ref.v_ref, bf16[3,1280,512]{2,1,0:T(8,128)(2,1)} %get-tuple-element.65.q_ref.k_ref.v_ref, bf16[3,1280,512]{2,1,0:T(8,128)(2,1)} %get-tuple-element.65.q_ref.k_ref.v_ref, s32[1,512]{1,0:T(1,128)} %sub.16.p_ref), custom_call_target="tpu_custom_call" | custom-call | flops 6710886400 | bytes 5242880 | tf_op jit(solution)/shard_map/pallas_call | solution.py:263
  163.6 4.0 shard_map.266
  170.3 4.0 shard_map.268
  174.2 25.4 %collective-permute-done.5 = bf16[320,2048]{1,0:T(8,128)(2,1)S(1)} collective-permute-done((bf16[320,2048]{1,0:T(8,128)(2,1)}, bf16[320,2048]{1,0:T(8,128)(2,1)S(1)}, u32[]{:S(2)}, u32[]{:S(2)}) %collective-permute-start.5) | collective-permute-done | bytes 1310752 | tf_op jit(solution)/shard_map/ppermute | solution.py:35
  199.6 2.9 add_convert_fusion.12
  202.6 5.5 collective-permute-start.6
  211.5 16.2 %collective-permute-done.14.c_ref = bf16[320,2048]{1,0:T(8,128)(2,1)} collective-permute-done((bf16[320,2048]{1,0:T(8,128)(2,1)S(1)}, bf16[320,2048]{1,0:T(8,128)(2,1)}, u32[]{:S(2)}, u32[]{:S(2)}) %collective-permute-start.14) | collective-permute-done | bytes 1310752 | tf_op jit(solution)/shard_map/ppermute | solution.py:35
  229.4 4.0 shard_map.267
  233.4 20.4 %collective-permute-done.6 = bf16[320,2048]{1,0:T(8,128)(2,1)} collective-permute-done((bf16[320,2048]{1,0:T(8,128)(2,1)}, bf16[320,2048]{1,0:T(8,128)(2,1)}, u32[]{:S(2)}, u32[]{:S(2)}) %collective-permute-start.6) | collective-permute-done | bytes 1310752 | tf_op jit(solution)/shard_map/ppermute | solution.py:35
  253.8 4.9 add_convert_fusion.11
  258.7 4.6 collective-permute-start.7
  271.7 4.0 shard_map.265
  275.6 14.1 %collective-permute-done.7 = bf16[320,2048]{1,0:T(8,128)(2,1)S(1)} collective-permute-done((bf16[320,2048]{1,0:T(8,128)(2,1)}, bf16[320,2048]{1,0:T(8,128)(2,1)S(1)}, u32[]{:S(2)}, u32[]{:S(2)}) %collective-permute-start.7) | collective-permute-done | bytes 1310752 | tf_op jit(solution)/shard_map/ppermute | solution.py:35
  289.7 7.5 collective-permute-done.9
  297.3 3.0 multiply_reduce_fusion.1
  302.2 24.1 %collective-permute-start.10 = (bf16[320,2048]{1,0:T(8,128)(2,1)}, bf16[320,2048]{1,0:T(8,128)(2,1)}, u32[]{:S(2)}, u32[]{:S(2)}) collective-permute-start(bf16[320,2048]{1,0:T(8,128)(2,1)} %multiply_convert_fusion.n_ref), channel_id=1, source_target_pairs={{0,1},{1,0},{2,3},{3,2},{4,5},{5,4},{6,7},{7,6},{8,9},{9,8},{10,11... | collective-permute-start | bytes 3932168 | tf_op jit(solution)/shard_map/ppermute | solution.py:35
  329.7 23.8 %collective-permute-done.16 = bf16[320,2048]{1,0:T(8,128)(2,1)} collective-permute-done((bf16[320,2048]{1,0:T(8,128)(2,1)}, bf16[320,2048]{1,0:T(8,128)(2,1)}, u32[]{:S(2)}, u32[]{:S(2)}) %collective-permute-start.16) | collective-permute-done | bytes 1310752 | tf_op jit(solution)/shard_map/ppermute | solution.py:35
  356.7 21.5 %collective-permute-done.10.n_ref = bf16[320,2048]{1,0:T(8,128)(2,1)} collective-permute-done((bf16[320,2048]{1,0:T(8,128)(2,1)}, bf16[320,2048]{1,0:T(8,128)(2,1)}, u32[]{:S(2)}, u32[]{:S(2)}) %collective-permute-start.10) | collective-permute-done | bytes 1310752 | tf_op jit(solution)/shard_map/ppermute | solution.py:35
  379.0 28.8 %shard_map.269 = (bf16[320,2048]{1,0:T(8,128)(2,1)}, bf16[320,2048]{1,0:T(8,128)(2,1)}, f32[48,2048]{1,0:T(8,128)}, f32[48,2048]{1,0:T(8,128)}) custom-call(bf16[320,2048]{1,0:T(8,128)(2,1)} %multiply_convert_fusion.n_ref, bf16[320,2048]{1,0:T(8,128)(2,1)} %c_ref, bf16[2048,2048]{1,0:T(8,128)(2,1)} %all-gather.14.cloned.1.call-done.wg_ref, ...), custom_call_target="tpu_custom_call" | custom-call | flops 16106127360 | bytes 25165824 | tf_op jit(solution)/shard_map/pallas_call | solution.py:401
  410.6 28.8 %shard_map.271 = (bf16[320,2048]{1,0:T(8,128)(2,1)}, bf16[320,2048]{1,0:T(8,128)(2,1)}, f32[48,2048]{1,0:T(8,128)}, f32[48,2048]{1,0:T(8,128)}) custom-call(bf16[320,2048]{1,0:T(8,128)(2,1)} %collective-permute-done.10.n_ref, bf16[320,2048]{1,0:T(8,128)(2,1)} %collective-permute-done.14.c_ref, bf16[2048,2048]{1,0:T(8,128)(2,1)} %all-gather.14.cloned.1.call-done.wg_ref, ...), custom_call_target="tpu_custom_call" | custom-call | flops 16106127360 | bytes 25165824 | tf_op jit(solution)/shard_map/pallas_call | solution.py:401
  442.6 22.7 %collective-permute-done.12 = bf16[320,2048]{1,0:T(8,128)(2,1)} collective-permute-done((bf16[320,2048]{1,0:T(8,128)(2,1)S(1)}, bf16[320,2048]{1,0:T(8,128)(2,1)}, u32[]{:S(2)}, u32[]{:S(2)}) %collective-permute-start.12) | collective-permute-done | bytes 1310752 | tf_op jit(solution)/shard_map/ppermute | solution.py:35
  467.9 28.7 %shard_map.270 = (bf16[320,2048]{1,0:T(8,128)(2,1)}, bf16[320,2048]{1,0:T(8,128)(2,1)}, f32[48,2048]{1,0:T(8,128)}, f32[48,2048]{1,0:T(8,128)}) custom-call(bf16[320,2048]{1,0:T(8,128)(2,1)} %broadcast_select_fusion.5.n_ref, bf16[320,2048]{1,0:T(8,128)(2,1)} %broadcast_select_fusion.4.c_ref, bf16[2048,2048]{1,0:T(8,128)(2,1)} %all-gather.14.cloned.1.call-done.wg_ref, ...), custom_call_target="tpu_custom_call" | custom-call | flops 16106127360 | bytes 25165824 | tf_op jit(solution)/shard_map/pallas_call | solution.py:401
  500.7 28.8 %shard_map.272 = (bf16[320,2048]{1,0:T(8,128)(2,1)}, bf16[320,2048]{1,0:T(8,128)(2,1)}, f32[48,2048]{1,0:T(8,128)}, f32[48,2048]{1,0:T(8,128)}) custom-call(bf16[320,2048]{1,0:T(8,128)(2,1)} %broadcast_select_fusion.3.n_ref, bf16[320,2048]{1,0:T(8,128)(2,1)} %broadcast_select_fusion.2.c_ref, bf16[2048,2048]{1,0:T(8,128)(2,1)} %all-gather.14.cloned.1.call-done.wg_ref, ...), custom_call_target="tpu_custom_call" | custom-call | flops 16106127360 | bytes 25165824 | tf_op jit(solution)/shard_map/pallas_call | solution.py:401
  536.5 19.0 %collective-permute-done.25 = bf16[320,2048]{1,0:T(8,128)(2,1)} collective-permute-done((bf16[320,2048]{1,0:T(8,128)(2,1)}, bf16[320,2048]{1,0:T(8,128)(2,1)}, u32[]{:S(2)}, u32[]{:S(2)}) %collective-permute-start.25) | collective-permute-done | bytes 1310752 | tf_op jit(solution)/shard_map/ppermute | solution.py:35
  555.6 3.3 add_convert_fusion.5
  558.9 5.5 collective-permute-start.26
  567.4 8.2 all-reduce.12
  618.1 5.4 add_convert_fusion.8
  627.2 4.5 add_convert_fusion.4
  631.7 5.6 collective-permute-start.27
  641.7 38.3 %collective-permute-done.27 = bf16[320,2048]{1,0:T(8,128)(2,1)} collective-permute-done((bf16[320,2048]{1,0:T(8,128)(2,1)}, bf16[320,2048]{1,0:T(8,128)(2,1)}, u32[]{:S(2)}, u32[]{:S(2)}) %collective-permute-start.27) | collective-permute-done | bytes 1310752 | tf_op jit(solution)/shard_map/ppermute | solution.py:35
  680.0 5.2 collective-permute-done.29
  687.9 5.4 fusion.339
  697.3 24.2 %collective-permute-done.30.refs_1_ = bf16[320,2048]{1,0:T(8,128)(2,1)S(1)} collective-permute-done((bf16[320,2048]{1,0:T(8,128)(2,1)S(1)}, bf16[320,2048]{1,0:T(8,128)(2,1)S(1)}, u32[]{:S(2)}, u32[]{:S(2)}) %collective-permute-start.30) | collective-permute-done | bytes 1310752 | tf_op jit(solution)/shard_map/ppermute | solution.py:35
  730.1 4.8 shard_map.273
  735.0 4.9 shard_map.274
  740.2 13.2 %collective-permute-done.34 = bf16[320,2048]{1,0:T(8,128)(2,1)} collective-permute-done((bf16[320,2048]{1,0:T(8,128)(2,1)}, bf16[320,2048]{1,0:T(8,128)(2,1)}, u32[]{:S(2)}, u32[]{:S(2)}) %collective-permute-start.34) | collective-permute-done | bytes 1310752 | tf_op jit(solution)/shard_map/ppermute | solution.py:35
  755.9 5.0 shard_map.275
  761.2 20.3 %collective-permute-done.32 = bf16[320,2048]{1,0:T(8,128)(2,1)S(1)} collective-permute-done((bf16[320,2048]{1,0:T(8,128)(2,1)}, bf16[320,2048]{1,0:T(8,128)(2,1)S(1)}, u32[]{:S(2)}, u32[]{:S(2)}) %collective-permute-start.32) | collective-permute-done | bytes 1310752 | tf_op jit(solution)/shard_map/ppermute | solution.py:35
  782.7 4.8 shard_map.276
  787.6 29.3 %shard_map.277.d_ref = bf16[3,1280,512]{2,1,0:T(8,128)(2,1)} custom-call(bf16[3,1280,512]{2,1,0:T(8,128)(2,1)} %get-tuple-element.65.q_ref.k_ref.v_ref, bf16[3,1280,512]{2,1,0:T(8,128)(2,1)} %get-tuple-element.65.q_ref.k_ref.v_ref, bf16[3,1280,512]{2,1,0:T(8,128)(2,1)} %get-tuple-element.65.q_ref.k_ref.v_ref, ...), custom_call_target="tpu_custom_call" | custom-call | flops 16777216000 | bytes 10485760 | tf_op jit(solution)/shard_map/pallas_call | solution.py:326
  820.4 6.6 shard_map.278
  829.1 6.5 shard_map.279
  835.6 3.9 collective-permute-start.35
  840.6 6.6 shard_map.280
  847.2 6.4 shard_map.281
  858.7 35.1 %all-reduce.16.cloned.1.call-done = (bf16[1,48,2048]{2,1,0:T(8,128)(2,1)}, bf16[1,64,2048]{2,1,0:T(8,128)(2,1)}) async-done(((bf16[1,48,2048]{2,1,0:T(8,128)(2,1)}, bf16[1,64,2048]{2,1,0:T(8,128)(2,1)}), (bf16[1,48,2048]{2,1,0:T(8,128)(2,1)}, bf16[1,64,2048]{2,1,0:T(8,128)(2,1)})) %all-reduce.16.cloned.1.call-update) | async-done | bytes 458768 | tf_op jit(solution)/shard_map/psum | solution.py:588
  893.9 9.6 all_gather.50
  903.8 3.3 add_convert_fusion.2
  907.1 4.4 collective-permute-start.36
  915.6 23.7 %collective-permute-done.36 = bf16[320,2048]{1,0:T(8,128)(2,1)} collective-permute-done((bf16[320,2048]{1,0:T(8,128)(2,1)}, bf16[320,2048]{1,0:T(8,128)(2,1)}, u32[]{:S(2)}, u32[]{:S(2)}) %collective-permute-start.36) | collective-permute-done | bytes 1310752 | tf_op jit(solution)/shard_map/ppermute | solution.py:35
  939.3 4.9 add_convert_fusion.1
  944.2 8.4 collective-permute-start.37
  958.6 20.6 %collective-permute-done.37 = bf16[320,2048]{1,0:T(8,128)(2,1)} collective-permute-done((bf16[320,2048]{1,0:T(8,128)(2,1)}, bf16[320,2048]{1,0:T(8,128)(2,1)}, u32[]{:S(2)}, u32[]{:S(2)}) %collective-permute-start.37) | collective-permute-done | bytes 1310752 | tf_op jit(solution)/shard_map/ppermute | solution.py:35
  979.2 5.2 collective-permute-done.39
  987.2 4.0 fusion.7
  (299 shorter events, 138.1 us)
Async XLA Ops:
  7.2 48.8 %copy-start = (bf16[5,8,2048,16]{2,3,1,0:T(8,128)(2,1)S(1)}, bf16[5,8,2048,16]{2,3,1,0:T(8,128)(2,1)}, u32[]{:S(2)}) copy-start(bf16[5,8,2048,16]{2,3,1,0:T(8,128)(2,1)} %param.32) | copy-start | bytes 7864324
  7.2 106.0 %all-gather.10.cloned.1.call-start = ((), (), s32[]{:S(2)}) async-start(), calls=%async_computation | async-start | bytes 7077888 | tf_op jit(solution)/shard_map/all_gather | solution.py:501
  9.4 154.2 %all-gather.12.cloned.1.call-start = ((), (), s32[]{:S(2)}) async-start(), calls=%async_computation.1 | async-start | bytes 2359296 | tf_op jit(solution)/shard_map/all_gather | solution.py:504
  10.2 368.8 %all-gather.14.cloned.1.call-start = ((), (), s32[]{:S(2)}) async-start(), calls=%async_computation.2 | async-start | bytes 9437184 | tf_op jit(solution)/shard_map/all_gather | solution.py:505
  10.9 368.1 %all-gather.16.cloned.1.call-start = ((), (), s32[]{:S(2)}) async-start(), calls=%async_computation.3 | async-start | bytes 9437184 | tf_op jit(solution)/shard_map/all_gather | solution.py:506
  11.5 367.5 %all-gather.18.cloned.1.call-start = ((), (), s32[]{:S(2)}) async-start(), calls=%async_computation.4 | async-start | bytes 9437184 | tf_op jit(solution)/shard_map/all_gather | solution.py:507
  12.1 627.0 %all-gather.24.cloned.1.call-start = ((), (), s32[]{:S(2)}) async-start(), calls=%async_computation.7 | async-start | bytes 1769472 | tf_op jit(solution)/shard_map/all_gather | solution.py:451
  12.2 40.4 %copy-start.57 = (s32[1,20]{1,0:T(1,128)S(1)}, s32[1,20]{1,0:T(1,128)}, u32[]{:S(2)}) copy-start(s32[1,20]{1,0:T(1,128)} %param.38) | copy-start | bytes 244
  16.0 32.1 %collective-permute-start = (bf16[320,2048]{1,0:T(8,128)(2,1)}, bf16[320,2048]{1,0:T(8,128)(2,1)}, u32[]{:S(2)}, u32[]{:S(2)}) collective-permute-start(bf16[320,2048]{1,0:T(8,128)(2,1)} %fusion.2.refs_1_), channel_id=1, source_target_pairs={{0,1},{1,0},{2,3},{3,2},{4,5},{5,4},{6,7},{7,6},{8,9},{9,8},{10,11... | collective-permute-start | bytes 3932168 | tf_op jit(solution)/shard_map/ppermute | solution.py:35
  19.0 32.2 %collective-permute-start.3 = (bf16[320,2048]{1,0:T(8,128)(2,1)}, bf16[320,2048]{1,0:T(8,128)(2,1)}, u32[]{:S(2)}, u32[]{:S(2)}) collective-permute-start(bf16[320,2048]{1,0:T(8,128)(2,1)} %fusion.2.refs_1_), channel_id=1, source_target_pairs={{1,2},{2,1},{5,6},{6,5},{9,10},{10,9},{13,14},{14,13},{17,18},{18,... | collective-permute-start | bytes 3932168 | tf_op jit(solution)/shard_map/ppermute | solution.py:35
  48.1 7.9 collective-permute-start.1
  51.3 34.5 %collective-permute-start.4 = (bf16[320,2048]{1,0:T(8,128)(2,1)}, bf16[320,2048]{1,0:T(8,128)(2,1)}, u32[]{:S(2)}, u32[]{:S(2)}) collective-permute-start(bf16[320,2048]{1,0:T(8,128)(2,1)} %collective-permute-done.3), channel_id=1, source_target_pairs={{1,0},{2,3},{5,4},{6,7},{9,8},{10,11},{13,12},{14,15},{17,16},{18,... | collective-permute-start | bytes 3932168 | tf_op jit(solution)/shard_map/ppermute | solution.py:35
  56.0 56.0 %collective-permute-start.2 = (bf16[320,2048]{1,0:T(8,128)(2,1)}, bf16[320,2048]{1,0:T(8,128)(2,1)S(1)}, u32[]{:S(2)}, u32[]{:S(2)}) collective-permute-start(bf16[320,2048]{1,0:T(8,128)(2,1)} %collective-permute-done.1), channel_id=1, source_target_pairs={{1,0},{2,3},{5,4},{6,7},{9,8},{10,11},{13,12},{14,15},{17,16},{18,... | collective-permute-start | bytes 3932168 | tf_op jit(solution)/shard_map/ppermute | solution.py:35
  167.7 32.0 %collective-permute-start.5 = (bf16[320,2048]{1,0:T(8,128)(2,1)}, bf16[320,2048]{1,0:T(8,128)(2,1)S(1)}, u32[]{:S(2)}, u32[]{:S(2)}) collective-permute-start(bf16[320,2048]{1,0:T(8,128)(2,1)} %get-tuple-element.68), channel_id=1, source_target_pairs={{0,1},{3,2},{4,5},{7,6},{8,9},{11,10},{12,13},{15,14},{16,17},{19,... | collective-permute-start | bytes 3932168 | tf_op jit(solution)/shard_map/ppermute | solution.py:35
  170.2 57.4 %collective-permute-start.14 = (bf16[320,2048]{1,0:T(8,128)(2,1)S(1)}, bf16[320,2048]{1,0:T(8,128)(2,1)}, u32[]{:S(2)}, u32[]{:S(2)}) collective-permute-start(bf16[320,2048]{1,0:T(8,128)(2,1)S(1)} %copy-done.23), channel_id=1, source_target_pairs={{0,1},{1,0},{2,3},{3,2},{4,5},{5,4},{6,7},{7,6},{8,9},{9,8},{10,11... | collective-permute-start | bytes 3932168 | tf_op jit(solution)/shard_map/ppermute | solution.py:35
  202.6 51.3 %copy-start.30 = (bf16[320,2048]{1,0:T(8,128)(2,1)S(1)}, bf16[320,2048]{1,0:T(8,128)(2,1)}, u32[]{:S(2)}) copy-start(bf16[320,2048]{1,0:T(8,128)(2,1)} %get-tuple-element.68) | copy-start | bytes 3932164
  202.6 51.3 %collective-permute-start.6 = (bf16[320,2048]{1,0:T(8,128)(2,1)}, bf16[320,2048]{1,0:T(8,128)(2,1)}, u32[]{:S(2)}, u32[]{:S(2)}) collective-permute-start(bf16[320,2048]{1,0:T(8,128)(2,1)} %add_convert_fusion.12), channel_id=1, source_target_pairs={{0,1},{1,2},{4,5},{5,6},{8,9},{9,10},{12,13},{13,14},{16,17},{17,1... | collective-permute-start | bytes 3932168 | tf_op jit(solution)/shard_map/ppermute | solution.py:35
  208.0 45.8 %collective-permute-start.8 = (bf16[320,2048]{1,0:T(8,128)(2,1)}, bf16[320,2048]{1,0:T(8,128)(2,1)}, u32[]{:S(2)}, u32[]{:S(2)}) collective-permute-start(bf16[320,2048]{1,0:T(8,128)(2,1)} %add_convert_fusion.12), channel_id=1, source_target_pairs={{3,2},{2,1},{7,6},{6,5},{11,10},{10,9},{15,14},{14,13},{19,18},{18... | collective-permute-start | bytes 3932168 | tf_op jit(solution)/shard_map/ppermute | solution.py:35
  209.7 59.2 %collective-permute-start.17 = (bf16[320,2048]{1,0:T(8,128)(2,1)S(1)}, bf16[320,2048]{1,0:T(8,128)(2,1)}, u32[]{:S(2)}, u32[]{:S(2)}) collective-permute-start(bf16[320,2048]{1,0:T(8,128)(2,1)S(1)} %copy-done.23), channel_id=1, source_target_pairs={{1,2},{2,1},{5,6},{6,5},{9,10},{10,9},{13,14},{14,13},{17,18},{18,... | collective-permute-start | bytes 3932168 | tf_op jit(solution)/shard_map/ppermute | solution.py:35
  227.6 42.7 %collective-permute-start.15 = (bf16[320,2048]{1,0:T(8,128)(2,1)}, bf16[320,2048]{1,0:T(8,128)(2,1)}, u32[]{:S(2)}, u32[]{:S(2)}) collective-permute-start(bf16[320,2048]{1,0:T(8,128)(2,1)} %collective-permute-done.14.c_ref), channel_id=1, source_target_pairs={{1,2},{2,1},{5,6},{6,5},{9,10},{10,9},{13,14},{14,13},{17,18},{18,... | collective-permute-start | bytes 3932168 | tf_op jit(solution)/shard_map/ppermute | solution.py:35
  258.7 31.0 %collective-permute-start.7 = (bf16[320,2048]{1,0:T(8,128)(2,1)}, bf16[320,2048]{1,0:T(8,128)(2,1)S(1)}, u32[]{:S(2)}, u32[]{:S(2)}) collective-permute-start(bf16[320,2048]{1,0:T(8,128)(2,1)} %get-tuple-element.128), channel_id=1, source_target_pairs={{0,1},{1,2},{2,3},{4,5},{5,6},{6,7},{8,9},{9,10},{10,11},{12,13},{... | collective-permute-start | bytes 3932168 | tf_op jit(solution)/shard_map/ppermute | solution.py:35
  263.3 33.9 %collective-permute-start.9 = (bf16[320,2048]{1,0:T(8,128)(2,1)}, bf16[320,2048]{1,0:T(8,128)(2,1)}, u32[]{:S(2)}, u32[]{:S(2)}) collective-permute-start(bf16[320,2048]{1,0:T(8,128)(2,1)} %get-tuple-element.129), channel_id=1, source_target_pairs={{3,2},{2,1},{1,0},{7,6},{6,5},{5,4},{11,10},{10,9},{9,8},{15,14},{... | collective-permute-start | bytes 3932168 | tf_op jit(solution)/shard_map/ppermute | solution.py:35
  264.7 36.2 %copy-start.38 = (f32[2048]{0:T(1024)}, f32[2048]{0:T(1024)S(1)}, u32[]{:S(2)}) copy-start(f32[2048]{0:T(1024)S(1)} %convert_element_type.799) | copy-start | bytes 24580
  268.9 28.4 %copy-start.9 = (bf16[320,2048]{1,0:T(8,128)(2,1)S(1)}, bf16[320,2048]{1,0:T(8,128)(2,1)}, u32[]{:S(2)}) copy-start(bf16[320,2048]{1,0:T(8,128)(2,1)} %param.21) | copy-start | bytes 3932164
  268.9 58.2 %collective-permute-start.19 = (bf16[320,2048]{1,0:T(8,128)(2,1)}, bf16[320,2048]{1,0:T(8,128)(2,1)}, u32[]{:S(2)}, u32[]{:S(2)}) collective-permute-start(bf16[320,2048]{1,0:T(8,128)(2,1)} %collective-permute-done.17), channel_id=1, source_target_pairs={{1,0},{2,3},{5,4},{6,7},{9,8},{10,11},{13,12},{14,15},{17,16},{18,... | collective-permute-start | bytes 3932168 | tf_op jit(solution)/shard_map/ppermute | solution.py:35
  270.4 83.1 %collective-permute-start.16 = (bf16[320,2048]{1,0:T(8,128)(2,1)}, bf16[320,2048]{1,0:T(8,128)(2,1)}, u32[]{:S(2)}, u32[]{:S(2)}) collective-permute-start(bf16[320,2048]{1,0:T(8,128)(2,1)} %collective-permute-done.15), channel_id=1, source_target_pairs={{1,0},{2,3},{5,4},{6,7},{9,8},{10,11},{13,12},{14,15},{17,16},{18,... | collective-permute-start | bytes 3932168 | tf_op jit(solution)/shard_map/ppermute | solution.py:35
  302.2 76.0 %collective-permute-start.10 = (bf16[320,2048]{1,0:T(8,128)(2,1)}, bf16[320,2048]{1,0:T(8,128)(2,1)}, u32[]{:S(2)}, u32[]{:S(2)}) collective-permute-start(bf16[320,2048]{1,0:T(8,128)(2,1)} %multiply_convert_fusion.n_ref), channel_id=1, source_target_pairs={{0,1},{1,0},{2,3},{3,2},{4,5},{5,4},{6,7},{7,6},{8,9},{9,8},{10,11... | collective-permute-start | bytes 3932168 | tf_op jit(solution)/shard_map/ppermute | solution.py:35
  356.0 51.9 %collective-permute-start.13 = (bf16[320,2048]{1,0:T(8,128)(2,1)}, bf16[320,2048]{1,0:T(8,128)(2,1)S(1)}, u32[]{:S(2)}, u32[]{:S(2)}) collective-permute-start(bf16[320,2048]{1,0:T(8,128)(2,1)} %multiply_convert_fusion.n_ref), channel_id=1, source_target_pairs={{1,2},{2,1},{5,6},{6,5},{9,10},{10,9},{13,14},{14,13},{17,18},{18,... | collective-permute-start | bytes 3932168 | tf_op jit(solution)/shard_map/ppermute | solution.py:35
  378.2 30.9 %collective-permute-start.11 = (bf16[320,2048]{1,0:T(8,128)(2,1)}, bf16[320,2048]{1,0:T(8,128)(2,1)S(1)}, u32[]{:S(2)}, u32[]{:S(2)}) collective-permute-start(bf16[320,2048]{1,0:T(8,128)(2,1)} %collective-permute-done.10.n_ref), channel_id=1, source_target_pairs={{1,2},{2,1},{5,6},{6,5},{9,10},{10,9},{13,14},{14,13},{17,18},{18,... | collective-permute-start | bytes 3932168 | tf_op jit(solution)/shard_map/ppermute | solution.py:35
  407.8 33.6 %collective-permute-start.18 = (bf16[320,2048]{1,0:T(8,128)(2,1)S(1)}, bf16[320,2048]{1,0:T(8,128)(2,1)S(1)}, u32[]{:S(2)}, u32[]{:S(2)}) collective-permute-start(bf16[320,2048]{1,0:T(8,128)(2,1)S(1)} %collective-permute-done.13), channel_id=1, source_target_pairs={{1,0},{2,3},{5,4},{6,7},{9,8},{10,11},{13,12},{14,15},{17,16},{18,... | collective-permute-start | bytes 3932168 | tf_op jit(solution)/shard_map/ppermute | solution.py:35
  409.1 56.2 %collective-permute-start.12 = (bf16[320,2048]{1,0:T(8,128)(2,1)S(1)}, bf16[320,2048]{1,0:T(8,128)(2,1)}, u32[]{:S(2)}, u32[]{:S(2)}) collective-permute-start(bf16[320,2048]{1,0:T(8,128)(2,1)S(1)} %collective-permute-done.11), channel_id=1, source_target_pairs={{1,0},{2,3},{5,4},{6,7},{9,8},{10,11},{13,12},{14,15},{17,16},{18,... | collective-permute-start | bytes 3932168 | tf_op jit(solution)/shard_map/ppermute | solution.py:35
  496.6 34.7 %collective-permute-start.20 = (bf16[320,2048]{1,0:T(8,128)(2,1)}, bf16[320,2048]{1,0:T(8,128)(2,1)S(1)}, u32[]{:S(2)}, u32[]{:S(2)}) collective-permute-start(bf16[320,2048]{1,0:T(8,128)(2,1)} %get-tuple-element.73), channel_id=1, source_target_pairs={{0,1},{3,2},{4,5},{7,6},{8,9},{11,10},{12,13},{15,14},{16,17},{19,... | collective-permute-start | bytes 3932168 | tf_op jit(solution)/shard_map/ppermute | solution.py:35
  498.0 31.5 %copy-start.34 = (f32[48,2048]{1,0:T(8,128)S(1)}, f32[48,2048]{1,0:T(8,128)}, u32[]{:S(2)}) copy-start(f32[48,2048]{1,0:T(8,128)} %get-tuple-element.106) | copy-start | bytes 1179652
  498.0 31.5 %copy-start.35 = (f32[48,2048]{1,0:T(8,128)S(1)}, f32[48,2048]{1,0:T(8,128)}, u32[]{:S(2)}) copy-start(f32[48,2048]{1,0:T(8,128)} %get-tuple-element.107) | copy-start | bytes 1179652
  498.0 31.5 %copy-start.36 = (f32[48,2048]{1,0:T(8,128)S(1)}, f32[48,2048]{1,0:T(8,128)}, u32[]{:S(2)}) copy-start(f32[48,2048]{1,0:T(8,128)} %get-tuple-element.109) | copy-start | bytes 1179652
  498.1 57.5 %collective-permute-start.25 = (bf16[320,2048]{1,0:T(8,128)(2,1)}, bf16[320,2048]{1,0:T(8,128)(2,1)}, u32[]{:S(2)}, u32[]{:S(2)}) collective-permute-start(bf16[320,2048]{1,0:T(8,128)(2,1)} %get-tuple-element.77), channel_id=1, source_target_pairs={{0,1},{3,2},{4,5},{7,6},{8,9},{11,10},{12,13},{15,14},{16,17},{19,... | collective-permute-start | bytes 3932168 | tf_op jit(solution)/shard_map/ppermute | solution.py:35
  531.3 362.5 %all-reduce.16.cloned.1.call-start = ((), (), s32[]{:S(2)}) async-start(), calls=%async_computation.8 | async-start | bytes 917504 | tf_op jit(solution)/shard_map/psum | solution.py:588
  533.3 32.8 %copy-start.58 = (u32[32]{0:T(128)S(1)}, u32[32]{0:T(128)}, u32[]{:S(2)}) copy-start(u32[32]{0:T(128)} %constant.139) | copy-start | bytes 388
  533.3 82.4 %copy-start.33 = (f32[48,2048]{1,0:T(8,128)S(1)}, f32[48,2048]{1,0:T(8,128)}, u32[]{:S(2)}) copy-start(f32[48,2048]{1,0:T(8,128)} %get-tuple-element.96) | copy-start | bytes 1179652
  533.3 83.7 %collective-permute-start.21 = (bf16[320,2048]{1,0:T(8,128)(2,1)S(1)}, bf16[320,2048]{1,0:T(8,128)(2,1)S(1)}, u32[]{:S(2)}, u32[]{:S(2)}) collective-permute-start(bf16[320,2048]{1,0:T(8,128)(2,1)S(1)} %add_convert_fusion.9), channel_id=1, source_target_pairs={{0,1},{1,2},{4,5},{5,6},{8,9},{9,10},{12,13},{13,14},{16,17},{17,1... | collective-permute-start | bytes 3932168 | tf_op jit(solution)/shard_map/ppermute | solution.py:35
  534.8 82.2 %collective-permute-start.23 = (bf16[320,2048]{1,0:T(8,128)(2,1)S(1)}, bf16[320,2048]{1,0:T(8,128)(2,1)}, u32[]{:S(2)}, u32[]{:S(2)}) collective-permute-start(bf16[320,2048]{1,0:T(8,128)(2,1)S(1)} %add_convert_fusion.9), channel_id=1, source_target_pairs={{3,2},{2,1},{7,6},{6,5},{11,10},{10,9},{15,14},{14,13},{19,18},{18... | collective-permute-start | bytes 3932168 | tf_op jit(solution)/shard_map/ppermute | solution.py:35
  558.9 68.3 %collective-permute-start.26 = (bf16[320,2048]{1,0:T(8,128)(2,1)}, bf16[320,2048]{1,0:T(8,128)(2,1)}, u32[]{:S(2)}, u32[]{:S(2)}) collective-permute-start(bf16[320,2048]{1,0:T(8,128)(2,1)} %add_convert_fusion.5), channel_id=1, source_target_pairs={{0,1},{1,2},{4,5},{5,6},{8,9},{9,10},{12,13},{13,14},{16,17},{17,1... | collective-permute-start | bytes 3932168 | tf_op jit(solution)/shard_map/ppermute | solution.py:35
  564.3 62.9 %collective-permute-start.28 = (bf16[320,2048]{1,0:T(8,128)(2,1)}, bf16[320,2048]{1,0:T(8,128)(2,1)}, u32[]{:S(2)}, u32[]{:S(2)}) collective-permute-start(bf16[320,2048]{1,0:T(8,128)(2,1)} %add_convert_fusion.5), channel_id=1, source_target_pairs={{3,2},{2,1},{7,6},{6,5},{11,10},{10,9},{15,14},{14,13},{19,18},{18... | collective-permute-start | bytes 3932168 | tf_op jit(solution)/shard_map/ppermute | solution.py:35
  623.5 64.3 %collective-permute-start.22 = (bf16[320,2048]{1,0:T(8,128)(2,1)}, bf16[320,2048]{1,0:T(8,128)(2,1)}, u32[]{:S(2)}, u32[]{:S(2)}) collective-permute-start(bf16[320,2048]{1,0:T(8,128)(2,1)} %get-tuple-element.126), channel_id=1, source_target_pairs={{0,1},{1,2},{2,3},{4,5},{5,6},{6,7},{8,9},{9,10},{10,11},{12,13},{... | collective-permute-start | bytes 3932168 | tf_op jit(solution)/shard_map/ppermute | solution.py:35
  625.9 62.0 %collective-permute-start.24 = (bf16[320,2048]{1,0:T(8,128)(2,1)}, bf16[320,2048]{1,0:T(8,128)(2,1)}, u32[]{:S(2)}, u32[]{:S(2)}) collective-permute-start(bf16[320,2048]{1,0:T(8,128)(2,1)} %get-tuple-element.127), channel_id=1, source_target_pairs={{3,2},{2,1},{1,0},{7,6},{6,5},{5,4},{11,10},{10,9},{9,8},{15,14},{... | collective-permute-start | bytes 3932168 | tf_op jit(solution)/shard_map/ppermute | solution.py:35
  631.7 48.2 %collective-permute-start.27 = (bf16[320,2048]{1,0:T(8,128)(2,1)}, bf16[320,2048]{1,0:T(8,128)(2,1)}, u32[]{:S(2)}, u32[]{:S(2)}) collective-permute-start(bf16[320,2048]{1,0:T(8,128)(2,1)} %get-tuple-element.124), channel_id=1, source_target_pairs={{0,1},{1,2},{2,3},{4,5},{5,6},{6,7},{8,9},{9,10},{10,11},{12,13},{... | collective-permute-start | bytes 3932168 | tf_op jit(solution)/shard_map/ppermute | solution.py:35
  637.4 47.8 %collective-permute-start.29 = (bf16[320,2048]{1,0:T(8,128)(2,1)}, bf16[320,2048]{1,0:T(8,128)(2,1)}, u32[]{:S(2)}, u32[]{:S(2)}) collective-permute-start(bf16[320,2048]{1,0:T(8,128)(2,1)} %get-tuple-element.125), channel_id=1, source_target_pairs={{3,2},{2,1},{1,0},{7,6},{6,5},{5,4},{11,10},{10,9},{9,8},{15,14},{... | collective-permute-start | bytes 3932168 | tf_op jit(solution)/shard_map/ppermute | solution.py:35
  641.0 44.2 %copy-start.6 = (f32[320,2048]{1,0:T(8,128)S(1)}, f32[320,2048]{1,0:T(8,128)}, u32[]{:S(2)}) copy-start(f32[320,2048]{1,0:T(8,128)} %copy-done.5) | copy-start | bytes 7864324
  641.0 44.2 %copy-start.19 = (bf16[320,2048]{1,0:T(8,128)(2,1)S(1)}, bf16[320,2048]{1,0:T(8,128)(2,1)}, u32[]{:S(2)}) copy-start(bf16[320,2048]{1,0:T(8,128)(2,1)} %get-tuple-element.76) | copy-start | bytes 3932164
  641.0 44.2 %copy-start.39 = (f32[2048]{0:T(1024)S(1)}, f32[2048]{0:T(1024)}, u32[]{:S(2)}) copy-start(f32[2048]{0:T(1024)} %copy-done.38) | copy-start | bytes 24580
  693.3 35.8 %copy-start.12 = (bf16[320,2048]{1,0:T(8,128)(2,1)}, bf16[320,2048]{1,0:T(8,128)(2,1)S(1)}, u32[]{:S(2)}) copy-start(bf16[320,2048]{1,0:T(8,128)(2,1)S(1)} %get-tuple-element.112.refs_1_) | copy-start | bytes 3932164
  693.3 28.2 %collective-permute-start.30 = (bf16[320,2048]{1,0:T(8,128)(2,1)S(1)}, bf16[320,2048]{1,0:T(8,128)(2,1)S(1)}, u32[]{:S(2)}, u32[]{:S(2)}) collective-permute-start(bf16[320,2048]{1,0:T(8,128)(2,1)S(1)} %get-tuple-element.112.refs_1_), channel_id=1, source_target_pairs={{0,1},{1,0},{2,3},{3,2},{4,5},{5,4},{6,7},{7,6},{8,9},{9,8},{10,11... | collective-permute-start | bytes 3932168 | tf_op jit(solution)/shard_map/ppermute | solution.py:35
  695.3 28.5 %collective-permute-start.33 = (bf16[320,2048]{1,0:T(8,128)(2,1)S(1)}, bf16[320,2048]{1,0:T(8,128)(2,1)}, u32[]{:S(2)}, u32[]{:S(2)}) collective-permute-start(bf16[320,2048]{1,0:T(8,128)(2,1)S(1)} %get-tuple-element.112.refs_1_), channel_id=1, source_target_pairs={{1,2},{2,1},{5,6},{6,5},{9,10},{10,9},{13,14},{14,13},{17,18},{18,... | collective-permute-start | bytes 3932168 | tf_op jit(solution)/shard_map/ppermute | solution.py:35
  721.5 6.4 collective-permute-start.31
  723.8 29.6 %collective-permute-start.34 = (bf16[320,2048]{1,0:T(8,128)(2,1)}, bf16[320,2048]{1,0:T(8,128)(2,1)}, u32[]{:S(2)}, u32[]{:S(2)}) collective-permute-start(bf16[320,2048]{1,0:T(8,128)(2,1)} %collective-permute-done.33), channel_id=1, source_target_pairs={{1,0},{2,3},{5,4},{6,7},{9,8},{10,11},{13,12},{14,15},{17,16},{18,... | collective-permute-start | bytes 3932168 | tf_op jit(solution)/shard_map/ppermute | solution.py:35
  727.9 53.6 %collective-permute-start.32 = (bf16[320,2048]{1,0:T(8,128)(2,1)}, bf16[320,2048]{1,0:T(8,128)(2,1)S(1)}, u32[]{:S(2)}, u32[]{:S(2)}) collective-permute-start(bf16[320,2048]{1,0:T(8,128)(2,1)} %collective-permute-done.31), channel_id=1, source_target_pairs={{1,0},{2,3},{5,4},{6,7},{9,8},{10,11},{13,12},{14,15},{17,16},{18,... | collective-permute-start | bytes 3932168 | tf_op jit(solution)/shard_map/ppermute | solution.py:35
  787.6 29.3 %copy-start.11 = (bf16[1280,128]{1,0:T(8,128)(2,1)S(1)}, bf16[1280,128]{1,0:T(8,128)(2,1)}, u32[]{:S(2)}) copy-start(bf16[1280,128]{1,0:T(8,128)(2,1)} %get-tuple-element.104) | copy-start | bytes 983044
  835.6 68.2 %collective-permute-start.35 = (bf16[320,2048]{1,0:T(8,128)(2,1)}, bf16[320,2048]{1,0:T(8,128)(2,1)}, u32[]{:S(2)}, u32[]{:S(2)}) collective-permute-start(bf16[320,2048]{1,0:T(8,128)(2,1)} %get-tuple-element.89), channel_id=1, source_target_pairs={{0,1},{3,2},{4,5},{7,6},{8,9},{11,10},{12,13},{15,14},{16,17},{19,... | collective-permute-start | bytes 3932168 | tf_op jit(solution)/shard_map/ppermute | solution.py:35
  857.0 97.1 %all-gather.20.cloned.1.call-start = ((), (), s32[]{:S(2)}) async-start(), calls=%async_computation.5 | async-start | bytes 1769472 | tf_op jit(solution)/shard_map/all_gather | solution.py:451
  893.8 97.4 %all-gather.22.cloned.1.call-start = ((), (), s32[]{:S(2)}) async-start(), calls=%async_computation.6 | async-start | bytes 2359296 | tf_op jit(solution)/shard_map/all_gather | solution.py:451
  907.1 32.2 %collective-permute-start.36 = (bf16[320,2048]{1,0:T(8,128)(2,1)}, bf16[320,2048]{1,0:T(8,128)(2,1)}, u32[]{:S(2)}, u32[]{:S(2)}) collective-permute-start(bf16[320,2048]{1,0:T(8,128)(2,1)} %add_convert_fusion.2), channel_id=1, source_target_pairs={{0,1},{1,2},{4,5},{5,6},{8,9},{9,10},{12,13},{13,14},{16,17},{17,1... | collective-permute-start | bytes 3932168 | tf_op jit(solution)/shard_map/ppermute | solution.py:35
  911.5 27.8 %collective-permute-start.38 = (bf16[320,2048]{1,0:T(8,128)(2,1)}, bf16[320,2048]{1,0:T(8,128)(2,1)}, u32[]{:S(2)}, u32[]{:S(2)}) collective-permute-start(bf16[320,2048]{1,0:T(8,128)(2,1)} %add_convert_fusion.2), channel_id=1, source_target_pairs={{3,2},{2,1},{7,6},{6,5},{11,10},{10,9},{15,14},{14,13},{19,18},{18... | collective-permute-start | bytes 3932168 | tf_op jit(solution)/shard_map/ppermute | solution.py:35
  944.2 35.1 %collective-permute-start.37 = (bf16[320,2048]{1,0:T(8,128)(2,1)}, bf16[320,2048]{1,0:T(8,128)(2,1)}, u32[]{:S(2)}, u32[]{:S(2)}) collective-permute-start(bf16[320,2048]{1,0:T(8,128)(2,1)} %get-tuple-element.121), channel_id=1, source_target_pairs={{0,1},{1,2},{2,3},{4,5},{5,6},{6,7},{8,9},{9,10},{10,11},{12,13},{... | collective-permute-start | bytes 3932168 | tf_op jit(solution)/shard_map/ppermute | solution.py:35
  952.6 31.8 %collective-permute-start.39 = (bf16[320,2048]{1,0:T(8,128)(2,1)}, bf16[320,2048]{1,0:T(8,128)(2,1)}, u32[]{:S(2)}, u32[]{:S(2)}) collective-permute-start(bf16[320,2048]{1,0:T(8,128)(2,1)} %get-tuple-element.122), channel_id=1, source_target_pairs={{3,2},{2,1},{1,0},{7,6},{6,5},{5,4},{11,10},{10,9},{9,8},{15,14},{... | collective-permute-start | bytes 3932168 | tf_op jit(solution)/shard_map/ppermute | solution.py:35
  (44 other events, 351.9 us)
Sparse Core Ops, SparseCore 0:
  10.5 48.2 all-gather.9
  60.6 27.8 all-gather.11
  90.4 54.3 all-gather.13
  146.6 54.3 all-gather.15
  202.8 54.3 all-gather.17
  531.5 24.5 all-gather.23
  857.2 36.6 all-reduce.15
  895.9 25.2 all-gather.19
  923.2 27.8 all-gather.21

commit v2 on v1

--- a/solution.py
+++ b/solution.py
@@ -13,6 +13,8 @@
 QT = 256
 RANK_PAD = 128
 VMEM_LIMIT = 60 * 1024 * 1024
+LINE = 4
+MESH = pl.DeviceIdType.MESH
 
 eps = 1e-05
 theta = 130000.0
@@ -35,12 +37,16 @@
     return lax.ppermute(value, "tensor", pairs)
 
 
-def line_gather(value, edge):
+def line_gather_start(value):
     one = permute(value, [(0, 1), (1, 0), (2, 3), (3, 2)])
     mid = permute(value, [(1, 2), (2, 1)])
+    return one, mid
+
+
+def line_gather_finish(value, one, mid, edge):
     two_edge = permute(mid, [(1, 0), (2, 3)])
     two_mid = permute(one, [(1, 2), (2, 1)])
-    three_edge = permute(two_mid, [(1, 0), (2, 3)])
+    three_edge = permute(one, [(2, 0), (1, 3)])
     two = jnp.where(edge, two_edge, two_mid)
     three = jnp.where(edge, three_edge, mid)
     return [value, one, two, three]
@@ -91,120 +97,411 @@
     return values * cosine + other * sine
 
 
-def project_body(rope, groups, *refs):
-    if rope:
-        slot_ref, x_ref, w_ref, e_ref, a_ref, cos_ref, sin_ref = refs[:7]
-    else:
-        slot_ref, x_ref, w_ref, e_ref, a_ref = refs[:5]
-    y_ref, l_ref = refs[-2:]
-    group = pl.program_id(0)
-
-    @pl.when(group == 0)
+SIDES = (1, -1)
+
+
+def far_of(place, side):
+    return place if side == 1 else LINE - 1 - place
+
+
+def greet(place):
+    barrier = pltpu.get_barrier_semaphore()
+    for side in SIDES:
+
+        @pl.when(far_of(place, side) < LINE - 1)
+        def _():
+            pl.semaphore_signal(
+                barrier, inc=1, device_id={"tensor": place + side}, device_id_type=MESH
+            )
+
+    edge = (place == 0) | (place == LINE - 1)
+
+    @pl.when(edge)
+    def _():
+        pl.semaphore_wait(barrier, 1)
+
+    @pl.when(jnp.logical_not(edge))
+    def _():
+        pl.semaphore_wait(barrier, 2)
+
+
+def chunk_rows(chunk, rows):
+    return pl.ds(chunk * rows, rows)
+
+
+class Gather:
+    def __init__(self, place, buf, send, recv, chunks):
+        self.place, self.buf, self.sems, self.chunks = place, buf, (send, recv), chunks
+        self.rows = buf.shape[1] // chunks
+
+    def copy(self, side, step, chunk, shard, target):
+        where = self.buf.at[shard, chunk_rows(chunk, self.rows)]
+        spot = (0 if side == 1 else 1, step - 1, chunk)
+        return pltpu.make_async_remote_copy(
+            src_ref=where,
+            dst_ref=where,
+            send_sem=self.sems[0].at[spot],
+            recv_sem=self.sems[1].at[spot],
+            device_id={"tensor": target},
+            device_id_type=MESH,
+        )
+
+    def each_send(self, step, chunk, act):
+        for side in SIDES:
+            far = far_of(self.place, side)
+
+            @pl.when((far < LINE - 1) & (far >= step - 1))
+            def _():
+                shard = self.place - side * (step - 1)
+                act(self.copy(side, step, chunk, shard, self.place + side))
+
+    def send(self, step, chunk):
+        self.each_send(step, chunk, lambda copy: copy.start())
+
+    def arrive(self, step, chunk):
+        for side in SIDES:
+
+            @pl.when(far_of(self.place, side) >= step)
+            def _():
+                shard = self.place - side * step
+                self.copy(side, step, chunk, shard, self.place - side).wait_recv()
+
+    def drain(self):
+        for step in range(1, LINE):
+            for chunk in range(self.chunks):
+                self.each_send(step, chunk, lambda copy: copy.wait_send())
+
+
+class Sum:
+    def __init__(self, place, part, held, send, recv, chunks):
+        self.place, self.part, self.held = place, part, held
+        self.sems, self.chunks = (send, recv), chunks
+        self.rows = part.shape[1] // chunks
+
+    def copy(self, side, step, chunk, shard, target):
+        rows = chunk_rows(chunk, self.rows)
+        index = 0 if side == 1 else 1
+        spot = (index, step - 1, chunk)
+        return pltpu.make_async_remote_copy(
+            src_ref=self.part.at[shard, rows],
+            dst_ref=self.held.at[index, step - 1, rows],
+            send_sem=self.sems[0].at[spot],
+            recv_sem=self.sems[1].at[spot],
+            device_id={"tensor": target},
+            device_id_type=MESH,
+        )
+
+    def send(self, step, chunk):
+        rows = chunk_rows(chunk, self.rows)
+        for index, side in enumerate(SIDES):
+            far = far_of(self.place, side)
+            shard = self.place + side * (LINE - step)
+            if step > 1:
+
+                @pl.when((far >= 1) & (far <= step - 1))
+                def _():
+                    self.copy(side, step - 1, chunk, self.place, self.place - side).wait_recv()
+                    self.part[shard, rows] = (
+                        self.part[shard, rows].astype(f32)
+                        + self.held[index, step - 2, rows].astype(f32)
+                    ).astype(bf16)
+
+            @pl.when(far <= step - 1)
+            def _():
+                self.copy(side, step, chunk, shard, self.place + side).start()
+
+    def total(self, chunk, out):
+        rows = chunk_rows(chunk, self.rows)
+        out[rows] = self.part[self.place, rows].astype(f32)
+        for index, side in enumerate(SIDES):
+
+            @pl.when(far_of(self.place, side) >= 1)
+            def _():
+                self.copy(side, LINE - 1, chunk, self.place, self.place - side).wait_recv()
+                out[rows] += self.held[index, LINE - 2, rows].astype(f32)
+
+    def drain(self):
+        for step in range(1, LINE):
+            for chunk in range(self.chunks):
+                for side in SIDES:
+                    far = far_of(self.place, side)
+                    shard = self.place + side * (LINE - step)
+
+                    @pl.when(far <= step - 1)
+                    def _():
+                        self.copy(side, step, chunk, shard, self.place + side).wait_send()
+
+
+def line_sems(chunks):
+    return [pltpu.SemaphoreType.DMA((2, LINE - 1, chunks))] * 2
+
+
+def fetch(pairs, sems):
+    copies = [pltpu.make_async_copy(src, dst, sems.at[i]) for i, (src, dst) in enumerate(pairs)]
+    for copy in copies:
+        copy.start()
+    return copies
+
+
+IN_VMEM = pl.BlockSpec(memory_space=pltpu.VMEM)
+IN_HBM = pl.BlockSpec(memory_space=pl.ANY)
+
+
+def comm_params(number):
+    return pltpu.CompilerParams(
+        vmem_limit_bytes=VMEM_LIMIT, collective_id=number, has_side_effects=True
+    )
+
+
+def gather_norm_body(x_ref, gain_ref, buf, send, recv):
+    place = lax.axis_index("tensor")
+    greet(place)
+    rows = x_ref[...].astype(f32)
+    rms = lax.rsqrt(jnp.mean(rows * rows, axis=1, keepdims=True) + eps)
+    buf[place] = (rows * rms * gain_ref[...]).astype(bf16)
+    gather = Gather(place, buf, send, recv, 1)
+    gather.send(1, 0)
+    for step in range(1, LINE):
+        gather.arrive(step, 0)
+        if step < LINE - 1:
+            gather.send(step + 1, 0)
+    gather.drain()
+
+
+def gather_norm(x, gain):
+    rows, features = x.shape
+    return pl.pallas_call(
+        gather_norm_body,
+        in_specs=[IN_VMEM, IN_VMEM],
+        out_specs=IN_VMEM,
+        out_shape=jax.ShapeDtypeStruct((LINE, rows, features), bf16),
+        scratch_shapes=line_sems(1),
+        compiler_params=comm_params(0),
+    )(x, gain[None, :])
+
+
+def project_body(groups, x_ref, w_ref, e_ref, a_ref, cos_ref, sin_ref, y_ref, l_ref):
+    tile = pl.program_id(0)
+
+    @pl.when(tile == 0)
     def _():
         l_ref[...] = nt(x_ref[...], e_ref[...]).astype(bf16)
 
     total = nn(x_ref[...], w_ref[...]) + nn(l_ref[...], a_ref[...])
-    if rope:
-
-        @pl.when(group < groups - 1)
-        def _():
-            y_ref[0] = turn(total, cos_ref[...], sin_ref[...]).astype(bf16)
-
-        @pl.when(group == groups - 1)
-        def _():
-            y_ref[0] = total.astype(bf16)
-    else:
+
+    @pl.when(tile < pl.num_programs(0) // groups * (groups - 1))
+    def _():
+        y_ref[0] = turn(total, cos_ref[...], sin_ref[...]).astype(bf16)
+
+    @pl.when(tile >= pl.num_programs(0) // groups * (groups - 1))
+    def _():
         y_ref[0] = total.astype(bf16)
 
 
-def project(slot, x, weight, entry, exits, groups, rows_total, tables, before):
+def project(x, weight, entry, exits, groups, tables, tile=256):
     rows, features = x.shape
-    width = weight.shape[1] // groups
-    in_specs = [
-        pl.BlockSpec((rows, features), lambda g, s: (0, 0)),
-        pl.BlockSpec((features, width), lambda g, s: (0, g)),
-        pl.BlockSpec((RANK_PAD, features), lambda g, s: (0, 0)),
-        pl.BlockSpec((RANK_PAD, width), lambda g, s: (0, g)),
-    ]
-    operands = [x, weight, entry, exits]
-    if tables is not None:
-        in_specs += [pl.BlockSpec((rows, tables[0].shape[1]), lambda g, s: (s[0], 0))] * 2
-        operands += list(tables)
-    aliases = {}
-    if before is not None:
-        aliases = {len(operands) + 1: 0, len(operands) + 2: 1}
-        in_specs += [pl.BlockSpec(memory_space=pl.ANY)] * 2
-        operands += list(before)
+    width = exits.shape[1] // groups
+    per = width // tile
     return pl.pallas_call(
-        functools.partial(project_body, tables is not None, groups),
-        grid_spec=pltpu.PrefetchScalarGridSpec(
-            num_scalar_prefetch=1,
-            grid=(groups,),
-            in_specs=in_specs,
-            out_specs=[
-                pl.BlockSpec((1, rows, width), lambda g, s: (g, s[0], 0)),
-                pl.BlockSpec((rows, RANK_PAD), lambda g, s: (s[0], 0)),
-            ],
-        ),
+        functools.partial(project_body, groups),
+        grid=(groups * per,),
+        in_specs=[
+            pl.BlockSpec((rows, features), lambda i: (0, 0)),
+            pl.BlockSpec((features, tile), lambda i: (0, i)),
+            pl.BlockSpec((RANK_PAD, features), lambda i: (0, 0)),
+            pl.BlockSpec((RANK_PAD, tile), lambda i: (0, i)),
+            pl.BlockSpec((rows, tables[0].shape[1]), lambda i: (0, 0)),
+            pl.BlockSpec((rows, tables[0].shape[1]), lambda i: (0, 0)),
+        ],
+        out_specs=[
+            pl.BlockSpec((1, rows, tile), lambda i: (i // per, 0, i % per)),
+            pl.BlockSpec((rows, RANK_PAD), lambda i: (0, 0)),
+        ],
         out_shape=[
-            jax.ShapeDtypeStruct((groups, rows_total, width), bf16),
-            jax.ShapeDtypeStruct((rows_total, RANK_PAD), bf16),
-        ],
-        input_output_aliases=aliases,
+            jax.ShapeDtypeStruct((groups, rows, width), bf16),
+            jax.ShapeDtypeStruct((rows, RANK_PAD), bf16),
+        ],
         compiler_params=pltpu.CompilerParams(vmem_limit_bytes=VMEM_LIMIT),
         cost_estimate=pl.CostEstimate(
-            flops=2 * rows * features * weight.shape[1],
-            bytes_accessed=2 * weight.size + 4 * x.size,
-            transcendentals=0,
+            flops=2 * rows * features * exits.shape[1], bytes_accessed=2 * rows * features, transcendentals=0
         ),
-    )(slot, *operands)
-
-
-def collect_body(groups, slot_ref, d_ref, w_ref, a_ref, e_ref, y_ref, b_ref):
-    tile = pl.program_id(0)
-    width = d_ref.shape[2]
-
-    @pl.when(tile == 0)
-    def _():
-        low = nt(d_ref[0], a_ref[:, :width])
-        for g in range(1, groups):
-            low += nt(d_ref[g], a_ref[:, g * width : (g + 1) * width])
-        b_ref[...] = low.astype(bf16)
-
-    total = nn(b_ref[...], e_ref[...])
-    for g in range(groups):
-        total += nt(d_ref[g], w_ref[:, g * width : (g + 1) * width])
-    y_ref[...] = total.astype(bf16)
-
-
-def collect(slot, d, weight, exits, entry, rows, tile=1024):
-    groups, _, width = d.shape
-    features = weight.shape[0]
+    )(x, weight, entry, exits, *tables)
+
+
+def middle_body(
+    chunks, d_ref, w_ref, a_ref, e_ref, x_ref, gain_ref, mid_ref, buf, low_ref,
+    part, held, wv, wsem, s_send, s_recv, g_send, g_recv,
+):
+    place = lax.axis_index("tensor")
+    width = d_ref.shape[1]
+    (load,) = fetch([(w_ref.at[:, 3 * width :], wv)], wsem)
+    greet(place)
+    load.wait()
+    rows = part.shape[1]
+    summed = Sum(place, part, held, s_send, s_recv, chunks)
+    gather = Gather(place, buf, g_send, g_recv, chunks)
+    for slot in (3, 2, 1, 0):
+        shard = place ^ slot
+        mine = pl.ds(pl.multiple_of(shard * rows, rows), rows)
+        d = d_ref[mine]
+        low = nt(d, a_ref[...]).astype(bf16)
+        low_ref[mine] = low
+        part[shard] = (nt(d, wv[...]) + nn(low, e_ref[...])).astype(bf16)
+        if slot == 3:
+            for chunk in range(chunks):
+                summed.send(1, chunk)
+    size = rows // chunks
+    for turn_ in range(chunks + 2):
+        if turn_ < chunks:
+            summed.send(2, turn_)
+            summed.send(3, turn_)
+            summed.total(turn_, mid_ref)
+            here = chunk_rows(turn_, size)
+            value = mid_ref[here] + x_ref[here].astype(f32)
+            mid_ref[here] = value
+            rms = lax.rsqrt(jnp.mean(value * value, axis=1, keepdims=True) + eps)
+            buf[place, here] = (value * rms * gain_ref[...]).astype(bf16)
+            gather.send(1, turn_)
+        for step in (1, 2):
+            chunk = turn_ - step
+            if 0 <= chunk < chunks:
+                gather.arrive(step, chunk)
+                gather.send(step + 1, chunk)
+    for chunk in range(chunks):
+        gather.arrive(3, chunk)
+    summed.drain()
+    gather.drain()
+
+
+def middle_rows(attended, weight, exits, entry, x, gain, chunks=4):
+    rows, features = x.shape
+    width = attended.shape[1]
     return pl.pallas_call(
-        functools.partial(collect_body, groups),
-        grid_spec=pltpu.PrefetchScalarGridSpec(
-            num_scalar_prefetch=1,
-            grid=(features // tile,),
-            in_specs=[
-                pl.BlockSpec((groups, rows, width), lambda i, s: (0, s[0], 0)),
-                pl.BlockSpec((tile, groups * width), lambda i, s: (i, 0)),
-                pl.BlockSpec((RANK_PAD, groups * width), lambda i, s: (0, 0)),
-                pl.BlockSpec((RANK_PAD, tile), lambda i, s: (0, i)),
-            ],
-            out_specs=[
-                pl.BlockSpec((rows, tile), lambda i, s: (0, i)),
-                pl.BlockSpec((rows, RANK_PAD), lambda i, s: (0, 0)),
-            ],
-        ),
+        functools.partial(middle_body, chunks),
+        in_specs=[IN_VMEM, IN_HBM, IN_VMEM, IN_VMEM, IN_VMEM, IN_VMEM],
+        out_specs=[IN_VMEM] * 3,
+        out_shape=[
+            jax.ShapeDtypeStruct((rows, features), f32),
+            jax.ShapeDtypeStruct((LINE, rows, features), bf16),
+            jax.ShapeDtypeStruct((LINE * rows, RANK_PAD), bf16),
+        ],
+        scratch_shapes=[
+            pltpu.VMEM((LINE, rows, features), bf16),
+            pltpu.VMEM((2, LINE - 1, rows, features), bf16),
+            pltpu.VMEM((features, width), bf16),
+            pltpu.SemaphoreType.DMA((1,)),
+        ]
+        + line_sems(chunks)
+        + line_sems(chunks),
+        compiler_params=comm_params(1),
+    )(attended, weight, exits, entry, x, gain[None, :])
+
+
+def branch_body(b_ref, w_ref, e_ref, a_ref, buf, y_ref, l_ref, wv, wsem, send, recv):
+    place = lax.axis_index("tensor")
+    rows = b_ref.shape[0]
+    width = y_ref.shape[2]
+    (load,) = fetch([(w_ref.at[:, 3 * width :], wv)], wsem)
+    greet(place)
+    buf[place] = b_ref[...]
+    gather = Gather(place, buf, send, recv, 1)
+    gather.send(1, 0)
+    load.wait()
+    for slot in range(LINE):
+        if slot:
+            gather.arrive(slot, 0)
+            if slot < LINE - 1:
+                gather.send(slot + 1, 0)
+        shard = place ^ slot
+        mine = pl.ds(pl.multiple_of(shard * rows, rows), rows)
+        low = nt(buf[shard], e_ref[...]).astype(bf16)
+        l_ref[mine] = low
+        y_ref[0, mine] = (nn(buf[shard], wv[...]) + nn(low, a_ref[...])).astype(bf16)
+    gather.drain()
+
+
+def branch_back(branch, weight, entry, exits):
+    rows, features = branch.shape
+    width = exits.shape[1]
+    return pl.pallas_call(
+        branch_body,
+        in_specs=[IN_VMEM, IN_HBM, IN_VMEM, IN_VMEM],
+        out_specs=[IN_VMEM] * 3,
+        out_shape=[
+            jax.ShapeDtypeStruct((LINE, rows, features), bf16),
+            jax.ShapeDtypeStruct((1, LINE * rows, width), bf16),
+            jax.ShapeDtypeStruct((LINE * rows, RANK_PAD), bf16),
+        ],
+        scratch_shapes=[pltpu.VMEM((features, width), bf16), pltpu.SemaphoreType.DMA((1,))]
+        + line_sems(1),
+        compiler_params=comm_params(2),
+    )(branch, weight, entry, exits)
+
+
+def tokens_body(
+    chunks, d_ref, w_ref, a_ref, e_ref, x_ref, gain_ref, mid_ref, out_ref, low_ref,
+    part, held, acc, dv, wv, wsem, send, recv,
+):
+    place = lax.axis_index("tensor")
+    groups, _, width = d_ref.shape
+    loads = fetch([(d_ref, dv), (w_ref.at[:, : groups * width], wv)], wsem)
+    greet(place)
+    for load in loads:
+        load.wait()
+    rows = part.shape[1]
+    summed = Sum(place, part, held, send, recv, chunks)
+    for slot in (3, 2, 1, 0):
+        shard = place ^ slot
+        mine = pl.ds(pl.multiple_of(shard * rows, rows), rows)
+        d = jnp.concatenate([dv[g, mine] for g in range(groups)], axis=1)
+        low = nt(d, a_ref[...]).astype(bf16)
+        low_ref[mine] = low
+        part[shard] = (nt(d, wv[...]) + nn(low, e_ref[...])).astype(bf16)
+        if slot == 3:
+            for chunk in range(chunks):
+                summed.send(1, chunk)
+    size = rows // chunks
+    for chunk in range(chunks):
+        summed.send(2, chunk)
+        summed.send(3, chunk)
+        if chunk:
+            finish_tokens(summed, chunk - 1, size, acc, x_ref, gain_ref, mid_ref, out_ref)
+    finish_tokens(summed, chunks - 1, size, acc, x_ref, gain_ref, mid_ref, out_ref)
+    summed.drain()
+
+
+def finish_tokens(summed, chunk, size, acc, x_ref, gain_ref, mid_ref, out_ref):
+    summed.total(chunk, acc)
+    here = chunk_rows(chunk, size)
+    rows = x_ref[here].astype(f32)
+    rms = lax.rsqrt(jnp.mean(rows * rows, axis=1, keepdims=True) + eps)
+    scaled = acc[here] * gain_ref[...]
+    mean = jnp.mean(scaled * rows, axis=1, keepdims=True)
+    out_ref[here] = (mid_ref[here] + rms * (scaled - rows * (rms * rms) * mean)).astype(bf16)
+
+
+def tokens_back(head_grads, weight, exits, entry, x, gain, grad_middle, chunks=4):
+    rows, features = x.shape
+    groups, total, width = head_grads.shape
+    return pl.pallas_call(
+        functools.partial(tokens_body, chunks),
+        in_specs=[IN_HBM, IN_HBM] + [IN_VMEM] * 5,
+        out_specs=[IN_VMEM] * 2,
         out_shape=[
             jax.ShapeDtypeStruct((rows, features), bf16),
-            jax.ShapeDtypeStruct((rows, RANK_PAD), bf16),
-        ],
-        compiler_params=pltpu.CompilerParams(vmem_limit_bytes=VMEM_LIMIT),
-        cost_estimate=pl.CostEstimate(
-            flops=2 * rows * weight.size, bytes_accessed=2 * weight.size + 4 * rows * features, transcendentals=0
-        ),
-    )(slot, d, weight, exits, entry)
+            jax.ShapeDtypeStruct((total, RANK_PAD), bf16),
+        ],
+        scratch_shapes=[
+            pltpu.VMEM((LINE, rows, features), bf16),
+            pltpu.VMEM((2, LINE - 1, rows, features), bf16),
+            pltpu.VMEM((rows, features), f32),
+            pltpu.VMEM((groups, total, width), bf16),
+            pltpu.VMEM((features, groups * width), bf16),
+            pltpu.SemaphoreType.DMA((2,)),
+        ]
+        + line_sems(chunks),
+        compiler_params=comm_params(3),
+    )(head_grads, weight, exits, entry, x, gain[None, :], grad_middle)
 
 
 def tree_tiles(seg, rows, parent_row):
@@ -350,22 +647,22 @@
 
 
 def feed_body(
-    rank, n_ref, c_ref, wg_ref, wu_ref, wd_ref, xg_ref, xu_ref, xd_ref, e_ref, f_ref,
+    rank, slot_ref, n_ref, c_ref, wg_ref, wu_ref, wd_ref, xg_ref, xu_ref, xd_ref, e_ref, f_ref,
     res_ref, back_ref, unit_ref, model_ref, low, low_t, acc_res, acc_back, acc_low,
 ):
     tile = pl.program_id(0)
 
     @pl.when(tile == 0)
     def _():
-        first = nt(n_ref[...], e_ref[...]) + nt(c_ref[...], f_ref[...])
+        first = nt(n_ref[0], e_ref[...]) + nt(c_ref[...], f_ref[...])
         low[...] = first.astype(bf16)
         low_t[...] = first.T.astype(bf16)
         acc_res[...] = jnp.zeros_like(acc_res)
         acc_back[...] = jnp.zeros_like(acc_back)
         acc_low[...] = jnp.zeros_like(acc_low)
 
-    gate = nn(n_ref[...], wg_ref[...]) + nn(low[...], xg_ref[...])
-    rise = nn(n_ref[...], wu_ref[...]) + nn(low[...], xu_ref[...])
+    gate = nn(n_ref[0], wg_ref[...]) + nn(low[...], xg_ref[...])
+    rise = nn(n_ref[0], wu_ref[...]) + nn(low[...], xu_ref[...])
     grad_hidden = nn(c_ref[...], wd_ref[...]) + nn(low[...], xd_ref[...])
     sigmoid = jax.nn.sigmoid(gate)
     silu = gate * sigmoid
@@ -387,50 +684,50 @@
         joined_t = acc_low[...].T.astype(bf16)
         back_ref[...] = (acc_back[...] + nn(joined, e_ref[...])).astype(bf16)
         res_ref[...] = (acc_res[...] + nn(joined, f_ref[...])).astype(bf16)
-        model_ref[: 2 * rank] = nn(joined_t[: 2 * rank], n_ref[...])
+        model_ref[: 2 * rank] = nn(joined_t[: 2 * rank], n_ref[0])
         model_ref[2 * rank :] = nn(joined_t[2 * rank : 3 * rank], c_ref[...])
 
 
-def feed(normed, cot, w_gate, w_rise, w_fall, x_gate, x_rise, x_fall, entry, final, rank, tile=512):
-    rows, features = normed.shape
-    units = w_gate.shape[1]
-    whole = pl.BlockSpec((rows, features), lambda i: (0, 0))
-    weight = pl.BlockSpec((features, tile), lambda i: (0, i))
-    exits = pl.BlockSpec((RANK_PAD, tile), lambda i: (0, i))
-    entries = pl.BlockSpec((RANK_PAD, features), lambda i: (0, 0))
+def feed(slot, normed, cot, weight, x_gate, x_rise, x_fall, entry, final, rank, tile=512):
+    _, rows, features = normed.shape
+    units = weight.shape[1] // 3
+    tiles = units // tile
+    whole = pl.BlockSpec((rows, features), lambda i, s: (0, 0))
+    exits = pl.BlockSpec((RANK_PAD, tile), lambda i, s: (0, i))
+    entries = pl.BlockSpec((RANK_PAD, features), lambda i, s: (0, 0))
     return pl.pallas_call(
         functools.partial(feed_body, rank),
-        grid=(units // tile,),
-        in_specs=[whole, whole, weight, weight, weight, exits, exits, exits, entries, entries],
-        out_specs=[
-            whole,
-            whole,
-            pl.BlockSpec((3 * rank, tile), lambda i: (0, i)),
-            pl.BlockSpec((3 * rank, features), lambda i: (0, 0)),
-        ],
+        grid_spec=pltpu.PrefetchScalarGridSpec(
+            num_scalar_prefetch=1,
+            grid=(tiles,),
+            in_specs=[pl.BlockSpec((1, rows, features), lambda i, s: (s[0], 0, 0)), whole]
+            + [pl.BlockSpec((features, tile), lambda i, s, k=k: (0, k * tiles + i)) for k in range(3)]
+            + [exits, exits, exits, entries, entries],
+            out_specs=[
+                whole,
+                whole,
+                pl.BlockSpec((3 * rank, tile), lambda i, s: (0, i)),
+                pl.BlockSpec((3 * rank, features), lambda i, s: (0, 0)),
+            ],
+            scratch_shapes=[
+                pltpu.VMEM((rows, RANK_PAD), bf16),
+                pltpu.VMEM((RANK_PAD, rows), bf16),
+                pltpu.VMEM((rows, features), f32),
+                pltpu.VMEM((rows, features), f32),
+                pltpu.VMEM((rows, RANK_PAD), f32),
+            ],
+        ),
         out_shape=[
             jax.ShapeDtypeStruct((rows, features), bf16),
             jax.ShapeDtypeStruct((rows, features), bf16),
             jax.ShapeDtypeStruct((3 * rank, units), f32),
             jax.ShapeDtypeStruct((3 * rank, features), f32),
         ],
-        scratch_shapes=[
-            pltpu.VMEM((rows, RANK_PAD), bf16),
-            pltpu.VMEM((RANK_PAD, rows), bf16),
-            pltpu.VMEM((rows, features), f32),
-            pltpu.VMEM((rows, features), f32),
-            pltpu.VMEM((rows, RANK_PAD), f32),
-        ],
         compiler_params=pltpu.CompilerParams(vmem_limit_bytes=VMEM_LIMIT),
         cost_estimate=pl.CostEstimate(
-            flops=12 * rows * w_gate.size, bytes_accessed=6 * w_gate.size, transcendentals=0
+            flops=12 * rows * features * units, bytes_accessed=6 * features * units, transcendentals=0
         ),
-    )(normed, cot, w_gate, w_rise, w_fall, x_gate, x_rise, x_fall, entry, final)
-
-
-def norm_forward(rows, gain):
-    rms = lax.rsqrt(jnp.mean(rows * rows, axis=1, keepdims=True) + eps)
-    return (rows * rms * gain).astype(bf16), rms
+    )(slot, normed, cot, weight, weight, weight, x_gate, x_rise, x_fall, entry, final)
 
 
 def norm_backward(rows, rms, gain, grad):
@@ -488,8 +785,7 @@
     place = lax.axis_index("tensor")
     edge = (place == 0) | (place == 3)
     slots = [(place ^ s).reshape(1).astype(jnp.int32) for s in range(4)]
-    rows_here = tokens.astype(f32)
-    local_rows = rows_here.shape[0]
+    local_rows = tokens.shape[0]
     total = local_rows * lax.axis_size("tensor")
     blocks = parents.shape[1]
     seg = total // blocks
@@ -498,13 +794,15 @@
     gain_one = attention_gain.astype(f32)
     gain_two = feed_gain.astype(f32)
 
-    w_qkv = lax.all_gather(
-        jnp.concatenate([query_weight, key_weight, value_weight], axis=1), "dp", axis=0, tiled=True
-    )
-    w_output = lax.all_gather(output_weight, "dp", axis=0, tiled=True)
-    w_gate = lax.all_gather(gate_weight, "dp", axis=0, tiled=True)
-    w_rise = lax.all_gather(up_weight, "dp", axis=0, tiled=True)
-    w_fall = lax.all_gather(down_weight, "dp", axis=0, tiled=True)
+    w_heads = lax.all_gather(
+        jnp.concatenate([query_weight, key_weight, value_weight, output_weight], axis=1),
+        "dp",
+        axis=0,
+        tiled=True,
+    )
+    w_units = lax.all_gather(
+        jnp.concatenate([gate_weight, up_weight, down_weight], axis=1), "dp", axis=0, tiled=True
+    )
 
     entries = jnp.swapaxes(entry_maps, 2, 3)[:, pick]
     heads_exit = head_exits[:, pick]
@@ -528,57 +826,46 @@
     x_rise = place_rows(units_exit[1], rank)
     x_fall = place_rows(fall_entry, 2 * rank)
 
-    normed_one, rms_one = norm_forward(rows_here, gain_one)
-    full_one = line_gather(normed_one, edge)
-    state = None
-    for s in range(4):
-        state = project(slots[s], full_one[s], w_qkv, entry_one, exit_one, 3, total, tables, state)
-    qkv, low_one = state
-    cot_start, _ = lax.optimization_barrier((cotangent, full_one[3]))
-    full_cot = line_gather(cot_start, edge)
+    full_one = gather_norm(tokens, gain_one)
+    cot_tied, _ = lax.optimization_barrier((cotangent, full_one))
+    one, mid = line_gather_start(cot_tied)
+    flat_one = full_one.reshape(total, -1)
+    qkv, low_one = project(flat_one, w_heads, entry_one, exit_one, 3, tables)
     attended, lse = attend(qkv, leaf_parent, seg)
-    partial_one = [
-        collect(slots[s], attended, w_output, exit_out, final_one, local_rows) for s in (3, 2, 1, 0)
-    ][::-1]
-    middle = rows_here + line_scatter([p[0] for p in partial_one], place)
-
-    normed_two, rms_two = norm_forward(middle, gain_two)
-    full_two = line_gather(normed_two, edge)
-    fed = [
-        feed(
-            full_two[s], full_cot[s], w_gate, w_rise, w_fall, x_gate, x_rise, x_fall,
-            entry_two, final_two, rank,
+    one, mid, attended = lax.optimization_barrier((one, mid, attended))
+    full_cot = line_gather_finish(cot_tied, one, mid, edge)
+    middle, full_two, adapt_o = middle_rows(
+        attended[0], w_heads, exit_out, final_one, tokens, gain_two
+    )
+
+    fed = [None] * 4
+    tie = middle
+    for s in (3, 2, 1, 0):
+        slot, _ = lax.optimization_barrier((slots[s], tie))
+        fed[s] = feed(
+            slot, full_two, full_cot[s], w_units, x_gate, x_rise, x_fall, entry_two, final_two, rank
         )
-        for s in range(4)
-    ]
+        tie = fed[s][3]
+    rms_two = lax.rsqrt(jnp.mean(middle * middle, axis=1, keepdims=True) + eps)
     grad_middle = cotangent.astype(f32) + norm_backward(
         middle, rms_two, gain_two, line_scatter([f[1] for f in fed], place)
     )
-    result = (middle + line_scatter([f[0] for f in fed], place)).astype(bf16)
     unit_grads = functools.reduce(jnp.add, [f[2] for f in fed])
     model_grads = functools.reduce(jnp.add, [f[3] for f in fed])
 
-    full_branch = line_gather(grad_middle.astype(bf16), edge)
-    state = None
-    for s in range(4):
-        state = project(slots[s], full_branch[s], w_output, final_one, exit_out, 1, total, None, state)
-    grad_attended, back_o = state
+    full_branch, grad_attended, back_o = branch_back(
+        grad_middle.astype(bf16), w_heads, final_one, exit_out
+    )
+    res_parts, _ = lax.optimization_barrier(([f[0] for f in fed], back_o))
+    result = (middle + line_scatter(res_parts, place)).astype(bf16)
     head_grads = attend_back(qkv, attended, grad_attended, lse, leaf_parent, tables, seg)
-    partial_four = [
-        collect(slots[s], head_grads, w_qkv, exit_one, entry_one, local_rows) for s in (3, 2, 1, 0)
-    ][::-1]
-    grad_tokens = (
-        grad_middle
-        + norm_backward(rows_here, rms_one, gain_one, line_scatter([p[0] for p in partial_four], place))
-    ).astype(bf16)
+    grad_tokens, back_one = tokens_back(
+        head_grads, w_heads, exit_one, entry_one, tokens, gain_one, grad_middle
+    )
 
     out_grads = tn(back_o, attended[0])[:rank]
-    final_one_grads = functools.reduce(
-        jnp.add, [tn(partial_one[s][1], full_branch[s])[:rank] for s in range(4)]
-    )
-    entry_one_grads = functools.reduce(
-        jnp.add, [tn(partial_four[s][1], full_one[s])[: 3 * rank] for s in range(4)]
-    )
+    final_one_grads = tn(adapt_o, full_branch.reshape(total, -1))[:rank]
+    entry_one_grads = tn(back_one, flat_one)[: 3 * rank]
     head_parts = [
         tn(low_one[:, k * rank : (k + 1) * rank], head_grads[k]) for k in range(3)
     ]

time: 1020 us -> 984 us (0.965)
  Pallas kernels: 257 us -> 660 us
  waiting for transfers between devices: 438 us -> 108 us
  starting transfers between devices: 112 us -> 35.4 us
  other arithmetic: 96.4 us -> 62.5 us
    pallas_call x20 -> x9, Pallas kernels: 208 us -> 611 us  [the longest x1 189 us: middle_rows(): pl.pallas_call(functools.partial(middle_body, chunks), in_specs=[IN_VMEM,...]
    ppermute x40 -> x15, waiting for transfers between devices: 400 us -> 69.8 us  [permute(): return lax.ppermute(value, 'tensor', pairs)]
    ppermute x40 -> x15, starting transfers between devices: 112 us -> 35 us  [permute(): return lax.ppermute(value, 'tensor', pairs)]
    convert_element_type x8 -> x4, other arithmetic: 31.2 us -> 16.7 us  [add_rows(): return (left.astype(f32) + right.astype(f32)).astype(bf16)]
    select_n x8 -> x2, other arithmetic: 16.2 us -> 3.72 us  [the longest x1 2.52 us: line_gather_finish(): two = jnp.where(edge, two_edge, two_mid)]
  transfers between devices with their start and end apart: 49 -> 21, of which waited for: 22 -> 6; matrix products, arithmetic and copies ran while one was open for 10% -> 6% of each run, Pallas kernels for 18% -> 36%
where the time goes in v2:
time: 984 us; the launch traced here: 975 us
  Pallas kernels  660 us (67%)
  waiting for transfers between devices  108 us (11%)
  other arithmetic  62.5 us (6%)
  between operations  55.5 us (6%)
  starting transfers between devices  35.4 us (4%)
  local copies, waits for them, and re-layouts  23.4 us (2%)
  blocking collectives  17.7 us (2%)
  matrix products  12.5 us (1%)
    pallas_call x1, Pallas kernels, middle_rows(): pl.pallas_call(functools.partial(middle_body, chunks), in_specs=[IN_VMEM,...  189 us
    pallas_call x4, Pallas kernels, feed(): pl.pallas_call(functools.partial(feed_body, rank), grid_spec=pltpu.Prefet...  116 us
    pallas_call x1, Pallas kernels, tokens_back(): pl.pallas_call(functools.partial(tokens_body, chunks), in_specs=[IN_HBM,...  99.9 us
    pallas_call x1, Pallas kernels, gather_norm(): pl.pallas_call(gather_norm_body, in_specs=[IN_VMEM, IN_VMEM], out_specs=I...  95.1 us
    pallas_call x1, Pallas kernels, branch_back(): pl.pallas_call(branch_body, in_specs=[IN_VMEM, IN_HBM, IN_VMEM, IN_VMEM],...  91.4 us
    ppermute x15, waiting for transfers between devices, permute(): return lax.ppermute(value, 'tensor', pairs)  69.8 us
    psum x1, waiting for transfers between devices, local(): late = per_tree(lax.psum(entry_one_grads.astype(bf16), 'tensor'))  38.3 us
    ppermute x15, starting transfers between devices, permute(): return lax.ppermute(value, 'tensor', pairs)  35 us
  transfers between devices with their start and end apart: 21, of which 6 were waited for; matrix products, arithmetic and copies ran while one was open for 6% of the time, Pallas kernels for 36%

profile of v2, /device:TPU:0, one launch (start us, length us, event | category | flops | bytes accessed | tf_op | source)
XLA Modules:
  0.0 974.9 jit_solution(5909305468572847876)
XLA Ops:
  7.2 2.4 pad_maximum_fusion.3
  9.7 3.2 pad_maximum_fusion
  14.3 95.1 %shard_map.260 = bf16[4,320,2048]{2,1,0:T(8,128)(2,1)} custom-call(bf16[320,2048]{1,0:T(8,128)(2,1)} %x_ref.5, f32[1,2048]{1,0:T(1,128)} %bitcast.327), custom_call_target="tpu_custom_call" | custom-call | tf_op jit(solution)/shard_map/pallas_call | solution.py:273
  109.4 1.7 collective-permute-start.1
  115.1 19.8 %shard_map.261 = (bf16[3,1280,512]{2,1,0:T(8,128)(2,1)}, bf16[1280,128]{1,0:T(8,128)(2,1)}) custom-call(bf16[1280,2048]{1,0:T(8,128)(2,1)} %bitcast.321, bf16[2048,2048]{1,0:T(8,128)(2,1)} %all-gather.7.cloned.1.call-done.w_ref, bf16[128,2048]{1,0:T(8,128)(2,1)} %fusion.20.e_ref, bf16[128,1536]{1,0:T(8,128)(2,1)} %pad.50.a_ref, ...), custom_call_target="tpu_custom_call" | custom-call | flops 8053063680 | bytes 5242880 | tf_op jit(solution)/shard_map/pallas_call | solution.py:305
  134.9 19.3 %shard_map.262 = (bf16[1,1280,512]{2,1,0:T(8,128)(2,1)}, f32[4,2,1280]{2,1,0:T(2,128)}) custom-call(bf16[3,1280,512]{2,1,0:T(8,128)(2,1)} %get-tuple-element.49.q_ref.k_ref.v_ref, bf16[3,1280,512]{2,1,0:T(8,128)(2,1)} %get-tuple-element.49.q_ref.k_ref.v_ref, bf16[3,1280,512]{2,1,0:T(8,128)(2,1)} %get-tuple-element.49.q_ref.k_ref.v_ref, s32[1,512]{1,0:T(1,128)} %sub.13.p_ref), custom_call_target="tpu_custom_call" | custom-call | flops 6710886400 | bytes 5242880 | tf_op jit(solution)/shard_map/pallas_call | solution.py:560
  154.3 1.3 collective-permute-start.2
  156.3 1.3 collective-permute-start.3
  157.6 1.0 dynamic-slice_bitcast_fusion.1
  165.7 0.9 fusion.21.e_ref
  166.5 189.1 %shard_map.263 = (f32[320,2048]{1,0:T(8,128)}, bf16[4,320,2048]{2,1,0:T(8,128)(2,1)}, bf16[1280,128]{1,0:T(8,128)(2,1)}) custom-call(bf16[1280,512]{1,0:T(8,128)(2,1)} %bitcast.323, bf16[2048,2048]{1,0:T(8,128)(2,1)} %all-gather.7.cloned.1.call-done.w_ref, bf16[128,512]{1,0:T(8,128)(2,1)} %pad.51.a_ref, bf16[128,2048]{1,0:T(8,128)(2,1)} %pad.52.e_ref, ...), custom_call_target="tpu_custom_call" | custom-call | tf_op jit(solution)/shard_map/pallas_call | solution.py:379
  355.7 1.2 broadcast_select_fusion.1.c_ref
  356.9 2.5 broadcast_select_fusion.c_ref
  359.4 28.9 %shard_map.264 = (bf16[320,2048]{1,0:T(8,128)(2,1)}, bf16[320,2048]{1,0:T(8,128)(2,1)}, f32[48,2048]{1,0:T(8,128)}, f32[48,2048]{1,0:T(8,128)}) custom-call(s32[1]{0:T(128)} %bitcast.19.slot_ref, bf16[4,320,2048]{2,1,0:T(8,128)(2,1)} %get-tuple-element.54.n_ref, bf16[320,2048]{1,0:T(8,128)(2,1)} %broadcast_select_fusion.1.c_ref, ...), custom_call_target="tpu_custom_call" | custom-call | flops 16106127360 | bytes 25165824 | tf_op jit(solution)/shard_map/pallas_call | solution.py:698
  388.3 28.7 %shard_map.265 = (bf16[320,2048]{1,0:T(8,128)(2,1)}, bf16[320,2048]{1,0:T(8,128)(2,1)}, f32[48,2048]{1,0:T(8,128)}, f32[48,2048]{1,0:T(8,128)}) custom-call(s32[1]{0:T(128)} %bitcast.18.slot_ref, bf16[4,320,2048]{2,1,0:T(8,128)(2,1)} %get-tuple-element.54.n_ref, bf16[320,2048]{1,0:T(8,128)(2,1)} %broadcast_select_fusion.c_ref, ...), custom_call_target="tpu_custom_call" | custom-call | flops 16106127360 | bytes 25165824 | tf_op jit(solution)/shard_map/pallas_call | solution.py:698
  417.1 29.2 %shard_map.266 = (bf16[320,2048]{1,0:T(8,128)(2,1)}, bf16[320,2048]{1,0:T(8,128)(2,1)}, f32[48,2048]{1,0:T(8,128)}, f32[48,2048]{1,0:T(8,128)}) custom-call(s32[1]{0:T(128)} %bitcast.17.slot_ref, bf16[4,320,2048]{2,1,0:T(8,128)(2,1)} %get-tuple-element.54.n_ref, bf16[320,2048]{1,0:T(8,128)(2,1)} %collective-permute-done.c_ref, ...), custom_call_target="tpu_custom_call" | custom-call | flops 16106127360 | bytes 25165824 | tf_op jit(solution)/shard_map/pallas_call | solution.py:698
  446.3 1.6 collective-permute-start.5
  448.0 28.8 %shard_map.267 = (bf16[320,2048]{1,0:T(8,128)(2,1)}, bf16[320,2048]{1,0:T(8,128)(2,1)}, f32[48,2048]{1,0:T(8,128)}, f32[48,2048]{1,0:T(8,128)}) custom-call(s32[1]{0:T(128)} %bitcast.16.slot_ref, bf16[4,320,2048]{2,1,0:T(8,128)(2,1)} %get-tuple-element.54.n_ref, bf16[320,2048]{1,0:T(8,128)(2,1)} %c_ref, ...), custom_call_target="tpu_custom_call" | custom-call | flops 16106127360 | bytes 25165824 | tf_op jit(solution)/shard_map/pallas_call | solution.py:698
  476.8 2.0 add_convert_fusion.7
  479.1 1.0 copy-done.13
  480.1 3.4 add_convert_fusion.6
  483.5 2.4 collective-permute-start.6
  485.9 1.7 collective-permute-start.8
  489.0 7.9 all-reduce.12
  537.5 1.3 add_convert_fusion.8
  538.8 4.6 add_convert_fusion.5
  543.4 2.3 collective-permute-start.7
  545.7 1.3 collective-permute-start.9
  547.0 1.9 fusion.167
  551.2 1.3 slice_bitcast_fusion.20
  552.5 1.5 pad_maximum_fusion.1
  553.9 17.8 %collective-permute-done.7 = bf16[320,2048]{1,0:T(8,128)(2,1)} collective-permute-done((bf16[320,2048]{1,0:T(8,128)(2,1)}, bf16[320,2048]{1,0:T(8,128)(2,1)}, u32[]{:S(2)}, u32[]{:S(2)}) %collective-permute-start.7) | collective-permute-done | bytes 1310752 | tf_op jit(solution)/shard_map/ppermute | solution.py:37
  571.7 5.2 collective-permute-done.9
  576.9 2.7 multiply_reduce_fusion.1
  579.7 5.3 fusion.316
  585.0 91.4 %shard_map.268 = (bf16[4,320,2048]{2,1,0:T(8,128)(2,1)}, bf16[1,1280,512]{2,1,0:T(8,128)(2,1)}, bf16[1280,128]{1,0:T(8,128)(2,1)}) custom-call(bf16[320,2048]{1,0:T(8,128)(2,1)} %get-tuple-element.92.b_ref, bf16[2048,2048]{1,0:T(8,128)(2,1)} %all-gather.7.cloned.1.call-done.w_ref, bf16[128,2048]{1,0:T(8,128)(2,1)} %pad.52.e_ref, bf16[128,512]{1,0:T(8,128)(2,1)} %pad.51.a_ref), custom_call_target="tpu_custom_call" | custom-call | tf_op jit(solution)/shard_map/pallas_call | solution.py:426
  676.4 29.3 %shard_map.269.d_ref = bf16[3,1280,512]{2,1,0:T(8,128)(2,1)} custom-call(bf16[3,1280,512]{2,1,0:T(8,128)(2,1)} %get-tuple-element.49.q_ref.k_ref.v_ref, bf16[3,1280,512]{2,1,0:T(8,128)(2,1)} %get-tuple-element.49.q_ref.k_ref.v_ref, bf16[3,1280,512]{2,1,0:T(8,128)(2,1)} %get-tuple-element.49.q_ref.k_ref.v_ref, bf16[1,1280,512]{2,1,0:T(8,128)(2,1)} %get-tuple-element.51.o_ref, ...), custom_call_target="tpu_custom_call" | custom-call | flops 16777216000 | bytes 10485760 | tf_op jit(solution)/shard_map/pallas_call | solution.py:623
  705.8 1.8 fusion.6
  707.5 1.8 fusion.7
  709.3 3.4 fusion.319
  712.7 99.9 %shard_map.270 = (bf16[320,2048]{1,0:T(8,128)(2,1)}, bf16[1280,128]{1,0:T(8,128)(2,1)}) custom-call(bf16[3,1280,512]{2,1,0:T(8,128)(2,1)} %shard_map.269.d_ref, bf16[2048,2048]{1,0:T(8,128)(2,1)} %all-gather.7.cloned.1.call-done.w_ref, bf16[128,1536]{1,0:T(8,128)(2,1)} %pad.50.a_ref, bf16[128,2048]{1,0:T(8,128)(2,1)} %fusion.20.e_ref, ...), custom_call_target="tpu_custom_call" | custom-call | tf_op jit(solution)/shard_map/pallas_call | solution.py:486
  812.6 3.6 fusion.318
  817.3 4.6 collective-permute-start.10
  822.7 1.6 fusion.8
  824.3 38.3 %all-reduce.16.cloned.1.call-done = (bf16[1,48,2048]{2,1,0:T(8,128)(2,1)}, bf16[1,64,2048]{2,1,0:T(8,128)(2,1)}) async-done(((bf16[1,48,2048]{2,1,0:T(8,128)(2,1)}, bf16[1,64,2048]{2,1,0:T(8,128)(2,1)}), (bf16[1,48,2048]{2,1,0:T(8,128)(2,1)}, bf16[1,64,2048]{2,1,0:T(8,128)(2,1)})) %all-reduce.16.cloned.1.call-update) | async-done | bytes 458768 | tf_op jit(solution)/shard_map/psum | solution.py:875
  862.6 9.8 %all_gather.38 = bf16[8,64,512]{2,1,0:T(8,128)(2,1)S(1)} all-gather(bf16[1,64,512]{2,1,0:T(8,128)(2,1)S(1)} %pad_maximum_fusion.5), channel_id=1, replica_groups=mesh['dp'=8,'tensor'=4] {'dp'}, dimensions={0}, use_global_device_ids=true | all-gather | bytes 589824 | tf_op jit(solution)/shard_map/all_gather | solution.py:748
  872.8 3.3 add_convert_fusion.3
  876.1 4.4 collective-permute-start.11
  880.5 1.7 collective-permute-start.13
  883.6 1.0 pad_maximum_fusion.4
  884.6 23.7 %collective-permute-done.11 = bf16[320,2048]{1,0:T(8,128)(2,1)} collective-permute-done((bf16[320,2048]{1,0:T(8,128)(2,1)}, bf16[320,2048]{1,0:T(8,128)(2,1)}, u32[]{:S(2)}, u32[]{:S(2)}) %collective-permute-start.11) | collective-permute-done | bytes 1310752 | tf_op jit(solution)/shard_map/ppermute | solution.py:37
  908.3 5.4 add_convert_fusion.2
  913.7 8.3 collective-permute-start.12
  922.0 1.5 collective-permute-start.14
  923.6 1.9 fusion.93
  928.0 2.7 copy-done.20
  930.7 18.0 %collective-permute-done.12 = bf16[320,2048]{1,0:T(8,128)(2,1)} collective-permute-done((bf16[320,2048]{1,0:T(8,128)(2,1)}, bf16[320,2048]{1,0:T(8,128)(2,1)}, u32[]{:S(2)}, u32[]{:S(2)}) %collective-permute-start.12) | collective-permute-done | bytes 1310752 | tf_op jit(solution)/shard_map/ppermute | solution.py:37
  948.6 5.2 collective-permute-done.14
  953.9 3.6 add_convert_fusion
  957.5 2.1 fusion.29
  962.8 1.0 fusion.10
  963.8 1.0 fusion.9
  964.9 1.5 pad_maximum_fusion.2
  966.7 1.1 copy.66
  (145 shorter events, 26.9 us)
Async XLA Ops:
  7.2 107.0 %copy-start = (bf16[5,8,2048,16]{2,3,1,0:T(8,128)(2,1)S(1)}, bf16[5,8,2048,16]{2,3,1,0:T(8,128)(2,1)}, u32[]{:S(2)}) copy-start(bf16[5,8,2048,16]{2,3,1,0:T(8,128)(2,1)} %param.32) | copy-start | bytes 7864324
  7.2 107.9 %all-gather.7.cloned.1.call-start = ((), (), s32[]{:S(2)}) async-start(), calls=%async_computation | async-start | bytes 9437184 | tf_op jit(solution)/shard_map/all_gather | solution.py:797
  9.7 349.7 %all-gather.9.cloned.1.call-start = ((), (), s32[]{:S(2)}) async-start(), calls=%async_computation.1 | async-start | bytes 28311552 | tf_op jit(solution)/shard_map/all_gather | solution.py:803
  13.0 0.7 copy-start.22
  13.0 534.0 %all-gather.15.cloned.1.call-start = ((), (), s32[]{:S(2)}) async-start(), calls=%async_computation.4 | async-start | bytes 1769472 | tf_op jit(solution)/shard_map/all_gather | solution.py:748
  14.3 97.6 %copy-start.24 = (s32[1,20]{1,0:T(1,128)S(1)}, s32[1,20]{1,0:T(1,128)}, u32[]{:S(2)}) copy-start(s32[1,20]{1,0:T(1,128)} %param.38) | copy-start | bytes 244
  109.3 44.9 %collective-permute-start = (bf16[320,2048]{1,0:T(8,128)(2,1)}, bf16[320,2048]{1,0:T(8,128)(2,1)}, u32[]{:S(2)}, u32[]{:S(2)}) collective-permute-start(bf16[320,2048]{1,0:T(8,128)(2,1)} %c_ref), channel_id=1, source_target_pairs={{0,1},{1,0},{2,3},{3,2},{4,5},{5,4},{6,7},{7,6},{8,9},{9,8},{10,11... | collective-permute-start | bytes 3932168 | tf_op jit(solution)/shard_map/ppermute | solution.py:37
  109.4 44.8 %collective-permute-start.1 = (bf16[320,2048]{1,0:T(8,128)(2,1)}, bf16[320,2048]{1,0:T(8,128)(2,1)}, u32[]{:S(2)}, u32[]{:S(2)}) collective-permute-start(bf16[320,2048]{1,0:T(8,128)(2,1)} %c_ref), channel_id=1, source_target_pairs={{1,2},{2,1},{5,6},{6,5},{9,10},{10,9},{13,14},{14,13},{17,18},{18,... | collective-permute-start | bytes 3932168 | tf_op jit(solution)/shard_map/ppermute | solution.py:37
  134.9 25.9 %copy-start.23 = (bf16[2048]{0:T(1024)(128)(2,1)S(1)}, bf16[2048]{0:T(1024)(128)(2,1)}, u32[]{:S(2)}) copy-start(bf16[2048]{0:T(1024)(128)(2,1)} %param.24) | copy-start | bytes 12292
  154.3 201.4 %collective-permute-start.2 = (bf16[320,2048]{1,0:T(8,128)(2,1)}, bf16[320,2048]{1,0:T(8,128)(2,1)S(1)}, u32[]{:S(2)}, u32[]{:S(2)}) collective-permute-start(bf16[320,2048]{1,0:T(8,128)(2,1)} %collective-permute-done.c_ref), channel_id=1, source_target_pairs={{2,0},{1,3},{6,4},{5,7},{10,8},{9,11},{14,12},{13,15},{18,16},{17,... | collective-permute-start | bytes 3932168 | tf_op jit(solution)/shard_map/ppermute | solution.py:37
  155.6 201.3 %collective-permute-start.4 = (bf16[320,2048]{1,0:T(8,128)(2,1)}, bf16[320,2048]{1,0:T(8,128)(2,1)S(1)}, u32[]{:S(2)}, u32[]{:S(2)}) collective-permute-start(bf16[320,2048]{1,0:T(8,128)(2,1)} %collective-permute-done.c_ref), channel_id=1, source_target_pairs={{1,2},{2,1},{5,6},{6,5},{9,10},{10,9},{13,14},{14,13},{17,18},{18,... | collective-permute-start | bytes 3932168 | tf_op jit(solution)/shard_map/ppermute | solution.py:37
  156.3 200.6 %collective-permute-start.3 = (bf16[320,2048]{1,0:T(8,128)(2,1)}, bf16[320,2048]{1,0:T(8,128)(2,1)}, u32[]{:S(2)}, u32[]{:S(2)}) collective-permute-start(bf16[320,2048]{1,0:T(8,128)(2,1)} %collective-permute-done.1), channel_id=1, source_target_pairs={{1,0},{2,3},{5,4},{6,7},{9,8},{10,11},{13,12},{14,15},{17,16},{18,... | collective-permute-start | bytes 3932168 | tf_op jit(solution)/shard_map/ppermute | solution.py:37
  417.1 29.2 %copy-start.11 = (bf16[320,2048]{1,0:T(8,128)(2,1)S(1)}, bf16[320,2048]{1,0:T(8,128)(2,1)}, u32[]{:S(2)}) copy-start(bf16[320,2048]{1,0:T(8,128)(2,1)} %get-tuple-element.68) | copy-start | bytes 3932164
  446.3 30.4 %copy-start.17 = (f32[48,2048]{1,0:T(8,128)S(1)}, f32[48,2048]{1,0:T(8,128)}, u32[]{:S(2)}) copy-start(f32[48,2048]{1,0:T(8,128)} %get-tuple-element.87) | copy-start | bytes 1179652
  446.3 32.7 %collective-permute-start.5 = (bf16[320,2048]{1,0:T(8,128)(2,1)S(1)}, bf16[320,2048]{1,0:T(8,128)(2,1)S(1)}, u32[]{:S(2)}, u32[]{:S(2)}) collective-permute-start(bf16[320,2048]{1,0:T(8,128)(2,1)S(1)} %copy-done.11), channel_id=1, source_target_pairs={{0,1},{3,2},{4,5},{7,6},{8,9},{11,10},{12,13},{15,14},{16,17},{19,... | collective-permute-start | bytes 3932168 | tf_op jit(solution)/shard_map/ppermute | solution.py:37
  476.7 10.9 %copy-start.25 = (u32[32]{0:T(128)S(1)}, u32[32]{0:T(128)}, u32[]{:S(2)}) copy-start(u32[32]{0:T(128)} %constant.137) | copy-start | bytes 388
  476.8 60.7 %copy-start.16 = (f32[48,2048]{1,0:T(8,128)S(1)}, f32[48,2048]{1,0:T(8,128)}, u32[]{:S(2)}) copy-start(f32[48,2048]{1,0:T(8,128)} %get-tuple-element.57) | copy-start | bytes 1179652
  478.8 383.7 %all-reduce.16.cloned.1.call-start = ((), (), s32[]{:S(2)}) async-start(), calls=%async_computation.5 | async-start | bytes 917504 | tf_op jit(solution)/shard_map/psum | solution.py:875
  479.1 1.1 copy-start.13
  480.1 58.7 %copy-start.12 = (bf16[320,2048]{1,0:T(8,128)(2,1)S(1)}, bf16[320,2048]{1,0:T(8,128)(2,1)}, u32[]{:S(2)}) copy-start(bf16[320,2048]{1,0:T(8,128)(2,1)} %get-tuple-element.69) | copy-start | bytes 3932164
  483.5 55.2 %collective-permute-start.6 = (bf16[320,2048]{1,0:T(8,128)(2,1)}, bf16[320,2048]{1,0:T(8,128)(2,1)}, u32[]{:S(2)}, u32[]{:S(2)}) collective-permute-start(bf16[320,2048]{1,0:T(8,128)(2,1)} %add_convert_fusion.6), channel_id=1, source_target_pairs={{0,1},{1,2},{4,5},{5,6},{8,9},{9,10},{12,13},{13,14},{16,17},{17,1... | collective-permute-start | bytes 3932168 | tf_op jit(solution)/shard_map/ppermute | solution.py:37
  485.9 52.9 %collective-permute-start.8 = (bf16[320,2048]{1,0:T(8,128)(2,1)}, bf16[320,2048]{1,0:T(8,128)(2,1)}, u32[]{:S(2)}, u32[]{:S(2)}) collective-permute-start(bf16[320,2048]{1,0:T(8,128)(2,1)} %add_convert_fusion.6), channel_id=1, source_target_pairs={{3,2},{2,1},{7,6},{6,5},{11,10},{10,9},{15,14},{14,13},{19,18},{18... | collective-permute-start | bytes 3932168 | tf_op jit(solution)/shard_map/ppermute | solution.py:37
  543.4 28.4 %collective-permute-start.7 = (bf16[320,2048]{1,0:T(8,128)(2,1)}, bf16[320,2048]{1,0:T(8,128)(2,1)}, u32[]{:S(2)}, u32[]{:S(2)}) collective-permute-start(bf16[320,2048]{1,0:T(8,128)(2,1)} %get-tuple-element.101), channel_id=1, source_target_pairs={{0,1},{1,2},{2,3},{4,5},{5,6},{6,7},{8,9},{9,10},{10,11},{12,13},{... | collective-permute-start | bytes 3932168 | tf_op jit(solution)/shard_map/ppermute | solution.py:37
  545.7 31.2 %collective-permute-start.9 = (bf16[320,2048]{1,0:T(8,128)(2,1)}, bf16[320,2048]{1,0:T(8,128)(2,1)}, u32[]{:S(2)}, u32[]{:S(2)}) collective-permute-start(bf16[320,2048]{1,0:T(8,128)(2,1)} %get-tuple-element.102), channel_id=1, source_target_pairs={{3,2},{2,1},{1,0},{7,6},{6,5},{5,4},{11,10},{10,9},{9,8},{15,14},{... | collective-permute-start | bytes 3932168 | tf_op jit(solution)/shard_map/ppermute | solution.py:37
  547.0 2.0 copy-start.3
  552.5 24.4 %copy-start.5 = (f32[320,2048]{1,0:T(8,128)S(1)}, f32[320,2048]{1,0:T(8,128)}, u32[]{:S(2)}) copy-start(f32[320,2048]{1,0:T(8,128)} %get-tuple-element.52) | copy-start | bytes 7864324
  552.5 24.4 %copy-start.8 = (bf16[320,2048]{1,0:T(8,128)(2,1)S(1)}, bf16[320,2048]{1,0:T(8,128)(2,1)}, u32[]{:S(2)}) copy-start(bf16[320,2048]{1,0:T(8,128)(2,1)} %get-tuple-element.67) | copy-start | bytes 3932164
  552.5 24.4 %copy-start.21 = (f32[2048]{0:T(1024)S(1)}, f32[2048]{0:T(1024)}, u32[]{:S(2)}) copy-start(f32[2048]{0:T(1024)} %convert_element_type.696) | copy-start | bytes 24580
  676.4 29.4 %copy-start.9 = (bf16[1280,128]{1,0:T(8,128)(2,1)S(1)}, bf16[1280,128]{1,0:T(8,128)(2,1)}, u32[]{:S(2)}) copy-start(bf16[1280,128]{1,0:T(8,128)(2,1)} %get-tuple-element.83) | copy-start | bytes 983044
  705.8 3.6 copy-start.18
  712.7 99.9 %copy-start.15 = (bf16[128,2048]{1,0:T(8,128)(2,1)}, bf16[128,2048]{1,0:T(8,128)(2,1)S(1)}, u32[]{:S(2)}) copy-start(bf16[128,2048]{1,0:T(8,128)(2,1)S(1)} %fusion.319) | copy-start | bytes 1572868
  812.6 4.3 copy-start.7
  812.6 4.3 copy-start.19
  812.6 9.2 slice-start
  817.3 55.5 %collective-permute-start.10 = (bf16[320,2048]{1,0:T(8,128)(2,1)}, bf16[320,2048]{1,0:T(8,128)(2,1)}, u32[]{:S(2)}, u32[]{:S(2)}) collective-permute-start(bf16[320,2048]{1,0:T(8,128)(2,1)} %get-tuple-element.73), channel_id=1, source_target_pairs={{0,1},{3,2},{4,5},{7,6},{8,9},{11,10},{12,13},{15,14},{16,17},{19,... | collective-permute-start | bytes 3932168 | tf_op jit(solution)/shard_map/ppermute | solution.py:37
  822.6 100.9 %all-gather.11.cloned.1.call-start = ((), (), s32[]{:S(2)}) async-start(), calls=%async_computation.2 | async-start | bytes 1769472 | tf_op jit(solution)/shard_map/all_gather | solution.py:748
  862.6 94.9 %all-gather.13.cloned.1.call-start = ((), (), s32[]{:S(2)}) async-start(), calls=%async_computation.3 | async-start | bytes 2359296 | tf_op jit(solution)/shard_map/all_gather | solution.py:748
  876.1 32.2 %collective-permute-start.11 = (bf16[320,2048]{1,0:T(8,128)(2,1)}, bf16[320,2048]{1,0:T(8,128)(2,1)}, u32[]{:S(2)}, u32[]{:S(2)}) collective-permute-start(bf16[320,2048]{1,0:T(8,128)(2,1)} %add_convert_fusion.3), channel_id=1, source_target_pairs={{0,1},{1,2},{4,5},{5,6},{8,9},{9,10},{12,13},{13,14},{16,17},{17,1... | collective-permute-start | bytes 3932168 | tf_op jit(solution)/shard_map/ppermute | solution.py:37
  880.5 27.8 %collective-permute-start.13 = (bf16[320,2048]{1,0:T(8,128)(2,1)}, bf16[320,2048]{1,0:T(8,128)(2,1)}, u32[]{:S(2)}, u32[]{:S(2)}) collective-permute-start(bf16[320,2048]{1,0:T(8,128)(2,1)} %add_convert_fusion.3), channel_id=1, source_target_pairs={{3,2},{2,1},{7,6},{6,5},{11,10},{10,9},{15,14},{14,13},{19,18},{18... | collective-permute-start | bytes 3932168 | tf_op jit(solution)/shard_map/ppermute | solution.py:37
  913.7 35.0 %collective-permute-start.12 = (bf16[320,2048]{1,0:T(8,128)(2,1)}, bf16[320,2048]{1,0:T(8,128)(2,1)}, u32[]{:S(2)}, u32[]{:S(2)}) collective-permute-start(bf16[320,2048]{1,0:T(8,128)(2,1)} %get-tuple-element.99), channel_id=1, source_target_pairs={{0,1},{1,2},{2,3},{4,5},{5,6},{6,7},{8,9},{9,10},{10,11},{12,13},{... | collective-permute-start | bytes 3932168 | tf_op jit(solution)/shard_map/ppermute | solution.py:37
  922.0 31.8 %collective-permute-start.14 = (bf16[320,2048]{1,0:T(8,128)(2,1)}, bf16[320,2048]{1,0:T(8,128)(2,1)}, u32[]{:S(2)}, u32[]{:S(2)}) collective-permute-start(bf16[320,2048]{1,0:T(8,128)(2,1)} %get-tuple-element.100), channel_id=1, source_target_pairs={{3,2},{2,1},{1,0},{7,6},{6,5},{5,4},{11,10},{10,9},{9,8},{15,14},{... | collective-permute-start | bytes 3932168 | tf_op jit(solution)/shard_map/ppermute | solution.py:37
  923.5 2.0 copy-start.4
  927.8 26.1 %copy-start.6 = (f32[320,2048]{1,0:T(8,128)S(1)}, f32[320,2048]{1,0:T(8,128)}, u32[]{:S(2)}) copy-start(f32[320,2048]{1,0:T(8,128)} %get-tuple-element.52) | copy-start | bytes 7864324
  927.8 26.0 %copy-start.14 = (bf16[320,2048]{1,0:T(8,128)(2,1)S(1)}, bf16[320,2048]{1,0:T(8,128)(2,1)}, u32[]{:S(2)}) copy-start(bf16[320,2048]{1,0:T(8,128)(2,1)} %get-tuple-element.72) | copy-start | bytes 3932164
  928.0 2.7 copy-start.20
  957.5 2.2 copy-start.2
  964.9 1.9 copy-start.10
  964.9 3.0 copy-start.1
Sparse Core Ops, SparseCore 0:
  10.5 57.0 all-gather.6
  69.5 125.3 all-gather.8
  479.0 23.8 all-gather.14
  822.7 39.7 all-reduce.15
  864.5 25.5 all-gather.10
  891.9 27.8 all-gather.12

commit v3 on v2

--- a/solution.py
+++ b/solution.py
@@ -11,7 +11,6 @@
 HEAD_DIM = 64
 TRUNK, BRANCHES = 8, 4
 QT = 256
-RANK_PAD = 128
 VMEM_LIMIT = 60 * 1024 * 1024
 LINE = 4
 MESH = pl.DeviceIdType.MESH
@@ -43,31 +42,11 @@
     return one, mid
 
 
-def line_gather_finish(value, one, mid, edge):
+def line_gather_finish(one, mid):
     two_edge = permute(mid, [(1, 0), (2, 3)])
     two_mid = permute(one, [(1, 2), (2, 1)])
     three_edge = permute(one, [(2, 0), (1, 3)])
-    two = jnp.where(edge, two_edge, two_mid)
-    three = jnp.where(edge, three_edge, mid)
-    return [value, one, two, three]
-
-
-def add_rows(left, right):
-    return (left.astype(f32) + right.astype(f32)).astype(bf16)
-
-
-def line_scatter(parts, place):
-    right = [(0, 1), (1, 2), (2, 3)]
-    left = [(3, 2), (2, 1), (1, 0)]
-    first = permute(parts[3], [(0, 1), (3, 2)])
-    held = add_rows(parts[2], first)
-    second_right = permute(held, right[:2])
-    second_left = permute(held, left[:2])
-    base_right = jnp.where(place == 1, parts[3], parts[1])
-    base_left = jnp.where(place == 2, parts[3], parts[1])
-    third_right = permute(add_rows(base_right, second_right), right)
-    third_left = permute(add_rows(base_left, second_left), left)
-    return parts[0].astype(f32) + third_right.astype(f32) + third_left.astype(f32)
+    return two_edge, two_mid, three_edge, mid
 
 
 def rope_tables(blocks, seg):
@@ -166,8 +145,8 @@
                 shard = self.place - side * step
                 self.copy(side, step, chunk, shard, self.place - side).wait_recv()
 
-    def drain(self):
-        for step in range(1, LINE):
+    def drain(self, stop=LINE, start=1):
+        for step in range(start, stop):
             for chunk in range(self.chunks):
                 self.each_send(step, chunk, lambda copy: copy.wait_send())
 
@@ -191,20 +170,26 @@
             device_id_type=MESH,
         )
 
-    def send(self, step, chunk):
+    def add(self, step, chunk):
         rows = chunk_rows(chunk, self.rows)
         for index, side in enumerate(SIDES):
             far = far_of(self.place, side)
             shard = self.place + side * (LINE - step)
-            if step > 1:
-
-                @pl.when((far >= 1) & (far <= step - 1))
-                def _():
-                    self.copy(side, step - 1, chunk, self.place, self.place - side).wait_recv()
-                    self.part[shard, rows] = (
-                        self.part[shard, rows].astype(f32)
-                        + self.held[index, step - 2, rows].astype(f32)
-                    ).astype(bf16)
+
+            @pl.when((far >= 1) & (far <= step - 1))
+            def _():
+                self.copy(side, step - 1, chunk, self.place, self.place - side).wait_recv()
+                self.part[shard, rows] = (
+                    self.part[shard, rows].astype(f32)
+                    + self.held[index, step - 2, rows].astype(f32)
+                ).astype(bf16)
+
+    def send(self, step, chunk):
+        if step > 1:
+            self.add(step, chunk)
+        for side in SIDES:
+            far = far_of(self.place, side)
+            shard = self.place + side * (LINE - step)
 
             @pl.when(far <= step - 1)
             def _():
@@ -220,8 +205,8 @@
                 self.copy(side, LINE - 1, chunk, self.place, self.place - side).wait_recv()
                 out[rows] += self.held[index, LINE - 2, rows].astype(f32)
 
-    def drain(self):
-        for step in range(1, LINE):
+    def drain(self, stop=LINE):
+        for step in range(1, stop):
             for chunk in range(self.chunks):
                 for side in SIDES:
                     far = far_of(self.place, side)
@@ -253,79 +238,101 @@
     )
 
 
-def gather_norm_body(x_ref, gain_ref, buf, send, recv):
+def gather_norm_body(x_ref, gain_ref, wg_ref, wu_ref, wd_ref, buf, w_ref, wsem, send, recv):
     place = lax.axis_index("tensor")
+    width = wg_ref.shape[1]
+    loads = fetch(
+        [(w, w_ref.at[:, k * width : (k + 1) * width]) for k, w in enumerate((wg_ref, wu_ref, wd_ref))],
+        wsem,
+    )
     greet(place)
     rows = x_ref[...].astype(f32)
     rms = lax.rsqrt(jnp.mean(rows * rows, axis=1, keepdims=True) + eps)
     buf[place] = (rows * rms * gain_ref[...]).astype(bf16)
     gather = Gather(place, buf, send, recv, 1)
-    gather.send(1, 0)
-    for step in range(1, LINE):
+    for step in range(1, LINE - 1):
+        gather.send(step, 0)
         gather.arrive(step, 0)
-        if step < LINE - 1:
-            gather.send(step + 1, 0)
-    gather.drain()
-
-
-def gather_norm(x, gain):
+    gather.drain(stop=LINE - 1)
+    for load in loads:
+        load.wait()
+
+
+def gather_norm(x, gain, weights):
     rows, features = x.shape
+    deep, width = weights[0].shape
     return pl.pallas_call(
         gather_norm_body,
-        in_specs=[IN_VMEM, IN_VMEM],
-        out_specs=IN_VMEM,
-        out_shape=jax.ShapeDtypeStruct((LINE, rows, features), bf16),
-        scratch_shapes=line_sems(1),
+        in_specs=[IN_VMEM, IN_VMEM] + [IN_HBM] * 3,
+        out_specs=[IN_VMEM, IN_HBM],
+        out_shape=[
+            jax.ShapeDtypeStruct((LINE, rows, features), bf16),
+            jax.ShapeDtypeStruct((deep, 3 * width), bf16),
+        ],
+        scratch_shapes=[pltpu.SemaphoreType.DMA((3,))] + line_sems(1),
         compiler_params=comm_params(0),
-    )(x, gain[None, :])
-
-
-def project_body(groups, x_ref, w_ref, e_ref, a_ref, cos_ref, sin_ref, y_ref, l_ref):
-    tile = pl.program_id(0)
-
-    @pl.when(tile == 0)
-    def _():
-        l_ref[...] = nt(x_ref[...], e_ref[...]).astype(bf16)
-
-    total = nn(x_ref[...], w_ref[...]) + nn(l_ref[...], a_ref[...])
-
-    @pl.when(tile < pl.num_programs(0) // groups * (groups - 1))
-    def _():
-        y_ref[0] = turn(total, cos_ref[...], sin_ref[...]).astype(bf16)
-
-    @pl.when(tile >= pl.num_programs(0) // groups * (groups - 1))
-    def _():
-        y_ref[0] = total.astype(bf16)
-
-
-def project(x, weight, entry, exits, groups, tables, tile=256):
-    rows, features = x.shape
-    width = exits.shape[1] // groups
-    per = width // tile
+    )(x, gain[None, :], *weights)
+
+
+def project_body(
+    x_ref, w_ref, e_ref, a_ref, cos_ref, sin_ref, buf, y_ref, l_ref, wv, xsem, wsem, send, recv
+):
+    place = lax.axis_index("tensor")
+    groups, _, width = y_ref.shape
+    rows, rank = x_ref.shape[1], a_ref.shape[1]
+    edge = (place == 0) | (place == LINE - 1)
+    copies = []
+    for slot in range(LINE):
+        copy = pltpu.make_async_copy(x_ref.at[place ^ slot], buf.at[place ^ slot], xsem.at[slot])
+        if slot < LINE - 1:
+            copy.start()
+        else:
+            pl.when(jnp.logical_not(edge))(copy.start)
+        copies.append(copy)
+    (load,) = fetch([(w_ref.at[:, : groups * width], wv)], wsem)
+    greet(place)
+    for copy in copies[:-1]:
+        copy.wait()
+    gather = Gather(place, buf, send, recv, 1)
+    gather.send(LINE - 1, 0)
+    load.wait()
+    for slot in range(LINE):
+        if slot == LINE - 1:
+            pl.when(jnp.logical_not(edge))(copies[slot].wait)
+            gather.arrive(slot, 0)
+        shard = place ^ slot
+        mine = pl.ds(pl.multiple_of(shard * rows, rows), rows)
+        low = nt(buf[shard], e_ref[:groups].reshape(groups * rank, -1)).astype(bf16)
+        l_ref[mine] = low
+        for g in range(groups):
+            band = slice(g * width, (g + 1) * width)
+            value = nn(buf[shard], wv[:, band]) + nn(low[:, g * rank : (g + 1) * rank], a_ref[g])
+            if g < groups - 1:
+                value = turn(value, cos_ref[mine], sin_ref[mine])
+            y_ref[g, mine] = value.astype(bf16)
+    gather.drain(start=LINE - 1)
+
+
+def project(x, weight, entries, exits, tables):
+    _, rows, features = x.shape
+    groups, rank, width = exits.shape
     return pl.pallas_call(
-        functools.partial(project_body, groups),
-        grid=(groups * per,),
-        in_specs=[
-            pl.BlockSpec((rows, features), lambda i: (0, 0)),
-            pl.BlockSpec((features, tile), lambda i: (0, i)),
-            pl.BlockSpec((RANK_PAD, features), lambda i: (0, 0)),
-            pl.BlockSpec((RANK_PAD, tile), lambda i: (0, i)),
-            pl.BlockSpec((rows, tables[0].shape[1]), lambda i: (0, 0)),
-            pl.BlockSpec((rows, tables[0].shape[1]), lambda i: (0, 0)),
+        project_body,
+        in_specs=[IN_HBM, IN_HBM] + [IN_VMEM] * 4,
+        out_specs=[IN_VMEM] * 3,
+        out_shape=[
+            jax.ShapeDtypeStruct((LINE, rows, features), bf16),
+            jax.ShapeDtypeStruct((groups, LINE * rows, width), bf16),
+            jax.ShapeDtypeStruct((LINE * rows, groups * rank), bf16),
         ],
-        out_specs=[
-            pl.BlockSpec((1, rows, tile), lambda i: (i // per, 0, i % per)),
-            pl.BlockSpec((rows, RANK_PAD), lambda i: (0, 0)),
-        ],
-        out_shape=[
-            jax.ShapeDtypeStruct((groups, rows, width), bf16),
-            jax.ShapeDtypeStruct((rows, RANK_PAD), bf16),
-        ],
-        compiler_params=pltpu.CompilerParams(vmem_limit_bytes=VMEM_LIMIT),
-        cost_estimate=pl.CostEstimate(
-            flops=2 * rows * features * exits.shape[1], bytes_accessed=2 * rows * features, transcendentals=0
-        ),
-    )(x, weight, entry, exits, *tables)
+        scratch_shapes=[
+            pltpu.VMEM((features, groups * width), bf16),
+            pltpu.SemaphoreType.DMA((LINE,)),
+            pltpu.SemaphoreType.DMA((1,)),
+        ]
+        + line_sems(1),
+        compiler_params=comm_params(4),
+    )(x, weight, entries, exits, *tables)
 
 
 def middle_body(
@@ -346,7 +353,7 @@
         d = d_ref[mine]
         low = nt(d, a_ref[...]).astype(bf16)
         low_ref[mine] = low
-        part[shard] = (nt(d, wv[...]) + nn(low, e_ref[...])).astype(bf16)
+        part[shard] = (nt(d, wv[...]) + nn(low, e_ref[0])).astype(bf16)
         if slot == 3:
             for chunk in range(chunks):
                 summed.send(1, chunk)
@@ -373,7 +380,7 @@
     gather.drain()
 
 
-def middle_rows(attended, weight, exits, entry, x, gain, chunks=4):
+def middle_rows(attended, weight, exits, finals, x, gain, chunks=4):
     rows, features = x.shape
     width = attended.shape[1]
     return pl.pallas_call(
@@ -383,7 +390,7 @@
         out_shape=[
             jax.ShapeDtypeStruct((rows, features), f32),
             jax.ShapeDtypeStruct((LINE, rows, features), bf16),
-            jax.ShapeDtypeStruct((LINE * rows, RANK_PAD), bf16),
+            jax.ShapeDtypeStruct((LINE * rows, exits.shape[0]), bf16),
         ],
         scratch_shapes=[
             pltpu.VMEM((LINE, rows, features), bf16),
@@ -394,80 +401,141 @@
         + line_sems(chunks)
         + line_sems(chunks),
         compiler_params=comm_params(1),
-    )(attended, weight, exits, entry, x, gain[None, :])
-
-
-def branch_body(b_ref, w_ref, e_ref, a_ref, buf, y_ref, l_ref, wv, wsem, send, recv):
+    )(attended, weight, exits, finals, x, gain[None, :])
+
+
+def branch_body(
+    b_ref, w_ref, e_ref, a_ref, p_ref, buf, y_ref, l_ref, out_ref,
+    part, held, wv, wsem, send, recv, s_send, s_recv,
+):
     place = lax.axis_index("tensor")
     rows = b_ref.shape[0]
-    width = y_ref.shape[2]
-    (load,) = fetch([(w_ref.at[:, 3 * width :], wv)], wsem)
+    load, parts = fetch([(w_ref.at[:, 3 * y_ref.shape[2] :], wv), (p_ref, part)], wsem)
     greet(place)
     buf[place] = b_ref[...]
     gather = Gather(place, buf, send, recv, 1)
+    summed = Sum(place, part, held, s_send, s_recv, 1)
     gather.send(1, 0)
+    parts.wait()
+    summed.send(1, 0)
     load.wait()
     for slot in range(LINE):
         if slot:
             gather.arrive(slot, 0)
-            if slot < LINE - 1:
-                gather.send(slot + 1, 0)
+        if 0 < slot < LINE - 1:
+            gather.send(slot + 1, 0)
+        if slot == 1:
+            summed.send(2, 0)
+        if slot == 2:
+            summed.add(3, 0)
+            out_ref[0] = part[place]
+            for index, side in enumerate(SIDES):
+
+                @pl.when(far_of(place, side) < LINE - 1)
+                def _():
+                    out_ref[index + 1] = part[place + side]
+
+                @pl.when(far_of(place, side) == LINE - 1)
+                def _():
+                    out_ref[index + 1] = jnp.zeros_like(part[place])
+
         shard = place ^ slot
         mine = pl.ds(pl.multiple_of(shard * rows, rows), rows)
-        low = nt(buf[shard], e_ref[...]).astype(bf16)
+        low = nt(buf[shard], e_ref[0]).astype(bf16)
         l_ref[mine] = low
         y_ref[0, mine] = (nn(buf[shard], wv[...]) + nn(low, a_ref[...])).astype(bf16)
     gather.drain()
-
-
-def branch_back(branch, weight, entry, exits):
+    summed.drain(LINE - 1)
+
+
+def branch_back(branch, weight, finals, exits, parts):
     rows, features = branch.shape
-    width = exits.shape[1]
+    rank, width = exits.shape
     return pl.pallas_call(
         branch_body,
-        in_specs=[IN_VMEM, IN_HBM, IN_VMEM, IN_VMEM],
-        out_specs=[IN_VMEM] * 3,
+        in_specs=[IN_VMEM, IN_HBM, IN_VMEM, IN_VMEM, IN_HBM],
+        out_specs=[IN_VMEM] * 4,
         out_shape=[
             jax.ShapeDtypeStruct((LINE, rows, features), bf16),
             jax.ShapeDtypeStruct((1, LINE * rows, width), bf16),
-            jax.ShapeDtypeStruct((LINE * rows, RANK_PAD), bf16),
+            jax.ShapeDtypeStruct((LINE * rows, rank), bf16),
+            jax.ShapeDtypeStruct((3, rows, features), bf16),
         ],
-        scratch_shapes=[pltpu.VMEM((features, width), bf16), pltpu.SemaphoreType.DMA((1,))]
+        scratch_shapes=[
+            pltpu.VMEM((LINE, rows, features), bf16),
+            pltpu.VMEM((2, LINE - 1, rows, features), bf16),
+            pltpu.VMEM((features, width), bf16),
+            pltpu.SemaphoreType.DMA((2,)),
+        ]
+        + line_sems(1)
         + line_sems(1),
         compiler_params=comm_params(2),
-    )(branch, weight, entry, exits)
+    )(branch, weight, finals, exits, parts)
 
 
 def tokens_body(
-    chunks, d_ref, w_ref, a_ref, e_ref, x_ref, gain_ref, mid_ref, out_ref, low_ref,
-    part, held, acc, dv, wv, wsem, send, recv,
+    chunks, d_ref, w_ref, a_ref, e_ref, x_ref, gain_ref, mid_ref, n_ref, b_ref, lone_ref, lo_ref, bo_ref, o_ref,
+    out_ref, model_ref, head_ref,
+    part, held, acc, dv, wv, midv, nv, bv, low, block, extra, wsem, send, recv, x_send, x_recv,
 ):
     place = lax.axis_index("tensor")
-    groups, _, width = d_ref.shape
-    loads = fetch([(d_ref, dv), (w_ref.at[:, : groups * width], wv)], wsem)
+    groups, total, width = d_ref.shape
+    rank = a_ref.shape[1]
+    loads = fetch(
+        [(d_ref, dv), (w_ref.at[:, : groups * width], wv), (n_ref, nv), (b_ref, bv), (mid_ref, midv)],
+        wsem,
+    )
+    block[...] = jnp.zeros_like(block)
+    for g in range(groups):
+        block[g * rank : (g + 1) * rank, g * width : (g + 1) * width] = a_ref[g]
     greet(place)
-    for load in loads:
+    for load in loads[:2]:
         load.wait()
     rows = part.shape[1]
     summed = Sum(place, part, held, send, recv, chunks)
+    entry = e_ref[:groups].reshape(groups * rank, -1)
     for slot in (3, 2, 1, 0):
         shard = place ^ slot
         mine = pl.ds(pl.multiple_of(shard * rows, rows), rows)
         d = jnp.concatenate([dv[g, mine] for g in range(groups)], axis=1)
-        low = nt(d, a_ref[...]).astype(bf16)
-        low_ref[mine] = low
-        part[shard] = (nt(d, wv[...]) + nn(low, e_ref[...])).astype(bf16)
+        mine_low = nt(d, block[...]).astype(bf16)
+        low[mine] = mine_low
+        part[shard] = (nt(d, wv[...]) + nn(mine_low, entry)).astype(bf16)
         if slot == 3:
             for chunk in range(chunks):
                 summed.send(1, chunk)
+    summed.send(2, 0)
+    for load in loads[2:]:
+        load.wait()
+
+    def turned(value):
+        return value.astype(f32).T.astype(bf16)
+
+    joined = nn(turned(low[...]), nv[...].reshape(total, -1))
+    final = nn(turned(lo_ref[...]), bv[...].reshape(total, -1))
+    extra[place] = jnp.concatenate([joined, final], axis=0).astype(bf16)
+    gather = Gather(place, extra, x_send, x_recv, 1)
+    gather.send(1, 0)
+    summed.send(3, 0)
+    low_one = turned(lone_ref[...])
+    for g in range(groups):
+        band = slice(g * rank, (g + 1) * rank)
+        head_ref[band] = nn(low_one[band], dv[g]).astype(bf16)
+    head_ref[groups * rank :] = nn(turned(bo_ref[...]), o_ref[...]).astype(bf16)
     size = rows // chunks
-    for chunk in range(chunks):
+    for chunk in range(1, chunks):
         summed.send(2, chunk)
         summed.send(3, chunk)
-        if chunk:
-            finish_tokens(summed, chunk - 1, size, acc, x_ref, gain_ref, mid_ref, out_ref)
-    finish_tokens(summed, chunks - 1, size, acc, x_ref, gain_ref, mid_ref, out_ref)
+        gather.arrive(chunk, 0)
+        if chunk < LINE - 1:
+            gather.send(chunk + 1, 0)
+        finish_tokens(summed, chunk - 1, size, acc, x_ref, gain_ref, midv, out_ref)
+    model_ref[...] = functools.reduce(
+        jnp.add, [extra[shard].astype(f32) for shard in range(LINE)]
+    ).astype(bf16)
+    finish_tokens(summed, chunks - 1, size, acc, x_ref, gain_ref, midv, out_ref)
     summed.drain()
+    gather.drain()
 
 
 def finish_tokens(summed, chunk, size, acc, x_ref, gain_ref, mid_ref, out_ref):
@@ -480,16 +548,22 @@
     out_ref[here] = (mid_ref[here] + rms * (scaled - rows * (rms * rms) * mean)).astype(bf16)
 
 
-def tokens_back(head_grads, weight, exits, entry, x, gain, grad_middle, chunks=4):
+def tokens_back(
+    head_grads, weight, exits, entries, x, gain, grad_middle, normed, branch, low_one, low_out, back_out, attended
+):
+    chunks = LINE
     rows, features = x.shape
     groups, total, width = head_grads.shape
+    rank = exits.shape[1]
+    deep = (groups + 1) * rank
     return pl.pallas_call(
         functools.partial(tokens_body, chunks),
-        in_specs=[IN_HBM, IN_HBM] + [IN_VMEM] * 5,
-        out_specs=[IN_VMEM] * 2,
+        in_specs=[IN_HBM, IN_HBM] + [IN_VMEM] * 4 + [IN_HBM] * 3 + [IN_VMEM] * 4,
+        out_specs=[IN_VMEM] * 3,
         out_shape=[
             jax.ShapeDtypeStruct((rows, features), bf16),
-            jax.ShapeDtypeStruct((total, RANK_PAD), bf16),
+            jax.ShapeDtypeStruct((deep, features), bf16),
+            jax.ShapeDtypeStruct((deep, width), bf16),
         ],
         scratch_shapes=[
             pltpu.VMEM((LINE, rows, features), bf16),
@@ -497,11 +571,21 @@
             pltpu.VMEM((rows, features), f32),
             pltpu.VMEM((groups, total, width), bf16),
             pltpu.VMEM((features, groups * width), bf16),
-            pltpu.SemaphoreType.DMA((2,)),
+            pltpu.VMEM((rows, features), f32),
+            pltpu.VMEM((LINE, rows, features), bf16),
+            pltpu.VMEM((LINE, rows, features), bf16),
+            pltpu.VMEM((total, groups * rank), bf16),
+            pltpu.VMEM((groups * rank, groups * width), bf16),
+            pltpu.VMEM((LINE, deep, features), bf16),
+            pltpu.SemaphoreType.DMA((5,)),
         ]
-        + line_sems(chunks),
+        + line_sems(chunks)
+        + line_sems(1),
         compiler_params=comm_params(3),
-    )(head_grads, weight, exits, entry, x, gain[None, :], grad_middle)
+    )(
+        head_grads, weight, exits, entries, x, gain[None, :], grad_middle, normed, branch,
+        low_one, low_out, back_out, attended,
+    )
 
 
 def tree_tiles(seg, rows, parent_row):
@@ -647,105 +731,196 @@
 
 
 def feed_body(
-    rank, slot_ref, n_ref, c_ref, wg_ref, wu_ref, wd_ref, xg_ref, xu_ref, xd_ref, e_ref, f_ref,
-    res_ref, back_ref, unit_ref, model_ref, low, low_t, acc_res, acc_back, acc_low,
+    rank, tile, chunks,
+    n_ref, c0_ref, c1_ref, c2e_ref, c2m_ref, c3e_ref, c3m_ref, w_ref, mid_ref,
+    xu_in, xd_in, e_in, f_in, gain_ref,
+    grad_ref, low_grad_ref, res_ref, unit_ref, model_ref,
+    x_ref, e_ref, f_ref, midv, nbuf, cbuf, wbuf, low, low_t, acc_res, acc_back, acc_low, part, held, resv,
+    nsem, csem, wsem, rsem, msem, send, recv,
 ):
-    tile = pl.program_id(0)
-
-    @pl.when(tile == 0)
-    def _():
-        first = nt(n_ref[0], e_ref[...]) + nt(c_ref[...], f_ref[...])
+    place = lax.axis_index("tensor")
+    edge = (place == 0) | (place == LINE - 1)
+    units = unit_ref.shape[1]
+    tiles = units // tile
+    summed = Sum(place, part, held, send, recv, chunks)
+
+    def load_rows(order, act):
+        into = order % 2
+        slot = LINE - 1 - order
+        act(pltpu.make_async_copy(n_ref.at[place ^ slot], nbuf.at[into], nsem.at[into]))
+        for number, at_edge, inside in (
+            (3, c3e_ref, c3m_ref),
+            (2, c2e_ref, c2m_ref),
+            (1, c1_ref, c1_ref),
+            (0, c0_ref, c0_ref),
+        ):
+            if at_edge is inside:
+
+                @pl.when(slot == number)
+                def _():
+                    act(pltpu.make_async_copy(inside, cbuf.at[into], csem.at[into]))
+            else:
+
+                @pl.when((slot == number) & edge)
+                def _():
+                    act(pltpu.make_async_copy(at_edge, cbuf.at[into], csem.at[into]))
+
+                @pl.when((slot == number) & jnp.logical_not(edge))
+                def _():
+                    act(pltpu.make_async_copy(inside, cbuf.at[into], csem.at[into]))
+
+    def load_weights(index, into, act):
+        for k in range(3):
+            columns = pl.ds(pl.multiple_of(k * units + index * tile, tile), tile)
+            act(pltpu.make_async_copy(w_ref.at[:, columns], wbuf.at[into, k], wsem.at[into, k]))
+
+    def start(copy):
+        copy.start()
+
+    def wait(copy):
+        copy.wait()
+
+    load_rows(jnp.int32(0), start)
+    load_weights(0, 0, start)
+    (load_middle,) = fetch([(mid_ref, midv)], msem)
+    for padded in (x_ref, e_ref, f_ref):
+        padded[...] = jnp.zeros_like(padded)
+    x_ref[0, :rank] = xu_in[0]
+    x_ref[1, rank : 2 * rank] = xu_in[1]
+    x_ref[2, 2 * rank :] = xd_in[...]
+    e_ref[: 2 * rank] = e_in[3:].reshape(2 * rank, -1)
+    f_ref[2 * rank :] = f_in[1]
+    unit_ref[...] = jnp.zeros_like(unit_ref)
+    model_ref[...] = jnp.zeros_like(model_ref)
+    greet(place)
+
+    def one_shard(order, carry):
+        into = order % 2
+        shard = place ^ (LINE - 1 - order)
+        load_rows(order, wait)
+
+        @pl.when(order < LINE - 1)
+        def _():
+            load_rows(order + 1, start)
+
+        first = nt(nbuf[into], e_ref[...]) + nt(cbuf[into], f_ref[...])
         low[...] = first.astype(bf16)
         low_t[...] = first.T.astype(bf16)
         acc_res[...] = jnp.zeros_like(acc_res)
         acc_back[...] = jnp.zeros_like(acc_back)
         acc_low[...] = jnp.zeros_like(acc_low)
 
-    gate = nn(n_ref[0], wg_ref[...]) + nn(low[...], xg_ref[...])
-    rise = nn(n_ref[0], wu_ref[...]) + nn(low[...], xu_ref[...])
-    grad_hidden = nn(c_ref[...], wd_ref[...]) + nn(low[...], xd_ref[...])
-    sigmoid = jax.nn.sigmoid(gate)
-    silu = gate * sigmoid
-    hidden = (silu * rise).astype(bf16)
-    grad_gate = (grad_hidden * rise * sigmoid * (1.0 + gate * (1.0 - sigmoid))).astype(bf16)
-    grad_rise = (grad_hidden * silu).astype(bf16)
-    acc_back[...] += nt(grad_gate, wg_ref[...]) + nt(grad_rise, wu_ref[...])
-    acc_res[...] += nt(hidden, wd_ref[...])
-    acc_low[...] += (
-        nt(grad_gate, xg_ref[...]) + nt(grad_rise, xu_ref[...]) + nt(hidden, xd_ref[...])
-    )
-    unit_ref[:rank] = nn(low_t[:rank], grad_gate)
-    unit_ref[rank : 2 * rank] = nn(low_t[rank : 2 * rank], grad_rise)
-    unit_ref[2 * rank :] = nn(low_t[2 * rank : 3 * rank], hidden)
-
-    @pl.when(tile == pl.num_programs(0) - 1)
-    def _():
+        def one_tile(index, carry):
+            stage = order * tiles + index
+            at = stage % 2
+            load_weights(index, at, wait)
+
+            @pl.when(stage < LINE * tiles - 1)
+            def _():
+                load_weights((index + 1) % tiles, 1 - at, start)
+
+            columns = pl.ds(pl.multiple_of(index * tile, tile), tile)
+            x_gate, x_rise, x_fall = x_ref[0, :, columns], x_ref[1, :, columns], x_ref[2, :, columns]
+            gate = nn(nbuf[into], wbuf[at, 0]) + nn(low[...], x_gate)
+            rise = nn(nbuf[into], wbuf[at, 1]) + nn(low[...], x_rise)
+            grad_hidden = nn(cbuf[into], wbuf[at, 2]) + nn(low[...], x_fall)
+            sigmoid = jax.nn.sigmoid(gate)
+            silu = gate * sigmoid
+            hidden = (silu * rise).astype(bf16)
+            grad_gate = (grad_hidden * rise * sigmoid * (1.0 + gate * (1.0 - sigmoid))).astype(bf16)
+            grad_rise = (grad_hidden * silu).astype(bf16)
+            acc_back[...] += nt(grad_gate, wbuf[at, 0]) + nt(grad_rise, wbuf[at, 1])
+            acc_res[...] += nt(hidden, wbuf[at, 2])
+            acc_low[...] += nt(grad_gate, x_gate) + nt(grad_rise, x_rise) + nt(hidden, x_fall)
+            unit_ref[:rank, columns] += nn(low_t[:rank], grad_gate)
+            unit_ref[rank : 2 * rank, columns] += nn(low_t[rank : 2 * rank], grad_rise)
+            unit_ref[2 * rank :, columns] += nn(low_t[2 * rank : 3 * rank], hidden)
+            return carry
+
+        lax.fori_loop(0, tiles, one_tile, 0)
         joined = acc_low[...].astype(bf16)
         joined_t = acc_low[...].T.astype(bf16)
-        back_ref[...] = (acc_back[...] + nn(joined, e_ref[...])).astype(bf16)
-        res_ref[...] = (acc_res[...] + nn(joined, f_ref[...])).astype(bf16)
-        model_ref[: 2 * rank] = nn(joined_t[: 2 * rank], n_ref[0])
-        model_ref[2 * rank :] = nn(joined_t[2 * rank : 3 * rank], c_ref[...])
-
-
-def feed(slot, normed, cot, weight, x_gate, x_rise, x_fall, entry, final, rank, tile=512):
+        part[shard] = (acc_back[...] + nn(joined, e_ref[...])).astype(bf16)
+
+        @pl.when(order > 0)
+        def _():
+            pltpu.make_async_copy(resv, res_ref.at[shard], rsem.at[0]).wait()
+
+        resv[...] = (acc_res[...] + nn(joined, f_ref[...])).astype(bf16)
+        pltpu.make_async_copy(resv, res_ref.at[shard], rsem.at[0]).start()
+        for step in (1, 2, 3):
+
+            @pl.when(order == step - 1)
+            def _():
+                for chunk in range(chunks):
+                    summed.send(step, chunk)
+
+        model_ref[: 2 * rank] += nn(joined_t[: 2 * rank], nbuf[into])
+        model_ref[2 * rank :] += nn(joined_t[2 * rank : 3 * rank], cbuf[into])
+        return carry
+
+    lax.fori_loop(0, LINE, one_shard, 0)
+    size = part.shape[1] // chunks
+    last = (LINE - 1) % 2
+    load_middle.wait()
+    for chunk in range(chunks):
+        summed.total(chunk, acc_back)
+        here = chunk_rows(chunk, size)
+        middle = midv[here]
+        rms = lax.rsqrt(jnp.mean(middle * middle, axis=1, keepdims=True) + eps)
+        scaled = acc_back[here] * gain_ref[...]
+        mean = jnp.mean(scaled * middle, axis=1, keepdims=True)
+        grad = cbuf[last, here].astype(f32) + rms * (scaled - middle * (rms * rms) * mean)
+        grad_ref[here] = grad
+        low_grad_ref[here] = grad.astype(bf16)
+    pltpu.make_async_copy(resv, res_ref.at[place], rsem.at[0]).wait()
+    summed.drain()
+
+
+def feed(normed, cots, weight, middle, units_exit, fall_entry, entries, finals, gain, tile=512, chunks=4):
     _, rows, features = normed.shape
     units = weight.shape[1] // 3
-    tiles = units // tile
-    whole = pl.BlockSpec((rows, features), lambda i, s: (0, 0))
-    exits = pl.BlockSpec((RANK_PAD, tile), lambda i, s: (0, i))
-    entries = pl.BlockSpec((RANK_PAD, features), lambda i, s: (0, 0))
+    rank = fall_entry.shape[0]
     return pl.pallas_call(
-        functools.partial(feed_body, rank),
-        grid_spec=pltpu.PrefetchScalarGridSpec(
-            num_scalar_prefetch=1,
-            grid=(tiles,),
-            in_specs=[pl.BlockSpec((1, rows, features), lambda i, s: (s[0], 0, 0)), whole]
-            + [pl.BlockSpec((features, tile), lambda i, s, k=k: (0, k * tiles + i)) for k in range(3)]
-            + [exits, exits, exits, entries, entries],
-            out_specs=[
-                whole,
-                whole,
-                pl.BlockSpec((3 * rank, tile), lambda i, s: (0, i)),
-                pl.BlockSpec((3 * rank, features), lambda i, s: (0, 0)),
-            ],
-            scratch_shapes=[
-                pltpu.VMEM((rows, RANK_PAD), bf16),
-                pltpu.VMEM((RANK_PAD, rows), bf16),
-                pltpu.VMEM((rows, features), f32),
-                pltpu.VMEM((rows, features), f32),
-                pltpu.VMEM((rows, RANK_PAD), f32),
-            ],
-        ),
+        functools.partial(feed_body, rank, tile, chunks),
+        in_specs=[IN_HBM] * 9 + [IN_VMEM] * 5,
+        out_specs=[IN_VMEM, IN_VMEM, IN_HBM, IN_VMEM, IN_VMEM],
         out_shape=[
+            jax.ShapeDtypeStruct((rows, features), f32),
             jax.ShapeDtypeStruct((rows, features), bf16),
-            jax.ShapeDtypeStruct((rows, features), bf16),
+            jax.ShapeDtypeStruct((LINE, rows, features), bf16),
             jax.ShapeDtypeStruct((3 * rank, units), f32),
             jax.ShapeDtypeStruct((3 * rank, features), f32),
         ],
-        compiler_params=pltpu.CompilerParams(vmem_limit_bytes=VMEM_LIMIT),
-        cost_estimate=pl.CostEstimate(
-            flops=12 * rows * features * units, bytes_accessed=6 * features * units, transcendentals=0
-        ),
-    )(slot, normed, cot, weight, weight, weight, x_gate, x_rise, x_fall, entry, final)
-
-
-def norm_backward(rows, rms, gain, grad):
-    scaled = grad * gain
-    return rms * (scaled - rows * (rms * rms) * jnp.mean(scaled * rows, axis=1, keepdims=True))
-
-
-def stack_rows(blocks, rows=RANK_PAD):
-    joined = jnp.concatenate(blocks, axis=0)
-    return jnp.pad(joined, ((0, rows - joined.shape[0]), (0, 0)))
-
-
-def place_rows(block, start):
-    return jnp.pad(block, ((start, RANK_PAD - start - block.shape[0]), (0, 0)))
+        scratch_shapes=[
+            pltpu.VMEM((3, 3 * rank, units), bf16),
+            pltpu.VMEM((3 * rank, features), bf16),
+            pltpu.VMEM((3 * rank, features), bf16),
+            pltpu.VMEM((rows, features), f32),
+            pltpu.VMEM((2, rows, features), bf16),
+            pltpu.VMEM((2, rows, features), bf16),
+            pltpu.VMEM((2, 3, features, tile), bf16),
+            pltpu.VMEM((rows, 3 * rank), bf16),
+            pltpu.VMEM((3 * rank, rows), bf16),
+            pltpu.VMEM((rows, features), f32),
+            pltpu.VMEM((rows, features), f32),
+            pltpu.VMEM((rows, 3 * rank), f32),
+            pltpu.VMEM((LINE, rows, features), bf16),
+            pltpu.VMEM((2, LINE - 1, rows, features), bf16),
+            pltpu.VMEM((rows, features), bf16),
+            pltpu.SemaphoreType.DMA((2,)),
+            pltpu.SemaphoreType.DMA((2,)),
+            pltpu.SemaphoreType.DMA((2, 3)),
+            pltpu.SemaphoreType.DMA((1,)),
+            pltpu.SemaphoreType.DMA((1,)),
+        ]
+        + line_sems(chunks),
+        compiler_params=comm_params(5),
+    )(normed, *cots, weight, middle, units_exit, fall_entry, entries, finals, gain[None, :])
 
 
 def per_tree(block):
-    return lax.all_gather(block.astype(bf16), "dp", axis=0, tiled=False)
+    return lax.all_gather(block, "dp", axis=0, tiled=False)
 
 
 def by_adapter(gathered, picks, adapters):
@@ -780,11 +955,7 @@
     adapter_pick,
 ):
     pick = adapter_pick[0]
-    picks = lax.all_gather(adapter_pick, "dp", axis=0, tiled=True)
     adapters, rank = entry_maps.shape[1], entry_maps.shape[3]
-    place = lax.axis_index("tensor")
-    edge = (place == 0) | (place == 3)
-    slots = [(place ^ s).reshape(1).astype(jnp.int32) for s in range(4)]
     local_rows = tokens.shape[0]
     total = local_rows * lax.axis_size("tensor")
     blocks = parents.shape[1]
@@ -800,9 +971,6 @@
         axis=0,
         tiled=True,
     )
-    w_units = lax.all_gather(
-        jnp.concatenate([gate_weight, up_weight, down_weight], axis=1), "dp", axis=0, tiled=True
-    )
 
     entries = jnp.swapaxes(entry_maps, 2, 3)[:, pick]
     heads_exit = head_exits[:, pick]
@@ -810,84 +978,65 @@
     out_entry = jnp.swapaxes(output_entry, 1, 2)[pick]
     fall_entry = jnp.swapaxes(down_entry, 1, 2)[pick]
     finals = final_exits[:, pick]
-    width = heads_exit.shape[2]
-    entry_one = stack_rows([entries[0], entries[1], entries[2]])
-    exit_one = stack_rows(
-        [
-            jnp.pad(heads_exit[k], ((0, 0), (k * width, (2 - k) * width)))
-            for k in range(3)
-        ]
-    )
-    final_one = place_rows(finals[0], 0)
-    exit_out = place_rows(out_entry, 0)
-    entry_two = stack_rows([entries[3], entries[4]])
-    final_two = place_rows(finals[1], 2 * rank)
-    x_gate = place_rows(units_exit[0], 0)
-    x_rise = place_rows(units_exit[1], rank)
-    x_fall = place_rows(fall_entry, 2 * rank)
-
-    full_one = gather_norm(tokens, gain_one)
-    cot_tied, _ = lax.optimization_barrier((cotangent, full_one))
+
+    most_one, units_here = gather_norm(tokens, gain_one, (gate_weight, up_weight, down_weight))
+    w_units = lax.all_gather(units_here, "dp", axis=0, tiled=True)
+    cot_tied, _ = lax.optimization_barrier((cotangent, most_one))
     one, mid = line_gather_start(cot_tied)
-    flat_one = full_one.reshape(total, -1)
-    qkv, low_one = project(flat_one, w_heads, entry_one, exit_one, 3, tables)
+    full_one, qkv, low_one = project(most_one, w_heads, entries, heads_exit, tables)
+    one, mid, qkv = lax.optimization_barrier((one, mid, qkv))
+    cots = (cotangent, one) + line_gather_finish(one, mid)
     attended, lse = attend(qkv, leaf_parent, seg)
-    one, mid, attended = lax.optimization_barrier((one, mid, attended))
-    full_cot = line_gather_finish(cot_tied, one, mid, edge)
     middle, full_two, adapt_o = middle_rows(
-        attended[0], w_heads, exit_out, final_one, tokens, gain_two
-    )
-
-    fed = [None] * 4
-    tie = middle
-    for s in (3, 2, 1, 0):
-        slot, _ = lax.optimization_barrier((slots[s], tie))
-        fed[s] = feed(
-            slot, full_two, full_cot[s], w_units, x_gate, x_rise, x_fall, entry_two, final_two, rank
-        )
-        tie = fed[s][3]
-    rms_two = lax.rsqrt(jnp.mean(middle * middle, axis=1, keepdims=True) + eps)
-    grad_middle = cotangent.astype(f32) + norm_backward(
-        middle, rms_two, gain_two, line_scatter([f[1] for f in fed], place)
-    )
-    unit_grads = functools.reduce(jnp.add, [f[2] for f in fed])
-    model_grads = functools.reduce(jnp.add, [f[3] for f in fed])
-
-    full_branch, grad_attended, back_o = branch_back(
-        grad_middle.astype(bf16), w_heads, final_one, exit_out
-    )
-    res_parts, _ = lax.optimization_barrier(([f[0] for f in fed], back_o))
-    result = (middle + line_scatter(res_parts, place)).astype(bf16)
+        attended[0], w_heads, out_entry, finals, tokens, gain_two
+    )
+
+    grad_middle, branch, res_parts, unit_grads, model_grads = feed(
+        full_two, cots, w_units, middle, units_exit, fall_entry, entries, finals, gain_two
+    )
+    early = jnp.concatenate(
+        [unit_grads.astype(bf16), jnp.full((rank, unit_grads.shape[1]), pick).astype(bf16)]
+    )
+    model_low = model_grads.astype(bf16)
+    branch, early, model_low = lax.optimization_barrier((branch, early, model_low))
+    early = per_tree(early)
+    model_sum = lax.psum(model_low, "tensor")
+
+    full_branch, grad_attended, back_o, res_rows = branch_back(
+        branch, w_heads, finals, out_entry, res_parts
+    )
+    from_left = permute(res_rows[1], [(0, 1), (1, 2), (2, 3)])
+    from_right = permute(res_rows[2], [(3, 2), (2, 1), (1, 0)])
     head_grads = attend_back(qkv, attended, grad_attended, lse, leaf_parent, tables, seg)
-    grad_tokens, back_one = tokens_back(
-        head_grads, w_heads, exit_one, entry_one, tokens, gain_one, grad_middle
-    )
-
-    out_grads = tn(back_o, attended[0])[:rank]
-    final_one_grads = tn(adapt_o, full_branch.reshape(total, -1))[:rank]
-    entry_one_grads = tn(back_one, flat_one)[: 3 * rank]
-    head_parts = [
-        tn(low_one[:, k * rank : (k + 1) * rank], head_grads[k]) for k in range(3)
-    ]
-    early = per_tree(
-        lax.psum(jnp.concatenate([model_grads, final_one_grads]).astype(bf16), "tensor")
-    )
-    late = per_tree(lax.psum(entry_one_grads.astype(bf16), "tensor"))
-    unit_all = per_tree(unit_grads)
-    head_all = per_tree(jnp.concatenate(head_parts + [out_grads]))
-
-    early = by_adapter(early, picks, adapters)
-    late = by_adapter(late, picks, adapters)
-    unit_all = by_adapter(unit_all, picks, adapters)
-    head_all = by_adapter(head_all, picks, adapters)
+    head_grads, model_sum = lax.optimization_barrier((head_grads, model_sum))
+    model_all = per_tree(model_sum)
+    grad_tokens, late_model, late_head = tokens_back(
+        head_grads, w_heads, heads_exit, entries, tokens, gain_one, grad_middle,
+        full_one, full_branch, low_one, adapt_o, back_o, attended[0],
+    )
+    late = per_tree(
+        jnp.concatenate([late_model, late_head.reshape(rank, -1)], axis=0)
+    )
+    result = (
+        middle
+        + res_rows[0].astype(f32)
+        + from_left.astype(f32)
+        + from_right.astype(f32)
+    ).astype(bf16)
+
+    picks = early[:, 3 * rank, 0].astype(f32)
+    unit_all = by_adapter(early[:, : 3 * rank], picks, adapters)
+    model_all = by_adapter(model_all, picks, adapters)
+    late_model = by_adapter(late[:, : 4 * rank], picks, adapters)
+    head_all = by_adapter(late[:, 4 * rank :].reshape((late.shape[0],) + late_head.shape), picks, adapters)
 
     def cut(block, index):
         return block[:, index * rank : (index + 1) * rank]
 
     grad_entries = jnp.stack(
-        [cut(late, 0), cut(late, 1), cut(late, 2), cut(early, 0), cut(early, 1)]
+        [cut(late_model, 0), cut(late_model, 1), cut(late_model, 2), cut(model_all, 0), cut(model_all, 1)]
     ).swapaxes(2, 3)
-    grad_finals = jnp.stack([cut(early, 3), cut(early, 2)])
+    grad_finals = jnp.stack([cut(late_model, 3), cut(model_all, 2)])
     grad_heads = jnp.stack([cut(head_all, k) for k in range(3)])
     grad_output = cut(head_all, 3).swapaxes(1, 2)
     grad_units = jnp.stack([cut(unit_all, 0), cut(unit_all, 1)])

time: 984 us -> 875 us (0.89)
  waiting for transfers between devices: 108 us -> 0.65 us
  Pallas kernels: 660 us -> 721 us
  other arithmetic: 62.5 us -> 36.6 us
  blocking collectives: 17.7 us -> 0 us
  starting transfers between devices: 35.4 us -> 19.4 us
  matrix products: 12.5 us -> 0 us
    ppermute x15 -> x7, waiting for transfers between devices: 69.8 us -> 0.02 us  [permute(): return lax.ppermute(value, 'tensor', pairs)]
    pallas_call x7 -> x4, Pallas kernels: 322 us -> 369 us  [the longest x1 110 us: feed(): pl.pallas_call(functools.partial(feed_body, rank, tile, chunks), in_specs...]
    psum x1, waiting for transfers between devices: 38.3 us -> 0.01 us  [local(): model_sum = lax.psum(model_low, 'tensor')]
    pallas_call x1, Pallas kernels: 99.9 us -> 121 us  [tokens_back(): pl.pallas_call(functools.partial(tokens_body, chunks), in_specs=[IN_HBM,...]
    convert_element_type x8 -> x4, other arithmetic: 28.2 us -> 7.6 us  [the longest x1 4.02 us: local(): result = (middle + res_rows[0].astype(f32) + from_left.astype(f32) + from...]
    ppermute x15 -> x7, starting transfers between devices: 35 us -> 19.1 us  [permute(): return lax.ppermute(value, 'tensor', pairs)]
    dot_general x6 -> x0, matrix products: 12.5 us -> none  [tn(): lax.dot_general(left, right, (((0,), (0,)), ((), ())), preferred_element_...]
  transfers between devices with their start and end apart: 21 -> 13, of which waited for: 6 -> 0; matrix products, arithmetic and copies ran while one was open for 6% -> 4% of each run, Pallas kernels for 36% -> 71%
where the time goes in v3:
time: 875 us; the launch traced here: 865 us
  Pallas kernels  721 us (82%)
  between operations  56.2 us (6%)
  other arithmetic  36.6 us (4%)
  local copies, waits for them, and re-layouts  31.1 us (4%)
  starting transfers between devices  19.4 us (2%)
    pallas_call x1, Pallas kernels, middle_rows(): pl.pallas_call(functools.partial(middle_body, chunks), in_specs=[IN_VMEM,...  182 us
    pallas_call x1, Pallas kernels, tokens_back(): pl.pallas_call(functools.partial(tokens_body, chunks), in_specs=[IN_HBM,...  121 us
    pallas_call x1, Pallas kernels, feed(): pl.pallas_call(functools.partial(feed_body, rank, tile, chunks), in_specs...  110 us
    pallas_call x1, Pallas kernels, gather_norm(): pl.pallas_call(gather_norm_body, in_specs=[IN_VMEM, IN_VMEM] + [IN_HBM] *...  100 us
    pallas_call x1, Pallas kernels, branch_back(): pl.pallas_call(branch_body, in_specs=[IN_VMEM, IN_HBM, IN_VMEM, IN_VMEM,...  97.8 us
    pallas_call x1, Pallas kernels, project(): pl.pallas_call(project_body, in_specs=[IN_HBM, IN_HBM] + [IN_VMEM] * 4, o...  61.8 us
    pallas_call x1, Pallas kernels, attend_back(): pl.pallas_call(functools.partial(attend_back_body, seg), grid=(pairs,), i...  29.1 us
    pallas_call x1, Pallas kernels, attend(): pl.pallas_call(functools.partial(attend_body, seg), grid=(pairs,), in_spe...  19.3 us
  transfers between devices with their start and end apart: 13, of which 0 were waited for; matrix products, arithmetic and copies ran while one was open for 4% of the time, Pallas kernels for 71%

profile of v3, /device:TPU:0, one launch (start us, length us, event | category | flops | bytes accessed | tf_op | source)
XLA Modules:
  0.0 864.6 jit_solution(18217951722521161501)
XLA Ops:
  7.2 2.4 pad_maximum_fusion.2
  9.8 0.6 broadcast_in_dim.290
  10.4 100.1 %shard_map.260 = (bf16[4,320,2048]{2,1,0:T(8,128)(2,1)}, bf16[256,6144]{1,0:T(8,128)(2,1)}) custom-call(bf16[320,2048]{1,0:T(8,128)(2,1)} %x_ref.5, f32[1,2048]{1,0:T(1,128)} %bitcast.298, bf16[256,2048]{1,0:T(8,128)(2,1)} %wg_ref.1, bf16[256,2048]{1,0:T(8,128)(2,1)} %wu_ref.1, bf16[256,2048]{1,0:T(8,128)(2,1)} %wd_ref.1), custom_call_target="tpu_custom_call" | custom-call | tf_op jit(solution)/shard_map/pallas_call | solution.py:264
  110.6 1.7 collective-permute-start.1
  112.3 4.9 collective-permute-start
  117.8 1.4 dynamic-slice_bitcast_fusion.4.a_ref
  119.3 0.7 dynamic-slice_bitcast_fusion.e_ref.e_in
  120.0 61.8 %shard_map.261 = (bf16[4,320,2048]{2,1,0:T(8,128)(2,1)}, bf16[3,1280,512]{2,1,0:T(8,128)(2,1)}, bf16[1280,48]{1,0:T(8,128)(2,1)}) custom-call(bf16[4,320,2048]{2,1,0:T(8,128)(2,1)} %get-tuple-element.39.x_ref, bf16[2048,2048]{1,0:T(8,128)(2,1)} %all-gather.9.cloned.1.call-done.w_ref, bf16[5,16,2048]{2,1,0:T(8,128)(2,1)} %dynamic-slice_bitcast_fusion.e_ref.e_in, ...), custom_call_target="tpu_custom_call" | custom-call | tf_op jit(solution)/shard_map/pallas_call | solution.py:319
  181.8 1.5 collective-permute-start.4
  183.3 0.7 collective-permute-start.3
  184.1 1.3 collective-permute-start.2
  185.5 0.7 sub.10.p_ref
  186.2 0.6 broadcast_in_dim.291
  186.8 1.3 dynamic-slice_bitcast_fusion.5.a_ref
  188.1 1.5 dynamic-slice_bitcast_fusion.3.xd_in
  189.6 1.7 dynamic-slice_bitcast_fusion.1
  191.3 19.3 %shard_map.262 = (bf16[1,1280,512]{2,1,0:T(8,128)(2,1)}, f32[4,2,1280]{2,1,0:T(2,128)}) custom-call(bf16[3,1280,512]{2,1,0:T(8,128)(2,1)} %get-tuple-element.42.q_ref.k_ref.v_ref, bf16[3,1280,512]{2,1,0:T(8,128)(2,1)} %get-tuple-element.42.q_ref.k_ref.v_ref, bf16[3,1280,512]{2,1,0:T(8,128)(2,1)} %get-tuple-element.42.q_ref.k_ref.v_ref, s32[1,512]{1,0:T(1,128)} %sub.10.p_ref), custom_call_target="tpu_custom_call" | custom-call | flops 6710886400 | bytes 5242880 | tf_op jit(solution)/shard_map/pallas_call | solution.py:644
  210.6 181.7 %shard_map.263 = (f32[320,2048]{1,0:T(8,128)}, bf16[4,320,2048]{2,1,0:T(8,128)(2,1)}, bf16[1280,16]{1,0:T(8,128)(2,1)}) custom-call(bf16[1280,512]{1,0:T(8,128)(2,1)} %bitcast.295, bf16[2048,2048]{1,0:T(8,128)(2,1)} %all-gather.9.cloned.1.call-done.w_ref, bf16[16,512]{1,0:T(8,128)(2,1)} %dynamic-slice_bitcast_fusion.5.a_ref, ...), custom_call_target="tpu_custom_call" | custom-call | tf_op jit(solution)/shard_map/pallas_call | solution.py:386
  392.4 1.0 copy-done.11
  393.4 0.4 copy-done.12
  393.8 109.7 %shard_map.264 = (f32[320,2048]{1,0:T(8,128)}, bf16[320,2048]{1,0:T(8,128)(2,1)}, bf16[4,320,2048]{2,1,0:T(8,128)(2,1)}, f32[48,2048]{1,0:T(8,128)}, f32[48,2048]{1,0:T(8,128)}) custom-call(bf16[4,320,2048]{2,1,0:T(8,128)(2,1)} %get-tuple-element.45.n_ref, bf16[320,2048]{1,0:T(8,128)(2,1)} %c0_ref.1, bf16[320,2048]{1,0:T(8,128)(2,1)} %collective-permute-done.c1_ref, ...), custom_call_target="tpu_custom_call" | custom-call | tf_op jit(solution)/shard_map/pallas_call | solution.py:884
  503.5 1.0 convert_element_type.831
  504.5 1.7 convert_element_type.833
  506.2 0.7 concatenate.10
  507.0 0.5 all-gather.13.cloned.1.call-update
  507.6 97.8 %shard_map.265 = (bf16[4,320,2048]{2,1,0:T(8,128)(2,1)}, bf16[1,1280,512]{2,1,0:T(8,128)(2,1)}, bf16[1280,16]{1,0:T(8,128)(2,1)}, bf16[3,320,2048]{2,1,0:T(8,128)(2,1)}) custom-call(bf16[320,2048]{1,0:T(8,128)(2,1)} %get-tuple-element.52.b_ref, bf16[2048,2048]{1,0:T(8,128)(2,1)} %all-gather.9.cloned.1.call-done.w_ref, ...), custom_call_target="tpu_custom_call" | custom-call | tf_op jit(solution)/shard_map/pallas_call | solution.py:454
  605.4 29.1 %shard_map.266.d_ref = bf16[3,1280,512]{2,1,0:T(8,128)(2,1)} custom-call(bf16[3,1280,512]{2,1,0:T(8,128)(2,1)} %get-tuple-element.42.q_ref.k_ref.v_ref, bf16[3,1280,512]{2,1,0:T(8,128)(2,1)} %get-tuple-element.42.q_ref.k_ref.v_ref, bf16[3,1280,512]{2,1,0:T(8,128)(2,1)} %get-tuple-element.42.q_ref.k_ref.v_ref, bf16[1,1280,512]{2,1,0:T(8,128)(2,1)} %get-tuple-element.43.o_ref, ...), custom_call_target="tpu_custom_call" | custom-call | flops 16777216000 | bytes 10485760 | tf_op jit(solution)/shard_map/pallas_call | solution.py:707
  634.5 3.5 slice_bitcast_fusion.1
  638.1 7.7 collective-permute-start.5
  645.8 1.3 collective-permute-start.6
  647.1 121.2 %shard_map.267 = (bf16[320,2048]{1,0:T(8,128)(2,1)}, bf16[64,2048]{1,0:T(8,128)(2,1)}, bf16[64,512]{1,0:T(8,128)(2,1)}) custom-call(bf16[3,1280,512]{2,1,0:T(8,128)(2,1)} %shard_map.266.d_ref, bf16[2048,2048]{1,0:T(8,128)(2,1)} %all-gather.9.cloned.1.call-done.w_ref, bf16[3,16,512]{2,1,0:T(8,128)(2,1)} %dynamic-slice_bitcast_fusion.4.a_ref, ...), custom_call_target="tpu_custom_call" | custom-call | tf_op jit(solution)/shard_map/pallas_call | solution.py:559
  768.3 0.9 reshape.1262
  769.2 1.7 pad_maximum_fusion.4
  771.0 4.0 fusion.2
  775.0 0.9 slice_convert_fusion
  775.9 0.6 fusion.280
  817.1 1.8 fusion.79
  821.0 1.2 slice_bitcast_fusion.4
  822.2 1.5 pad_maximum_fusion
  823.8 1.9 fusion.153
  825.6 1.8 fusion.162
  829.3 1.6 copy-done.9
  830.9 1.1 slice_bitcast_fusion.2
  832.0 2.0 fusion.230
  834.0 1.2 fusion.279
  835.1 1.2 fusion.272
  836.3 1.2 fusion.265
  837.5 1.2 fusion.258
  839.0 0.4 fusion.15
  839.4 0.4 fusion.23
  839.8 0.4 fusion.31
  840.7 0.4 fusion.47
  841.5 0.4 fusion.63
  842.3 1.0 slice_bitcast_fusion.3
  843.4 1.2 copy-done.6
  844.6 1.0 fusion.7
  846.2 0.8 slice_bitcast_fusion.12
  847.0 2.5 fusion.6
  849.5 2.4 fusion.5
  851.9 1.1 fusion.4
  853.0 1.1 fusion.3
  854.1 1.5 pad_maximum_fusion.1
  855.5 0.9 pad_maximum_fusion.3
  856.5 1.1 copy.66
  (93 shorter events, 6.5 us)
Async XLA Ops:
  7.2 112.1 %copy-start = (bf16[5,8,2048,16]{2,3,1,0:T(8,128)(2,1)S(1)}, bf16[5,8,2048,16]{2,3,1,0:T(8,128)(2,1)}, u32[]{:S(2)}) copy-start(bf16[5,8,2048,16]{2,3,1,0:T(8,128)(2,1)} %param.32) | copy-start | bytes 7864324
  7.2 2.6 copy-start.15
  7.2 112.8 %all-gather.9.cloned.1.call-start = ((), (), s32[]{:S(2)}) async-start(), calls=%async_computation | async-start | bytes 9437184 | tf_op jit(solution)/shard_map/all_gather | solution.py:968
  9.7 382.7 %all-gather.11.cloned.1.call-start = ((), (), s32[]{:S(2)}) async-start(), calls=%async_computation.1 | async-start | bytes 28311552 | tf_op jit(solution)/shard_map/all_gather | solution.py:983
  110.5 523.9 %all-reduce.3.cloned.1.call-start = ((), (), s32[]{:S(2)}) async-start(), calls=%async_computation.2 | async-start | bytes 393216 | tf_op jit(solution)/shard_map/psum | solution.py:1003
  110.6 71.2 %collective-permute-start.1 = (bf16[320,2048]{1,0:T(8,128)(2,1)}, bf16[320,2048]{1,0:T(8,128)(2,1)}, u32[]{:S(2)}, u32[]{:S(2)}) collective-permute-start(bf16[320,2048]{1,0:T(8,128)(2,1)} %c0_ref.1), channel_id=1, source_target_pairs={{1,2},{2,1},{5,6},{6,5},{9,10},{10,9},{13,14},{14,13},{17,18},{18,... | collective-permute-start | bytes 3932168 | tf_op jit(solution)/shard_map/ppermute | solution.py:36
  112.3 69.5 %collective-permute-start = (bf16[320,2048]{1,0:T(8,128)(2,1)}, bf16[320,2048]{1,0:T(8,128)(2,1)}, u32[]{:S(2)}, u32[]{:S(2)}) collective-permute-start(bf16[320,2048]{1,0:T(8,128)(2,1)} %c0_ref.1), channel_id=1, source_target_pairs={{0,1},{1,0},{2,3},{3,2},{4,5},{5,4},{6,7},{7,6},{8,9},{9,8},{10,11... | collective-permute-start | bytes 3932168 | tf_op jit(solution)/shard_map/ppermute | solution.py:36
  120.0 65.4 %copy-start.17 = (s32[1,20]{1,0:T(1,128)S(1)}, s32[1,20]{1,0:T(1,128)}, u32[]{:S(2)}) copy-start(s32[1,20]{1,0:T(1,128)} %param.38) | copy-start | bytes 244
  120.0 66.2 %copy-start.16 = (bf16[2048]{0:T(1024)(128)(2,1)S(1)}, bf16[2048]{0:T(1024)(128)(2,1)}, u32[]{:S(2)}) copy-start(bf16[2048]{0:T(1024)(128)(2,1)} %param.24) | copy-start | bytes 12292
  181.8 210.5 %collective-permute-start.4 = (bf16[320,2048]{1,0:T(8,128)(2,1)}, bf16[320,2048]{1,0:T(8,128)(2,1)S(1)}, u32[]{:S(2)}, u32[]{:S(2)}) collective-permute-start(bf16[320,2048]{1,0:T(8,128)(2,1)} %collective-permute-done.c1_ref), channel_id=1, source_target_pairs={{2,0},{1,3},{6,4},{5,7},{10,8},{9,11},{14,12},{13,15},{18,16},{17,... | collective-permute-start | bytes 3932168 | tf_op jit(solution)/shard_map/ppermute | solution.py:36
  183.3 209.0 %collective-permute-start.3 = (bf16[320,2048]{1,0:T(8,128)(2,1)}, bf16[320,2048]{1,0:T(8,128)(2,1)S(1)}, u32[]{:S(2)}, u32[]{:S(2)}) collective-permute-start(bf16[320,2048]{1,0:T(8,128)(2,1)} %collective-permute-done.c1_ref), channel_id=1, source_target_pairs={{1,2},{2,1},{5,6},{6,5},{9,10},{10,9},{13,14},{14,13},{17,18},{18,... | collective-permute-start | bytes 3932168 | tf_op jit(solution)/shard_map/ppermute | solution.py:36
  184.1 208.2 %collective-permute-start.2 = (bf16[320,2048]{1,0:T(8,128)(2,1)}, bf16[320,2048]{1,0:T(8,128)(2,1)}, u32[]{:S(2)}, u32[]{:S(2)}) collective-permute-start(bf16[320,2048]{1,0:T(8,128)(2,1)} %collective-permute-done.1.c3m_ref), channel_id=1, source_target_pairs={{1,0},{2,3},{5,4},{6,7},{9,8},{10,11},{13,12},{14,15},{17,16},{18,... | collective-permute-start | bytes 3932168 | tf_op jit(solution)/shard_map/ppermute | solution.py:36
  392.3 1.1 copy-start.11
  392.4 1.5 copy-start.12
  507.0 268.0 %all-gather.13.cloned.1.call-start = ((), (), s32[]{:S(2)}) async-start(), calls=%async_computation.3 | async-start | bytes 2359296 | tf_op jit(solution)/shard_map/all_gather | solution.py:923
  507.5 316.2 %all-gather.17.cloned.1.call-start = ((), (), s32[]{:S(2)}) async-start(), calls=%async_computation.5 | async-start | bytes 1769472 | tf_op jit(solution)/shard_map/all_gather | solution.py:923
  634.5 197.5 %all-gather.15.cloned.1.call-start = ((), (), s32[]{:S(2)}) async-start(), calls=%async_computation.4 | async-start | bytes 2949120 | tf_op jit(solution)/shard_map/all_gather | solution.py:923
  638.1 132.9 %collective-permute-start.5 = (bf16[320,2048]{1,0:T(8,128)(2,1)}, bf16[320,2048]{1,0:T(8,128)(2,1)}, u32[]{:S(2)}, u32[]{:S(2)}) collective-permute-start(bf16[320,2048]{1,0:T(8,128)(2,1)} %get-tuple-element.70), channel_id=1, source_target_pairs={{0,1},{1,2},{2,3},{4,5},{5,6},{6,7},{8,9},{9,10},{10,11},{12,13},{... | collective-permute-start | bytes 3932168 | tf_op jit(solution)/shard_map/ppermute | solution.py:36
  645.8 125.1 %collective-permute-start.6 = (bf16[320,2048]{1,0:T(8,128)(2,1)}, bf16[320,2048]{1,0:T(8,128)(2,1)}, u32[]{:S(2)}, u32[]{:S(2)}) collective-permute-start(bf16[320,2048]{1,0:T(8,128)(2,1)} %get-tuple-element.71), channel_id=1, source_target_pairs={{3,2},{2,1},{1,0},{7,6},{6,5},{5,4},{11,10},{10,9},{9,8},{15,14},{... | collective-permute-start | bytes 3932168 | tf_op jit(solution)/shard_map/ppermute | solution.py:36
  647.1 123.9 %copy-start.5 = (f32[320,2048]{1,0:T(8,128)S(1)}, f32[320,2048]{1,0:T(8,128)}, u32[]{:S(2)}) copy-start(f32[320,2048]{1,0:T(8,128)} %get-tuple-element.44.mid_ref) | copy-start | bytes 7864324
  775.0 43.9 %copy-start.4 = (bf16[512,2048]{1,0:T(8,128)(2,1)S(1)}, bf16[512,2048]{1,0:T(8,128)(2,1)}, u32[]{:S(2)}) copy-start(bf16[512,2048]{1,0:T(8,128)(2,1)} %all-gather.13.cloned.1.call-done) | copy-start | bytes 6291460
  823.8 3.6 copy-start.3
  829.3 1.6 copy-start.9
  832.0 6.7 copy-start.2
  842.3 2.3 copy-start.6
  842.3 3.3 copy-start.14
  846.1 5.8 copy-start.10
  849.5 4.6 copy-start.7
  849.5 4.6 copy-start.8
  854.1 2.4 copy-start.13
  854.1 3.5 copy-start.1
Sparse Core Ops, SparseCore 0:
  10.5 57.0 all-gather.8
  110.7 128.0 all-gather.10
  507.1 40.2 all-reduce.2
  549.9 27.3 all-gather.12
  634.6 27.9 all-gather.16
  771.1 32.2 all-gather.14

commit v4 on v3

--- a/solution.py
+++ b/solution.py
@@ -34,19 +34,6 @@
 
 def permute(value, pairs):
     return lax.ppermute(value, "tensor", pairs)
-
-
-def line_gather_start(value):
-    one = permute(value, [(0, 1), (1, 0), (2, 3), (3, 2)])
-    mid = permute(value, [(1, 2), (2, 1)])
-    return one, mid
-
-
-def line_gather_finish(one, mid):
-    two_edge = permute(mid, [(1, 0), (2, 3)])
-    two_mid = permute(one, [(1, 2), (2, 1)])
-    three_edge = permute(one, [(2, 0), (1, 3)])
-    return two_edge, two_mid, three_edge, mid
 
 
 def rope_tables(blocks, seg):
@@ -83,8 +70,10 @@
     return place if side == 1 else LINE - 1 - place
 
 
-def greet(place):
+def greet(place, partners=()):
     barrier = pltpu.get_barrier_semaphore()
+    for partner in partners:
+        pl.semaphore_signal(barrier, inc=1, device_id={"dp": partner}, device_id_type=MESH)
     for side in SIDES:
 
         @pl.when(far_of(place, side) < LINE - 1)
@@ -97,11 +86,11 @@
 
     @pl.when(edge)
     def _():
-        pl.semaphore_wait(barrier, 1)
+        pl.semaphore_wait(barrier, 1 + len(partners))
 
     @pl.when(jnp.logical_not(edge))
     def _():
-        pl.semaphore_wait(barrier, 2)
+        pl.semaphore_wait(barrier, 2 + len(partners))
 
 
 def chunk_rows(chunk, rows):
@@ -238,13 +227,8 @@
     )
 
 
-def gather_norm_body(x_ref, gain_ref, wg_ref, wu_ref, wd_ref, buf, w_ref, wsem, send, recv):
+def gather_norm_body(x_ref, gain_ref, buf, send, recv):
     place = lax.axis_index("tensor")
-    width = wg_ref.shape[1]
-    loads = fetch(
-        [(w, w_ref.at[:, k * width : (k + 1) * width]) for k, w in enumerate((wg_ref, wu_ref, wd_ref))],
-        wsem,
-    )
     greet(place)
     rows = x_ref[...].astype(f32)
     rms = lax.rsqrt(jnp.mean(rows * rows, axis=1, keepdims=True) + eps)
@@ -254,24 +238,18 @@
         gather.send(step, 0)
         gather.arrive(step, 0)
     gather.drain(stop=LINE - 1)
-    for load in loads:
-        load.wait()
-
-
-def gather_norm(x, gain, weights):
+
+
+def gather_norm(x, gain):
     rows, features = x.shape
-    deep, width = weights[0].shape
     return pl.pallas_call(
         gather_norm_body,
-        in_specs=[IN_VMEM, IN_VMEM] + [IN_HBM] * 3,
-        out_specs=[IN_VMEM, IN_HBM],
-        out_shape=[
-            jax.ShapeDtypeStruct((LINE, rows, features), bf16),
-            jax.ShapeDtypeStruct((deep, 3 * width), bf16),
-        ],
-        scratch_shapes=[pltpu.SemaphoreType.DMA((3,))] + line_sems(1),
+        in_specs=[IN_VMEM, IN_VMEM],
+        out_specs=IN_VMEM,
+        out_shape=jax.ShapeDtypeStruct((LINE, rows, features), bf16),
+        scratch_shapes=line_sems(1),
         compiler_params=comm_params(0),
-    )(x, gain[None, :], *weights)
+    )(x, gain[None, :])
 
 
 def project_body(
@@ -336,14 +314,27 @@
 
 
 def middle_body(
-    chunks, d_ref, w_ref, a_ref, e_ref, x_ref, gain_ref, mid_ref, buf, low_ref,
-    part, held, wv, wsem, s_send, s_recv, g_send, g_recv,
+    chunks, d_ref, w_ref, c_ref, before_ref, after_ref, a_ref, e_ref, x_ref, gain_ref, mid_ref, buf, cbuf, low_ref,
+    part, held, wv, wsem, s_send, s_recv, g_send, g_recv, c_send, c_recv,
 ):
     place = lax.axis_index("tensor")
     width = d_ref.shape[1]
-    (load,) = fetch([(w_ref.at[:, 3 * width :], wv)], wsem)
+    load, own = fetch([(w_ref.at[:, 3 * width :], wv), (c_ref, cbuf.at[place])], wsem)
+
+    def neighbours(act):
+        @pl.when(place > 0)
+        def _():
+            act(pltpu.make_async_copy(before_ref, cbuf.at[place - 1], wsem.at[2]))
+
+        @pl.when(place < LINE - 1)
+        def _():
+            act(pltpu.make_async_copy(after_ref, cbuf.at[place + 1], wsem.at[3]))
+
+    neighbours(lambda copy: copy.start())
     greet(place)
     load.wait()
+    own.wait()
+    cots = Gather(place, cbuf, c_send, c_recv, 1)
     rows = part.shape[1]
     summed = Sum(place, part, held, s_send, s_recv, chunks)
     gather = Gather(place, buf, g_send, g_recv, chunks)
@@ -357,8 +348,13 @@
         if slot == 3:
             for chunk in range(chunks):
                 summed.send(1, chunk)
+    neighbours(lambda copy: copy.wait())
+    cots.send(2, 0)
     size = rows // chunks
     for turn_ in range(chunks + 2):
+        if turn_ == 2:
+            cots.arrive(2, 0)
+            cots.send(3, 0)
         if turn_ < chunks:
             summed.send(2, turn_)
             summed.send(3, turn_)
@@ -376,19 +372,22 @@
                 gather.send(step + 1, chunk)
     for chunk in range(chunks):
         gather.arrive(3, chunk)
+    cots.arrive(3, 0)
     summed.drain()
     gather.drain()
-
-
-def middle_rows(attended, weight, exits, finals, x, gain, chunks=4):
+    cots.drain(start=2)
+
+
+def middle_rows(attended, weight, cot, before, after, exits, finals, x, gain, chunks=4):
     rows, features = x.shape
     width = attended.shape[1]
     return pl.pallas_call(
         functools.partial(middle_body, chunks),
-        in_specs=[IN_VMEM, IN_HBM, IN_VMEM, IN_VMEM, IN_VMEM, IN_VMEM],
-        out_specs=[IN_VMEM] * 3,
+        in_specs=[IN_VMEM] + [IN_HBM] * 4 + [IN_VMEM] * 4,
+        out_specs=[IN_VMEM] * 4,
         out_shape=[
             jax.ShapeDtypeStruct((rows, features), f32),
+            jax.ShapeDtypeStruct((LINE, rows, features), bf16),
             jax.ShapeDtypeStruct((LINE, rows, features), bf16),
             jax.ShapeDtypeStruct((LINE * rows, exits.shape[0]), bf16),
         ],
@@ -396,16 +395,17 @@
             pltpu.VMEM((LINE, rows, features), bf16),
             pltpu.VMEM((2, LINE - 1, rows, features), bf16),
             pltpu.VMEM((features, width), bf16),
-            pltpu.SemaphoreType.DMA((1,)),
+            pltpu.SemaphoreType.DMA((4,)),
         ]
         + line_sems(chunks)
-        + line_sems(chunks),
+        + line_sems(chunks)
+        + line_sems(1),
         compiler_params=comm_params(1),
-    )(attended, weight, exits, finals, x, gain[None, :])
+    )(attended, weight, cot, before, after, exits, finals, x, gain[None, :])
 
 
 def branch_body(
-    b_ref, w_ref, e_ref, a_ref, p_ref, buf, y_ref, l_ref, out_ref,
+    b_ref, w_ref, e_ref, a_ref, p_ref, buf, y_ref, l_ref, own_ref, right_ref, left_ref,
     part, held, wv, wsem, send, recv, s_send, s_recv,
 ):
     place = lax.axis_index("tensor")
@@ -428,16 +428,16 @@
             summed.send(2, 0)
         if slot == 2:
             summed.add(3, 0)
-            out_ref[0] = part[place]
-            for index, side in enumerate(SIDES):
+            own_ref[...] = part[place]
+            for out_ref, side in ((right_ref, 1), (left_ref, -1)):
 
                 @pl.when(far_of(place, side) < LINE - 1)
                 def _():
-                    out_ref[index + 1] = part[place + side]
+                    out_ref[...] = part[place + side]
 
                 @pl.when(far_of(place, side) == LINE - 1)
                 def _():
-                    out_ref[index + 1] = jnp.zeros_like(part[place])
+                    out_ref[...] = jnp.zeros_like(out_ref)
 
         shard = place ^ slot
         mine = pl.ds(pl.multiple_of(shard * rows, rows), rows)
@@ -454,13 +454,13 @@
     return pl.pallas_call(
         branch_body,
         in_specs=[IN_VMEM, IN_HBM, IN_VMEM, IN_VMEM, IN_HBM],
-        out_specs=[IN_VMEM] * 4,
+        out_specs=[IN_VMEM] * 6,
         out_shape=[
             jax.ShapeDtypeStruct((LINE, rows, features), bf16),
             jax.ShapeDtypeStruct((1, LINE * rows, width), bf16),
             jax.ShapeDtypeStruct((LINE * rows, rank), bf16),
-            jax.ShapeDtypeStruct((3, rows, features), bf16),
-        ],
+        ]
+        + [jax.ShapeDtypeStruct((rows, features), bf16)] * 3,
         scratch_shapes=[
             pltpu.VMEM((LINE, rows, features), bf16),
             pltpu.VMEM((2, LINE - 1, rows, features), bf16),
@@ -476,9 +476,11 @@
 def tokens_body(
     chunks, d_ref, w_ref, a_ref, e_ref, x_ref, gain_ref, mid_ref, n_ref, b_ref, lone_ref, lo_ref, bo_ref, o_ref,
     out_ref, model_ref, head_ref,
-    part, held, acc, dv, wv, midv, nv, bv, low, block, extra, wsem, send, recv, x_send, x_recv,
+    part, held, acc, dv, wv, midv, nv, bv, low, block, extra, wsem, send, recv, x_send, x_recv, t_send, t_recv,
 ):
     place = lax.axis_index("tensor")
+    tree = lax.axis_index("dp")
+    trees = Trees(tree, (model_ref, head_ref), t_send, t_recv)
     groups, total, width = d_ref.shape
     rank = a_ref.shape[1]
     loads = fetch(
@@ -488,7 +490,7 @@
     block[...] = jnp.zeros_like(block)
     for g in range(groups):
         block[g * rank : (g + 1) * rank, g * width : (g + 1) * width] = a_ref[g]
-    greet(place)
+    greet(place, trees.partners)
     for load in loads[:2]:
         load.wait()
     rows = part.shape[1]
@@ -520,22 +522,79 @@
     low_one = turned(lone_ref[...])
     for g in range(groups):
         band = slice(g * rank, (g + 1) * rank)
-        head_ref[band] = nn(low_one[band], dv[g]).astype(bf16)
-    head_ref[groups * rank :] = nn(turned(bo_ref[...]), o_ref[...]).astype(bf16)
+        head_ref[tree, band] = nn(low_one[band], dv[g]).astype(bf16)
+    head_ref[tree, groups * rank :] = nn(turned(bo_ref[...]), o_ref[...]).astype(bf16)
     size = rows // chunks
-    for chunk in range(1, chunks):
+
+    def finish(chunk):
+        finish_tokens(summed, chunk, size, acc, x_ref, gain_ref, midv, out_ref)
+
+    gather.arrive(1, 0)
+    gather.send(2, 0)
+    summed.send(2, 1)
+    gather.arrive(2, 0)
+    gather.send(3, 0)
+    finish(0)
+    summed.send(3, 1)
+    gather.arrive(3, 0)
+    model_ref[tree] = functools.reduce(
+        jnp.add, [extra[shard].astype(f32) for shard in range(LINE)]
+    ).astype(bf16)
+    trees.send(0)
+    for chunk in range(2, chunks):
         summed.send(2, chunk)
         summed.send(3, chunk)
-        gather.arrive(chunk, 0)
-        if chunk < LINE - 1:
-            gather.send(chunk + 1, 0)
-        finish_tokens(summed, chunk - 1, size, acc, x_ref, gain_ref, midv, out_ref)
-    model_ref[...] = functools.reduce(
-        jnp.add, [extra[shard].astype(f32) for shard in range(LINE)]
-    ).astype(bf16)
-    finish_tokens(summed, chunks - 1, size, acc, x_ref, gain_ref, midv, out_ref)
+        if chunk - 1 < trees.rounds:
+            trees.arrive(chunk - 2)
+            trees.send(chunk - 1)
+        finish(chunk - 1)
+    for number in range(chunks - 1, trees.rounds):
+        trees.arrive(number - 1)
+        trees.send(number)
+    finish(chunks - 1)
+    trees.arrive(trees.rounds - 1)
     summed.drain()
     gather.drain()
+    trees.drain()
+
+
+class Trees:
+    def __init__(self, tree, refs, send, recv):
+        self.tree, self.refs, self.sems = tree, refs, (send, recv)
+        self.rounds = refs[0].shape[0].bit_length() - 1
+        self.partners = [self.partner(number) for number in range(self.rounds)]
+
+    def partner(self, number):
+        size = 1 << number
+        return self.tree + size - 2 * size * ((self.tree // size) % 2)
+
+    def copies(self, number, owner):
+        size = 1 << number
+        here = pl.ds((owner // size) * size, size)
+        return [
+            pltpu.make_async_remote_copy(
+                src_ref=ref.at[here],
+                dst_ref=ref.at[here],
+                send_sem=self.sems[0].at[number, k],
+                recv_sem=self.sems[1].at[number, k],
+                device_id={"dp": self.partner(number)},
+                device_id_type=MESH,
+            )
+            for k, ref in enumerate(self.refs)
+        ]
+
+    def send(self, number):
+        for copy in self.copies(number, self.tree):
+            copy.start()
+
+    def arrive(self, number):
+        for copy in self.copies(number, self.partner(number)):
+            copy.wait_recv()
+
+    def drain(self):
+        for number in range(self.rounds):
+            for copy in self.copies(number, self.tree):
+                copy.wait_send()
 
 
 def finish_tokens(summed, chunk, size, acc, x_ref, gain_ref, mid_ref, out_ref):
@@ -556,14 +615,16 @@
     groups, total, width = head_grads.shape
     rank = exits.shape[1]
     deep = (groups + 1) * rank
+    trees = lax.axis_size("dp")
+    sems = pltpu.SemaphoreType.DMA((trees.bit_length() - 1, 2))
     return pl.pallas_call(
         functools.partial(tokens_body, chunks),
         in_specs=[IN_HBM, IN_HBM] + [IN_VMEM] * 4 + [IN_HBM] * 3 + [IN_VMEM] * 4,
         out_specs=[IN_VMEM] * 3,
         out_shape=[
             jax.ShapeDtypeStruct((rows, features), bf16),
-            jax.ShapeDtypeStruct((deep, features), bf16),
-            jax.ShapeDtypeStruct((deep, width), bf16),
+            jax.ShapeDtypeStruct((trees, deep, features), bf16),
+            jax.ShapeDtypeStruct((trees, deep, width), bf16),
         ],
         scratch_shapes=[
             pltpu.VMEM((LINE, rows, features), bf16),
@@ -580,7 +641,8 @@
             pltpu.SemaphoreType.DMA((5,)),
         ]
         + line_sems(chunks)
-        + line_sems(1),
+        + line_sems(1)
+        + [sems, sems],
         compiler_params=comm_params(3),
     )(
         head_grads, weight, exits, entries, x, gain[None, :], grad_middle, normed, branch,
@@ -732,42 +794,22 @@
 
 def feed_body(
     rank, tile, chunks,
-    n_ref, c0_ref, c1_ref, c2e_ref, c2m_ref, c3e_ref, c3m_ref, w_ref, mid_ref,
+    n_ref, c_ref, w_ref, mid_ref,
     xu_in, xd_in, e_in, f_in, gain_ref,
     grad_ref, low_grad_ref, res_ref, unit_ref, model_ref,
     x_ref, e_ref, f_ref, midv, nbuf, cbuf, wbuf, low, low_t, acc_res, acc_back, acc_low, part, held, resv,
     nsem, csem, wsem, rsem, msem, send, recv,
 ):
     place = lax.axis_index("tensor")
-    edge = (place == 0) | (place == LINE - 1)
     units = unit_ref.shape[1]
     tiles = units // tile
     summed = Sum(place, part, held, send, recv, chunks)
 
     def load_rows(order, act):
         into = order % 2
-        slot = LINE - 1 - order
-        act(pltpu.make_async_copy(n_ref.at[place ^ slot], nbuf.at[into], nsem.at[into]))
-        for number, at_edge, inside in (
-            (3, c3e_ref, c3m_ref),
-            (2, c2e_ref, c2m_ref),
-            (1, c1_ref, c1_ref),
-            (0, c0_ref, c0_ref),
-        ):
-            if at_edge is inside:
-
-                @pl.when(slot == number)
-                def _():
-                    act(pltpu.make_async_copy(inside, cbuf.at[into], csem.at[into]))
-            else:
-
-                @pl.when((slot == number) & edge)
-                def _():
-                    act(pltpu.make_async_copy(at_edge, cbuf.at[into], csem.at[into]))
-
-                @pl.when((slot == number) & jnp.logical_not(edge))
-                def _():
-                    act(pltpu.make_async_copy(inside, cbuf.at[into], csem.at[into]))
+        shard = place ^ (LINE - 1 - order)
+        act(pltpu.make_async_copy(n_ref.at[shard], nbuf.at[into], nsem.at[into]))
+        act(pltpu.make_async_copy(c_ref.at[shard], cbuf.at[into], csem.at[into]))
 
     def load_weights(index, into, act):
         for k in range(3):
@@ -883,7 +925,7 @@
     rank = fall_entry.shape[0]
     return pl.pallas_call(
         functools.partial(feed_body, rank, tile, chunks),
-        in_specs=[IN_HBM] * 9 + [IN_VMEM] * 5,
+        in_specs=[IN_HBM] * 4 + [IN_VMEM] * 5,
         out_specs=[IN_VMEM, IN_VMEM, IN_HBM, IN_VMEM, IN_VMEM],
         out_shape=[
             jax.ShapeDtypeStruct((rows, features), f32),
@@ -916,21 +958,79 @@
         ]
         + line_sems(chunks),
         compiler_params=comm_params(5),
-    )(normed, *cots, weight, middle, units_exit, fall_entry, entries, finals, gain[None, :])
+    )(normed, cots, weight, middle, units_exit, fall_entry, entries, finals, gain[None, :])
 
 
 def per_tree(block):
     return lax.all_gather(block, "dp", axis=0, tiled=False)
 
 
-def by_adapter(gathered, picks, adapters):
-    out = []
-    for a in range(adapters):
-        total = 0.0
-        for tree in range(gathered.shape[0]):
-            total += jnp.where(picks[tree] == a, gathered[tree].astype(f32), 0.0)
-        out.append(total)
-    return jnp.stack(out)
+def combine_body(rank, pick_ref, early, model, late, head, entry_ref, final_ref, unit_ref, down_ref, exit_ref, out_ref):
+    for ref in (entry_ref, final_ref, unit_ref, down_ref, exit_ref, out_ref):
+        ref[...] = jnp.zeros_like(ref)
+
+    def one_tree(tree, carry):
+        pick = pick_ref[tree]
+
+        def block(ref, index):
+            return ref[tree, index * rank : (index + 1) * rank].astype(f32)
+
+        for k in range(3):
+            entry_ref[k, pick] += block(late, k)
+            exit_ref[k, pick] += block(head, k)
+        final_ref[0, pick] += block(late, 3)
+        out_ref[pick] += block(head, 3)
+        for k in range(2):
+            entry_ref[3 + k, pick] += block(model, k)
+            unit_ref[k, pick] += block(early, k)
+        final_ref[1, pick] += block(model, 2)
+        down_ref[pick] += block(early, 2)
+        return carry
+
+    lax.fori_loop(0, early.shape[0], one_tree, 0)
+
+
+def combine(picks, early, model, late, head, adapters, steps=4):
+    trees, _, features = early.shape
+    rank = late.shape[1] // 4
+    width = head.shape[2]
+    wide, narrow = features // steps, width // steps
+
+    def taken(array, tile):
+        return pl.BlockSpec((trees, array.shape[1], tile), lambda i, p: (0, 0, i))
+
+    def given(lead, tile):
+        shape = lead + (adapters, rank, tile)
+        return pl.BlockSpec(shape, lambda i, p: (0,) * (len(shape) - 1) + (i,))
+
+    def shape(lead, full):
+        return jax.ShapeDtypeStruct(lead + (adapters, rank, full), f32)
+
+    return pl.pallas_call(
+        functools.partial(combine_body, rank),
+        grid_spec=pltpu.PrefetchScalarGridSpec(
+            num_scalar_prefetch=1,
+            grid=(steps,),
+            in_specs=[taken(early, wide), taken(model, wide), taken(late, wide), taken(head, narrow)],
+            out_specs=[
+                given((5,), wide),
+                given((2,), wide),
+                given((2,), wide),
+                given((), wide),
+                given((3,), narrow),
+                given((), narrow),
+            ],
+        ),
+        out_shape=[
+            shape((5,), features),
+            shape((2,), features),
+            shape((2,), features),
+            shape((), features),
+            shape((3,), width),
+            shape((), width),
+        ],
+        compiler_params=pltpu.CompilerParams(vmem_limit_bytes=VMEM_LIMIT),
+    )(picks, early, model, late, head)
 
 
 def local(
@@ -972,27 +1072,29 @@
         tiled=True,
     )
 
+    w_units = lax.all_gather(
+        jnp.concatenate([gate_weight, up_weight, down_weight], axis=1), "dp", axis=0, tiled=True
+    )
     entries = jnp.swapaxes(entry_maps, 2, 3)[:, pick]
     heads_exit = head_exits[:, pick]
-    units_exit = unit_exits[:, pick]
-    out_entry = jnp.swapaxes(output_entry, 1, 2)[pick]
-    fall_entry = jnp.swapaxes(down_entry, 1, 2)[pick]
-    finals = final_exits[:, pick]
-
-    most_one, units_here = gather_norm(tokens, gain_one, (gate_weight, up_weight, down_weight))
-    w_units = lax.all_gather(units_here, "dp", axis=0, tiled=True)
-    cot_tied, _ = lax.optimization_barrier((cotangent, most_one))
-    one, mid = line_gather_start(cot_tied)
+
+    most_one = gather_norm(tokens, gain_one)
     full_one, qkv, low_one = project(most_one, w_heads, entries, heads_exit, tables)
-    one, mid, qkv = lax.optimization_barrier((one, mid, qkv))
-    cots = (cotangent, one) + line_gather_finish(one, mid)
+    cot_tied, qkv = lax.optimization_barrier((cotangent, qkv))
+    before = permute(cot_tied, [(0, 1), (1, 2), (2, 3)])
+    after = permute(cot_tied, [(3, 2), (2, 1), (1, 0)])
     attended, lse = attend(qkv, leaf_parent, seg)
-    middle, full_two, adapt_o = middle_rows(
-        attended[0], w_heads, out_entry, finals, tokens, gain_two
+    late_pick, attended = lax.optimization_barrier((pick, attended))
+    units_exit = unit_exits[:, late_pick]
+    out_entry = jnp.swapaxes(output_entry, 1, 2)[late_pick]
+    fall_entry = jnp.swapaxes(down_entry, 1, 2)[late_pick]
+    finals = final_exits[:, late_pick]
+    middle, full_two, full_cot, adapt_o = middle_rows(
+        attended[0], w_heads, cotangent, before, after, out_entry, finals, tokens, gain_two
     )
 
     grad_middle, branch, res_parts, unit_grads, model_grads = feed(
-        full_two, cots, w_units, middle, units_exit, fall_entry, entries, finals, gain_two
+        full_two, full_cot, w_units, middle, units_exit, fall_entry, entries, finals, gain_two
     )
     early = jnp.concatenate(
         [unit_grads.astype(bf16), jnp.full((rank, unit_grads.shape[1]), pick).astype(bf16)]
@@ -1002,45 +1104,35 @@
     early = per_tree(early)
     model_sum = lax.psum(model_low, "tensor")
 
-    full_branch, grad_attended, back_o, res_rows = branch_back(
+    full_branch, grad_attended, back_o, res_own, res_right, res_left = branch_back(
         branch, w_heads, finals, out_entry, res_parts
     )
-    from_left = permute(res_rows[1], [(0, 1), (1, 2), (2, 3)])
-    from_right = permute(res_rows[2], [(3, 2), (2, 1), (1, 0)])
+    grad_attended, res_right, res_left = lax.optimization_barrier((grad_attended, res_right, res_left))
+    from_left = permute(res_right, [(0, 1), (1, 2), (2, 3)])
+    from_right = permute(res_left, [(3, 2), (2, 1), (1, 0)])
     head_grads = attend_back(qkv, attended, grad_attended, lse, leaf_parent, tables, seg)
-    head_grads, model_sum = lax.optimization_barrier((head_grads, model_sum))
+    head_grads, model_sum, from_left, from_right = lax.optimization_barrier(
+        (head_grads, model_sum, from_left, from_right)
+    )
     model_all = per_tree(model_sum)
     grad_tokens, late_model, late_head = tokens_back(
         head_grads, w_heads, heads_exit, entries, tokens, gain_one, grad_middle,
         full_one, full_branch, low_one, adapt_o, back_o, attended[0],
     )
-    late = per_tree(
-        jnp.concatenate([late_model, late_head.reshape(rank, -1)], axis=0)
-    )
     result = (
         middle
-        + res_rows[0].astype(f32)
+        + res_own.astype(f32)
         + from_left.astype(f32)
         + from_right.astype(f32)
     ).astype(bf16)
 
-    picks = early[:, 3 * rank, 0].astype(f32)
-    unit_all = by_adapter(early[:, : 3 * rank], picks, adapters)
-    model_all = by_adapter(model_all, picks, adapters)
-    late_model = by_adapter(late[:, : 4 * rank], picks, adapters)
-    head_all = by_adapter(late[:, 4 * rank :].reshape((late.shape[0],) + late_head.shape), picks, adapters)
-
-    def cut(block, index):
-        return block[:, index * rank : (index + 1) * rank]
-
-    grad_entries = jnp.stack(
-        [cut(late_model, 0), cut(late_model, 1), cut(late_model, 2), cut(model_all, 0), cut(model_all, 1)]
-    ).swapaxes(2, 3)
-    grad_finals = jnp.stack([cut(late_model, 3), cut(model_all, 2)])
-    grad_heads = jnp.stack([cut(head_all, k) for k in range(3)])
-    grad_output = cut(head_all, 3).swapaxes(1, 2)
-    grad_units = jnp.stack([cut(unit_all, 0), cut(unit_all, 1)])
-    grad_down = cut(unit_all, 2).swapaxes(1, 2)
+    picks = early[:, 3 * rank, 0].astype(jnp.int32)
+    grad_entries, grad_finals, grad_units, grad_down, grad_heads, grad_output = combine(
+        picks, early, model_all, late_model, late_head, adapters
+    )
+    grad_entries = grad_entries.swapaxes(2, 3)
+    grad_output = grad_output.swapaxes(1, 2)
+    grad_down = grad_down.swapaxes(1, 2)
     return (
         result,
         grad_tokens,

time: 875 us -> 761 us (0.87)
  between operations: 56.2 us -> 15.1 us
  Pallas kernels: 721 us -> 692 us
  other arithmetic: 36.6 us -> 14.7 us
  local copies, waits for them, and re-layouts: 31.1 us -> 11.7 us
    pallas_call x1, Pallas kernels: 61.8 us -> 44.5 us  [project(): pl.pallas_call(project_body, in_specs=[IN_HBM, IN_HBM] + [IN_VMEM] * 4, o...]
    unnamed x21 -> x0, other arithmetic: 11.6 us -> none
    unnamed x48 -> x25, local copies, waits for them, and re-layouts: 12.5 us -> 3.58 us
    pallas_call x2 -> x3, Pallas kernels: 282 us -> 274 us  [the longest x1 198 us: middle_rows(): pl.pallas_call(functools.partial(middle_body, chunks), in_specs=[IN_VMEM]...]
    ppermute x7 -> x4, starting transfers between devices: 19.1 us -> 15.2 us  [permute(): return lax.ppermute(value, 'tensor', pairs)]
  transfers between devices with their start and end apart: 13 -> 9, of which waited for: 0 -> 0; matrix products, arithmetic and copies ran while one was open for 4% -> 2% of each run, Pallas kernels for 71% -> 76%
where the time goes in v4:
time: 761 us; the launch traced here: 750 us
  Pallas kernels  692 us (91%)
  starting transfers between devices  15.4 us (2%)
  between operations  15.1 us (2%)
  other arithmetic  14.7 us (2%)
  local copies, waits for them, and re-layouts  11.7 us (2%)
    pallas_call x1, Pallas kernels, middle_rows(): pl.pallas_call(functools.partial(middle_body, chunks), in_specs=[IN_VMEM]...  198 us
    pallas_call x1, Pallas kernels, tokens_back(): pl.pallas_call(functools.partial(tokens_body, chunks), in_specs=[IN_HBM,...  118 us
    pallas_call x1, Pallas kernels, feed(): pl.pallas_call(functools.partial(feed_body, rank, tile, chunks), in_specs...  110 us
    pallas_call x1, Pallas kernels, branch_back(): pl.pallas_call(branch_body, in_specs=[IN_VMEM, IN_HBM, IN_VMEM, IN_VMEM,...  97.7 us
    pallas_call x1, Pallas kernels, gather_norm(): pl.pallas_call(gather_norm_body, in_specs=[IN_VMEM, IN_VMEM], out_specs=I...  67.2 us
    pallas_call x1, Pallas kernels, project(): pl.pallas_call(project_body, in_specs=[IN_HBM, IN_HBM] + [IN_VMEM] * 4, o...  44.5 us
    pallas_call x1, Pallas kernels, attend_back(): pl.pallas_call(functools.partial(attend_back_body, seg), grid=(pairs,), i...  29.1 us
    pallas_call x1, Pallas kernels, attend(): pl.pallas_call(functools.partial(attend_body, seg), grid=(pairs,), in_spe...  19.3 us
  transfers between devices with their start and end apart: 9, of which 0 were waited for; matrix products, arithmetic and copies ran while one was open for 2% of the time, Pallas kernels for 76%

profile of v4, /device:TPU:0, one launch (start us, length us, event | category | flops | bytes accessed | tf_op | source)
XLA Modules:
  0.0 749.9 jit_solution(240130516283785071)
XLA Ops:
  7.2 0.0 copy-start
  7.2 0.0 all-gather.7.cloned.1.call-start
  7.2 2.4 pad_maximum_fusion.1
  9.7 0.0 all-gather.7.cloned.1.call-update
  9.7 0.0 all-gather.9.cloned.1.call-start
  9.7 3.2 pad_maximum_fusion
  12.9 0.0 copy-start.9
  12.9 0.0 all-gather.9.cloned.1.call-update
  12.9 0.0 all-reduce.3.cloned.1.call-start
  13.6 0.0 copy-done.9
  13.7 0.6 broadcast_in_dim.22
  14.3 67.2 %shard_map.260.x_ref = bf16[4,320,2048]{2,1,0:T(8,128)(2,1)} custom-call(bf16[320,2048]{1,0:T(8,128)(2,1)} %x_ref.5, f32[1,2048]{1,0:T(1,128)} %bitcast.43), custom_call_target="tpu_custom_call" | custom-call | tf_op jit(solution)/shard_map/pallas_call | solution.py:245
  81.4 1.4 dynamic-slice_bitcast_fusion.4.a_ref
  82.9 0.0 copy-done
  82.9 0.7 dynamic-slice_bitcast_fusion.e_ref.e_in
  83.6 0.0 copy-start.4
  83.6 44.5 %shard_map.261 = (bf16[4,320,2048]{2,1,0:T(8,128)(2,1)}, bf16[3,1280,512]{2,1,0:T(8,128)(2,1)}, bf16[1280,48]{1,0:T(8,128)(2,1)}) custom-call(bf16[4,320,2048]{2,1,0:T(8,128)(2,1)} %shard_map.260.x_ref, bf16[2048,2048]{1,0:T(8,128)(2,1)} %all-gather.7.cloned.1.call-done.w_ref, bf16[5,16,2048]{2,1,0:T(8,128)(2,1)} %dynamic-slice_bitcast_fusion.e_ref.e_in, ...), custom_call_target="tpu_custom_call" | custom-call | tf_op jit(solution)/shard_map/pallas_call | solution.py:297
  128.1 0.0 copy-done.4
  128.1 1.5 collective-permute-start.1
  129.6 5.6 collective-permute-start
  135.3 0.0 copy-done.11
  135.3 0.1 add_bitcast_fusion
  135.4 0.1 broadcast_in_dim.19
  135.4 0.7 sub.10.p_ref
  136.1 0.0 copy-done.10
  136.1 0.6 broadcast_in_dim.23
  136.7 1.3 dynamic-slice_bitcast_fusion.5.a_ref
  138.0 1.5 dynamic-slice_bitcast_fusion.3.xd_in
  139.5 1.7 dynamic-slice_bitcast_fusion.1
  141.2 19.3 %shard_map.262 = (bf16[1,1280,512]{2,1,0:T(8,128)(2,1)}, f32[4,2,1280]{2,1,0:T(2,128)}) custom-call(bf16[3,1280,512]{2,1,0:T(8,128)(2,1)} %get-tuple-element.52.q_ref.k_ref.v_ref, bf16[3,1280,512]{2,1,0:T(8,128)(2,1)} %get-tuple-element.52.q_ref.k_ref.v_ref, bf16[3,1280,512]{2,1,0:T(8,128)(2,1)} %get-tuple-element.52.q_ref.k_ref.v_ref, s32[1,512]{1,0:T(1,128)} %sub.10.p_ref), custom_call_target="tpu_custom_call" | custom-call | flops 6710886400 | bytes 5242880 | tf_op jit(solution)/shard_map/pallas_call | solution.py:706
  160.5 0.0 collective-permute-done.1.after_ref
  160.5 0.0 copy-start.8
  160.5 0.0 collective-permute-done.before_ref
  160.6 1.0 copy-done.8
  161.6 197.5 %shard_map.263 = (f32[320,2048]{1,0:T(8,128)}, bf16[4,320,2048]{2,1,0:T(8,128)(2,1)}, bf16[4,320,2048]{2,1,0:T(8,128)(2,1)}, bf16[1280,16]{1,0:T(8,128)(2,1)}) custom-call(bf16[1280,512]{1,0:T(8,128)(2,1)} %bitcast.38, bf16[2048,2048]{1,0:T(8,128)(2,1)} %all-gather.7.cloned.1.call-done.w_ref, bf16[320,2048]{1,0:T(8,128)(2,1)} %c_ref.1, ...), custom_call_target="tpu_custom_call" | custom-call | tf_op jit(solution)/shard_map/pallas_call | solution.py:384
  359.1 0.0 all-gather.9.cloned.1.call-done.w_ref
  359.1 110.2 %shard_map.264 = (f32[320,2048]{1,0:T(8,128)}, bf16[320,2048]{1,0:T(8,128)(2,1)}, bf16[4,320,2048]{2,1,0:T(8,128)(2,1)}, f32[48,2048]{1,0:T(8,128)}, f32[48,2048]{1,0:T(8,128)}) custom-call(bf16[4,320,2048]{2,1,0:T(8,128)(2,1)} %get-tuple-element.58.n_ref, bf16[4,320,2048]{2,1,0:T(8,128)(2,1)} %get-tuple-element.59.c_ref, ...), custom_call_target="tpu_custom_call" | custom-call | tf_op jit(solution)/shard_map/pallas_call | solution.py:926
  469.3 1.0 convert_element_type.29
  470.4 1.7 convert_element_type.31
  472.1 0.7 concatenate.11
  472.8 0.0 all-reduce.3.cloned.1.call-update
  472.8 0.0 all-gather.11.cloned.1.call-start
  472.9 0.5 all-gather.11.cloned.1.call-update
  473.4 0.0 all-gather.13.cloned.1.call-start
  473.4 97.7 %shard_map.265 = (bf16[4,320,2048]{2,1,0:T(8,128)(2,1)}, bf16[1,1280,512]{2,1,0:T(8,128)(2,1)}, bf16[1280,16]{1,0:T(8,128)(2,1)}, bf16[320,2048]{1,0:T(8,128)(2,...) custom-call(bf16[320,2048]{1,0:T(8,128)(2,1)} %get-tuple-element.63.b_ref, ...), custom_call_target="tpu_custom_call" | custom-call | tf_op jit(solution)/shard_map/pallas_call | solution.py:454
  571.1 6.8 collective-permute-start.2
  577.9 1.3 collective-permute-start.3
  579.2 29.1 %shard_map.266.d_ref = bf16[3,1280,512]{2,1,0:T(8,128)(2,1)} custom-call(bf16[3,1280,512]{2,1,0:T(8,128)(2,1)} %get-tuple-element.52.q_ref.k_ref.v_ref, bf16[3,1280,512]{2,1,0:T(8,128)(2,1)} %get-tuple-element.52.q_ref.k_ref.v_ref, bf16[3,1280,512]{2,1,0:T(8,128)(2,1)} %get-tuple-element.52.q_ref.k_ref.v_ref, bf16[1,1280,512]{2,1,0:T(8,128)(2,1)} %get-tuple-element.54.o_ref, ...), custom_call_target="tpu_custom_call" | custom-call | flops 16777216000 | bytes 10485760 | tf_op jit(solution)/shard_map/pallas_call | solution.py:769
  608.3 0.0 collective-permute-done.2
  608.3 0.0 copy-start.6
  608.3 0.0 collective-permute-done.3
  608.3 0.0 copy-start.7
  608.3 0.0 all-gather.13.cloned.1.call-update
  608.3 1.0 copy-done.6
  609.3 0.4 copy-done.7
  609.8 118.0 %shard_map.267 = (bf16[320,2048]{1,0:T(8,128)(2,1)}, bf16[8,64,2048]{2,1,0:T(8,128)(2,1)}, bf16[8,64,512]{2,1,0:T(8,128)(2,1)}) custom-call(bf16[3,1280,512]{2,1,0:T(8,128)(2,1)} %shard_map.266.d_ref, bf16[2048,2048]{1,0:T(8,128)(2,1)} %all-gather.7.cloned.1.call-done.w_ref, bf16[3,16,512]{2,1,0:T(8,128)(2,1)} %dynamic-slice_bitcast_fusion.4.a_ref, ...), custom_call_target="tpu_custom_call" | custom-call | tf_op jit(solution)/shard_map/pallas_call | solution.py:620
  727.8 0.0 copy-done.2
  727.8 0.0 copy-done.5
  727.8 3.6 add_convert_fusion
  731.5 1.5 fusion.pick_ref
  732.9 8.9 %shard_map.268 = (f32[5,8,16,2048]{3,2,1,0:T(8,128)}, f32[2,8,16,2048]{3,2,1,0:T(8,128)}, f32[2,8,16,2048]{3,2,1,0:T(8,128)}, f32[8,16,2048]{2,1,0:T(8,128)}, f3...) custom-call(s32[8]{0:T(128)} %fusion.pick_ref, bf16[8,64,2048]{2,1,0:T(8,128)(2,1)} %bitcast.41, ...), custom_call_target="tpu_custom_call" | custom-call | tf_op jit(solution)/shard_map/pallas_call | solution.py:1009
  741.8 0.0 copy-done.3
  741.8 1.1 copy.35
  742.9 0.0 copy-done.1
  (10 shorter events, 0.0 us)
Async XLA Ops:
  7.2 75.7 %copy-start = (bf16[5,8,2048,16]{2,3,1,0:T(8,128)(2,1)S(1)}, bf16[5,8,2048,16]{2,3,1,0:T(8,128)(2,1)}, u32[]{:S(2)}) copy-start(bf16[5,8,2048,16]{2,3,1,0:T(8,128)(2,1)} %param.32) | copy-start | bytes 7864324
  7.2 76.5 %all-gather.7.cloned.1.call-start = ((), (), s32[]{:S(2)}) async-start(), calls=%async_computation | async-start | bytes 9437184 | tf_op jit(solution)/shard_map/all_gather | solution.py:1068
  9.7 349.4 %all-gather.9.cloned.1.call-start = ((), (), s32[]{:S(2)}) async-start(), calls=%async_computation.1 | async-start | bytes 28311552 | tf_op jit(solution)/shard_map/all_gather | solution.py:1075
  12.9 0.7 copy-start.9
  12.9 595.3 %all-reduce.3.cloned.1.call-start = ((), (), s32[]{:S(2)}) async-start(), calls=%async_computation.2 | async-start | bytes 393216 | tf_op jit(solution)/shard_map/psum | solution.py:1105
  83.6 44.5 %copy-start.4 = (bf16[320,2048]{1,0:T(8,128)(2,1)S(1)}, bf16[320,2048]{1,0:T(8,128)(2,1)}, u32[]{:S(2)}) copy-start(bf16[320,2048]{1,0:T(8,128)(2,1)} %c_ref.1) | copy-start | bytes 3932164
  83.6 51.7 %copy-start.11 = (s32[1,20]{1,0:T(1,128)S(1)}, s32[1,20]{1,0:T(1,128)}, u32[]{:S(2)}) copy-start(s32[1,20]{1,0:T(1,128)} %param.38) | copy-start | bytes 244
  83.6 52.5 %copy-start.10 = (bf16[2048]{0:T(1024)(128)(2,1)S(1)}, bf16[2048]{0:T(1024)(128)(2,1)}, u32[]{:S(2)}) copy-start(bf16[2048]{0:T(1024)(128)(2,1)} %param.24) | copy-start | bytes 12292
  128.1 32.4 %collective-permute-start.1 = (bf16[320,2048]{1,0:T(8,128)(2,1)S(1)}, bf16[320,2048]{1,0:T(8,128)(2,1)S(1)}, u32[]{:S(2)}, u32[]{:S(2)}) collective-permute-start(bf16[320,2048]{1,0:T(8,128)(2,1)S(1)} %copy-done.4), channel_id=1, source_target_pairs={{3,2},{2,1},{1,0},{7,6},{6,5},{5,4},{11,10},{10,9},{9,8},{15,14},{... | collective-permute-start | bytes 3932168 | tf_op jit(solution)/shard_map/ppermute | solution.py:36
  129.6 30.9 %collective-permute-start = (bf16[320,2048]{1,0:T(8,128)(2,1)S(1)}, bf16[320,2048]{1,0:T(8,128)(2,1)}, u32[]{:S(2)}, u32[]{:S(2)}) collective-permute-start(bf16[320,2048]{1,0:T(8,128)(2,1)S(1)} %copy-done.4), channel_id=1, source_target_pairs={{0,1},{1,2},{2,3},{4,5},{5,6},{6,7},{8,9},{9,10},{10,11},{12,13},{... | collective-permute-start | bytes 3932168 | tf_op jit(solution)/shard_map/ppermute | solution.py:36
  160.5 1.1 copy-start.8
  472.8 258.7 %all-gather.11.cloned.1.call-start = ((), (), s32[]{:S(2)}) async-start(), calls=%async_computation.3 | async-start | bytes 2359296 | tf_op jit(solution)/shard_map/all_gather | solution.py:965
  473.4 259.5 %all-gather.13.cloned.1.call-start = ((), (), s32[]{:S(2)}) async-start(), calls=%async_computation.4 | async-start | bytes 1769472 | tf_op jit(solution)/shard_map/all_gather | solution.py:965
  571.1 37.2 %collective-permute-start.2 = (bf16[320,2048]{1,0:T(8,128)(2,1)}, bf16[320,2048]{1,0:T(8,128)(2,1)S(1)}, u32[]{:S(2)}, u32[]{:S(2)}) collective-permute-start(bf16[320,2048]{1,0:T(8,128)(2,1)} %get-tuple-element.72), channel_id=1, source_target_pairs={{0,1},{1,2},{2,3},{4,5},{5,6},{6,7},{8,9},{9,10},{10,11},{12,13},{... | collective-permute-start | bytes 3932168 | tf_op jit(solution)/shard_map/ppermute | solution.py:36
  577.9 30.4 %collective-permute-start.3 = (bf16[320,2048]{1,0:T(8,128)(2,1)}, bf16[320,2048]{1,0:T(8,128)(2,1)S(1)}, u32[]{:S(2)}, u32[]{:S(2)}) collective-permute-start(bf16[320,2048]{1,0:T(8,128)(2,1)} %get-tuple-element.73), channel_id=1, source_target_pairs={{3,2},{2,1},{1,0},{7,6},{6,5},{5,4},{11,10},{10,9},{9,8},{15,14},{... | collective-permute-start | bytes 3932168 | tf_op jit(solution)/shard_map/ppermute | solution.py:36
  608.3 1.1 copy-start.6
  608.3 1.5 copy-start.7
  609.8 118.0 %copy-start.2 = (f32[320,2048]{1,0:T(8,128)S(1)}, f32[320,2048]{1,0:T(8,128)}, u32[]{:S(2)}) copy-start(f32[320,2048]{1,0:T(8,128)} %get-tuple-element.57.mid_ref) | copy-start | bytes 7864324
  609.8 118.0 %copy-start.5 = (bf16[320,2048]{1,0:T(8,128)(2,1)S(1)}, bf16[320,2048]{1,0:T(8,128)(2,1)}, u32[]{:S(2)}) copy-start(bf16[320,2048]{1,0:T(8,128)(2,1)} %get-tuple-element.65) | copy-start | bytes 3932164
  732.9 8.9 %copy-start.3 = (bf16[320,2048]{1,0:T(8,128)(2,1)S(1)}, bf16[320,2048]{1,0:T(8,128)(2,1)}, u32[]{:S(2)}) copy-start(bf16[320,2048]{1,0:T(8,128)(2,1)} %get-tuple-element.105) | copy-start | bytes 3932164
  732.9 10.0 %copy-start.1 = (bf16[5,8,2048,16]{2,3,1,0:T(8,128)(2,1)S(1)}, bf16[5,8,2048,16]{2,3,1,0:T(8,128)(2,1)}, u32[]{:S(2)}) copy-start(bf16[5,8,2048,16]{2,3,1,0:T(8,128)(2,1)} %param.32) | copy-start | bytes 7864324
Sparse Core Ops, SparseCore 0:
  10.5 57.0 all-gather.6
  70.1 125.3 all-gather.8
  472.9 40.0 all-reduce.2
  515.5 27.3 all-gather.10
  608.5 26.4 all-gather.12

commit v5 on v4

--- a/solution.py
+++ b/solution.py
@@ -98,15 +98,17 @@
 
 
 class Gather:
-    def __init__(self, place, buf, send, recv, chunks):
+    def __init__(self, place, buf, send, recv, chunks, own=None):
         self.place, self.buf, self.sems, self.chunks = place, buf, (send, recv), chunks
         self.rows = buf.shape[1] // chunks
+        self.own = own
 
     def copy(self, side, step, chunk, shard, target):
-        where = self.buf.at[shard, chunk_rows(chunk, self.rows)]
+        rows = chunk_rows(chunk, self.rows)
+        where = self.buf.at[shard, rows]
         spot = (0 if side == 1 else 1, step - 1, chunk)
         return pltpu.make_async_remote_copy(
-            src_ref=where,
+            src_ref=where if self.own is None or step > 1 else self.own.at[rows],
             dst_ref=where,
             send_sem=self.sems[0].at[spot],
             recv_sem=self.sems[1].at[spot],
@@ -227,16 +229,19 @@
     )
 
 
-def gather_norm_body(x_ref, gain_ref, buf, send, recv):
+def gather_norm_body(x_ref, gain_ref, buf, own, sem, send, recv):
     place = lax.axis_index("tensor")
     greet(place)
     rows = x_ref[...].astype(f32)
     rms = lax.rsqrt(jnp.mean(rows * rows, axis=1, keepdims=True) + eps)
-    buf[place] = (rows * rms * gain_ref[...]).astype(bf16)
-    gather = Gather(place, buf, send, recv, 1)
-    for step in range(1, LINE - 1):
-        gather.send(step, 0)
-        gather.arrive(step, 0)
+    own[...] = (rows * rms * gain_ref[...]).astype(bf16)
+    gather = Gather(place, buf, send, recv, 1, own)
+    gather.send(1, 0)
+    (kept,) = fetch([(own, buf.at[place])], sem)
+    gather.arrive(1, 0)
+    gather.send(2, 0)
+    kept.wait()
+    gather.arrive(2, 0)
     gather.drain(stop=LINE - 1)
 
 
@@ -245,20 +250,47 @@
     return pl.pallas_call(
         gather_norm_body,
         in_specs=[IN_VMEM, IN_VMEM],
-        out_specs=IN_VMEM,
+        out_specs=IN_HBM,
         out_shape=jax.ShapeDtypeStruct((LINE, rows, features), bf16),
-        scratch_shapes=line_sems(1),
+        scratch_shapes=[pltpu.VMEM((rows, features), bf16), pltpu.SemaphoreType.DMA((1,))]
+        + line_sems(1),
         compiler_params=comm_params(0),
     )(x, gain[None, :])
 
 
 def project_body(
-    x_ref, w_ref, e_ref, a_ref, cos_ref, sin_ref, buf, y_ref, l_ref, wv, xsem, wsem, send, recv
+    x_ref, w_ref, e_ref, a_ref, cos_ref, sin_ref, kept_ref, y_ref, l_ref,
+    buf, yv, wv, xsem, wsem, ysem, send, recv,
 ):
     place = lax.axis_index("tensor")
     groups, _, width = y_ref.shape
     rows, rank = x_ref.shape[1], a_ref.shape[1]
     edge = (place == 0) | (place == LINE - 1)
+    last = place ^ (LINE - 1)
+
+    def passed(side):
+        shard = place - side * (LINE - 2)
+        index = 0 if side == 1 else 1
+        return pltpu.make_async_remote_copy(
+            src_ref=x_ref.at[shard],
+            dst_ref=buf.at[shard],
+            send_sem=send.at[index],
+            recv_sem=recv.at[index],
+            device_id={"tensor": place + side},
+            device_id_type=MESH,
+        )
+
+    def came(side):
+        index = 0 if side == 1 else 1
+        return pltpu.make_async_remote_copy(
+            src_ref=x_ref.at[last],
+            dst_ref=buf.at[last],
+            send_sem=send.at[index],
+            recv_sem=recv.at[index],
+            device_id={"tensor": place - side},
+            device_id_type=MESH,
+        )
+
     copies = []
     for slot in range(LINE):
         copy = pltpu.make_async_copy(x_ref.at[place ^ slot], buf.at[place ^ slot], xsem.at[slot])
@@ -269,16 +301,20 @@
         copies.append(copy)
     (load,) = fetch([(w_ref.at[:, : groups * width], wv)], wsem)
     greet(place)
+    for side in SIDES:
+        pl.when(far_of(place, side) == LINE - 2)(passed(side).start)
     for copy in copies[:-1]:
         copy.wait()
-    gather = Gather(place, buf, send, recv, 1)
-    gather.send(LINE - 1, 0)
     load.wait()
+    outs = []
     for slot in range(LINE):
+        shard = place ^ slot
         if slot == LINE - 1:
             pl.when(jnp.logical_not(edge))(copies[slot].wait)
-            gather.arrive(slot, 0)
-        shard = place ^ slot
+            for side in SIDES:
+                pl.when(far_of(place, side) == LINE - 1)(came(side).wait_recv)
+            kept = pltpu.make_async_copy(buf.at[last], kept_ref.at[last], xsem.at[slot])
+            pl.when(edge)(kept.start)
         mine = pl.ds(pl.multiple_of(shard * rows, rows), rows)
         low = nt(buf[shard], e_ref[:groups].reshape(groups * rank, -1)).astype(bf16)
         l_ref[mine] = low
@@ -287,8 +323,15 @@
             value = nn(buf[shard], wv[:, band]) + nn(low[:, g * rank : (g + 1) * rank], a_ref[g])
             if g < groups - 1:
                 value = turn(value, cos_ref[mine], sin_ref[mine])
-            y_ref[g, mine] = value.astype(bf16)
-    gather.drain(start=LINE - 1)
+            yv[g, mine] = value.astype(bf16)
+            out = pltpu.make_async_copy(yv.at[g, mine], y_ref.at[g, mine], ysem.at[slot, g])
+            out.start()
+            outs.append(out)
+    pl.when(edge)(kept.wait)
+    for out in outs:
+        out.wait()
+    for side in SIDES:
+        pl.when(far_of(place, side) == LINE - 2)(passed(side).wait_send)
 
 
 def project(x, weight, entries, exits, tables):
@@ -297,29 +340,34 @@
     return pl.pallas_call(
         project_body,
         in_specs=[IN_HBM, IN_HBM] + [IN_VMEM] * 4,
-        out_specs=[IN_VMEM] * 3,
+        out_specs=[IN_HBM, IN_HBM, IN_VMEM],
         out_shape=[
             jax.ShapeDtypeStruct((LINE, rows, features), bf16),
             jax.ShapeDtypeStruct((groups, LINE * rows, width), bf16),
             jax.ShapeDtypeStruct((LINE * rows, groups * rank), bf16),
         ],
         scratch_shapes=[
+            pltpu.VMEM((LINE, rows, features), bf16),
+            pltpu.VMEM((groups, LINE * rows, width), bf16),
             pltpu.VMEM((features, groups * width), bf16),
             pltpu.SemaphoreType.DMA((LINE,)),
             pltpu.SemaphoreType.DMA((1,)),
-        ]
-        + line_sems(1),
+            pltpu.SemaphoreType.DMA((LINE, groups)),
+            pltpu.SemaphoreType.DMA((2,)),
+            pltpu.SemaphoreType.DMA((2,)),
+        ],
+        input_output_aliases={0: 0},
         compiler_params=comm_params(4),
     )(x, weight, entries, exits, *tables)
 
 
 def middle_body(
     chunks, d_ref, w_ref, c_ref, before_ref, after_ref, a_ref, e_ref, x_ref, gain_ref, mid_ref, buf, cbuf, low_ref,
-    part, held, wv, wsem, s_send, s_recv, g_send, g_recv, c_send, c_recv,
+    part, held, own, wv, wsem, nsem, s_send, s_recv, g_send, g_recv, c_send, c_recv,
 ):
     place = lax.axis_index("tensor")
     width = d_ref.shape[1]
-    load, own = fetch([(w_ref.at[:, 3 * width :], wv), (c_ref, cbuf.at[place])], wsem)
+    load, own_cot = fetch([(w_ref.at[:, 3 * width :], wv), (c_ref, cbuf.at[place])], wsem)
 
     def neighbours(act):
         @pl.when(place > 0)
@@ -333,11 +381,10 @@
     neighbours(lambda copy: copy.start())
     greet(place)
     load.wait()
-    own.wait()
-    cots = Gather(place, cbuf, c_send, c_recv, 1)
+    cots = Gather(place, cbuf, c_send, c_recv, chunks)
     rows = part.shape[1]
     summed = Sum(place, part, held, s_send, s_recv, chunks)
-    gather = Gather(place, buf, g_send, g_recv, chunks)
+    gather = Gather(place, buf, g_send, g_recv, chunks, own)
     for slot in (3, 2, 1, 0):
         shard = place ^ slot
         mine = pl.ds(pl.multiple_of(shard * rows, rows), rows)
@@ -346,33 +393,42 @@
         low_ref[mine] = low
         part[shard] = (nt(d, wv[...]) + nn(low, e_ref[0])).astype(bf16)
         if slot == 3:
-            for chunk in range(chunks):
-                summed.send(1, chunk)
+            summed.send(1, 0)
     neighbours(lambda copy: copy.wait())
-    cots.send(2, 0)
     size = rows // chunks
-    for turn_ in range(chunks + 2):
-        if turn_ == 2:
-            cots.arrive(2, 0)
-            cots.send(3, 0)
-        if turn_ < chunks:
-            summed.send(2, turn_)
-            summed.send(3, turn_)
-            summed.total(turn_, mid_ref)
-            here = chunk_rows(turn_, size)
+    kept = []
+    for now in range(chunks + 3):
+        if now + 1 < chunks:
+            summed.send(1, now + 1)
+        if now < chunks:
+            summed.send(2, now)
+            summed.send(3, now)
+            cots.send(2, now)
+        chunk = now - 1
+        if 0 <= chunk < chunks:
+            summed.total(chunk, mid_ref)
+            here = chunk_rows(chunk, size)
             value = mid_ref[here] + x_ref[here].astype(f32)
             mid_ref[here] = value
             rms = lax.rsqrt(jnp.mean(value * value, axis=1, keepdims=True) + eps)
-            buf[place, here] = (value * rms * gain_ref[...]).astype(bf16)
-            gather.send(1, turn_)
+            own[here] = (value * rms * gain_ref[...]).astype(bf16)
+            gather.send(1, chunk)
+            copy = pltpu.make_async_copy(own.at[here], buf.at[place, here], nsem.at[chunk])
+            copy.start()
+            kept.append(copy)
+            cots.arrive(2, chunk)
+            cots.send(3, chunk)
         for step in (1, 2):
-            chunk = turn_ - step
+            chunk = now - 1 - step
             if 0 <= chunk < chunks:
                 gather.arrive(step, chunk)
                 gather.send(step + 1, chunk)
     for chunk in range(chunks):
+        cots.arrive(3, chunk)
         gather.arrive(3, chunk)
-    cots.arrive(3, 0)
+    own_cot.wait()
+    for copy in kept:
+        copy.wait()
     summed.drain()
     gather.drain()
     cots.drain(start=2)
@@ -384,7 +440,7 @@
     return pl.pallas_call(
         functools.partial(middle_body, chunks),
         in_specs=[IN_VMEM] + [IN_HBM] * 4 + [IN_VMEM] * 4,
-        out_specs=[IN_VMEM] * 4,
+        out_specs=[IN_VMEM, IN_HBM, IN_HBM, IN_VMEM],
         out_shape=[
             jax.ShapeDtypeStruct((rows, features), f32),
             jax.ShapeDtypeStruct((LINE, rows, features), bf16),
@@ -394,19 +450,21 @@
         scratch_shapes=[
             pltpu.VMEM((LINE, rows, features), bf16),
             pltpu.VMEM((2, LINE - 1, rows, features), bf16),
+            pltpu.VMEM((rows, features), bf16),
             pltpu.VMEM((features, width), bf16),
             pltpu.SemaphoreType.DMA((4,)),
+            pltpu.SemaphoreType.DMA((chunks,)),
         ]
         + line_sems(chunks)
         + line_sems(chunks)
-        + line_sems(1),
+        + line_sems(chunks),
         compiler_params=comm_params(1),
     )(attended, weight, cot, before, after, exits, finals, x, gain[None, :])
 
 
 def branch_body(
-    b_ref, w_ref, e_ref, a_ref, p_ref, buf, y_ref, l_ref, own_ref, right_ref, left_ref,
-    part, held, wv, wsem, send, recv, s_send, s_recv,
+    b_ref, w_ref, e_ref, a_ref, p_ref, kept_ref, y_ref, l_ref, own_ref, right_ref, left_ref,
+    buf, part, held, wv, ksem, wsem, send, recv, s_send, s_recv,
 ):
     place = lax.axis_index("tensor")
     rows = b_ref.shape[0]
@@ -419,6 +477,7 @@
     parts.wait()
     summed.send(1, 0)
     load.wait()
+    kept = []
     for slot in range(LINE):
         if slot:
             gather.arrive(slot, 0)
@@ -444,6 +503,11 @@
         low = nt(buf[shard], e_ref[0]).astype(bf16)
         l_ref[mine] = low
         y_ref[0, mine] = (nn(buf[shard], wv[...]) + nn(low, a_ref[...])).astype(bf16)
+        copy = pltpu.make_async_copy(buf.at[shard], kept_ref.at[shard], ksem.at[slot])
+        copy.start()
+        kept.append(copy)
+    for copy in kept:
+        copy.wait()
     gather.drain()
     summed.drain(LINE - 1)
 
@@ -454,7 +518,7 @@
     return pl.pallas_call(
         branch_body,
         in_specs=[IN_VMEM, IN_HBM, IN_VMEM, IN_VMEM, IN_HBM],
-        out_specs=[IN_VMEM] * 6,
+        out_specs=[IN_HBM] + [IN_VMEM] * 5,
         out_shape=[
             jax.ShapeDtypeStruct((LINE, rows, features), bf16),
             jax.ShapeDtypeStruct((1, LINE * rows, width), bf16),
@@ -463,8 +527,10 @@
         + [jax.ShapeDtypeStruct((rows, features), bf16)] * 3,
         scratch_shapes=[
             pltpu.VMEM((LINE, rows, features), bf16),
+            pltpu.VMEM((LINE, rows, features), bf16),
             pltpu.VMEM((2, LINE - 1, rows, features), bf16),
             pltpu.VMEM((features, width), bf16),
+            pltpu.SemaphoreType.DMA((LINE,)),
             pltpu.SemaphoreType.DMA((2,)),
         ]
         + line_sems(1)
@@ -476,11 +542,12 @@
 def tokens_body(
     chunks, d_ref, w_ref, a_ref, e_ref, x_ref, gain_ref, mid_ref, n_ref, b_ref, lone_ref, lo_ref, bo_ref, o_ref,
     out_ref, model_ref, head_ref,
-    part, held, acc, dv, wv, midv, nv, bv, low, block, extra, wsem, send, recv, x_send, x_recv, t_send, t_recv,
+    part, held, acc, dv, wv, midv, nv, bv, low, block, extra, wsem, send, recv, x_send, x_recv, t_send, t_recv, h_send, h_recv,
 ):
     place = lax.axis_index("tensor")
     tree = lax.axis_index("dp")
-    trees = Trees(tree, (model_ref, head_ref), t_send, t_recv)
+    trees = Trees(tree, model_ref, t_send, t_recv)
+    heads = Trees(tree, head_ref, h_send, h_recv)
     groups, total, width = d_ref.shape
     rank = a_ref.shape[1]
     loads = fetch(
@@ -495,6 +562,7 @@
         load.wait()
     rows = part.shape[1]
     summed = Sum(place, part, held, send, recv, chunks)
+    gather = Gather(place, extra, x_send, x_recv, 1)
     entry = e_ref[:groups].reshape(groups * rank, -1)
     for slot in (3, 2, 1, 0):
         shard = place ^ slot
@@ -506,7 +574,6 @@
         if slot == 3:
             for chunk in range(chunks):
                 summed.send(1, chunk)
-    summed.send(2, 0)
     for load in loads[2:]:
         load.wait()
 
@@ -516,85 +583,87 @@
     joined = nn(turned(low[...]), nv[...].reshape(total, -1))
     final = nn(turned(lo_ref[...]), bv[...].reshape(total, -1))
     extra[place] = jnp.concatenate([joined, final], axis=0).astype(bf16)
-    gather = Gather(place, extra, x_send, x_recv, 1)
     gather.send(1, 0)
-    summed.send(3, 0)
+    for chunk in range(chunks):
+        summed.send(2, chunk)
     low_one = turned(lone_ref[...])
     for g in range(groups):
         band = slice(g * rank, (g + 1) * rank)
         head_ref[tree, band] = nn(low_one[band], dv[g]).astype(bf16)
     head_ref[tree, groups * rank :] = nn(turned(bo_ref[...]), o_ref[...]).astype(bf16)
-    size = rows // chunks
-
-    def finish(chunk):
-        finish_tokens(summed, chunk, size, acc, x_ref, gain_ref, midv, out_ref)
-
+    heads.send(0)
     gather.arrive(1, 0)
     gather.send(2, 0)
-    summed.send(2, 1)
+    summed.send(3, 0)
     gather.arrive(2, 0)
     gather.send(3, 0)
-    finish(0)
     summed.send(3, 1)
+    heads.advance(1)
     gather.arrive(3, 0)
     model_ref[tree] = functools.reduce(
         jnp.add, [extra[shard].astype(f32) for shard in range(LINE)]
     ).astype(bf16)
     trees.send(0)
-    for chunk in range(2, chunks):
-        summed.send(2, chunk)
-        summed.send(3, chunk)
-        if chunk - 1 < trees.rounds:
-            trees.arrive(chunk - 2)
-            trees.send(chunk - 1)
-        finish(chunk - 1)
-    for number in range(chunks - 1, trees.rounds):
-        trees.arrive(number - 1)
-        trees.send(number)
-    finish(chunks - 1)
-    trees.arrive(trees.rounds - 1)
+    summed.send(3, 2)
+    trees.advance(1)
+    heads.advance(2)
+    summed.send(3, 3)
+    size = rows // chunks
+
+    def finish(chunk):
+        finish_tokens(summed, chunk, size, acc, x_ref, gain_ref, midv, out_ref)
+
+    finish(0)
+    trees.advance(2)
+    finish(1)
+    for number in range(3, trees.rounds):
+        trees.advance(number)
+        heads.advance(number)
+    finish(2)
+    finish(3)
+    for blocks in (trees, heads):
+        blocks.arrive(blocks.rounds - 1)
+        blocks.drain()
     summed.drain()
     gather.drain()
-    trees.drain()
 
 
 class Trees:
-    def __init__(self, tree, refs, send, recv):
-        self.tree, self.refs, self.sems = tree, refs, (send, recv)
-        self.rounds = refs[0].shape[0].bit_length() - 1
+    def __init__(self, tree, ref, send, recv):
+        self.tree, self.ref, self.sems = tree, ref, (send, recv)
+        self.rounds = ref.shape[0].bit_length() - 1
         self.partners = [self.partner(number) for number in range(self.rounds)]
 
     def partner(self, number):
         size = 1 << number
         return self.tree + size - 2 * size * ((self.tree // size) % 2)
 
-    def copies(self, number, owner):
+    def copy(self, number, owner):
         size = 1 << number
         here = pl.ds((owner // size) * size, size)
-        return [
-            pltpu.make_async_remote_copy(
-                src_ref=ref.at[here],
-                dst_ref=ref.at[here],
-                send_sem=self.sems[0].at[number, k],
-                recv_sem=self.sems[1].at[number, k],
-                device_id={"dp": self.partner(number)},
-                device_id_type=MESH,
-            )
-            for k, ref in enumerate(self.refs)
-        ]
+        return pltpu.make_async_remote_copy(
+            src_ref=self.ref.at[here],
+            dst_ref=self.ref.at[here],
+            send_sem=self.sems[0].at[number],
+            recv_sem=self.sems[1].at[number],
+            device_id={"dp": self.partner(number)},
+            device_id_type=MESH,
+        )
 
     def send(self, number):
-        for copy in self.copies(number, self.tree):
-            copy.start()
+        self.copy(number, self.tree).start()
 
     def arrive(self, number):
-        for copy in self.copies(number, self.partner(number)):
-            copy.wait_recv()
+        self.copy(number, self.partner(number)).wait_recv()
+
+    def advance(self, number):
+        if number < self.rounds:
+            self.arrive(number - 1)
+            self.send(number)
 
     def drain(self):
         for number in range(self.rounds):
-            for copy in self.copies(number, self.tree):
-                copy.wait_send()
+            self.copy(number, self.tree).wait_send()
 
 
 def finish_tokens(summed, chunk, size, acc, x_ref, gain_ref, mid_ref, out_ref):
@@ -616,7 +685,7 @@
     rank = exits.shape[1]
     deep = (groups + 1) * rank
     trees = lax.axis_size("dp")
-    sems = pltpu.SemaphoreType.DMA((trees.bit_length() - 1, 2))
+    sems = pltpu.SemaphoreType.DMA((trees.bit_length() - 1,))
     return pl.pallas_call(
         functools.partial(tokens_body, chunks),
         in_specs=[IN_HBM, IN_HBM] + [IN_VMEM] * 4 + [IN_HBM] * 3 + [IN_VMEM] * 4,
@@ -642,7 +711,7 @@
         ]
         + line_sems(chunks)
         + line_sems(1)
-        + [sems, sems],
+        + [sems] * 4,
         compiler_params=comm_params(3),
     )(
         head_grads, weight, exits, entries, x, gain[None, :], grad_middle, normed, branch,
@@ -794,7 +863,7 @@
 
 def feed_body(
     rank, tile, chunks,
-    n_ref, c_ref, w_ref, mid_ref,
+    n_ref, c_ref, wg_ref, wu_ref, wd_ref, mid_ref,
     xu_in, xd_in, e_in, f_in, gain_ref,
     grad_ref, low_grad_ref, res_ref, unit_ref, model_ref,
     x_ref, e_ref, f_ref, midv, nbuf, cbuf, wbuf, low, low_t, acc_res, acc_back, acc_low, part, held, resv,
@@ -812,8 +881,8 @@
         act(pltpu.make_async_copy(c_ref.at[shard], cbuf.at[into], csem.at[into]))
 
     def load_weights(index, into, act):
-        for k in range(3):
-            columns = pl.ds(pl.multiple_of(k * units + index * tile, tile), tile)
+        columns = pl.ds(pl.multiple_of(index * tile, tile), tile)
+        for k, w_ref in enumerate((wg_ref, wu_ref, wd_ref)):
             act(pltpu.make_async_copy(w_ref.at[:, columns], wbuf.at[into, k], wsem.at[into, k]))
 
     def start(copy):
@@ -919,13 +988,13 @@
     summed.drain()
 
 
-def feed(normed, cots, weight, middle, units_exit, fall_entry, entries, finals, gain, tile=512, chunks=4):
+def feed(normed, cots, weights, middle, units_exit, fall_entry, entries, finals, gain, tile=512, chunks=4):
     _, rows, features = normed.shape
-    units = weight.shape[1] // 3
+    units = weights[0].shape[1]
     rank = fall_entry.shape[0]
     return pl.pallas_call(
         functools.partial(feed_body, rank, tile, chunks),
-        in_specs=[IN_HBM] * 4 + [IN_VMEM] * 5,
+        in_specs=[IN_HBM] * 6 + [IN_VMEM] * 5,
         out_specs=[IN_VMEM, IN_VMEM, IN_HBM, IN_VMEM, IN_VMEM],
         out_shape=[
             jax.ShapeDtypeStruct((rows, features), f32),
@@ -958,7 +1027,29 @@
         ]
         + line_sems(chunks),
         compiler_params=comm_params(5),
-    )(normed, cots, weight, middle, units_exit, fall_entry, entries, finals, gain[None, :])
+    )(normed, cots, *weights, middle, units_exit, fall_entry, entries, finals, gain[None, :])
+
+
+def pick_body(pick_ref, *refs):
+    count = len(refs) // 2
+    for source, target in zip(refs[:count], refs[count:]):
+        target[...] = source[...].reshape(target.shape)
+
+
+def picked(pick, arrays):
+    shapes = [a.shape[:1] + a.shape[2:] for a in arrays]
+    return pl.pallas_call(
+        pick_body,
+        grid_spec=pltpu.PrefetchScalarGridSpec(
+            num_scalar_prefetch=1,
+            grid=(1,),
+            in_specs=[
+                pl.BlockSpec(a.shape[:1] + (1,) + a.shape[2:], lambda i, p: (0, p[0], 0, 0)) for a in arrays
+            ],
+            out_specs=[pl.BlockSpec(shape, lambda i, p: (0, 0, 0)) for shape in shapes],
+        ),
+        out_shape=[jax.ShapeDtypeStruct(shape, bf16) for shape in shapes],
+    )(pick, *arrays)
 
 
 def per_tree(block):
@@ -1072,11 +1163,21 @@
         tiled=True,
     )
 
-    w_units = lax.all_gather(
-        jnp.concatenate([gate_weight, up_weight, down_weight], axis=1), "dp", axis=0, tiled=True
-    )
-    entries = jnp.swapaxes(entry_maps, 2, 3)[:, pick]
-    heads_exit = head_exits[:, pick]
+    w_units = [
+        lax.all_gather(w, "dp", axis=0, tiled=True) for w in (gate_weight, up_weight, down_weight)
+    ]
+    entries, heads_exit, units_exit, out_entry, fall_entry, finals = picked(
+        adapter_pick,
+        (
+            jnp.swapaxes(entry_maps, 2, 3),
+            head_exits,
+            unit_exits,
+            jnp.swapaxes(output_entry, 1, 2)[None],
+            jnp.swapaxes(down_entry, 1, 2)[None],
+            final_exits,
+        ),
+    )
+    out_entry, fall_entry = out_entry[0], fall_entry[0]
 
     most_one = gather_norm(tokens, gain_one)
     full_one, qkv, low_one = project(most_one, w_heads, entries, heads_exit, tables)
@@ -1084,11 +1185,6 @@
     before = permute(cot_tied, [(0, 1), (1, 2), (2, 3)])
     after = permute(cot_tied, [(3, 2), (2, 1), (1, 0)])
     attended, lse = attend(qkv, leaf_parent, seg)
-    late_pick, attended = lax.optimization_barrier((pick, attended))
-    units_exit = unit_exits[:, late_pick]
-    out_entry = jnp.swapaxes(output_entry, 1, 2)[late_pick]
-    fall_entry = jnp.swapaxes(down_entry, 1, 2)[late_pick]
-    finals = final_exits[:, late_pick]
     middle, full_two, full_cot, adapt_o = middle_rows(
         attended[0], w_heads, cotangent, before, after, out_entry, finals, tokens, gain_two
     )

time: 761 us -> 851 us (1.12)
  Pallas kernels: 692 us -> 791 us
    pallas_call x1, Pallas kernels: 198 us -> 303 us  [middle_rows(): pl.pallas_call(functools.partial(middle_body, chunks), in_specs=[IN_VMEM]...]
  transfers between devices with their start and end apart: 9 -> 11, of which waited for: 0 -> 2; matrix products, arithmetic and copies ran while one was open for 2% -> 1% of each run, Pallas kernels for 76% -> 80%
where the time goes in v5:
time: 851 us; the launch traced here: 842 us
  Pallas kernels  791 us (93%)
  between operations  15.4 us (2%)
  starting transfers between devices  13.8 us (2%)
  other arithmetic  11.4 us (1%)
    pallas_call x1, Pallas kernels, middle_rows(): pl.pallas_call(functools.partial(middle_body, chunks), in_specs=[IN_VMEM]...  303 us
    pallas_call x1, Pallas kernels, tokens_back(): pl.pallas_call(functools.partial(tokens_body, chunks), in_specs=[IN_HBM,...  119 us
    pallas_call x1, Pallas kernels, feed(): pl.pallas_call(functools.partial(feed_body, rank, tile, chunks), in_specs...  108 us
    pallas_call x1, Pallas kernels, branch_back(): pl.pallas_call(branch_body, in_specs=[IN_VMEM, IN_HBM, IN_VMEM, IN_VMEM,...  100 us
    pallas_call x1, Pallas kernels, gather_norm(): pl.pallas_call(gather_norm_body, in_specs=[IN_VMEM, IN_VMEM], out_specs=I...  64.9 us
    pallas_call x1, Pallas kernels, project(): pl.pallas_call(project_body, in_specs=[IN_HBM, IN_HBM] + [IN_VMEM] * 4, o...  36.7 us
    pallas_call x1, Pallas kernels, attend_back(): pl.pallas_call(functools.partial(attend_back_body, seg), grid=(pairs,), i...  29.1 us
    pallas_call x1, Pallas kernels, attend(): pl.pallas_call(functools.partial(attend_body, seg), grid=(pairs,), in_spe...  19.3 us
  transfers between devices with their start and end apart: 11, of which 2 were waited for; matrix products, arithmetic and copies ran while one was open for 1% of the time, Pallas kernels for 80%

profile of v5, /device:TPU:0, one launch (start us, length us, event | category | flops | bytes accessed | tf_op | source)
XLA Modules:
  0.0 842.1 jit_solution(16452559982010415761)
XLA Ops:
  7.2 0.0 all-gather.9.cloned.1.call-start
  7.2 2.3 pad_maximum_fusion
  9.5 0.0 copy-start.7
  9.5 0.0 all-gather.9.cloned.1.call-update
  9.5 0.0 all-gather.11.cloned.1.call-start
  9.6 0.7 all-gather.11.cloned.1.call-update
  10.3 0.0 all-gather.13.cloned.1.call-start
  10.3 0.7 all-gather.13.cloned.1.call-update
  11.0 0.0 all-gather.15.cloned.1.call-start
  11.1 0.5 all-gather.15.cloned.1.call-update
  11.6 0.0 all-reduce.3.cloned.1.call-start
  12.3 0.0 copy-done.7
  12.3 0.6 broadcast_in_dim.30
  12.9 64.9 %shard_map.260.x_ref = bf16[4,320,2048]{2,1,0:T(8,128)(2,1)} custom-call(bf16[320,2048]{1,0:T(8,128)(2,1)} %x_ref.5, f32[1,2048]{1,0:T(1,128)} %bitcast.28), custom_call_target="tpu_custom_call" | custom-call | tf_op jit(solution)/shard_map/pallas_call | solution.py:250
  77.8 2.0 shard_map.261
  79.9 0.0 all-gather.9.cloned.1.call-done.w_ref
  79.9 0.0 copy-start.2
  79.9 0.0 copy-start.9
  79.9 0.0 copy-start.8
  79.9 36.7 %shard_map.262 = (bf16[4,320,2048]{2,1,0:T(8,128)(2,1)}, bf16[3,1280,512]{2,1,0:T(8,128)(2,1)}, bf16[1280,48]{1,0:T(8,128)(2,1)}) custom-call(bf16[4,320,2048]{2,1,0:T(8,128)(2,1)} %shard_map.260.x_ref, bf16[2048,2048]{1,0:T(8,128)(2,1)} %all-gather.9.cloned.1.call-done.w_ref, ...), custom_call_target="tpu_custom_call", output_to_operand_aliasing={{0}: (0, {})} | custom-call | tf_op jit(solution)/shard_map/pallas_call | solution.py:340
  116.6 0.0 copy-done.2
  116.6 1.5 collective-permute-start.1
  118.1 5.6 collective-permute-start
  123.7 0.0 copy-done.9
  123.7 0.1 add_bitcast_fusion
  123.8 0.1 broadcast_in_dim.27
  123.8 0.7 sub.10.p_ref
  124.5 0.0 copy-done.8
  124.5 0.6 broadcast_in_dim.31
  125.1 19.3 %shard_map.263 = (bf16[1,1280,512]{2,1,0:T(8,128)(2,1)}, f32[4,2,1280]{2,1,0:T(2,128)}) custom-call(bf16[3,1280,512]{2,1,0:T(8,128)(2,1)} %get-tuple-element.58.q_ref.k_ref.v_ref, bf16[3,1280,512]{2,1,0:T(8,128)(2,1)} %get-tuple-element.58.q_ref.k_ref.v_ref, bf16[3,1280,512]{2,1,0:T(8,128)(2,1)} %get-tuple-element.58.q_ref.k_ref.v_ref, s32[1,512]{1,0:T(1,128)} %sub.10.p_ref), custom_call_target="tpu_custom_call" | custom-call | flops 6710886400 | bytes 5242880 | tf_op jit(solution)/shard_map/pallas_call | solution.py:775
  144.4 2.7 collective-permute-done.1.after_ref
  147.1 1.2 collective-permute-done.before_ref
  148.3 0.0 copy-done.6
  148.3 303.4 %shard_map.264 = (f32[320,2048]{1,0:T(8,128)}, bf16[4,320,2048]{2,1,0:T(8,128)(2,1)}, bf16[4,320,2048]{2,1,0:T(8,128)(2,1)}, bf16[1280,16]{1,0:T(8,128)(2,1)}) custom-call(bf16[1280,512]{1,0:T(8,128)(2,1)} %bitcast.20, bf16[2048,2048]{1,0:T(8,128)(2,1)} %all-gather.9.cloned.1.call-done.w_ref, bf16[320,2048]{1,0:T(8,128)(2,1)} %c_ref.1, ...), custom_call_target="tpu_custom_call" | custom-call | tf_op jit(solution)/shard_map/pallas_call | solution.py:440
  451.7 0.0 all-gather.11.cloned.1.call-done.wg_ref
  451.7 0.0 all-gather.13.cloned.1.call-done.wu_ref
  451.8 0.0 all-gather.15.cloned.1.call-done.wd_ref
  451.8 107.8 %shard_map.265 = (f32[320,2048]{1,0:T(8,128)}, bf16[320,2048]{1,0:T(8,128)(2,1)}, bf16[4,320,2048]{2,1,0:T(8,128)(2,1)}, f32[48,2048]{1,0:T(8,128)}, f32[48,2048]{1,0:T(8,128)}) custom-call(bf16[4,320,2048]{2,1,0:T(8,128)(2,1)} %get-tuple-element.64.n_ref, bf16[4,320,2048]{2,1,0:T(8,128)(2,1)} %get-tuple-element.65.c_ref, ...), custom_call_target="tpu_custom_call" | custom-call | tf_op jit(solution)/shard_map/pallas_call | solution.py:995
  559.6 1.0 convert_element_type.32
  560.7 1.7 convert_element_type.35
  562.4 0.7 concatenate.7
  563.1 0.0 all-reduce.3.cloned.1.call-update
  563.1 0.0 all-gather.17.cloned.1.call-start
  563.2 0.5 all-gather.17.cloned.1.call-update
  563.7 0.0 all-gather.19.cloned.1.call-start
  563.7 100.2 %shard_map.266 = (bf16[4,320,2048]{2,1,0:T(8,128)(2,1)}, bf16[1,1280,512]{2,1,0:T(8,128)(2,1)}, bf16[1280,16]{1,0:T(8,128)(2,1)}, bf16[320,2048]{1,0:T(8,128)(2,...) custom-call(bf16[320,2048]{1,0:T(8,128)(2,1)} %get-tuple-element.71.b_ref, ...), custom_call_target="tpu_custom_call" | custom-call | tf_op jit(solution)/shard_map/pallas_call | solution.py:518
  663.9 5.2 collective-permute-start.2
  669.1 1.3 collective-permute-start.3
  670.4 29.1 %shard_map.267.d_ref = bf16[3,1280,512]{2,1,0:T(8,128)(2,1)} custom-call(bf16[3,1280,512]{2,1,0:T(8,128)(2,1)} %get-tuple-element.58.q_ref.k_ref.v_ref, bf16[3,1280,512]{2,1,0:T(8,128)(2,1)} %get-tuple-element.58.q_ref.k_ref.v_ref, bf16[3,1280,512]{2,1,0:T(8,128)(2,1)} %get-tuple-element.58.q_ref.k_ref.v_ref, bf16[1,1280,512]{2,1,0:T(8,128)(2,1)} %get-tuple-element.59.o_ref, ...), custom_call_target="tpu_custom_call" | custom-call | flops 16777216000 | bytes 10485760 | tf_op jit(solution)/shard_map/pallas_call | solution.py:838
  699.5 0.0 collective-permute-done.2
  699.5 0.0 copy-start.4
  699.5 0.0 collective-permute-done.3
  699.5 0.0 copy-start.5
  699.5 0.0 all-gather.19.cloned.1.call-update
  699.6 1.0 copy-done.4
  700.6 0.4 copy-done.5
  701.0 119.1 %shard_map.268 = (bf16[320,2048]{1,0:T(8,128)(2,1)}, bf16[8,64,2048]{2,1,0:T(8,128)(2,1)}, bf16[8,64,512]{2,1,0:T(8,128)(2,1)}) custom-call(bf16[3,1280,512]{2,1,0:T(8,128)(2,1)} %shard_map.267.d_ref, bf16[2048,2048]{1,0:T(8,128)(2,1)} %all-gather.9.cloned.1.call-done.w_ref, bf16[3,16,512]{2,1,0:T(8,128)(2,1)} %get-tuple-element.56.a_ref, ...), custom_call_target="tpu_custom_call" | custom-call | tf_op jit(solution)/shard_map/pallas_call | solution.py:689
  820.1 0.0 copy-done
  820.1 0.0 copy-done.3
  820.1 3.6 add_convert_fusion
  823.7 1.5 fusion.pick_ref
  825.2 8.5 %shard_map.269 = (f32[5,8,16,2048]{3,2,1,0:T(8,128)}, f32[2,8,16,2048]{3,2,1,0:T(8,128)}, f32[2,8,16,2048]{3,2,1,0:T(8,128)}, f32[8,16,2048]{2,1,0:T(8,128)}, f3...) custom-call(s32[8]{0:T(128)} %fusion.pick_ref, bf16[8,64,2048]{2,1,0:T(8,128)(2,1)} %bitcast.24, ...), custom_call_target="tpu_custom_call" | custom-call | tf_op jit(solution)/shard_map/pallas_call | solution.py:1100
  833.7 0.0 copy-done.1
  833.7 1.1 copy.34
  (7 shorter events, 0.0 us)
Async XLA Ops:
  7.2 72.7 %all-gather.9.cloned.1.call-start = ((), (), s32[]{:S(2)}) async-start(), calls=%async_computation | async-start | bytes 9437184 | tf_op jit(solution)/shard_map/all_gather | solution.py:1159
  9.5 2.8 copy-start.7
  9.5 442.2 %all-gather.11.cloned.1.call-start = ((), (), s32[]{:S(2)}) async-start(), calls=%async_computation.1 | async-start | bytes 9437184 | tf_op jit(solution)/shard_map/all_gather | solution.py:1167
  10.3 441.5 %all-gather.13.cloned.1.call-start = ((), (), s32[]{:S(2)}) async-start(), calls=%async_computation.2 | async-start | bytes 9437184 | tf_op jit(solution)/shard_map/all_gather | solution.py:1167
  11.0 440.8 %all-gather.15.cloned.1.call-start = ((), (), s32[]{:S(2)}) async-start(), calls=%async_computation.3 | async-start | bytes 9437184 | tf_op jit(solution)/shard_map/all_gather | solution.py:1167
  11.6 687.9 %all-reduce.3.cloned.1.call-start = ((), (), s32[]{:S(2)}) async-start(), calls=%async_computation.4 | async-start | bytes 393216 | tf_op jit(solution)/shard_map/psum | solution.py:1201
  79.9 36.7 %copy-start.2 = (bf16[320,2048]{1,0:T(8,128)(2,1)S(1)}, bf16[320,2048]{1,0:T(8,128)(2,1)}, u32[]{:S(2)}) copy-start(bf16[320,2048]{1,0:T(8,128)(2,1)} %c_ref.1) | copy-start | bytes 3932164
  79.9 43.8 %copy-start.9 = (s32[1,20]{1,0:T(1,128)S(1)}, s32[1,20]{1,0:T(1,128)}, u32[]{:S(2)}) copy-start(s32[1,20]{1,0:T(1,128)} %param.38) | copy-start | bytes 244
  79.9 44.6 %copy-start.8 = (bf16[2048]{0:T(1024)(128)(2,1)S(1)}, bf16[2048]{0:T(1024)(128)(2,1)}, u32[]{:S(2)}) copy-start(bf16[2048]{0:T(1024)(128)(2,1)} %param.24) | copy-start | bytes 12292
  116.6 30.5 %collective-permute-start.1 = (bf16[320,2048]{1,0:T(8,128)(2,1)S(1)}, bf16[320,2048]{1,0:T(8,128)(2,1)S(1)}, u32[]{:S(2)}, u32[]{:S(2)}) collective-permute-start(bf16[320,2048]{1,0:T(8,128)(2,1)S(1)} %copy-done.2), channel_id=1, source_target_pairs={{3,2},{2,1},{1,0},{7,6},{6,5},{5,4},{11,10},{10,9},{9,8},{15,14},{... | collective-permute-start | bytes 3932168 | tf_op jit(solution)/shard_map/ppermute | solution.py:36
  118.1 30.2 %collective-permute-start = (bf16[320,2048]{1,0:T(8,128)(2,1)S(1)}, bf16[320,2048]{1,0:T(8,128)(2,1)}, u32[]{:S(2)}, u32[]{:S(2)}) collective-permute-start(bf16[320,2048]{1,0:T(8,128)(2,1)S(1)} %copy-done.2), channel_id=1, source_target_pairs={{0,1},{1,2},{2,3},{4,5},{5,6},{6,7},{8,9},{9,10},{10,11},{12,13},{... | collective-permute-start | bytes 3932168 | tf_op jit(solution)/shard_map/ppermute | solution.py:36
  147.1 1.2 copy-start.6
  563.1 260.6 %all-gather.17.cloned.1.call-start = ((), (), s32[]{:S(2)}) async-start(), calls=%async_computation.5 | async-start | bytes 2359296 | tf_op jit(solution)/shard_map/all_gather | solution.py:1056
  563.7 261.5 %all-gather.19.cloned.1.call-start = ((), (), s32[]{:S(2)}) async-start(), calls=%async_computation.6 | async-start | bytes 1769472 | tf_op jit(solution)/shard_map/all_gather | solution.py:1056
  663.9 35.6 %collective-permute-start.2 = (bf16[320,2048]{1,0:T(8,128)(2,1)}, bf16[320,2048]{1,0:T(8,128)(2,1)S(1)}, u32[]{:S(2)}, u32[]{:S(2)}) collective-permute-start(bf16[320,2048]{1,0:T(8,128)(2,1)} %get-tuple-element.80), channel_id=1, source_target_pairs={{0,1},{1,2},{2,3},{4,5},{5,6},{6,7},{8,9},{9,10},{10,11},{12,13},{... | collective-permute-start | bytes 3932168 | tf_op jit(solution)/shard_map/ppermute | solution.py:36
  669.1 30.4 %collective-permute-start.3 = (bf16[320,2048]{1,0:T(8,128)(2,1)}, bf16[320,2048]{1,0:T(8,128)(2,1)S(1)}, u32[]{:S(2)}, u32[]{:S(2)}) collective-permute-start(bf16[320,2048]{1,0:T(8,128)(2,1)} %get-tuple-element.81), channel_id=1, source_target_pairs={{3,2},{2,1},{1,0},{7,6},{6,5},{5,4},{11,10},{10,9},{9,8},{15,14},{... | collective-permute-start | bytes 3932168 | tf_op jit(solution)/shard_map/ppermute | solution.py:36
  699.5 1.1 copy-start.4
  699.5 1.5 copy-start.5
  701.0 119.1 %copy-start = (f32[320,2048]{1,0:T(8,128)S(1)}, f32[320,2048]{1,0:T(8,128)}, u32[]{:S(2)}) copy-start(f32[320,2048]{1,0:T(8,128)} %get-tuple-element.63.mid_ref) | copy-start | bytes 7864324
  701.0 119.1 %copy-start.3 = (bf16[320,2048]{1,0:T(8,128)(2,1)S(1)}, bf16[320,2048]{1,0:T(8,128)(2,1)}, u32[]{:S(2)}) copy-start(bf16[320,2048]{1,0:T(8,128)(2,1)} %get-tuple-element.73) | copy-start | bytes 3932164
  825.2 8.5 %copy-start.1 = (bf16[320,2048]{1,0:T(8,128)(2,1)S(1)}, bf16[320,2048]{1,0:T(8,128)(2,1)}, u32[]{:S(2)}) copy-start(bf16[320,2048]{1,0:T(8,128)(2,1)} %get-tuple-element.111) | copy-start | bytes 3932164
Sparse Core Ops, SparseCore 0:
  10.5 57.0 all-gather.8
  69.5 54.4 all-gather.10
  125.8 54.3 all-gather.12
  182.0 54.3 all-gather.14
  563.2 44.0 all-reduce.2
  609.8 27.3 all-gather.16
  699.7 27.3 all-gather.18

commit v6 on v5

--- a/solution.py
+++ b/solution.py
@@ -175,16 +175,22 @@
                     + self.held[index, step - 2, rows].astype(f32)
                 ).astype(bf16)
 
-    def send(self, step, chunk):
-        if step > 1:
+    def send(self, step, chunk, least=0, most=LINE):
+        if step > 1 and most > 0:
             self.add(step, chunk)
         for side in SIDES:
             far = far_of(self.place, side)
             shard = self.place + side * (LINE - step)
 
-            @pl.when(far <= step - 1)
+            @pl.when((far <= step - 1) & (far >= least) & (far <= most))
             def _():
                 self.copy(side, step, chunk, shard, self.place + side).start()
+
+    def begin(self, step, chunk):
+        self.send(step, chunk, most=0)
+
+    def relay(self, step, chunk):
+        self.send(step, chunk, least=1)
 
     def total(self, chunk, out):
         rows = chunk_rows(chunk, self.rows)
@@ -393,36 +399,39 @@
         low_ref[mine] = low
         part[shard] = (nt(d, wv[...]) + nn(low, e_ref[0])).astype(bf16)
         if slot == 3:
-            summed.send(1, 0)
+            summed.begin(1, 0)
+    for chunk in range(chunks):
+        for step in (1, 2, 3):
+            if chunk or step > 1:
+                summed.begin(step, chunk)
     neighbours(lambda copy: copy.wait())
     size = rows // chunks
     kept = []
-    for now in range(chunks + 3):
-        if now + 1 < chunks:
-            summed.send(1, now + 1)
-        if now < chunks:
-            summed.send(2, now)
-            summed.send(3, now)
-            cots.send(2, now)
-        chunk = now - 1
-        if 0 <= chunk < chunks:
-            summed.total(chunk, mid_ref)
-            here = chunk_rows(chunk, size)
-            value = mid_ref[here] + x_ref[here].astype(f32)
-            mid_ref[here] = value
-            rms = lax.rsqrt(jnp.mean(value * value, axis=1, keepdims=True) + eps)
-            own[here] = (value * rms * gain_ref[...]).astype(bf16)
-            gather.send(1, chunk)
-            copy = pltpu.make_async_copy(own.at[here], buf.at[place, here], nsem.at[chunk])
-            copy.start()
-            kept.append(copy)
-            cots.arrive(2, chunk)
-            cots.send(3, chunk)
-        for step in (1, 2):
-            chunk = now - 1 - step
-            if 0 <= chunk < chunks:
-                gather.arrive(step, chunk)
-                gather.send(step + 1, chunk)
+    for chunk in range(chunks):
+        summed.relay(2, chunk)
+        summed.relay(3, chunk)
+        cots.send(2, chunk)
+        if chunk:
+            cots.arrive(2, chunk - 1)
+            cots.send(3, chunk - 1)
+        summed.total(chunk, mid_ref)
+        here = chunk_rows(chunk, size)
+        value = mid_ref[here] + x_ref[here].astype(f32)
+        mid_ref[here] = value
+        rms = lax.rsqrt(jnp.mean(value * value, axis=1, keepdims=True) + eps)
+        own[here] = (value * rms * gain_ref[...]).astype(bf16)
+        copy = pltpu.make_async_copy(own.at[here], buf.at[place, here], nsem.at[chunk])
+        copy.start()
+        kept.append(copy)
+        if chunk == chunks - 1:
+            for before in range(chunks):
+                gather.send(1, before)
+    cots.arrive(2, chunks - 1)
+    cots.send(3, chunks - 1)
+    for step in (1, 2):
+        for chunk in range(chunks):
+            gather.arrive(step, chunk)
+            gather.send(step + 1, chunk)
     for chunk in range(chunks):
         cots.arrive(3, chunk)
         gather.arrive(3, chunk)
@@ -463,8 +472,9 @@
 
 
 def branch_body(
-    b_ref, w_ref, e_ref, a_ref, p_ref, kept_ref, y_ref, l_ref, own_ref, right_ref, left_ref,
-    buf, part, held, wv, ksem, wsem, send, recv, s_send, s_recv,
+    b_ref, w_ref, e_ref, a_ref, p_ref, d_ref, lo_ref, y_ref, own_ref, right_ref, left_ref,
+    final_ref, exit_ref,
+    buf, part, held, wv, wsem, send, recv, s_send, s_recv,
 ):
     place = lax.axis_index("tensor")
     rows = b_ref.shape[0]
@@ -477,7 +487,6 @@
     parts.wait()
     summed.send(1, 0)
     load.wait()
-    kept = []
     for slot in range(LINE):
         if slot:
             gather.arrive(slot, 0)
@@ -500,49 +509,46 @@
 
         shard = place ^ slot
         mine = pl.ds(pl.multiple_of(shard * rows, rows), rows)
-        low = nt(buf[shard], e_ref[0]).astype(bf16)
-        l_ref[mine] = low
-        y_ref[0, mine] = (nn(buf[shard], wv[...]) + nn(low, a_ref[...])).astype(bf16)
-        copy = pltpu.make_async_copy(buf.at[shard], kept_ref.at[shard], ksem.at[slot])
-        copy.start()
-        kept.append(copy)
-    for copy in kept:
-        copy.wait()
+        low = nt(buf[shard], e_ref[0])
+        y_ref[0, mine] = (nn(buf[shard], wv[...]) + nn(low.astype(bf16), a_ref[...])).astype(bf16)
+        final = nn(lo_ref[mine].astype(f32).T.astype(bf16), buf[shard])
+        leave = nn(low.T.astype(bf16), d_ref[mine])
+        final_ref[...] = final if slot == 0 else final_ref[...] + final
+        exit_ref[...] = leave if slot == 0 else exit_ref[...] + leave
     gather.drain()
     summed.drain(LINE - 1)
 
 
-def branch_back(branch, weight, finals, exits, parts):
+def branch_back(branch, weight, finals, exits, parts, attended, low_out):
     rows, features = branch.shape
     rank, width = exits.shape
     return pl.pallas_call(
         branch_body,
-        in_specs=[IN_VMEM, IN_HBM, IN_VMEM, IN_VMEM, IN_HBM],
-        out_specs=[IN_HBM] + [IN_VMEM] * 5,
-        out_shape=[
-            jax.ShapeDtypeStruct((LINE, rows, features), bf16),
-            jax.ShapeDtypeStruct((1, LINE * rows, width), bf16),
-            jax.ShapeDtypeStruct((LINE * rows, rank), bf16),
-        ]
-        + [jax.ShapeDtypeStruct((rows, features), bf16)] * 3,
+        in_specs=[IN_VMEM, IN_HBM, IN_VMEM, IN_VMEM, IN_HBM, IN_VMEM, IN_VMEM],
+        out_specs=[IN_VMEM] * 6,
+        out_shape=[jax.ShapeDtypeStruct((1, LINE * rows, width), bf16)]
+        + [jax.ShapeDtypeStruct((rows, features), bf16)] * 3
+        + [
+            jax.ShapeDtypeStruct((rank, features), f32),
+            jax.ShapeDtypeStruct((rank, width), f32),
+        ],
         scratch_shapes=[
             pltpu.VMEM((LINE, rows, features), bf16),
             pltpu.VMEM((LINE, rows, features), bf16),
             pltpu.VMEM((2, LINE - 1, rows, features), bf16),
             pltpu.VMEM((features, width), bf16),
-            pltpu.SemaphoreType.DMA((LINE,)),
             pltpu.SemaphoreType.DMA((2,)),
         ]
         + line_sems(1)
         + line_sems(1),
         compiler_params=comm_params(2),
-    )(branch, weight, finals, exits, parts)
+    )(branch, weight, finals, exits, parts, attended, low_out)
 
 
 def tokens_body(
-    chunks, d_ref, w_ref, a_ref, e_ref, x_ref, gain_ref, mid_ref, n_ref, b_ref, lone_ref, lo_ref, bo_ref, o_ref,
+    chunks, d_ref, w_ref, a_ref, e_ref, x_ref, gain_ref, mid_ref, n_ref, lone_ref, final_ref, exit_ref,
     out_ref, model_ref, head_ref,
-    part, held, acc, dv, wv, midv, nv, bv, low, block, extra, wsem, send, recv, x_send, x_recv, t_send, t_recv, h_send, h_recv,
+    part, held, acc, dv, wv, midv, nv, low, block, extra, wsem, send, recv, x_send, x_recv, t_send, t_recv, h_send, h_recv,
 ):
     place = lax.axis_index("tensor")
     tree = lax.axis_index("dp")
@@ -551,7 +557,7 @@
     groups, total, width = d_ref.shape
     rank = a_ref.shape[1]
     loads = fetch(
-        [(d_ref, dv), (w_ref.at[:, : groups * width], wv), (n_ref, nv), (b_ref, bv), (mid_ref, midv)],
+        [(d_ref, dv), (w_ref.at[:, : groups * width], wv), (n_ref, nv), (mid_ref, midv)],
         wsem,
     )
     block[...] = jnp.zeros_like(block)
@@ -564,16 +570,26 @@
     summed = Sum(place, part, held, send, recv, chunks)
     gather = Gather(place, extra, x_send, x_recv, 1)
     entry = e_ref[:groups].reshape(groups * rank, -1)
-    for slot in (3, 2, 1, 0):
+
+    def rows_of(slot):
         shard = place ^ slot
         mine = pl.ds(pl.multiple_of(shard * rows, rows), rows)
-        d = jnp.concatenate([dv[g, mine] for g in range(groups)], axis=1)
-        mine_low = nt(d, block[...]).astype(bf16)
-        low[mine] = mine_low
-        part[shard] = (nt(d, wv[...]) + nn(mine_low, entry)).astype(bf16)
-        if slot == 3:
-            for chunk in range(chunks):
-                summed.send(1, chunk)
+        return shard, mine, jnp.concatenate([dv[g, mine] for g in range(groups)], axis=1)
+
+    def lower(slot):
+        _, mine, d = rows_of(slot)
+        low[mine] = nt(d, block[...]).astype(bf16)
+
+    def partial(slot):
+        shard, mine, d = rows_of(slot)
+        part[shard] = (nt(d, wv[...]) + nn(low[mine], entry)).astype(bf16)
+
+    lower(3)
+    partial(3)
+    summed.begin(1, 0)
+    summed.begin(1, 1)
+    for slot in (2, 1, 0):
+        lower(slot)
     for load in loads[2:]:
         load.wait()
 
@@ -581,40 +597,48 @@
         return value.astype(f32).T.astype(bf16)
 
     joined = nn(turned(low[...]), nv[...].reshape(total, -1))
-    final = nn(turned(lo_ref[...]), bv[...].reshape(total, -1))
-    extra[place] = jnp.concatenate([joined, final], axis=0).astype(bf16)
+    extra[place] = jnp.concatenate([joined, final_ref[...]], axis=0).astype(bf16)
     gather.send(1, 0)
-    for chunk in range(chunks):
-        summed.send(2, chunk)
+    for chunk in range(2, chunks):
+        summed.begin(1, chunk)
+    for slot in (2, 1, 0):
+        partial(slot)
+    for step in (2, 3):
+        for chunk in range(chunks):
+            summed.begin(step, chunk)
+    summed.relay(2, 0)
+    summed.relay(2, 1)
+    gather.arrive(1, 0)
+    gather.send(2, 0)
+    summed.relay(2, 2)
     low_one = turned(lone_ref[...])
     for g in range(groups):
         band = slice(g * rank, (g + 1) * rank)
         head_ref[tree, band] = nn(low_one[band], dv[g]).astype(bf16)
-    head_ref[tree, groups * rank :] = nn(turned(bo_ref[...]), o_ref[...]).astype(bf16)
+    head_ref[tree, groups * rank :] = exit_ref[...].astype(bf16)
     heads.send(0)
-    gather.arrive(1, 0)
-    gather.send(2, 0)
-    summed.send(3, 0)
+    summed.relay(2, 3)
     gather.arrive(2, 0)
     gather.send(3, 0)
-    summed.send(3, 1)
     heads.advance(1)
+    summed.relay(3, 0)
     gather.arrive(3, 0)
     model_ref[tree] = functools.reduce(
         jnp.add, [extra[shard].astype(f32) for shard in range(LINE)]
     ).astype(bf16)
     trees.send(0)
-    summed.send(3, 2)
+    heads.advance(2)
+    summed.relay(3, 1)
     trees.advance(1)
-    heads.advance(2)
-    summed.send(3, 3)
+    summed.relay(3, 2)
+    summed.relay(3, 3)
+    trees.advance(2)
     size = rows // chunks
 
     def finish(chunk):
         finish_tokens(summed, chunk, size, acc, x_ref, gain_ref, midv, out_ref)
 
     finish(0)
-    trees.advance(2)
     finish(1)
     for number in range(3, trees.rounds):
         trees.advance(number)
@@ -677,7 +701,7 @@
 
 
 def tokens_back(
-    head_grads, weight, exits, entries, x, gain, grad_middle, normed, branch, low_one, low_out, back_out, attended
+    head_grads, weight, exits, entries, x, gain, grad_middle, normed, low_one, final_grads, exit_grads
 ):
     chunks = LINE
     rows, features = x.shape
@@ -688,7 +712,7 @@
     sems = pltpu.SemaphoreType.DMA((trees.bit_length() - 1,))
     return pl.pallas_call(
         functools.partial(tokens_body, chunks),
-        in_specs=[IN_HBM, IN_HBM] + [IN_VMEM] * 4 + [IN_HBM] * 3 + [IN_VMEM] * 4,
+        in_specs=[IN_HBM, IN_HBM] + [IN_VMEM] * 4 + [IN_HBM] * 2 + [IN_VMEM] * 3,
         out_specs=[IN_VMEM] * 3,
         out_shape=[
             jax.ShapeDtypeStruct((rows, features), bf16),
@@ -703,19 +727,18 @@
             pltpu.VMEM((features, groups * width), bf16),
             pltpu.VMEM((rows, features), f32),
             pltpu.VMEM((LINE, rows, features), bf16),
-            pltpu.VMEM((LINE, rows, features), bf16),
             pltpu.VMEM((total, groups * rank), bf16),
             pltpu.VMEM((groups * rank, groups * width), bf16),
             pltpu.VMEM((LINE, deep, features), bf16),
-            pltpu.SemaphoreType.DMA((5,)),
+            pltpu.SemaphoreType.DMA((4,)),
         ]
         + line_sems(chunks)
         + line_sems(1)
         + [sems] * 4,
         compiler_params=comm_params(3),
     )(
-        head_grads, weight, exits, entries, x, gain[None, :], grad_middle, normed, branch,
-        low_one, low_out, back_out, attended,
+        head_grads, weight, exits, entries, x, gain[None, :], grad_middle, normed,
+        low_one, final_grads, exit_grads,
     )
 
 
@@ -1200,8 +1223,8 @@
     early = per_tree(early)
     model_sum = lax.psum(model_low, "tensor")
 
-    full_branch, grad_attended, back_o, res_own, res_right, res_left = branch_back(
-        branch, w_heads, finals, out_entry, res_parts
+    grad_attended, res_own, res_right, res_left, final_grads, exit_grads = branch_back(
+        branch, w_heads, finals, out_entry, res_parts, attended[0], adapt_o
     )
     grad_attended, res_right, res_left = lax.optimization_barrier((grad_attended, res_right, res_left))
     from_left = permute(res_right, [(0, 1), (1, 2), (2, 3)])
@@ -1213,7 +1236,7 @@
     model_all = per_tree(model_sum)
     grad_tokens, late_model, late_head = tokens_back(
         head_grads, w_heads, heads_exit, entries, tokens, gain_one, grad_middle,
-        full_one, full_branch, low_one, adapt_o, back_o, attended[0],
+        full_one, low_one, final_grads, exit_grads,
     )
     result = (
         middle

time: 851 us -> 834 us (0.980)
  Pallas kernels: 791 us -> 773 us
    pallas_call x1, Pallas kernels: 119 us -> 100 us  [tokens_back(): pl.pallas_call(functools.partial(tokens_body, chunks), in_specs=[IN_HBM,...]
where the time goes in v6:
time: 834 us; the launch traced here: 824 us
  Pallas kernels  773 us (93%)
  between operations  15.4 us (2%)
  starting transfers between devices  14.1 us (2%)
  other arithmetic  11.4 us (1%)
    pallas_call x1, Pallas kernels, middle_rows(): pl.pallas_call(functools.partial(middle_body, chunks), in_specs=[IN_VMEM]...  303 us
    pallas_call x1, Pallas kernels, feed(): pl.pallas_call(functools.partial(feed_body, rank, tile, chunks), in_specs...  108 us
    pallas_call x1, Pallas kernels, branch_back(): pl.pallas_call(branch_body, in_specs=[IN_VMEM, IN_HBM, IN_VMEM, IN_VMEM,...  100 us
    pallas_call x1, Pallas kernels, tokens_back(): pl.pallas_call(functools.partial(tokens_body, chunks), in_specs=[IN_HBM,...  100 us
    pallas_call x1, Pallas kernels, gather_norm(): pl.pallas_call(gather_norm_body, in_specs=[IN_VMEM, IN_VMEM], out_specs=I...  64.9 us
    pallas_call x1, Pallas kernels, project(): pl.pallas_call(project_body, in_specs=[IN_HBM, IN_HBM] + [IN_VMEM] * 4, o...  36.7 us
    pallas_call x1, Pallas kernels, attend_back(): pl.pallas_call(functools.partial(attend_back_body, seg), grid=(pairs,), i...  29.1 us
    pallas_call x1, Pallas kernels, attend(): pl.pallas_call(functools.partial(attend_body, seg), grid=(pairs,), in_spe...  19.3 us
  transfers between devices with their start and end apart: 11, of which 2 were waited for; matrix products, arithmetic and copies ran while one was open for 1% of the time, Pallas kernels for 80%

profile of v6, /device:TPU:0, one launch (start us, length us, event | category | flops | bytes accessed | tf_op | source)
XLA Modules:
  0.0 823.8 jit_solution(1856170518791979190)
XLA Ops:
  7.2 0.0 all-gather.9.cloned.1.call-start
  7.2 2.3 pad_maximum_fusion
  9.5 0.0 copy-start.7
  9.5 0.0 all-gather.9.cloned.1.call-update
  9.5 0.0 all-gather.11.cloned.1.call-start
  9.6 0.7 all-gather.11.cloned.1.call-update
  10.3 0.0 all-gather.13.cloned.1.call-start
  10.3 0.7 all-gather.13.cloned.1.call-update
  11.0 0.0 all-gather.15.cloned.1.call-start
  11.1 0.5 all-gather.15.cloned.1.call-update
  11.6 0.0 all-reduce.3.cloned.1.call-start
  12.3 0.0 copy-done.7
  12.3 0.6 broadcast_in_dim.30
  12.9 64.9 %shard_map.260.x_ref = bf16[4,320,2048]{2,1,0:T(8,128)(2,1)} custom-call(bf16[320,2048]{1,0:T(8,128)(2,1)} %x_ref.5, f32[1,2048]{1,0:T(1,128)} %bitcast.28), custom_call_target="tpu_custom_call" | custom-call | tf_op jit(solution)/shard_map/pallas_call | solution.py:256
  77.8 2.0 shard_map.261
  79.9 0.0 all-gather.9.cloned.1.call-done.w_ref
  79.9 0.0 copy-start.2
  79.9 0.0 copy-start.9
  79.9 0.0 copy-start.8
  79.9 36.7 %shard_map.262 = (bf16[4,320,2048]{2,1,0:T(8,128)(2,1)}, bf16[3,1280,512]{2,1,0:T(8,128)(2,1)}, bf16[1280,48]{1,0:T(8,128)(2,1)}) custom-call(bf16[4,320,2048]{2,1,0:T(8,128)(2,1)} %shard_map.260.x_ref, bf16[2048,2048]{1,0:T(8,128)(2,1)} %all-gather.9.cloned.1.call-done.w_ref, ...), custom_call_target="tpu_custom_call", output_to_operand_aliasing={{0}: (0, {})} | custom-call | tf_op jit(solution)/shard_map/pallas_call | solution.py:346
  116.6 0.0 copy-done.2
  116.6 1.5 collective-permute-start.1
  118.1 5.6 collective-permute-start
  123.7 0.0 copy-done.9
  123.7 0.1 add_bitcast_fusion
  123.8 0.1 broadcast_in_dim.27
  123.8 0.7 sub.10.p_ref
  124.5 0.0 copy-done.8
  124.5 0.6 broadcast_in_dim.31
  125.1 19.3 %shard_map.263 = (bf16[1,1280,512]{2,1,0:T(8,128)(2,1)}, f32[4,2,1280]{2,1,0:T(2,128)}) custom-call(bf16[3,1280,512]{2,1,0:T(8,128)(2,1)} %get-tuple-element.58.q_ref.k_ref.v_ref, bf16[3,1280,512]{2,1,0:T(8,128)(2,1)} %get-tuple-element.58.q_ref.k_ref.v_ref, bf16[3,1280,512]{2,1,0:T(8,128)(2,1)} %get-tuple-element.58.q_ref.k_ref.v_ref, s32[1,512]{1,0:T(1,128)} %sub.10.p_ref), custom_call_target="tpu_custom_call" | custom-call | flops 6710886400 | bytes 5242880 | tf_op jit(solution)/shard_map/pallas_call | solution.py:798
  144.4 2.7 collective-permute-done.1.after_ref
  147.1 1.2 collective-permute-done.before_ref
  148.3 0.0 copy-done.6
  148.3 303.5 %shard_map.264 = (f32[320,2048]{1,0:T(8,128)}, bf16[4,320,2048]{2,1,0:T(8,128)(2,1)}, bf16[4,320,2048]{2,1,0:T(8,128)(2,1)}, bf16[1280,16]{1,0:T(8,128)(2,1)}) custom-call(bf16[1280,512]{1,0:T(8,128)(2,1)} %bitcast.20, bf16[2048,2048]{1,0:T(8,128)(2,1)} %all-gather.9.cloned.1.call-done.w_ref, bf16[320,2048]{1,0:T(8,128)(2,1)} %c_ref.1, ...), custom_call_target="tpu_custom_call" | custom-call | tf_op jit(solution)/shard_map/pallas_call | solution.py:449
  451.7 0.0 all-gather.11.cloned.1.call-done.wg_ref
  451.8 0.0 all-gather.13.cloned.1.call-done.wu_ref
  451.8 0.0 all-gather.15.cloned.1.call-done.wd_ref
  451.8 107.8 %shard_map.265 = (f32[320,2048]{1,0:T(8,128)}, bf16[320,2048]{1,0:T(8,128)(2,1)}, bf16[4,320,2048]{2,1,0:T(8,128)(2,1)}, f32[48,2048]{1,0:T(8,128)}, f32[48,2048]{1,0:T(8,128)}) custom-call(bf16[4,320,2048]{2,1,0:T(8,128)(2,1)} %get-tuple-element.64.n_ref, bf16[4,320,2048]{2,1,0:T(8,128)(2,1)} %get-tuple-element.65.c_ref, ...), custom_call_target="tpu_custom_call" | custom-call | tf_op jit(solution)/shard_map/pallas_call | solution.py:1018
  559.7 1.0 convert_element_type.32
  560.7 1.7 convert_element_type.35
  562.4 0.7 concatenate.7
  563.1 0.0 all-reduce.3.cloned.1.call-update
  563.1 0.0 all-gather.17.cloned.1.call-start
  563.2 0.5 all-gather.17.cloned.1.call-update
  563.7 0.0 all-gather.19.cloned.1.call-start
  563.7 100.5 %shard_map.266 = (bf16[1,1280,512]{2,1,0:T(8,128)(2,1)}, bf16[320,2048]{1,0:T(8,128)(2,1)}, bf16[320,2048]{1,0:T(8,128)(2,1)}, bf16[320,2048]{1,0:T(8,128)(2,1)}, f32[16,2048]{1,0:T(8,128)}, /*index=5*/f32[16,512]{1,0:T(8,128)}) custom-call(bf16[320,2048]{1,0:T(8,128)(2,1)} %get-tuple-element.71.b_ref, ...), custom_call_target="tpu_custom_call" | custom-call | tf_op jit(solution)/shard_map/pallas_call | solution.py:525
  664.2 5.5 collective-permute-start.2
  669.7 1.3 collective-permute-start.3
  671.0 29.1 %shard_map.267.d_ref = bf16[3,1280,512]{2,1,0:T(8,128)(2,1)} custom-call(bf16[3,1280,512]{2,1,0:T(8,128)(2,1)} %get-tuple-element.58.q_ref.k_ref.v_ref, bf16[3,1280,512]{2,1,0:T(8,128)(2,1)} %get-tuple-element.58.q_ref.k_ref.v_ref, bf16[3,1280,512]{2,1,0:T(8,128)(2,1)} %get-tuple-element.58.q_ref.k_ref.v_ref, bf16[1,1280,512]{2,1,0:T(8,128)(2,1)} %get-tuple-element.59.o_ref, ...), custom_call_target="tpu_custom_call" | custom-call | flops 16777216000 | bytes 10485760 | tf_op jit(solution)/shard_map/pallas_call | solution.py:861
  700.1 0.0 collective-permute-done.2
  700.1 0.0 copy-start.4
  700.1 0.0 collective-permute-done.3
  700.1 0.0 copy-start.5
  700.1 0.0 all-gather.19.cloned.1.call-update
  700.1 1.0 copy-done.4
  701.1 0.4 copy-done.5
  701.6 100.2 %shard_map.268 = (bf16[320,2048]{1,0:T(8,128)(2,1)}, bf16[8,64,2048]{2,1,0:T(8,128)(2,1)}, bf16[8,64,512]{2,1,0:T(8,128)(2,1)}) custom-call(bf16[3,1280,512]{2,1,0:T(8,128)(2,1)} %shard_map.267.d_ref, bf16[2048,2048]{1,0:T(8,128)(2,1)} %all-gather.9.cloned.1.call-done.w_ref, bf16[3,16,512]{2,1,0:T(8,128)(2,1)} %get-tuple-element.56.a_ref, ...), custom_call_target="tpu_custom_call" | custom-call | tf_op jit(solution)/shard_map/pallas_call | solution.py:713
  801.8 0.0 copy-done
  801.8 0.0 copy-done.3
  801.8 3.6 add_convert_fusion
  805.4 1.5 fusion.pick_ref
  806.9 8.5 %shard_map.269 = (f32[5,8,16,2048]{3,2,1,0:T(8,128)}, f32[2,8,16,2048]{3,2,1,0:T(8,128)}, f32[2,8,16,2048]{3,2,1,0:T(8,128)}, f32[8,16,2048]{2,1,0:T(8,128)}, f3...) custom-call(s32[8]{0:T(128)} %fusion.pick_ref, bf16[8,64,2048]{2,1,0:T(8,128)(2,1)} %bitcast.24, ...), custom_call_target="tpu_custom_call" | custom-call | tf_op jit(solution)/shard_map/pallas_call | solution.py:1123
  815.4 0.0 copy-done.1
  815.4 1.1 copy.34
  (7 shorter events, 0.0 us)
Async XLA Ops:
  7.2 72.7 %all-gather.9.cloned.1.call-start = ((), (), s32[]{:S(2)}) async-start(), calls=%async_computation | async-start | bytes 9437184 | tf_op jit(solution)/shard_map/all_gather | solution.py:1182
  9.5 2.8 copy-start.7
  9.5 442.2 %all-gather.11.cloned.1.call-start = ((), (), s32[]{:S(2)}) async-start(), calls=%async_computation.1 | async-start | bytes 9437184 | tf_op jit(solution)/shard_map/all_gather | solution.py:1190
  10.3 441.5 %all-gather.13.cloned.1.call-start = ((), (), s32[]{:S(2)}) async-start(), calls=%async_computation.2 | async-start | bytes 9437184 | tf_op jit(solution)/shard_map/all_gather | solution.py:1190
  11.0 440.8 %all-gather.15.cloned.1.call-start = ((), (), s32[]{:S(2)}) async-start(), calls=%async_computation.3 | async-start | bytes 9437184 | tf_op jit(solution)/shard_map/all_gather | solution.py:1190
  11.6 688.5 %all-reduce.3.cloned.1.call-start = ((), (), s32[]{:S(2)}) async-start(), calls=%async_computation.4 | async-start | bytes 393216 | tf_op jit(solution)/shard_map/psum | solution.py:1224
  79.9 36.7 %copy-start.2 = (bf16[320,2048]{1,0:T(8,128)(2,1)S(1)}, bf16[320,2048]{1,0:T(8,128)(2,1)}, u32[]{:S(2)}) copy-start(bf16[320,2048]{1,0:T(8,128)(2,1)} %c_ref.1) | copy-start | bytes 3932164
  79.9 43.8 %copy-start.9 = (s32[1,20]{1,0:T(1,128)S(1)}, s32[1,20]{1,0:T(1,128)}, u32[]{:S(2)}) copy-start(s32[1,20]{1,0:T(1,128)} %param.38) | copy-start | bytes 244
  79.9 44.6 %copy-start.8 = (bf16[2048]{0:T(1024)(128)(2,1)S(1)}, bf16[2048]{0:T(1024)(128)(2,1)}, u32[]{:S(2)}) copy-start(bf16[2048]{0:T(1024)(128)(2,1)} %param.24) | copy-start | bytes 12292
  116.6 30.5 %collective-permute-start.1 = (bf16[320,2048]{1,0:T(8,128)(2,1)S(1)}, bf16[320,2048]{1,0:T(8,128)(2,1)S(1)}, u32[]{:S(2)}, u32[]{:S(2)}) collective-permute-start(bf16[320,2048]{1,0:T(8,128)(2,1)S(1)} %copy-done.2), channel_id=1, source_target_pairs={{3,2},{2,1},{1,0},{7,6},{6,5},{5,4},{11,10},{10,9},{9,8},{15,14},{... | collective-permute-start | bytes 3932168 | tf_op jit(solution)/shard_map/ppermute | solution.py:36
  118.1 30.2 %collective-permute-start = (bf16[320,2048]{1,0:T(8,128)(2,1)S(1)}, bf16[320,2048]{1,0:T(8,128)(2,1)}, u32[]{:S(2)}, u32[]{:S(2)}) collective-permute-start(bf16[320,2048]{1,0:T(8,128)(2,1)S(1)} %copy-done.2), channel_id=1, source_target_pairs={{0,1},{1,2},{2,3},{4,5},{5,6},{6,7},{8,9},{9,10},{10,11},{12,13},{... | collective-permute-start | bytes 3932168 | tf_op jit(solution)/shard_map/ppermute | solution.py:36
  147.1 1.2 copy-start.6
  563.1 242.3 %all-gather.17.cloned.1.call-start = ((), (), s32[]{:S(2)}) async-start(), calls=%async_computation.5 | async-start | bytes 2359296 | tf_op jit(solution)/shard_map/all_gather | solution.py:1079
  563.7 243.2 %all-gather.19.cloned.1.call-start = ((), (), s32[]{:S(2)}) async-start(), calls=%async_computation.6 | async-start | bytes 1769472 | tf_op jit(solution)/shard_map/all_gather | solution.py:1079
  664.2 35.9 %collective-permute-start.2 = (bf16[320,2048]{1,0:T(8,128)(2,1)}, bf16[320,2048]{1,0:T(8,128)(2,1)S(1)}, u32[]{:S(2)}, u32[]{:S(2)}) collective-permute-start(bf16[320,2048]{1,0:T(8,128)(2,1)} %get-tuple-element.81), channel_id=1, source_target_pairs={{0,1},{1,2},{2,3},{4,5},{5,6},{6,7},{8,9},{9,10},{10,11},{12,13},{... | collective-permute-start | bytes 3932168 | tf_op jit(solution)/shard_map/ppermute | solution.py:36
  669.7 30.4 %collective-permute-start.3 = (bf16[320,2048]{1,0:T(8,128)(2,1)}, bf16[320,2048]{1,0:T(8,128)(2,1)S(1)}, u32[]{:S(2)}, u32[]{:S(2)}) collective-permute-start(bf16[320,2048]{1,0:T(8,128)(2,1)} %get-tuple-element.82), channel_id=1, source_target_pairs={{3,2},{2,1},{1,0},{7,6},{6,5},{5,4},{11,10},{10,9},{9,8},{15,14},{... | collective-permute-start | bytes 3932168 | tf_op jit(solution)/shard_map/ppermute | solution.py:36
  700.1 1.1 copy-start.4
  700.1 1.5 copy-start.5
  701.6 100.2 %copy-start = (f32[320,2048]{1,0:T(8,128)S(1)}, f32[320,2048]{1,0:T(8,128)}, u32[]{:S(2)}) copy-start(f32[320,2048]{1,0:T(8,128)} %get-tuple-element.63.mid_ref) | copy-start | bytes 7864324
  701.6 100.2 %copy-start.3 = (bf16[320,2048]{1,0:T(8,128)(2,1)S(1)}, bf16[320,2048]{1,0:T(8,128)(2,1)}, u32[]{:S(2)}) copy-start(bf16[320,2048]{1,0:T(8,128)(2,1)} %get-tuple-element.74) | copy-start | bytes 3932164
  806.9 8.5 %copy-start.1 = (bf16[320,2048]{1,0:T(8,128)(2,1)S(1)}, bf16[320,2048]{1,0:T(8,128)(2,1)}, u32[]{:S(2)}) copy-start(bf16[320,2048]{1,0:T(8,128)(2,1)} %get-tuple-element.111) | copy-start | bytes 3932164
Sparse Core Ops, SparseCore 0:
  10.5 57.0 all-gather.8
  69.5 54.4 all-gather.10
  125.8 54.3 all-gather.12
  182.0 54.3 all-gather.14
  563.2 44.0 all-reduce.2
  609.9 27.3 all-gather.16
  700.3 27.3 all-gather.18

commit v7 on v6

--- a/solution.py
+++ b/solution.py
@@ -98,17 +98,23 @@
 
 
 class Gather:
-    def __init__(self, place, buf, send, recv, chunks, own=None):
+    def __init__(self, place, buf, send, recv, chunks, own=None, beside=None):
         self.place, self.buf, self.sems, self.chunks = place, buf, (send, recv), chunks
         self.rows = buf.shape[1] // chunks
-        self.own = own
+        self.own, self.beside = own, beside
 
     def copy(self, side, step, chunk, shard, target):
         rows = chunk_rows(chunk, self.rows)
         where = self.buf.at[shard, rows]
-        spot = (0 if side == 1 else 1, step - 1, chunk)
+        index = 0 if side == 1 else 1
+        spot = (index, step - 1, chunk)
+        source = where
+        if step == 1 and self.own is not None:
+            source = self.own.at[rows]
+        if step == 2 and self.beside is not None:
+            source = self.beside[index].at[rows]
         return pltpu.make_async_remote_copy(
-            src_ref=where if self.own is None or step > 1 else self.own.at[rows],
+            src_ref=source,
             dst_ref=where,
             send_sem=self.sems[0].at[spot],
             recv_sem=self.sems[1].at[spot],
@@ -368,26 +374,15 @@
 
 
 def middle_body(
-    chunks, d_ref, w_ref, c_ref, before_ref, after_ref, a_ref, e_ref, x_ref, gain_ref, mid_ref, buf, cbuf, low_ref,
+    chunks, d_ref, w_ref, before_ref, after_ref, a_ref, e_ref, x_ref, gain_ref, mid_ref, buf, cbuf, low_ref,
     part, held, own, wv, wsem, nsem, s_send, s_recv, g_send, g_recv, c_send, c_recv,
 ):
     place = lax.axis_index("tensor")
     width = d_ref.shape[1]
-    load, own_cot = fetch([(w_ref.at[:, 3 * width :], wv), (c_ref, cbuf.at[place])], wsem)
-
-    def neighbours(act):
-        @pl.when(place > 0)
-        def _():
-            act(pltpu.make_async_copy(before_ref, cbuf.at[place - 1], wsem.at[2]))
-
-        @pl.when(place < LINE - 1)
-        def _():
-            act(pltpu.make_async_copy(after_ref, cbuf.at[place + 1], wsem.at[3]))
-
-    neighbours(lambda copy: copy.start())
+    (load,) = fetch([(w_ref.at[:, 3 * width :], wv)], wsem)
     greet(place)
     load.wait()
-    cots = Gather(place, cbuf, c_send, c_recv, chunks)
+    cots = Gather(place, cbuf, c_send, c_recv, chunks, beside=(before_ref, after_ref))
     rows = part.shape[1]
     summed = Sum(place, part, held, s_send, s_recv, chunks)
     gather = Gather(place, buf, g_send, g_recv, chunks, own)
@@ -404,7 +399,6 @@
         for step in (1, 2, 3):
             if chunk or step > 1:
                 summed.begin(step, chunk)
-    neighbours(lambda copy: copy.wait())
     size = rows // chunks
     kept = []
     for chunk in range(chunks):
@@ -435,7 +429,6 @@
     for chunk in range(chunks):
         cots.arrive(3, chunk)
         gather.arrive(3, chunk)
-    own_cot.wait()
     for copy in kept:
         copy.wait()
     summed.drain()
@@ -443,12 +436,12 @@
     cots.drain(start=2)
 
 
-def middle_rows(attended, weight, cot, before, after, exits, finals, x, gain, chunks=4):
+def middle_rows(attended, weight, before, after, exits, finals, x, gain, chunks=4):
     rows, features = x.shape
     width = attended.shape[1]
     return pl.pallas_call(
         functools.partial(middle_body, chunks),
-        in_specs=[IN_VMEM] + [IN_HBM] * 4 + [IN_VMEM] * 4,
+        in_specs=[IN_VMEM] + [IN_HBM] * 3 + [IN_VMEM] * 4,
         out_specs=[IN_VMEM, IN_HBM, IN_HBM, IN_VMEM],
         out_shape=[
             jax.ShapeDtypeStruct((rows, features), f32),
@@ -461,14 +454,14 @@
             pltpu.VMEM((2, LINE - 1, rows, features), bf16),
             pltpu.VMEM((rows, features), bf16),
             pltpu.VMEM((features, width), bf16),
-            pltpu.SemaphoreType.DMA((4,)),
+            pltpu.SemaphoreType.DMA((1,)),
             pltpu.SemaphoreType.DMA((chunks,)),
         ]
         + line_sems(chunks)
         + line_sems(chunks)
         + line_sems(chunks),
         compiler_params=comm_params(1),
-    )(attended, weight, cot, before, after, exits, finals, x, gain[None, :])
+    )(attended, weight, before, after, exits, finals, x, gain[None, :])
 
 
 def branch_body(
@@ -886,7 +879,7 @@
 
 def feed_body(
     rank, tile, chunks,
-    n_ref, c_ref, wg_ref, wu_ref, wd_ref, mid_ref,
+    n_ref, c_ref, before_ref, after_ref, far_ref, wg_ref, wu_ref, wd_ref, mid_ref,
     xu_in, xd_in, e_in, f_in, gain_ref,
     grad_ref, low_grad_ref, res_ref, unit_ref, model_ref,
     x_ref, e_ref, f_ref, midv, nbuf, cbuf, wbuf, low, low_t, acc_res, acc_back, acc_low, part, held, resv,
@@ -901,7 +894,14 @@
         into = order % 2
         shard = place ^ (LINE - 1 - order)
         act(pltpu.make_async_copy(n_ref.at[shard], nbuf.at[into], nsem.at[into]))
-        act(pltpu.make_async_copy(c_ref.at[shard], cbuf.at[into], csem.at[into]))
+
+        def take(source):
+            act(pltpu.make_async_copy(source, cbuf.at[into], csem.at[into]))
+
+        pl.when(shard == place)(lambda: take(c_ref))
+        pl.when(shard == place - 1)(lambda: take(before_ref))
+        pl.when(shard == place + 1)(lambda: take(after_ref))
+        pl.when((shard > place + 1) | (shard < place - 1))(lambda: take(far_ref.at[shard]))
 
     def load_weights(index, into, act):
         columns = pl.ds(pl.multiple_of(index * tile, tile), tile)
@@ -1017,7 +1017,7 @@
     rank = fall_entry.shape[0]
     return pl.pallas_call(
         functools.partial(feed_body, rank, tile, chunks),
-        in_specs=[IN_HBM] * 6 + [IN_VMEM] * 5,
+        in_specs=[IN_HBM] * 9 + [IN_VMEM] * 5,
         out_specs=[IN_VMEM, IN_VMEM, IN_HBM, IN_VMEM, IN_VMEM],
         out_shape=[
             jax.ShapeDtypeStruct((rows, features), f32),
@@ -1050,7 +1050,7 @@
         ]
         + line_sems(chunks),
         compiler_params=comm_params(5),
-    )(normed, cots, *weights, middle, units_exit, fall_entry, entries, finals, gain[None, :])
+    )(normed, *cots, *weights, middle, units_exit, fall_entry, entries, finals, gain[None, :])
 
 
 def pick_body(pick_ref, *refs):
@@ -1208,12 +1208,12 @@
     before = permute(cot_tied, [(0, 1), (1, 2), (2, 3)])
     after = permute(cot_tied, [(3, 2), (2, 1), (1, 0)])
     attended, lse = attend(qkv, leaf_parent, seg)
-    middle, full_two, full_cot, adapt_o = middle_rows(
-        attended[0], w_heads, cotangent, before, after, out_entry, finals, tokens, gain_two
+    middle, full_two, far_cot, adapt_o = middle_rows(
+        attended[0], w_heads, before, after, out_entry, finals, tokens, gain_two
     )
 
     grad_middle, branch, res_parts, unit_grads, model_grads = feed(
-        full_two, full_cot, w_units, middle, units_exit, fall_entry, entries, finals, gain_two
+        full_two, (cotangent, before, after, far_cot), w_units, middle, units_exit, fall_entry, entries, finals, gain_two
     )
     early = jnp.concatenate(
         [unit_grads.astype(bf16), jnp.full((rank, unit_grads.shape[1]), pick).astype(bf16)]

time: 834 us -> 726 us (0.87)
  Pallas kernels: 773 us -> 664 us
    pallas_call x1, Pallas kernels: 303 us -> 197 us  [middle_rows(): pl.pallas_call(functools.partial(middle_body, chunks), in_specs=[IN_VMEM]...]
  transfers between devices with their start and end apart: 11 -> 11, of which waited for: 2 -> 2; matrix products, arithmetic and copies ran while one was open for 1% -> 1% of each run, Pallas kernels for 80% -> 76%
where the time goes in v7:
time: 726 us; the launch traced here: 717 us
  Pallas kernels  664 us (91%)
  between operations  15.4 us (2%)
  starting transfers between devices  13.7 us (2%)
  other arithmetic  11.4 us (2%)
  waiting for transfers between devices  7.63 us (1%)
    pallas_call x1, Pallas kernels, middle_rows(): pl.pallas_call(functools.partial(middle_body, chunks), in_specs=[IN_VMEM]...  197 us
    pallas_call x1, Pallas kernels, feed(): pl.pallas_call(functools.partial(feed_body, rank, tile, chunks), in_specs...  108 us
    pallas_call x1, Pallas kernels, tokens_back(): pl.pallas_call(functools.partial(tokens_body, chunks), in_specs=[IN_HBM,...  100 us
    pallas_call x1, Pallas kernels, branch_back(): pl.pallas_call(branch_body, in_specs=[IN_VMEM, IN_HBM, IN_VMEM, IN_VMEM,...  97.5 us
    pallas_call x1, Pallas kernels, gather_norm(): pl.pallas_call(gather_norm_body, in_specs=[IN_VMEM, IN_VMEM], out_specs=I...  64.9 us
    pallas_call x1, Pallas kernels, project(): pl.pallas_call(project_body, in_specs=[IN_HBM, IN_HBM] + [IN_VMEM] * 4, o...  36.6 us
    pallas_call x1, Pallas kernels, attend_back(): pl.pallas_call(functools.partial(attend_back_body, seg), grid=(pairs,), i...  29.1 us
    pallas_call x1, Pallas kernels, attend(): pl.pallas_call(functools.partial(attend_body, seg), grid=(pairs,), in_spe...  19.3 us
  transfers between devices with their start and end apart: 11, of which 2 were waited for; matrix products, arithmetic and copies ran while one was open for 1% of the time, Pallas kernels for 76%

profile of v7, /device:TPU:0, one launch (start us, length us, event | category | flops | bytes accessed | tf_op | source)
XLA Modules:
  0.0 716.9 jit_solution(1993720620377413031)
XLA Ops:
  7.2 0.0 all-gather.9.cloned.1.call-start
  7.2 2.3 pad_maximum_fusion
  9.5 0.0 copy-start.7
  9.5 0.0 all-gather.9.cloned.1.call-update
  9.5 0.0 all-gather.11.cloned.1.call-start
  9.6 0.7 all-gather.11.cloned.1.call-update
  10.3 0.0 all-gather.13.cloned.1.call-start
  10.3 0.7 all-gather.13.cloned.1.call-update
  11.0 0.0 all-gather.15.cloned.1.call-start
  11.1 0.5 all-gather.15.cloned.1.call-update
  11.6 0.0 all-reduce.3.cloned.1.call-start
  12.3 0.0 copy-done.7
  12.3 0.6 broadcast_in_dim.30
  12.9 64.9 %shard_map.260.x_ref = bf16[4,320,2048]{2,1,0:T(8,128)(2,1)} custom-call(bf16[320,2048]{1,0:T(8,128)(2,1)} %x_ref.5, f32[1,2048]{1,0:T(1,128)} %bitcast.28), custom_call_target="tpu_custom_call" | custom-call | tf_op jit(solution)/shard_map/pallas_call | solution.py:262
  77.8 2.0 shard_map.261
  79.9 0.0 copy-start.9
  79.9 0.0 copy-start.8
  79.9 36.6 %shard_map.262 = (bf16[4,320,2048]{2,1,0:T(8,128)(2,1)}, bf16[3,1280,512]{2,1,0:T(8,128)(2,1)}, bf16[1280,48]{1,0:T(8,128)(2,1)}) custom-call(bf16[4,320,2048]{2,1,0:T(8,128)(2,1)} %shard_map.260.x_ref, bf16[2048,2048]{1,0:T(8,128)(2,1)} %all-gather.9.cloned.1.call-done.w_ref, ...), custom_call_target="tpu_custom_call", output_to_operand_aliasing={{0}: (0, {})} | custom-call | tf_op jit(solution)/shard_map/pallas_call | solution.py:352
  116.4 1.5 collective-permute-start.1
  118.0 4.6 collective-permute-start
  122.6 0.0 copy-done.9
  122.6 0.1 add_bitcast_fusion
  122.7 0.1 broadcast_in_dim.27
  122.8 0.7 sub.10.p_ref
  123.4 0.0 copy-done.8
  123.4 0.6 broadcast_in_dim.31
  124.0 19.3 %shard_map.263 = (bf16[1,1280,512]{2,1,0:T(8,128)(2,1)}, f32[4,2,1280]{2,1,0:T(2,128)}) custom-call(bf16[3,1280,512]{2,1,0:T(8,128)(2,1)} %get-tuple-element.58.q_ref.k_ref.v_ref, bf16[3,1280,512]{2,1,0:T(8,128)(2,1)} %get-tuple-element.58.q_ref.k_ref.v_ref, bf16[3,1280,512]{2,1,0:T(8,128)(2,1)} %get-tuple-element.58.q_ref.k_ref.v_ref, s32[1,512]{1,0:T(1,128)} %sub.10.p_ref), custom_call_target="tpu_custom_call" | custom-call | flops 6710886400 | bytes 5242880 | tf_op jit(solution)/shard_map/pallas_call | solution.py:791
  143.3 3.6 collective-permute-done.1.after_ref
  146.9 0.0 copy-start.1
  146.9 1.5 collective-permute-done.before_ref
  148.4 0.0 copy-start.2
  148.4 0.0 copy-done.1
  148.4 1.1 copy-done.2
  149.5 197.2 %shard_map.264 = (f32[320,2048]{1,0:T(8,128)}, bf16[4,320,2048]{2,1,0:T(8,128)(2,1)}, bf16[4,320,2048]{2,1,0:T(8,128)(2,1)}, bf16[1280,16]{1,0:T(8,128)(2,1)}) custom-call(bf16[1280,512]{1,0:T(8,128)(2,1)} %bitcast.20, bf16[2048,2048]{1,0:T(8,128)(2,1)} %all-gather.9.cloned.1.call-done.w_ref, bf16[320,2048]{1,0:T(8,128)(2,1)} %copy-done.2, ...), custom_call_target="tpu_custom_call" | custom-call | tf_op jit(solution)/shard_map/pallas_call | solution.py:442
  346.7 0.0 all-gather.11.cloned.1.call-done.wg_ref
  346.8 0.0 all-gather.13.cloned.1.call-done.wu_ref
  346.8 0.0 all-gather.15.cloned.1.call-done.wd_ref
  346.8 108.4 %shard_map.265 = (f32[320,2048]{1,0:T(8,128)}, bf16[320,2048]{1,0:T(8,128)(2,1)}, bf16[4,320,2048]{2,1,0:T(8,128)(2,1)}, f32[48,2048]{1,0:T(8,128)}, f32[48,2048]{1,0:T(8,128)}) custom-call(bf16[4,320,2048]{2,1,0:T(8,128)(2,1)} %get-tuple-element.64.n_ref, bf16[320,2048]{1,0:T(8,128)(2,1)} %c_ref.1, bf16[320,2048]{1,0:T(8,128)(2,1)} %copy-done.2, ...), custom_call_target="tpu_custom_call" | custom-call | tf_op jit(solution)/shard_map/pallas_call | solution.py:1018
  455.2 1.0 convert_element_type.32
  456.3 1.7 convert_element_type.35
  458.0 0.7 concatenate.7
  458.7 0.0 all-reduce.3.cloned.1.call-update
  458.7 0.0 all-gather.17.cloned.1.call-start
  458.8 0.5 all-gather.17.cloned.1.call-update
  459.3 0.0 all-gather.19.cloned.1.call-start
  459.3 97.5 %shard_map.266 = (bf16[1,1280,512]{2,1,0:T(8,128)(2,1)}, bf16[320,2048]{1,0:T(8,128)(2,1)}, bf16[320,2048]{1,0:T(8,128)(2,1)}, bf16[320,2048]{1,0:T(8,128)(2,1)}, f32[16,2048]{1,0:T(8,128)}, /*index=5*/f32[16,512]{1,0:T(8,128)}) custom-call(bf16[320,2048]{1,0:T(8,128)(2,1)} %get-tuple-element.71.b_ref, ...), custom_call_target="tpu_custom_call" | custom-call | tf_op jit(solution)/shard_map/pallas_call | solution.py:518
  556.8 6.0 collective-permute-start.2
  562.8 1.3 collective-permute-start.3
  564.1 29.1 %shard_map.267.d_ref = bf16[3,1280,512]{2,1,0:T(8,128)(2,1)} custom-call(bf16[3,1280,512]{2,1,0:T(8,128)(2,1)} %get-tuple-element.58.q_ref.k_ref.v_ref, bf16[3,1280,512]{2,1,0:T(8,128)(2,1)} %get-tuple-element.58.q_ref.k_ref.v_ref, bf16[3,1280,512]{2,1,0:T(8,128)(2,1)} %get-tuple-element.58.q_ref.k_ref.v_ref, bf16[1,1280,512]{2,1,0:T(8,128)(2,1)} %get-tuple-element.59.o_ref, ...), custom_call_target="tpu_custom_call" | custom-call | flops 16777216000 | bytes 10485760 | tf_op jit(solution)/shard_map/pallas_call | solution.py:854
  593.2 0.0 collective-permute-done.2
  593.2 0.0 copy-start.5
  593.2 0.0 collective-permute-done.3
  593.3 0.0 copy-start.6
  593.3 0.0 all-gather.19.cloned.1.call-update
  593.3 1.0 copy-done.5
  594.3 0.4 copy-done.6
  594.7 100.2 %shard_map.268 = (bf16[320,2048]{1,0:T(8,128)(2,1)}, bf16[8,64,2048]{2,1,0:T(8,128)(2,1)}, bf16[8,64,512]{2,1,0:T(8,128)(2,1)}) custom-call(bf16[3,1280,512]{2,1,0:T(8,128)(2,1)} %shard_map.267.d_ref, bf16[2048,2048]{1,0:T(8,128)(2,1)} %all-gather.9.cloned.1.call-done.w_ref, bf16[3,16,512]{2,1,0:T(8,128)(2,1)} %get-tuple-element.56.a_ref, ...), custom_call_target="tpu_custom_call" | custom-call | tf_op jit(solution)/shard_map/pallas_call | solution.py:706
  694.9 0.0 copy-done
  694.9 0.0 copy-done.4
  694.9 3.6 add_convert_fusion
  698.6 1.5 fusion.pick_ref
  700.0 8.5 %shard_map.269 = (f32[5,8,16,2048]{3,2,1,0:T(8,128)}, f32[2,8,16,2048]{3,2,1,0:T(8,128)}, f32[2,8,16,2048]{3,2,1,0:T(8,128)}, f32[8,16,2048]{2,1,0:T(8,128)}, f3...) custom-call(s32[8]{0:T(128)} %fusion.pick_ref, bf16[8,64,2048]{2,1,0:T(8,128)(2,1)} %bitcast.24, ...), custom_call_target="tpu_custom_call" | custom-call | tf_op jit(solution)/shard_map/pallas_call | solution.py:1123
  708.6 0.0 copy-done.3
  708.6 1.1 copy.34
  (7 shorter events, 0.0 us)
Async XLA Ops:
  7.2 72.7 %all-gather.9.cloned.1.call-start = ((), (), s32[]{:S(2)}) async-start(), calls=%async_computation | async-start | bytes 9437184 | tf_op jit(solution)/shard_map/all_gather | solution.py:1182
  9.5 2.8 copy-start.7
  9.5 337.2 %all-gather.11.cloned.1.call-start = ((), (), s32[]{:S(2)}) async-start(), calls=%async_computation.1 | async-start | bytes 9437184 | tf_op jit(solution)/shard_map/all_gather | solution.py:1190
  10.3 336.5 %all-gather.13.cloned.1.call-start = ((), (), s32[]{:S(2)}) async-start(), calls=%async_computation.2 | async-start | bytes 9437184 | tf_op jit(solution)/shard_map/all_gather | solution.py:1190
  11.0 335.8 %all-gather.15.cloned.1.call-start = ((), (), s32[]{:S(2)}) async-start(), calls=%async_computation.3 | async-start | bytes 9437184 | tf_op jit(solution)/shard_map/all_gather | solution.py:1190
  11.6 581.6 %all-reduce.3.cloned.1.call-start = ((), (), s32[]{:S(2)}) async-start(), calls=%async_computation.4 | async-start | bytes 393216 | tf_op jit(solution)/shard_map/psum | solution.py:1224
  79.9 42.7 %copy-start.9 = (s32[1,20]{1,0:T(1,128)S(1)}, s32[1,20]{1,0:T(1,128)}, u32[]{:S(2)}) copy-start(s32[1,20]{1,0:T(1,128)} %param.38) | copy-start | bytes 244
  79.9 43.6 %copy-start.8 = (bf16[2048]{0:T(1024)(128)(2,1)S(1)}, bf16[2048]{0:T(1024)(128)(2,1)}, u32[]{:S(2)}) copy-start(bf16[2048]{0:T(1024)(128)(2,1)} %param.24) | copy-start | bytes 12292
  116.4 30.5 %collective-permute-start.1 = (bf16[320,2048]{1,0:T(8,128)(2,1)}, bf16[320,2048]{1,0:T(8,128)(2,1)S(1)}, u32[]{:S(2)}, u32[]{:S(2)}) collective-permute-start(bf16[320,2048]{1,0:T(8,128)(2,1)} %c_ref.1), channel_id=1, source_target_pairs={{3,2},{2,1},{1,0},{7,6},{6,5},{5,4},{11,10},{10,9},{9,8},{15,14},{... | collective-permute-start | bytes 3932168 | tf_op jit(solution)/shard_map/ppermute | solution.py:36
  118.0 30.5 %collective-permute-start = (bf16[320,2048]{1,0:T(8,128)(2,1)}, bf16[320,2048]{1,0:T(8,128)(2,1)S(1)}, u32[]{:S(2)}, u32[]{:S(2)}) collective-permute-start(bf16[320,2048]{1,0:T(8,128)(2,1)} %c_ref.1), channel_id=1, source_target_pairs={{0,1},{1,2},{2,3},{4,5},{5,6},{6,7},{8,9},{9,10},{10,11},{12,13},{... | collective-permute-start | bytes 3932168 | tf_op jit(solution)/shard_map/ppermute | solution.py:36
  146.9 1.5 copy-start.1
  148.4 1.1 copy-start.2
  458.7 239.9 %all-gather.17.cloned.1.call-start = ((), (), s32[]{:S(2)}) async-start(), calls=%async_computation.5 | async-start | bytes 2359296 | tf_op jit(solution)/shard_map/all_gather | solution.py:1079
  459.3 240.8 %all-gather.19.cloned.1.call-start = ((), (), s32[]{:S(2)}) async-start(), calls=%async_computation.6 | async-start | bytes 1769472 | tf_op jit(solution)/shard_map/all_gather | solution.py:1079
  556.8 36.4 %collective-permute-start.2 = (bf16[320,2048]{1,0:T(8,128)(2,1)}, bf16[320,2048]{1,0:T(8,128)(2,1)S(1)}, u32[]{:S(2)}, u32[]{:S(2)}) collective-permute-start(bf16[320,2048]{1,0:T(8,128)(2,1)} %get-tuple-element.81), channel_id=1, source_target_pairs={{0,1},{1,2},{2,3},{4,5},{5,6},{6,7},{8,9},{9,10},{10,11},{12,13},{... | collective-permute-start | bytes 3932168 | tf_op jit(solution)/shard_map/ppermute | solution.py:36
  562.8 30.4 %collective-permute-start.3 = (bf16[320,2048]{1,0:T(8,128)(2,1)}, bf16[320,2048]{1,0:T(8,128)(2,1)S(1)}, u32[]{:S(2)}, u32[]{:S(2)}) collective-permute-start(bf16[320,2048]{1,0:T(8,128)(2,1)} %get-tuple-element.82), channel_id=1, source_target_pairs={{3,2},{2,1},{1,0},{7,6},{6,5},{5,4},{11,10},{10,9},{9,8},{15,14},{... | collective-permute-start | bytes 3932168 | tf_op jit(solution)/shard_map/ppermute | solution.py:36
  593.2 1.1 copy-start.5
  593.3 1.5 copy-start.6
  594.7 100.2 %copy-start = (f32[320,2048]{1,0:T(8,128)S(1)}, f32[320,2048]{1,0:T(8,128)}, u32[]{:S(2)}) copy-start(f32[320,2048]{1,0:T(8,128)} %get-tuple-element.63.mid_ref) | copy-start | bytes 7864324
  594.7 100.2 %copy-start.4 = (bf16[320,2048]{1,0:T(8,128)(2,1)S(1)}, bf16[320,2048]{1,0:T(8,128)(2,1)}, u32[]{:S(2)}) copy-start(bf16[320,2048]{1,0:T(8,128)(2,1)} %get-tuple-element.74) | copy-start | bytes 3932164
  700.0 8.5 %copy-start.3 = (bf16[320,2048]{1,0:T(8,128)(2,1)S(1)}, bf16[320,2048]{1,0:T(8,128)(2,1)}, u32[]{:S(2)}) copy-start(bf16[320,2048]{1,0:T(8,128)(2,1)} %get-tuple-element.111) | copy-start | bytes 3932164
Sparse Core Ops, SparseCore 0:
  10.5 57.0 all-gather.8
  69.5 54.3 all-gather.10
  125.8 54.3 all-gather.12
  182.0 54.3 all-gather.14
  458.8 40.8 all-reduce.2
  502.2 27.3 all-gather.16
  593.4 26.5 all-gather.18

commit v8 on v7

--- a/solution.py
+++ b/solution.py
@@ -98,10 +98,10 @@
 
 
 class Gather:
-    def __init__(self, place, buf, send, recv, chunks, own=None, beside=None):
+    def __init__(self, place, buf, send, recv, chunks, own=None):
         self.place, self.buf, self.sems, self.chunks = place, buf, (send, recv), chunks
         self.rows = buf.shape[1] // chunks
-        self.own, self.beside = own, beside
+        self.own = own
 
     def copy(self, side, step, chunk, shard, target):
         rows = chunk_rows(chunk, self.rows)
@@ -111,8 +111,6 @@
         source = where
         if step == 1 and self.own is not None:
             source = self.own.at[rows]
-        if step == 2 and self.beside is not None:
-            source = self.beside[index].at[rows]
         return pltpu.make_async_remote_copy(
             src_ref=source,
             dst_ref=where,
@@ -122,17 +120,17 @@
             device_id_type=MESH,
         )
 
-    def each_send(self, step, chunk, act):
+    def each_send(self, step, chunk, act, least=0, most=LINE):
         for side in SIDES:
             far = far_of(self.place, side)
 
-            @pl.when((far < LINE - 1) & (far >= step - 1))
+            @pl.when((far < LINE - 1) & (far >= step - 1) & (far >= least) & (far <= most))
             def _():
                 shard = self.place - side * (step - 1)
                 act(self.copy(side, step, chunk, shard, self.place + side))
 
-    def send(self, step, chunk):
-        self.each_send(step, chunk, lambda copy: copy.start())
+    def send(self, step, chunk, least=0, most=LINE):
+        self.each_send(step, chunk, lambda copy: copy.start(), least, most)
 
     def arrive(self, step, chunk):
         for side in SIDES:
@@ -141,6 +139,26 @@
             def _():
                 shard = self.place - side * step
                 self.copy(side, step, chunk, shard, self.place - side).wait_recv()
+
+    def relay(self, step, chunk):
+        for side in SIDES:
+            far = far_of(self.place, side)
+
+            @pl.when((far < LINE - 1) & (far >= step - 1))
+            def _():
+                before = self.place - side * (step - 1)
+                self.copy(side, step - 1, chunk, before, self.place - side).wait_recv()
+                self.copy(side, step, chunk, before, self.place + side).start()
+
+    def close(self):
+        for side in SIDES:
+
+            @pl.when(far_of(self.place, side) == LINE - 1)
+            def _():
+                for step in range(1, LINE):
+                    for chunk in range(self.chunks):
+                        shard = self.place - side * step
+                        self.copy(side, step, chunk, shard, self.place - side).wait_recv()
 
     def drain(self, stop=LINE, start=1):
         for step in range(start, stop):
@@ -270,12 +288,15 @@
     )(x, gain[None, :])
 
 
-def project_body(
-    x_ref, w_ref, e_ref, a_ref, cos_ref, sin_ref, kept_ref, y_ref, l_ref,
-    buf, yv, wv, xsem, wsem, ysem, send, recv,
+def front_body(
+    chunks, seg,
+    x_ref, w_ref, c_ref, e_ref, a_ref, cos_ref, sin_ref, p_ref, oe_ref, f_ref, tok_ref, gain_ref,
+    kept_ref, y_ref, mid_ref, n_ref, cot_ref, l_ref, att_ref, lse_ref, lo_ref,
+    buf, yv, wv, wo, part, held, own, midv, xsem, wsem, ysem, nsem, msem, send, recv,
+    s_send, s_recv, g_send, g_recv, c_send, c_recv,
 ):
     place = lax.axis_index("tensor")
-    groups, _, width = y_ref.shape
+    groups, total, width = y_ref.shape
     rows, rank = x_ref.shape[1], a_ref.shape[1]
     edge = (place == 0) | (place == LINE - 1)
     last = place ^ (LINE - 1)
@@ -311,10 +332,18 @@
         else:
             pl.when(jnp.logical_not(edge))(copy.start)
         copies.append(copy)
-    (load,) = fetch([(w_ref.at[:, : groups * width], wv)], wsem)
+    load, load_out = fetch(
+        [(w_ref.at[:, : groups * width], wv), (w_ref.at[:, groups * width :], wo)], wsem
+    )
     greet(place)
+    cots = Gather(place, cot_ref, c_send, c_recv, chunks, c_ref)
+    summed = Sum(place, part, held, s_send, s_recv, chunks)
+    gather = Gather(place, n_ref, g_send, g_recv, chunks, own)
     for side in SIDES:
         pl.when(far_of(place, side) == LINE - 2)(passed(side).start)
+    for chunk in range(chunks):
+        cots.send(1, chunk)
+
     for copy in copies[:-1]:
         copy.wait()
     load.wait()
@@ -339,60 +368,30 @@
             out = pltpu.make_async_copy(yv.at[g, mine], y_ref.at[g, mine], ysem.at[slot, g])
             out.start()
             outs.append(out)
-    pl.when(edge)(kept.wait)
-    for out in outs:
-        out.wait()
-    for side in SIDES:
-        pl.when(far_of(place, side) == LINE - 2)(passed(side).wait_send)
-
-
-def project(x, weight, entries, exits, tables):
-    _, rows, features = x.shape
-    groups, rank, width = exits.shape
-    return pl.pallas_call(
-        project_body,
-        in_specs=[IN_HBM, IN_HBM] + [IN_VMEM] * 4,
-        out_specs=[IN_HBM, IN_HBM, IN_VMEM],
-        out_shape=[
-            jax.ShapeDtypeStruct((LINE, rows, features), bf16),
-            jax.ShapeDtypeStruct((groups, LINE * rows, width), bf16),
-            jax.ShapeDtypeStruct((LINE * rows, groups * rank), bf16),
-        ],
-        scratch_shapes=[
-            pltpu.VMEM((LINE, rows, features), bf16),
-            pltpu.VMEM((groups, LINE * rows, width), bf16),
-            pltpu.VMEM((features, groups * width), bf16),
-            pltpu.SemaphoreType.DMA((LINE,)),
-            pltpu.SemaphoreType.DMA((1,)),
-            pltpu.SemaphoreType.DMA((LINE, groups)),
-            pltpu.SemaphoreType.DMA((2,)),
-            pltpu.SemaphoreType.DMA((2,)),
-        ],
-        input_output_aliases={0: 0},
-        compiler_params=comm_params(4),
-    )(x, weight, entries, exits, *tables)
-
-
-def middle_body(
-    chunks, d_ref, w_ref, before_ref, after_ref, a_ref, e_ref, x_ref, gain_ref, mid_ref, buf, cbuf, low_ref,
-    part, held, own, wv, wsem, nsem, s_send, s_recv, g_send, g_recv, c_send, c_recv,
-):
-    place = lax.axis_index("tensor")
-    width = d_ref.shape[1]
-    (load,) = fetch([(w_ref.at[:, 3 * width :], wv)], wsem)
-    greet(place)
-    load.wait()
-    cots = Gather(place, cbuf, c_send, c_recv, chunks, beside=(before_ref, after_ref))
-    rows = part.shape[1]
-    summed = Sum(place, part, held, s_send, s_recv, chunks)
-    gather = Gather(place, buf, g_send, g_recv, chunks, own)
+
+    pair = 2 * HEAD_DIM
+
+    def one_pair(j, carry):
+        lanes = pl.ds(pl.multiple_of(j * pair, pair), pair)
+        attend_pair(seg, yv, lanes, p_ref[...], j, att_ref, lse_ref)
+
+        @pl.when(j == 0)
+        def _():
+            for chunk in range(chunks):
+                cots.relay(2, chunk)
+
+        return carry
+
+    lax.fori_loop(0, width // pair, one_pair, 0)
+
+    load_out.wait()
     for slot in (3, 2, 1, 0):
         shard = place ^ slot
         mine = pl.ds(pl.multiple_of(shard * rows, rows), rows)
-        d = d_ref[mine]
-        low = nt(d, a_ref[...]).astype(bf16)
-        low_ref[mine] = low
-        part[shard] = (nt(d, wv[...]) + nn(low, e_ref[0])).astype(bf16)
+        d = att_ref[mine]
+        low = nt(d, oe_ref[...]).astype(bf16)
+        lo_ref[mine] = low
+        part[shard] = (nt(d, wo[...]) + nn(low, f_ref[0])).astype(bf16)
         if slot == 3:
             summed.begin(1, 0)
     for chunk in range(chunks):
@@ -400,68 +399,82 @@
             if chunk or step > 1:
                 summed.begin(step, chunk)
     size = rows // chunks
-    kept = []
+    stores = []
     for chunk in range(chunks):
         summed.relay(2, chunk)
         summed.relay(3, chunk)
-        cots.send(2, chunk)
-        if chunk:
-            cots.arrive(2, chunk - 1)
-            cots.send(3, chunk - 1)
-        summed.total(chunk, mid_ref)
+        cots.relay(3, chunk)
+        summed.total(chunk, midv)
         here = chunk_rows(chunk, size)
-        value = mid_ref[here] + x_ref[here].astype(f32)
-        mid_ref[here] = value
+        value = midv[here] + tok_ref[here].astype(f32)
+        midv[here] = value
         rms = lax.rsqrt(jnp.mean(value * value, axis=1, keepdims=True) + eps)
         own[here] = (value * rms * gain_ref[...]).astype(bf16)
-        copy = pltpu.make_async_copy(own.at[here], buf.at[place, here], nsem.at[chunk])
-        copy.start()
-        kept.append(copy)
-        if chunk == chunks - 1:
-            for before in range(chunks):
-                gather.send(1, before)
-    cots.arrive(2, chunks - 1)
-    cots.send(3, chunks - 1)
-    for step in (1, 2):
+        stores.append(pltpu.make_async_copy(own.at[here], n_ref.at[place, here], nsem.at[chunk]))
+        stores.append(pltpu.make_async_copy(midv.at[here], mid_ref.at[here], msem.at[chunk]))
+        gather.send(1, chunk, least=1)
+        for store in stores[-2:]:
+            store.start()
+    for chunk in range(chunks):
+        gather.send(1, chunk, most=0)
+    for step in (2, 3):
         for chunk in range(chunks):
-            gather.arrive(step, chunk)
-            gather.send(step + 1, chunk)
-    for chunk in range(chunks):
-        cots.arrive(3, chunk)
-        gather.arrive(3, chunk)
-    for copy in kept:
-        copy.wait()
+            gather.relay(step, chunk)
+    cots.close()
+    gather.close()
+    pl.when(edge)(kept.wait)
+    for out in outs + stores:
+        out.wait()
+    for side in SIDES:
+        pl.when(far_of(place, side) == LINE - 2)(passed(side).wait_send)
     summed.drain()
     gather.drain()
-    cots.drain(start=2)
-
-
-def middle_rows(attended, weight, before, after, exits, finals, x, gain, chunks=4):
-    rows, features = x.shape
-    width = attended.shape[1]
+    cots.drain()
+
+
+def front(x, weight, cot, entries, exits, tables, leaf_parent, out_entry, finals, tokens, gain, seg, chunks=4):
+    _, rows, features = x.shape
+    groups, rank, width = exits.shape
+    total = LINE * rows
+    shards = jax.ShapeDtypeStruct((LINE, rows, features), bf16)
     return pl.pallas_call(
-        functools.partial(middle_body, chunks),
-        in_specs=[IN_VMEM] + [IN_HBM] * 3 + [IN_VMEM] * 4,
-        out_specs=[IN_VMEM, IN_HBM, IN_HBM, IN_VMEM],
+        functools.partial(front_body, chunks, seg),
+        in_specs=[IN_HBM] * 3 + [IN_VMEM] * 9,
+        out_specs=[IN_HBM] * 5 + [IN_VMEM] * 4,
         out_shape=[
+            shards,
+            jax.ShapeDtypeStruct((groups, total, width), bf16),
             jax.ShapeDtypeStruct((rows, features), f32),
-            jax.ShapeDtypeStruct((LINE, rows, features), bf16),
-            jax.ShapeDtypeStruct((LINE, rows, features), bf16),
-            jax.ShapeDtypeStruct((LINE * rows, exits.shape[0]), bf16),
+            shards,
+            shards,
+            jax.ShapeDtypeStruct((total, groups * rank), bf16),
+            jax.ShapeDtypeStruct((total, width), bf16),
+            jax.ShapeDtypeStruct((width // (2 * HEAD_DIM), 2, total), f32),
+            jax.ShapeDtypeStruct((total, rank), bf16),
         ],
         scratch_shapes=[
             pltpu.VMEM((LINE, rows, features), bf16),
+            pltpu.VMEM((groups, total, width), bf16),
+            pltpu.VMEM((features, groups * width), bf16),
+            pltpu.VMEM((features, width), bf16),
+            pltpu.VMEM((LINE, rows, features), bf16),
             pltpu.VMEM((2, LINE - 1, rows, features), bf16),
             pltpu.VMEM((rows, features), bf16),
-            pltpu.VMEM((features, width), bf16),
-            pltpu.SemaphoreType.DMA((1,)),
+            pltpu.VMEM((rows, features), f32),
+            pltpu.SemaphoreType.DMA((LINE,)),
+            pltpu.SemaphoreType.DMA((2,)),
+            pltpu.SemaphoreType.DMA((LINE, groups)),
             pltpu.SemaphoreType.DMA((chunks,)),
+            pltpu.SemaphoreType.DMA((chunks,)),
+            pltpu.SemaphoreType.DMA((2,)),
+            pltpu.SemaphoreType.DMA((2,)),
         ]
         + line_sems(chunks)
         + line_sems(chunks)
         + line_sems(chunks),
+        input_output_aliases={0: 0},
         compiler_params=comm_params(1),
-    )(attended, weight, before, after, exits, finals, x, gain[None, :])
+    )(x, weight, cot, entries, exits, *tables, leaf_parent, out_entry, finals, tokens, gain[None, :])
 
 
 def branch_body(
@@ -756,18 +769,18 @@
     return tiles
 
 
-def attend_body(seg, q_ref, k_ref, v_ref, p_ref, o_ref, lse_ref):
-    rows = q_ref.shape[1]
-    value_t = v_ref[0].T
+def attend_pair(seg, qkv_ref, lanes, parent_row, pair, o_ref, lse_ref):
+    rows = qkv_ref.shape[1]
+    value_t = qkv_ref[2, :, lanes].T
     lane = lax.broadcasted_iota(jnp.int32, (QT, 2 * HEAD_DIM), 1)
-    for start, pieces in tree_tiles(seg, rows, p_ref[...]):
-        query = q_ref[0, start : start + QT] * bf16(HEAD_DIM**-0.5)
+    for start, pieces in tree_tiles(seg, rows, parent_row):
+        query = qkv_ref[0, start : start + QT, lanes] * bf16(HEAD_DIM**-0.5)
         outs = []
         for h in range(2):
             own_query = jnp.where(lane // HEAD_DIM == h, query, bf16(0))
             scores = []
             for k0, count, mask in pieces:
-                s = nt(k_ref[0, k0 : k0 + count], own_query)
+                s = nt(qkv_ref[1, k0 : k0 + count, lanes], own_query)
                 scores.append(s if mask is None else jnp.where(mask, s, -1e30))
             top = functools.reduce(
                 jnp.maximum, [jnp.max(s, axis=0, keepdims=True) for s in scores]
@@ -781,33 +794,8 @@
                     weights.astype(bf16),
                 )
             outs.append(out / summed)
-            lse_ref[0, h : h + 1, start : start + QT] = top + jnp.log(summed)
-        o_ref[0, start : start + QT] = jnp.concatenate(outs, axis=0).T.astype(bf16)
-
-
-def attend(qkv, leaf_parent, seg):
-    _, rows, width = qkv.shape
-    pairs = width // (2 * HEAD_DIM)
-    return pl.pallas_call(
-        functools.partial(attend_body, seg),
-        grid=(pairs,),
-        in_specs=[
-            pl.BlockSpec((1, rows, 2 * HEAD_DIM), lambda j, g=g: (g, 0, j)) for g in range(3)
-        ]
-        + [pl.BlockSpec(leaf_parent.shape, lambda j: (0, 0))],
-        out_specs=[
-            pl.BlockSpec((1, rows, 2 * HEAD_DIM), lambda j: (0, 0, j)),
-            pl.BlockSpec((1, 2, rows), lambda j: (j, 0, 0)),
-        ],
-        out_shape=[
-            jax.ShapeDtypeStruct((1, rows, width), bf16),
-            jax.ShapeDtypeStruct((pairs, 2, rows), f32),
-        ],
-        compiler_params=pltpu.CompilerParams(vmem_limit_bytes=VMEM_LIMIT),
-        cost_estimate=pl.CostEstimate(
-            flops=8 * rows * rows * width, bytes_accessed=8 * rows * width, transcendentals=0
-        ),
-    )(qkv, qkv, qkv, leaf_parent)
+            lse_ref[pair, h : h + 1, start : start + QT] = top + jnp.log(summed)
+        o_ref[start : start + QT, lanes] = jnp.concatenate(outs, axis=0).T.astype(bf16)
 
 
 def attend_back_body(
@@ -816,7 +804,7 @@
     rows = q_ref.shape[1]
     scale = bf16(HEAD_DIM**-0.5)
     key_t = k_ref[0].T
-    weighed_t = (g_ref[0].astype(f32) * o_ref[0].astype(f32)).T
+    weighed_t = (g_ref[0].astype(f32) * o_ref[...].astype(f32)).T
     lane = lax.broadcasted_iota(jnp.int32, (QT, 2 * HEAD_DIM), 1)
     dk[...] = jnp.zeros_like(dk)
     dv[...] = jnp.zeros_like(dv)
@@ -856,7 +844,7 @@
         grid=(pairs,),
         in_specs=[pl.BlockSpec((1, rows, pair), lambda j, g=g: (g, 0, j)) for g in range(3)]
         + [
-            pl.BlockSpec((1, rows, pair), lambda j: (0, 0, j)),
+            pl.BlockSpec((rows, pair), lambda j: (0, j)),
             pl.BlockSpec((1, rows, pair), lambda j: (0, 0, j)),
             pl.BlockSpec((1, 2, rows), lambda j: (j, 0, 0)),
             pl.BlockSpec(leaf_parent.shape, lambda j: (0, 0)),
@@ -879,7 +867,7 @@
 
 def feed_body(
     rank, tile, chunks,
-    n_ref, c_ref, before_ref, after_ref, far_ref, wg_ref, wu_ref, wd_ref, mid_ref,
+    n_ref, c_ref, far_ref, wg_ref, wu_ref, wd_ref, mid_ref,
     xu_in, xd_in, e_in, f_in, gain_ref,
     grad_ref, low_grad_ref, res_ref, unit_ref, model_ref,
     x_ref, e_ref, f_ref, midv, nbuf, cbuf, wbuf, low, low_t, acc_res, acc_back, acc_low, part, held, resv,
@@ -898,10 +886,8 @@
         def take(source):
             act(pltpu.make_async_copy(source, cbuf.at[into], csem.at[into]))
 
-        pl.when(shard == place)(lambda: take(c_ref))
-        pl.when(shard == place - 1)(lambda: take(before_ref))
-        pl.when(shard == place + 1)(lambda: take(after_ref))
-        pl.when((shard > place + 1) | (shard < place - 1))(lambda: take(far_ref.at[shard]))
+        pl.when(order == LINE - 1)(lambda: take(c_ref))
+        pl.when(order < LINE - 1)(lambda: take(far_ref.at[shard]))
 
     def load_weights(index, into, act):
         columns = pl.ds(pl.multiple_of(index * tile, tile), tile)
@@ -1017,7 +1003,7 @@
     rank = fall_entry.shape[0]
     return pl.pallas_call(
         functools.partial(feed_body, rank, tile, chunks),
-        in_specs=[IN_HBM] * 9 + [IN_VMEM] * 5,
+        in_specs=[IN_HBM] * 7 + [IN_VMEM] * 5,
         out_specs=[IN_VMEM, IN_VMEM, IN_HBM, IN_VMEM, IN_VMEM],
         out_shape=[
             jax.ShapeDtypeStruct((rows, features), f32),
@@ -1203,17 +1189,12 @@
     out_entry, fall_entry = out_entry[0], fall_entry[0]
 
     most_one = gather_norm(tokens, gain_one)
-    full_one, qkv, low_one = project(most_one, w_heads, entries, heads_exit, tables)
-    cot_tied, qkv = lax.optimization_barrier((cotangent, qkv))
-    before = permute(cot_tied, [(0, 1), (1, 2), (2, 3)])
-    after = permute(cot_tied, [(3, 2), (2, 1), (1, 0)])
-    attended, lse = attend(qkv, leaf_parent, seg)
-    middle, full_two, far_cot, adapt_o = middle_rows(
-        attended[0], w_heads, before, after, out_entry, finals, tokens, gain_two
+    full_one, qkv, middle, full_two, full_cot, low_one, attended, lse, adapt_o = front(
+        most_one, w_heads, cotangent, entries, heads_exit, tables, leaf_parent, out_entry, finals, tokens, gain_two, seg
     )
 
     grad_middle, branch, res_parts, unit_grads, model_grads = feed(
-        full_two, (cotangent, before, after, far_cot), w_units, middle, units_exit, fall_entry, entries, finals, gain_two
+        full_two, (cotangent, full_cot), w_units, middle, units_exit, fall_entry, entries, finals, gain_two
     )
     early = jnp.concatenate(
         [unit_grads.astype(bf16), jnp.full((rank, unit_grads.shape[1]), pick).astype(bf16)]
@@ -1224,7 +1205,7 @@
     model_sum = lax.psum(model_low, "tensor")
 
     grad_attended, res_own, res_right, res_left, final_grads, exit_grads = branch_back(
-        branch, w_heads, finals, out_entry, res_parts, attended[0], adapt_o
+        branch, w_heads, finals, out_entry, res_parts, attended, adapt_o
     )
     grad_attended, res_right, res_left = lax.optimization_barrier((grad_attended, res_right, res_left))
     from_left = permute(res_right, [(0, 1), (1, 2), (2, 3)])

time: 726 us -> 698 us (0.961)
  Pallas kernels: 664 us -> 649 us
    pallas_call x3 -> x1, Pallas kernels: 253 us -> 231 us  [front(): pl.pallas_call(functools.partial(front_body, chunks, seg), in_specs=[IN_H...]
  transfers between devices with their start and end apart: 11 -> 9, of which waited for: 2 -> 0; matrix products, arithmetic and copies ran while one was open for 1% -> 1% of each run, Pallas kernels for 76% -> 77%
where the time goes in v8:
time: 698 us; the launch traced here: 689 us
  Pallas kernels  649 us (93%)
  between operations  15.4 us (2%)
  other arithmetic  11.4 us (2%)
    pallas_call x1, Pallas kernels, front(): pl.pallas_call(functools.partial(front_body, chunks, seg), in_specs=[IN_H...  231 us
    pallas_call x1, Pallas kernels, feed(): pl.pallas_call(functools.partial(feed_body, rank, tile, chunks), in_specs...  113 us
    pallas_call x1, Pallas kernels, branch_back(): pl.pallas_call(branch_body, in_specs=[IN_VMEM, IN_HBM, IN_VMEM, IN_VMEM,...  100 us
    pallas_call x1, Pallas kernels, tokens_back(): pl.pallas_call(functools.partial(tokens_body, chunks), in_specs=[IN_HBM,...  100 us
    pallas_call x1, Pallas kernels, gather_norm(): pl.pallas_call(gather_norm_body, in_specs=[IN_VMEM, IN_VMEM], out_specs=I...  64.9 us
    pallas_call x1, Pallas kernels, attend_back(): pl.pallas_call(functools.partial(attend_back_body, seg), grid=(pairs,), i...  29.1 us
  transfers between devices with their start and end apart: 9, of which 0 were waited for; matrix products, arithmetic and copies ran while one was open for 1% of the time, Pallas kernels for 77%

profile of v8, /device:TPU:0, one launch (start us, length us, event | category | flops | bytes accessed | tf_op | source)
XLA Modules:
  0.0 689.0 jit_solution(12565116030357129338)
XLA Ops:
  7.2 0.0 all-gather.9.cloned.1.call-start
  7.2 2.3 pad_maximum_fusion
  9.5 0.0 copy-start.7
  9.5 0.0 copy-start.5
  9.5 0.0 copy-start.6
  9.5 0.0 all-gather.9.cloned.1.call-update
  9.5 0.0 all-gather.11.cloned.1.call-start
  9.6 0.7 all-gather.11.cloned.1.call-update
  10.3 0.0 all-gather.13.cloned.1.call-start
  10.3 0.7 all-gather.13.cloned.1.call-update
  11.0 0.0 all-gather.15.cloned.1.call-start
  11.1 0.5 all-gather.15.cloned.1.call-update
  11.6 0.0 all-reduce.3.cloned.1.call-start
  12.3 0.0 copy-done.7
  12.3 0.1 add_bitcast_fusion
  12.4 0.1 broadcast_in_dim.27
  12.4 0.7 sub.10.p_ref
  13.1 0.0 copy-done.5
  13.1 0.6 broadcast_in_dim.30
  13.7 0.0 copy-done.6
  13.7 0.6 broadcast_in_dim.31
  14.3 64.9 %shard_map.260.x_ref = bf16[4,320,2048]{2,1,0:T(8,128)(2,1)} custom-call(bf16[320,2048]{1,0:T(8,128)(2,1)} %x_ref.3, f32[1,2048]{1,0:T(1,128)} %bitcast.25), custom_call_target="tpu_custom_call" | custom-call | tf_op jit(solution)/shard_map/pallas_call | solution.py:280
  79.3 2.0 shard_map.261
  81.3 0.0 all-gather.9.cloned.1.call-done.w_ref
  81.3 231.1 %shard_map.262 = (bf16[4,320,2048]{2,1,0:T(8,128)(2,1)}, bf16[3,1280,512]{2,1,0:T(8,128)(2,1)}, f32[320,2048]{1,0:T(8,128)}, bf16[4,320,2048]{2,1,0:T(8,128)(2,1...) custom-call(bf16[4,320,2048]{2,1,0:T(8,128)(2,1)} %shard_map.260.x_r, ...), custom_call_target="tpu_custom_call", output_to_operand_aliasing={{0}: (0, {})} | custom-call | tf_op jit(solution)/shard_map/pallas_call | solution.py:440
  312.4 0.0 all-gather.11.cloned.1.call-done.wg_ref
  312.4 0.0 all-gather.13.cloned.1.call-done.wu_ref
  312.4 0.0 all-gather.15.cloned.1.call-done.wd_ref
  312.4 112.8 %shard_map.263 = (f32[320,2048]{1,0:T(8,128)}, bf16[320,2048]{1,0:T(8,128)(2,1)}, bf16[4,320,2048]{2,1,0:T(8,128)(2,1)}, f32[48,2048]{1,0:T(8,128)}, f32[48,2048]{1,0:T(8,128)}) custom-call(bf16[4,320,2048]{2,1,0:T(8,128)(2,1)} %get-tuple-element.58.n_ref, bf16[320,2048]{1,0:T(8,128)(2,1)} %c_ref.3, bf16[4,320,2048]{2,1,0:T(8,128)(2,1)} %get-tuple-element.59.far_ref, ...), custom_call_target="tpu_custom_call" | custom-call | tf_op jit(solution)/shard_map/pallas_call | solution.py:1004
  425.3 1.0 convert_element_type.32
  426.3 1.7 convert_element_type.35
  428.0 0.7 concatenate.7
  428.7 0.0 all-reduce.3.cloned.1.call-update
  428.7 0.0 all-gather.17.cloned.1.call-start
  428.8 0.5 all-gather.17.cloned.1.call-update
  429.3 0.0 all-gather.19.cloned.1.call-start
  429.3 100.3 %shard_map.264 = (bf16[1,1280,512]{2,1,0:T(8,128)(2,1)}, bf16[320,2048]{1,0:T(8,128)(2,1)}, bf16[320,2048]{1,0:T(8,128)(2,1)}, bf16[320,2048]{1,0:T(8,128)(2,1)}, f32[16,2048]{1,0:T(8,128)}, /*index=5*/f32[16,512]{1,0:T(8,128)}) custom-call(bf16[320,2048]{1,0:T(8,128)(2,1)} %get-tuple-element.65.b_ref, ...), custom_call_target="tpu_custom_call" | custom-call | tf_op jit(solution)/shard_map/pallas_call | solution.py:531
  529.6 5.2 collective-permute-start
  534.9 1.3 collective-permute-start.1
  536.2 29.1 %shard_map.265.d_ref = bf16[3,1280,512]{2,1,0:T(8,128)(2,1)} custom-call(bf16[3,1280,512]{2,1,0:T(8,128)(2,1)} %get-tuple-element.70.q_ref.k_ref.v_ref, bf16[3,1280,512]{2,1,0:T(8,128)(2,1)} %get-tuple-element.70.q_ref.k_ref.v_ref, bf16[3,1280,512]{2,1,0:T(8,128)(2,1)} %get-tuple-element.70.q_ref.k_ref.v_ref, ...), custom_call_target="tpu_custom_call" | custom-call | flops 16777216000 | bytes 10485760 | tf_op jit(solution)/shard_map/pallas_call | solution.py:842
  565.3 0.0 all-reduce.3.cloned.1.call-done
  565.3 0.0 collective-permute-done
  565.3 0.0 copy-start.3
  565.3 0.0 collective-permute-done.1
  565.3 0.0 copy-start.4
  565.3 0.0 all-gather.19.cloned.1.call-update
  565.3 1.0 copy-done.3
  566.3 0.4 copy-done.4
  566.8 0.0 copy-start
  566.8 0.0 copy-start.2
  566.8 100.2 %shard_map.266 = (bf16[320,2048]{1,0:T(8,128)(2,1)}, bf16[8,64,2048]{2,1,0:T(8,128)(2,1)}, bf16[8,64,512]{2,1,0:T(8,128)(2,1)}) custom-call(bf16[3,1280,512]{2,1,0:T(8,128)(2,1)} %shard_map.265.d_ref, bf16[2048,2048]{1,0:T(8,128)(2,1)} %all-gather.9.cloned.1.call-done.w_ref, bf16[3,16,512]{2,1,0:T(8,128)(2,1)} %get-tuple-element.54.a_ref, ...), custom_call_target="tpu_custom_call" | custom-call | tf_op jit(solution)/shard_map/pallas_call | solution.py:719
  667.0 0.0 copy-done
  667.0 0.0 copy-done.2
  667.0 3.6 add_convert_fusion
  670.6 0.0 all-gather.17.cloned.1.call-done
  670.6 1.5 fusion.pick_ref
  672.1 0.0 all-gather.19.cloned.1.call-done
  672.1 0.0 copy-start.1
  672.1 8.5 %shard_map.267 = (f32[5,8,16,2048]{3,2,1,0:T(8,128)}, f32[2,8,16,2048]{3,2,1,0:T(8,128)}, f32[2,8,16,2048]{3,2,1,0:T(8,128)}, f32[8,16,2048]{2,1,0:T(8,128)}, f3...) custom-call(s32[8]{0:T(128)} %fusion.pick_ref, bf16[8,64,2048]{2,1,0:T(8,128)(2,1)} %bitcast.21, ...), custom_call_target="tpu_custom_call" | custom-call | tf_op jit(solution)/shard_map/pallas_call | solution.py:1109
  680.6 0.0 copy-done.1
  680.6 1.1 copy.34
Async XLA Ops:
  7.2 74.1 %all-gather.9.cloned.1.call-start = ((), (), s32[]{:S(2)}) async-start(), calls=%async_computation | async-start | bytes 9437184 | tf_op jit(solution)/shard_map/all_gather | solution.py:1168
  9.5 2.8 copy-start.7
  9.5 3.6 copy-start.5
  9.5 4.2 copy-start.6
  9.5 302.9 %all-gather.11.cloned.1.call-start = ((), (), s32[]{:S(2)}) async-start(), calls=%async_computation.1 | async-start | bytes 9437184 | tf_op jit(solution)/shard_map/all_gather | solution.py:1176
  10.3 302.1 %all-gather.13.cloned.1.call-start = ((), (), s32[]{:S(2)}) async-start(), calls=%async_computation.2 | async-start | bytes 9437184 | tf_op jit(solution)/shard_map/all_gather | solution.py:1176
  11.0 301.4 %all-gather.15.cloned.1.call-start = ((), (), s32[]{:S(2)}) async-start(), calls=%async_computation.3 | async-start | bytes 9437184 | tf_op jit(solution)/shard_map/all_gather | solution.py:1176
  11.6 553.7 %all-reduce.3.cloned.1.call-start = ((), (), s32[]{:S(2)}) async-start(), calls=%async_computation.4 | async-start | bytes 393216 | tf_op jit(solution)/shard_map/psum | solution.py:1205
  428.7 241.9 %all-gather.17.cloned.1.call-start = ((), (), s32[]{:S(2)}) async-start(), calls=%async_computation.5 | async-start | bytes 2359296 | tf_op jit(solution)/shard_map/all_gather | solution.py:1065
  429.3 242.8 %all-gather.19.cloned.1.call-start = ((), (), s32[]{:S(2)}) async-start(), calls=%async_computation.6 | async-start | bytes 1769472 | tf_op jit(solution)/shard_map/all_gather | solution.py:1065
  529.6 35.6 %collective-permute-start = (bf16[320,2048]{1,0:T(8,128)(2,1)}, bf16[320,2048]{1,0:T(8,128)(2,1)S(1)}, u32[]{:S(2)}, u32[]{:S(2)}) collective-permute-start(bf16[320,2048]{1,0:T(8,128)(2,1)} %get-tuple-element.77), channel_id=1, source_target_pairs={{0,1},{1,2},{2,3},{4,5},{5,6},{6,7},{8,9},{9,10},{10,11},{12,13},{... | collective-permute-start | bytes 3932168 | tf_op jit(solution)/shard_map/ppermute | solution.py:36
  534.9 30.4 %collective-permute-start.1 = (bf16[320,2048]{1,0:T(8,128)(2,1)}, bf16[320,2048]{1,0:T(8,128)(2,1)S(1)}, u32[]{:S(2)}, u32[]{:S(2)}) collective-permute-start(bf16[320,2048]{1,0:T(8,128)(2,1)} %get-tuple-element.78), channel_id=1, source_target_pairs={{3,2},{2,1},{1,0},{7,6},{6,5},{5,4},{11,10},{10,9},{9,8},{15,14},{... | collective-permute-start | bytes 3932168 | tf_op jit(solution)/shard_map/ppermute | solution.py:36
  565.3 1.1 copy-start.3
  565.3 1.5 copy-start.4
  566.8 100.2 %copy-start = (f32[320,2048]{1,0:T(8,128)S(1)}, f32[320,2048]{1,0:T(8,128)}, u32[]{:S(2)}) copy-start(f32[320,2048]{1,0:T(8,128)} %get-tuple-element.57.mid_ref) | copy-start | bytes 7864324
  566.8 100.2 %copy-start.2 = (bf16[320,2048]{1,0:T(8,128)(2,1)S(1)}, bf16[320,2048]{1,0:T(8,128)(2,1)}, u32[]{:S(2)}) copy-start(bf16[320,2048]{1,0:T(8,128)(2,1)} %get-tuple-element.69) | copy-start | bytes 3932164
  672.1 8.5 %copy-start.1 = (bf16[320,2048]{1,0:T(8,128)(2,1)S(1)}, bf16[320,2048]{1,0:T(8,128)(2,1)}, u32[]{:S(2)}) copy-start(bf16[320,2048]{1,0:T(8,128)(2,1)} %get-tuple-element.107) | copy-start | bytes 3932164
Sparse Core Ops, SparseCore 0:
  10.5 57.0 all-gather.8
  69.5 54.4 all-gather.10
  125.8 54.3 all-gather.12
  182.0 54.3 all-gather.14
  428.8 38.1 all-reduce.2
  469.5 27.4 all-gather.16
  565.4 25.8 all-gather.18

commit v9 on v8

--- a/solution.py
+++ b/solution.py
@@ -30,10 +30,6 @@
 
 def tn(left, right):
     return lax.dot_general(left, right, (((0,), (0,)), ((), ())), preferred_element_type=f32)
-
-
-def permute(value, pairs):
-    return lax.ppermute(value, "tensor", pairs)
 
 
 def rope_tables(blocks, seg):
@@ -553,8 +549,9 @@
 
 def tokens_body(
     chunks, d_ref, w_ref, a_ref, e_ref, x_ref, gain_ref, mid_ref, n_ref, lone_ref, final_ref, exit_ref,
-    out_ref, model_ref, head_ref,
-    part, held, acc, dv, wv, midv, nv, low, block, extra, wsem, send, recv, x_send, x_recv, t_send, t_recv, h_send, h_recv,
+    middle_ref, own_ref, left_ref, right_ref,
+    out_ref, model_ref, head_ref, res_ref,
+    part, held, acc, dv, wv, midv, nv, terms, low, block, extra, wsem, send, recv, x_send, x_recv, t_send, t_recv, h_send, h_recv,
 ):
     place = lax.axis_index("tensor")
     tree = lax.axis_index("dp")
@@ -563,7 +560,16 @@
     groups, total, width = d_ref.shape
     rank = a_ref.shape[1]
     loads = fetch(
-        [(d_ref, dv), (w_ref.at[:, : groups * width], wv), (n_ref, nv), (mid_ref, midv)],
+        [
+            (d_ref, dv),
+            (w_ref.at[:, : groups * width], wv),
+            (n_ref, nv),
+            (mid_ref, midv),
+            (middle_ref, acc),
+            (own_ref, terms.at[0]),
+            (left_ref, terms.at[1]),
+            (right_ref, terms.at[2]),
+        ],
         wsem,
     )
     block[...] = jnp.zeros_like(block)
@@ -623,6 +629,10 @@
         head_ref[tree, band] = nn(low_one[band], dv[g]).astype(bf16)
     head_ref[tree, groups * rank :] = exit_ref[...].astype(bf16)
     heads.send(0)
+    value = acc[...] + terms[0].astype(f32)
+    for index, side in enumerate(SIDES):
+        value += jnp.where(far_of(place, side) > 0, terms[index + 1].astype(f32), 0.0)
+    res_ref[...] = value.astype(bf16)
     summed.relay(2, 3)
     gather.arrive(2, 0)
     gather.send(3, 0)
@@ -707,7 +717,8 @@
 
 
 def tokens_back(
-    head_grads, weight, exits, entries, x, gain, grad_middle, normed, low_one, final_grads, exit_grads
+    head_grads, weight, exits, entries, x, gain, grad_middle, normed, low_one, final_grads, exit_grads,
+    middle, own, from_left, from_right,
 ):
     chunks = LINE
     rows, features = x.shape
@@ -718,12 +729,13 @@
     sems = pltpu.SemaphoreType.DMA((trees.bit_length() - 1,))
     return pl.pallas_call(
         functools.partial(tokens_body, chunks),
-        in_specs=[IN_HBM, IN_HBM] + [IN_VMEM] * 4 + [IN_HBM] * 2 + [IN_VMEM] * 3,
-        out_specs=[IN_VMEM] * 3,
+        in_specs=[IN_HBM, IN_HBM] + [IN_VMEM] * 4 + [IN_HBM] * 2 + [IN_VMEM] * 3 + [IN_HBM] * 4,
+        out_specs=[IN_VMEM] * 4,
         out_shape=[
             jax.ShapeDtypeStruct((rows, features), bf16),
             jax.ShapeDtypeStruct((trees, deep, features), bf16),
             jax.ShapeDtypeStruct((trees, deep, width), bf16),
+            jax.ShapeDtypeStruct((rows, features), bf16),
         ],
         scratch_shapes=[
             pltpu.VMEM((LINE, rows, features), bf16),
@@ -733,10 +745,11 @@
             pltpu.VMEM((features, groups * width), bf16),
             pltpu.VMEM((rows, features), f32),
             pltpu.VMEM((LINE, rows, features), bf16),
+            pltpu.VMEM((3, rows, features), bf16),
             pltpu.VMEM((total, groups * rank), bf16),
             pltpu.VMEM((groups * rank, groups * width), bf16),
             pltpu.VMEM((LINE, deep, features), bf16),
-            pltpu.SemaphoreType.DMA((4,)),
+            pltpu.SemaphoreType.DMA((8,)),
         ]
         + line_sems(chunks)
         + line_sems(1)
@@ -744,7 +757,7 @@
         compiler_params=comm_params(3),
     )(
         head_grads, weight, exits, entries, x, gain[None, :], grad_middle, normed,
-        low_one, final_grads, exit_grads,
+        low_one, final_grads, exit_grads, middle, own, from_left, from_right,
     )
 
 
@@ -799,8 +812,28 @@
 
 
 def attend_back_body(
-    seg, q_ref, k_ref, v_ref, o_ref, g_ref, lse_ref, p_ref, cos_ref, sin_ref, d_ref, dq_t, dk, dv
+    seg, q_ref, k_ref, v_ref, o_ref, g_ref, lse_ref, p_ref, cos_ref, sin_ref, right_ref, left_ref,
+    d_ref, from_left_ref, from_right_ref, dq_t, dk, dv, send, recv,
 ):
+    place = lax.axis_index("tensor")
+
+    def exchange(side, target):
+        index = 0 if side == 1 else 1
+        return pltpu.make_async_remote_copy(
+            src_ref=(right_ref, left_ref)[index],
+            dst_ref=(from_left_ref, from_right_ref)[index],
+            send_sem=send.at[index],
+            recv_sem=recv.at[index],
+            device_id={"tensor": target},
+            device_id_type=MESH,
+        )
+
+    @pl.when(pl.program_id(0) == 0)
+    def _():
+        greet(place)
+        for side in SIDES:
+            pl.when(far_of(place, side) < LINE - 1)(exchange(side, place + side).start)
+
     rows = q_ref.shape[1]
     scale = bf16(HEAD_DIM**-0.5)
     key_t = k_ref[0].T
@@ -834,8 +867,14 @@
     d_ref[1] = turn(dk[...], cosine, sine).astype(bf16)
     d_ref[2] = dv[...].astype(bf16)
 
-
-def attend_back(qkv, attended, grad, lse, leaf_parent, tables, seg):
+    @pl.when(pl.program_id(0) == pl.num_programs(0) - 1)
+    def _():
+        for side in SIDES:
+            pl.when(far_of(place, side) < LINE - 1)(exchange(side, place + side).wait_send)
+            pl.when(far_of(place, side) > 0)(exchange(side, place - side).wait_recv)
+
+
+def attend_back(qkv, attended, grad, lse, leaf_parent, tables, seg, right, left):
     _, rows, width = qkv.shape
     pairs = width // (2 * HEAD_DIM)
     pair = 2 * HEAD_DIM
@@ -850,32 +889,39 @@
             pl.BlockSpec(leaf_parent.shape, lambda j: (0, 0)),
             pl.BlockSpec((rows, pair), lambda j: (0, 0)),
             pl.BlockSpec((rows, pair), lambda j: (0, 0)),
+            IN_HBM,
+            IN_HBM,
         ],
-        out_specs=pl.BlockSpec((3, rows, pair), lambda j: (0, 0, j)),
-        out_shape=jax.ShapeDtypeStruct((3, rows, width), bf16),
+        out_specs=[pl.BlockSpec((3, rows, pair), lambda j: (0, 0, j)), IN_HBM, IN_HBM],
+        out_shape=[
+            jax.ShapeDtypeStruct((3, rows, width), bf16),
+            jax.ShapeDtypeStruct(right.shape, bf16),
+            jax.ShapeDtypeStruct(left.shape, bf16),
+        ],
         scratch_shapes=[
             pltpu.VMEM((pair, rows), f32),
             pltpu.VMEM((rows, pair), f32),
             pltpu.VMEM((rows, pair), f32),
+            pltpu.SemaphoreType.DMA((2,)),
+            pltpu.SemaphoreType.DMA((2,)),
         ],
-        compiler_params=pltpu.CompilerParams(vmem_limit_bytes=VMEM_LIMIT),
-        cost_estimate=pl.CostEstimate(
-            flops=20 * rows * rows * width, bytes_accessed=16 * rows * width, transcendentals=0
-        ),
-    )(qkv, qkv, qkv, attended, grad, lse, leaf_parent, *tables)
+        compiler_params=comm_params(4),
+    )(qkv, qkv, qkv, attended, grad, lse, leaf_parent, *tables, right, left)
 
 
 def feed_body(
     rank, tile, chunks,
     n_ref, c_ref, far_ref, wg_ref, wu_ref, wd_ref, mid_ref,
-    xu_in, xd_in, e_in, f_in, gain_ref,
-    grad_ref, low_grad_ref, res_ref, unit_ref, model_ref,
-    x_ref, e_ref, f_ref, midv, nbuf, cbuf, wbuf, low, low_t, acc_res, acc_back, acc_low, part, held, resv,
-    nsem, csem, wsem, rsem, msem, send, recv,
+    pick_ref, xu_in, xd_in, e_in, f_in, gain_ref,
+    grad_ref, low_grad_ref, res_ref, unit_out, model_out,
+    unit_ref, model_ref, x_ref, e_ref, f_ref, midv, nbuf, cbuf, wbuf, low, low_t, half_t, acc_res, acc_back, acc_low,
+    part, held, resv, nsem, csem, wsem, rsem, msem, send, recv,
 ):
     place = lax.axis_index("tensor")
     units = unit_ref.shape[1]
     tiles = units // tile
+    rows = part.shape[1]
+    half = rows // 2
     summed = Sum(place, part, held, send, recv, chunks)
 
     def load_rows(order, act):
@@ -914,73 +960,116 @@
     model_ref[...] = jnp.zeros_like(model_ref)
     greet(place)
 
-    def one_shard(order, carry):
-        into = order % 2
-        shard = place ^ (LINE - 1 - order)
-        load_rows(order, wait)
-
-        @pl.when(order < LINE - 1)
-        def _():
-            load_rows(order + 1, start)
-
-        first = nt(nbuf[into], e_ref[...]) + nt(cbuf[into], f_ref[...])
-        low[...] = first.astype(bf16)
-        low_t[...] = first.T.astype(bf16)
-        acc_res[...] = jnp.zeros_like(acc_res)
-        acc_back[...] = jnp.zeros_like(acc_back)
-        acc_low[...] = jnp.zeros_like(acc_low)
+    def one_block(n_rows, c_rows, count, turned, stage0, shard, here):
+        first = nt(n_rows(), e_ref[...]) + nt(c_rows(), f_ref[...])
+        low[:count] = first.astype(bf16)
+        turned[...] = first.T.astype(bf16)
+        acc_res[:count] = jnp.zeros((count, acc_res.shape[1]), f32)
+        acc_back[:count] = jnp.zeros((count, acc_back.shape[1]), f32)
+        acc_low[:count] = jnp.zeros((count, acc_low.shape[1]), f32)
 
         def one_tile(index, carry):
-            stage = order * tiles + index
+            stage = stage0 + index
             at = stage % 2
             load_weights(index, at, wait)
 
-            @pl.when(stage < LINE * tiles - 1)
+            @pl.when(stage < (LINE + 1) * tiles - 1)
             def _():
                 load_weights((index + 1) % tiles, 1 - at, start)
 
             columns = pl.ds(pl.multiple_of(index * tile, tile), tile)
             x_gate, x_rise, x_fall = x_ref[0, :, columns], x_ref[1, :, columns], x_ref[2, :, columns]
-            gate = nn(nbuf[into], wbuf[at, 0]) + nn(low[...], x_gate)
-            rise = nn(nbuf[into], wbuf[at, 1]) + nn(low[...], x_rise)
-            grad_hidden = nn(cbuf[into], wbuf[at, 2]) + nn(low[...], x_fall)
+            gate = nn(n_rows(), wbuf[at, 0]) + nn(low[:count], x_gate)
+            rise = nn(n_rows(), wbuf[at, 1]) + nn(low[:count], x_rise)
+            grad_hidden = nn(c_rows(), wbuf[at, 2]) + nn(low[:count], x_fall)
             sigmoid = jax.nn.sigmoid(gate)
             silu = gate * sigmoid
             hidden = (silu * rise).astype(bf16)
             grad_gate = (grad_hidden * rise * sigmoid * (1.0 + gate * (1.0 - sigmoid))).astype(bf16)
             grad_rise = (grad_hidden * silu).astype(bf16)
-            acc_back[...] += nt(grad_gate, wbuf[at, 0]) + nt(grad_rise, wbuf[at, 1])
-            acc_res[...] += nt(hidden, wbuf[at, 2])
-            acc_low[...] += nt(grad_gate, x_gate) + nt(grad_rise, x_rise) + nt(hidden, x_fall)
-            unit_ref[:rank, columns] += nn(low_t[:rank], grad_gate)
-            unit_ref[rank : 2 * rank, columns] += nn(low_t[rank : 2 * rank], grad_rise)
-            unit_ref[2 * rank :, columns] += nn(low_t[2 * rank : 3 * rank], hidden)
+            acc_back[:count] += nt(grad_gate, wbuf[at, 0]) + nt(grad_rise, wbuf[at, 1])
+            acc_res[:count] += nt(hidden, wbuf[at, 2])
+            acc_low[:count] += nt(grad_gate, x_gate) + nt(grad_rise, x_rise) + nt(hidden, x_fall)
+            unit_ref[:rank, columns] += nn(turned[:rank], grad_gate)
+            unit_ref[rank : 2 * rank, columns] += nn(turned[rank : 2 * rank], grad_rise)
+            unit_ref[2 * rank :, columns] += nn(turned[2 * rank : 3 * rank], hidden)
             return carry
 
         lax.fori_loop(0, tiles, one_tile, 0)
-        joined = acc_low[...].astype(bf16)
-        joined_t = acc_low[...].T.astype(bf16)
-        part[shard] = (acc_back[...] + nn(joined, e_ref[...])).astype(bf16)
-
-        @pl.when(order > 0)
+        joined = acc_low[:count].astype(bf16)
+        joined_t = acc_low[:count].T.astype(bf16)
+        part[shard, here] = (acc_back[:count] + nn(joined, e_ref[...])).astype(bf16)
+        return joined, joined_t
+
+    def model_grads(joined_t, n_rows, c_rows):
+        model_ref[: 2 * rank] += nn(joined_t[: 2 * rank], n_rows())
+        model_ref[2 * rank :] += nn(joined_t[2 * rank : 3 * rank], c_rows())
+
+    load_rows(jnp.int32(0), wait)
+    load_rows(jnp.int32(1), start)
+
+    def one_half(number, carry):
+        here = pl.ds(pl.multiple_of(number * half, half), half)
+
+        def n_rows():
+            return nbuf[0, here]
+
+        def c_rows():
+            return cbuf[0, here]
+
+        joined, joined_t = one_block(
+            n_rows, c_rows, half, half_t, number * tiles, place ^ (LINE - 1), here
+        )
+        for which in range(2):
+
+            @pl.when(number == which)
+            def _():
+                for chunk in range(which * chunks // 2, (which + 1) * chunks // 2):
+                    summed.begin(1, chunk)
+
+        resv[here] = (acc_res[:half] + nn(joined, f_ref[...])).astype(bf16)
+        model_grads(joined_t, n_rows, c_rows)
+        return carry
+
+    lax.fori_loop(0, 2, one_half, 0)
+    pltpu.make_async_copy(resv, res_ref.at[place ^ (LINE - 1)], rsem.at[0]).start()
+
+    def one_shard(order, carry):
+        into = order % 2
+        shard = place ^ (LINE - 1 - order)
+        load_rows(order, wait)
+
+        @pl.when(order < LINE - 1)
         def _():
-            pltpu.make_async_copy(resv, res_ref.at[shard], rsem.at[0]).wait()
-
-        resv[...] = (acc_res[...] + nn(joined, f_ref[...])).astype(bf16)
-        pltpu.make_async_copy(resv, res_ref.at[shard], rsem.at[0]).start()
-        for step in (1, 2, 3):
+            load_rows(order + 1, start)
+
+        def n_rows():
+            return nbuf[into]
+
+        def c_rows():
+            return cbuf[into]
+
+        joined, joined_t = one_block(
+            n_rows, c_rows, rows, low_t, (order + 1) * tiles, shard, slice(0, rows)
+        )
+        for step in (2, 3):
 
             @pl.when(order == step - 1)
             def _():
                 for chunk in range(chunks):
                     summed.send(step, chunk)
 
-        model_ref[: 2 * rank] += nn(joined_t[: 2 * rank], nbuf[into])
-        model_ref[2 * rank :] += nn(joined_t[2 * rank : 3 * rank], cbuf[into])
+        pltpu.make_async_copy(resv, res_ref.at[shard], rsem.at[0]).wait()
+        resv[...] = (acc_res[...] + nn(joined, f_ref[...])).astype(bf16)
+        pltpu.make_async_copy(resv, res_ref.at[shard], rsem.at[0]).start()
+        model_grads(joined_t, n_rows, c_rows)
         return carry
 
-    lax.fori_loop(0, LINE, one_shard, 0)
-    size = part.shape[1] // chunks
+    lax.fori_loop(1, LINE, one_shard, 0)
+    unit_out[: 3 * rank] = unit_ref[...].astype(bf16)
+    unit_out[3 * rank :] = jnp.full((rank, units), pick_ref[0, 0], f32).astype(bf16)
+    model_out[...] = model_ref[...].astype(bf16)
+    size = rows // chunks
     last = (LINE - 1) % 2
     load_middle.wait()
     for chunk in range(chunks):
@@ -997,22 +1086,24 @@
     summed.drain()
 
 
-def feed(normed, cots, weights, middle, units_exit, fall_entry, entries, finals, gain, tile=512, chunks=4):
+def feed(normed, cots, weights, middle, pick, units_exit, fall_entry, entries, finals, gain, tile=512, chunks=4):
     _, rows, features = normed.shape
     units = weights[0].shape[1]
     rank = fall_entry.shape[0]
     return pl.pallas_call(
         functools.partial(feed_body, rank, tile, chunks),
-        in_specs=[IN_HBM] * 7 + [IN_VMEM] * 5,
+        in_specs=[IN_HBM] * 7 + [pl.BlockSpec(memory_space=pltpu.SMEM)] + [IN_VMEM] * 5,
         out_specs=[IN_VMEM, IN_VMEM, IN_HBM, IN_VMEM, IN_VMEM],
         out_shape=[
             jax.ShapeDtypeStruct((rows, features), f32),
             jax.ShapeDtypeStruct((rows, features), bf16),
             jax.ShapeDtypeStruct((LINE, rows, features), bf16),
-            jax.ShapeDtypeStruct((3 * rank, units), f32),
-            jax.ShapeDtypeStruct((3 * rank, features), f32),
+            jax.ShapeDtypeStruct((4 * rank, units), bf16),
+            jax.ShapeDtypeStruct((3 * rank, features), bf16),
         ],
         scratch_shapes=[
+            pltpu.VMEM((3 * rank, units), f32),
+            pltpu.VMEM((3 * rank, features), f32),
             pltpu.VMEM((3, 3 * rank, units), bf16),
             pltpu.VMEM((3 * rank, features), bf16),
             pltpu.VMEM((3 * rank, features), bf16),
@@ -1022,6 +1113,7 @@
             pltpu.VMEM((2, 3, features, tile), bf16),
             pltpu.VMEM((rows, 3 * rank), bf16),
             pltpu.VMEM((3 * rank, rows), bf16),
+            pltpu.VMEM((3 * rank, rows // 2), bf16),
             pltpu.VMEM((rows, features), f32),
             pltpu.VMEM((rows, features), f32),
             pltpu.VMEM((rows, 3 * rank), f32),
@@ -1036,7 +1128,7 @@
         ]
         + line_sems(chunks),
         compiler_params=comm_params(5),
-    )(normed, *cots, *weights, middle, units_exit, fall_entry, entries, finals, gain[None, :])
+    )(normed, *cots, *weights, middle, pick, units_exit, fall_entry, entries, finals, gain[None, :])
 
 
 def pick_body(pick_ref, *refs):
@@ -1154,7 +1246,6 @@
     parents,
     adapter_pick,
 ):
-    pick = adapter_pick[0]
     adapters, rank = entry_maps.shape[1], entry_maps.shape[3]
     local_rows = tokens.shape[0]
     total = local_rows * lax.axis_size("tensor")
@@ -1193,38 +1284,25 @@
         most_one, w_heads, cotangent, entries, heads_exit, tables, leaf_parent, out_entry, finals, tokens, gain_two, seg
     )
 
-    grad_middle, branch, res_parts, unit_grads, model_grads = feed(
-        full_two, (cotangent, full_cot), w_units, middle, units_exit, fall_entry, entries, finals, gain_two
-    )
-    early = jnp.concatenate(
-        [unit_grads.astype(bf16), jnp.full((rank, unit_grads.shape[1]), pick).astype(bf16)]
-    )
-    model_low = model_grads.astype(bf16)
-    branch, early, model_low = lax.optimization_barrier((branch, early, model_low))
+    grad_middle, branch, res_parts, early, model_low = feed(
+        full_two, (cotangent, full_cot), w_units, middle, adapter_pick.astype(f32)[None, :],
+        units_exit, fall_entry, entries, finals, gain_two,
+    )
     early = per_tree(early)
     model_sum = lax.psum(model_low, "tensor")
 
     grad_attended, res_own, res_right, res_left, final_grads, exit_grads = branch_back(
         branch, w_heads, finals, out_entry, res_parts, attended, adapt_o
     )
-    grad_attended, res_right, res_left = lax.optimization_barrier((grad_attended, res_right, res_left))
-    from_left = permute(res_right, [(0, 1), (1, 2), (2, 3)])
-    from_right = permute(res_left, [(3, 2), (2, 1), (1, 0)])
-    head_grads = attend_back(qkv, attended, grad_attended, lse, leaf_parent, tables, seg)
-    head_grads, model_sum, from_left, from_right = lax.optimization_barrier(
-        (head_grads, model_sum, from_left, from_right)
-    )
+    head_grads, from_left, from_right = attend_back(
+        qkv, attended, grad_attended, lse, leaf_parent, tables, seg, res_right, res_left
+    )
+    head_grads, model_sum = lax.optimization_barrier((head_grads, model_sum))
     model_all = per_tree(model_sum)
-    grad_tokens, late_model, late_head = tokens_back(
+    grad_tokens, late_model, late_head, result = tokens_back(
         head_grads, w_heads, heads_exit, entries, tokens, gain_one, grad_middle,
-        full_one, low_one, final_grads, exit_grads,
-    )
-    result = (
-        middle
-        + res_own.astype(f32)
-        + from_left.astype(f32)
-        + from_right.astype(f32)
-    ).astype(bf16)
+        full_one, low_one, final_grads, exit_grads, middle, res_own, from_left, from_right,
+    )
 
     picks = early[:, 3 * rank, 0].astype(jnp.int32)
     grad_entries, grad_finals, grad_units, grad_down, grad_heads, grad_output = combine(

time: 698 us -> 692 us (level)
  Pallas kernels: 649 us -> 656 us
  transfers between devices with their start and end apart: 9 -> 7, of which waited for: 0 -> 0; matrix products, arithmetic and copies ran while one was open for 1% -> 1% of each run, Pallas kernels for 77% -> 78%
where the time goes in v9:
time: 692 us; the launch traced here: 683 us
  Pallas kernels  656 us (95%)
  between operations  15.3 us (2%)
    pallas_call x1, Pallas kernels, front(): pl.pallas_call(functools.partial(front_body, chunks, seg), in_specs=[IN_H...  231 us
    pallas_call x1, Pallas kernels, feed(): pl.pallas_call(functools.partial(feed_body, rank, tile, chunks), in_specs...  116 us
    pallas_call x1, Pallas kernels, tokens_back(): pl.pallas_call(functools.partial(tokens_body, chunks), in_specs=[IN_HBM,...  101 us
    pallas_call x1, Pallas kernels, branch_back(): pl.pallas_call(branch_body, in_specs=[IN_VMEM, IN_HBM, IN_VMEM, IN_VMEM,...  99.8 us
    pallas_call x1, Pallas kernels, gather_norm(): pl.pallas_call(gather_norm_body, in_specs=[IN_VMEM, IN_VMEM], out_specs=I...  64.9 us
    pallas_call x1, Pallas kernels, attend_back(): pl.pallas_call(functools.partial(attend_back_body, seg), grid=(pairs,), i...  33 us
  transfers between devices with their start and end apart: 7, of which 0 were waited for; matrix products, arithmetic and copies ran while one was open for 1% of the time, Pallas kernels for 78%

profile of v9, /device:TPU:0, one launch (start us, length us, event | category | flops | bytes accessed | tf_op | source)
XLA Modules:
  0.0 683.2 jit_solution(9113275737354933008)
XLA Ops:
  7.2 0.0 all-gather.9.cloned.1.call-start
  7.2 2.3 pad_maximum_fusion
  9.5 0.0 copy-start.4
  9.5 0.0 copy-start.2
  9.5 0.0 copy-start.3
  9.5 0.0 all-gather.9.cloned.1.call-update
  9.5 0.0 all-gather.11.cloned.1.call-start
  9.6 0.7 all-gather.11.cloned.1.call-update
  10.3 0.0 all-gather.13.cloned.1.call-start
  10.3 0.7 all-gather.13.cloned.1.call-update
  11.0 0.0 all-gather.15.cloned.1.call-start
  11.1 0.5 all-gather.15.cloned.1.call-update
  11.6 0.0 all-reduce.2.cloned.1.call-start
  12.3 0.0 copy-done.4
  12.3 0.1 add_bitcast_fusion
  12.4 0.1 broadcast_in_dim.29
  12.4 0.7 sub.10.p_ref
  13.1 0.0 copy-done.2
  13.1 0.6 broadcast_in_dim.33
  13.7 0.0 copy-done.3
  13.7 0.6 broadcast_in_dim.34
  14.3 64.9 %shard_map.260.x_ref = bf16[4,320,2048]{2,1,0:T(8,128)(2,1)} custom-call(bf16[320,2048]{1,0:T(8,128)(2,1)} %x_ref.3, f32[1,2048]{1,0:T(1,128)} %bitcast.27), custom_call_target="tpu_custom_call" | custom-call | tf_op jit(solution)/shard_map/pallas_call | solution.py:276
  79.2 2.0 shard_map.261
  81.2 0.0 all-gather.9.cloned.1.call-done.w_ref
  81.2 231.1 %shard_map.262 = (bf16[4,320,2048]{2,1,0:T(8,128)(2,1)}, bf16[3,1280,512]{2,1,0:T(8,128)(2,1)}, f32[320,2048]{1,0:T(8,128)}, bf16[4,320,2048]{2,1,0:T(8,128)(2,1...) custom-call(bf16[4,320,2048]{2,1,0:T(8,128)(2,1)} %shard_map.260.x_r, ...), custom_call_target="tpu_custom_call", output_to_operand_aliasing={{0}: (0, {})} | custom-call | tf_op jit(solution)/shard_map/pallas_call | solution.py:436
  312.3 0.0 all-gather.11.cloned.1.call-done.wg_ref
  312.4 0.0 all-gather.13.cloned.1.call-done.wu_ref
  312.4 0.0 all-gather.15.cloned.1.call-done.wd_ref
  312.4 116.5 %shard_map.263 = (f32[320,2048]{1,0:T(8,128)}, bf16[320,2048]{1,0:T(8,128)(2,1)}, bf16[4,320,2048]{2,1,0:T(8,128)(2,1)}, bf16[64,2048]{1,0:T(8,128)(2,1)}, bf16[48,2048]{1,0:T(8,128)(2,1)}) custom-call(bf16[4,320,2048]{2,1,0:T(8,128)(2,1)} %get-tuple-element.55.n_ref, bf16[320,2048]{1,0:T(8,128)(2,1)} %c_ref.3, ...), custom_call_target="tpu_custom_call" | custom-call | tf_op jit(solution)/shard_map/pallas_call | solution.py:1093
  428.9 0.0 all-reduce.2.cloned.1.call-update
  428.9 0.0 all-gather.17.cloned.1.call-start
  429.0 0.5 all-gather.17.cloned.1.call-update
  429.5 0.0 all-gather.19.cloned.1.call-start
  429.6 99.8 %shard_map.264 = (bf16[1,1280,512]{2,1,0:T(8,128)(2,1)}, bf16[320,2048]{1,0:T(8,128)(2,1)}, bf16[320,2048]{1,0:T(8,128)(2,1)}, bf16[320,2048]{1,0:T(8,128)(2,1)}, f32[16,2048]{1,0:T(8,128)}, /*index=5*/f32[16,512]{1,0:T(8,128)}) custom-call(bf16[320,2048]{1,0:T(8,128)(2,1)} %get-tuple-element.60.b_ref, ...), custom_call_target="tpu_custom_call" | custom-call | tf_op jit(solution)/shard_map/pallas_call | solution.py:527
  529.4 33.0 %shard_map.265 = (bf16[3,1280,512]{2,1,0:T(8,128)(2,1)}, bf16[320,2048]{1,0:T(8,128)(2,1)}, bf16[320,2048]{1,0:T(8,128)(2,1)}) custom-call(bf16[3,1280,512]{2,1,0:T(8,128)(2,1)} %get-tuple-element.53.q_ref.k_ref.v_ref, bf16[3,1280,512]{2,1,0:T(8,128)(2,1)} %get-tuple-element.53.q_ref.k_ref.v_ref, bf16[3,1280,512]{2,1,0:T(8,128)(2,1)} %get-tuple-element.53.q_ref.k_ref.v_ref, ...), custom_call_target="tpu_custom_call" | custom-call | tf_op jit(solution)/shard_map/pallas_call | solution.py:881
  562.5 0.0 all-reduce.2.cloned.1.call-done
  562.5 0.0 all-gather.19.cloned.1.call-update
  562.5 100.5 %shard_map.266 = (bf16[320,2048]{1,0:T(8,128)(2,1)}, bf16[8,64,2048]{2,1,0:T(8,128)(2,1)}, bf16[8,64,512]{2,1,0:T(8,128)(2,1)}, bf16[320,2048]{1,0:T(8,128)(2,1)}) custom-call(bf16[3,1280,512]{2,1,0:T(8,128)(2,1)} %get-tuple-element.69.d_ref, bf16[2048,2048]{1,0:T(8,128)(2,1)} %all-gather.9.cloned.1.call-done.w_ref, ...), custom_call_target="tpu_custom_call" | custom-call | tf_op jit(solution)/shard_map/pallas_call | solution.py:730
  663.0 0.0 all-gather.17.cloned.1.call-done
  663.1 1.5 fusion.pick_ref
  664.5 0.0 all-gather.19.cloned.1.call-done
  664.5 0.0 copy-start.1
  664.5 8.5 %shard_map.267 = (f32[5,8,16,2048]{3,2,1,0:T(8,128)}, f32[2,8,16,2048]{3,2,1,0:T(8,128)}, f32[2,8,16,2048]{3,2,1,0:T(8,128)}, f32[8,16,2048]{2,1,0:T(8,128)}, f3...) custom-call(s32[8]{0:T(128)} %fusion.pick_ref, bf16[8,64,2048]{2,1,0:T(8,128)(2,1)} %bitcast.21, ...), custom_call_target="tpu_custom_call" | custom-call | tf_op jit(solution)/shard_map/pallas_call | solution.py:1201
  673.1 0.0 copy-start
  673.1 0.0 copy-done.1
  673.1 1.1 copy.35
  674.1 0.7 copy-done
  674.8 1.1 copy.36
Async XLA Ops:
  7.2 74.1 %all-gather.9.cloned.1.call-start = ((), (), s32[]{:S(2)}) async-start(), calls=%async_computation | async-start | bytes 9437184 | tf_op jit(solution)/shard_map/all_gather | solution.py:1259
  9.5 2.8 copy-start.4
  9.5 3.6 copy-start.2
  9.5 4.2 copy-start.3
  9.5 302.8 %all-gather.11.cloned.1.call-start = ((), (), s32[]{:S(2)}) async-start(), calls=%async_computation.1 | async-start | bytes 9437184 | tf_op jit(solution)/shard_map/all_gather | solution.py:1267
  10.3 302.1 %all-gather.13.cloned.1.call-start = ((), (), s32[]{:S(2)}) async-start(), calls=%async_computation.2 | async-start | bytes 9437184 | tf_op jit(solution)/shard_map/all_gather | solution.py:1267
  11.0 301.4 %all-gather.15.cloned.1.call-start = ((), (), s32[]{:S(2)}) async-start(), calls=%async_computation.3 | async-start | bytes 9437184 | tf_op jit(solution)/shard_map/all_gather | solution.py:1267
  11.6 550.9 %all-reduce.2.cloned.1.call-start = ((), (), s32[]{:S(2)}) async-start(), calls=%async_computation.4 | async-start | bytes 393216 | tf_op jit(solution)/shard_map/psum | solution.py:1292
  428.9 234.1 %all-gather.17.cloned.1.call-start = ((), (), s32[]{:S(2)}) async-start(), calls=%async_computation.5 | async-start | bytes 2359296 | tf_op jit(solution)/shard_map/all_gather | solution.py:1157
  429.5 235.0 %all-gather.19.cloned.1.call-start = ((), (), s32[]{:S(2)}) async-start(), calls=%async_computation.6 | async-start | bytes 1769472 | tf_op jit(solution)/shard_map/all_gather | solution.py:1157
  664.5 8.5 %copy-start.1 = (bf16[320,2048]{1,0:T(8,128)(2,1)S(1)}, bf16[320,2048]{1,0:T(8,128)(2,1)}, u32[]{:S(2)}) copy-start(bf16[320,2048]{1,0:T(8,128)(2,1)} %get-tuple-element.98) | copy-start | bytes 3932164
  673.1 1.8 copy-start
Sparse Core Ops, SparseCore 0:
  10.5 57.0 all-gather.8
  69.5 54.3 all-gather.10
  125.8 54.3 all-gather.12
  182.0 54.3 all-gather.14
  429.1 38.5 all-reduce.1
  469.6 27.3 all-gather.16
  562.6 24.8 all-gather.18

commit v10 on v9

--- a/solution.py
+++ b/solution.py
@@ -473,80 +473,6 @@
     )(x, weight, cot, entries, exits, *tables, leaf_parent, out_entry, finals, tokens, gain[None, :])
 
 
-def branch_body(
-    b_ref, w_ref, e_ref, a_ref, p_ref, d_ref, lo_ref, y_ref, own_ref, right_ref, left_ref,
-    final_ref, exit_ref,
-    buf, part, held, wv, wsem, send, recv, s_send, s_recv,
-):
-    place = lax.axis_index("tensor")
-    rows = b_ref.shape[0]
-    load, parts = fetch([(w_ref.at[:, 3 * y_ref.shape[2] :], wv), (p_ref, part)], wsem)
-    greet(place)
-    buf[place] = b_ref[...]
-    gather = Gather(place, buf, send, recv, 1)
-    summed = Sum(place, part, held, s_send, s_recv, 1)
-    gather.send(1, 0)
-    parts.wait()
-    summed.send(1, 0)
-    load.wait()
-    for slot in range(LINE):
-        if slot:
-            gather.arrive(slot, 0)
-        if 0 < slot < LINE - 1:
-            gather.send(slot + 1, 0)
-        if slot == 1:
-            summed.send(2, 0)
-        if slot == 2:
-            summed.add(3, 0)
-            own_ref[...] = part[place]
-            for out_ref, side in ((right_ref, 1), (left_ref, -1)):
-
-                @pl.when(far_of(place, side) < LINE - 1)
-                def _():
-                    out_ref[...] = part[place + side]
-
-                @pl.when(far_of(place, side) == LINE - 1)
-                def _():
-                    out_ref[...] = jnp.zeros_like(out_ref)
-
-        shard = place ^ slot
-        mine = pl.ds(pl.multiple_of(shard * rows, rows), rows)
-        low = nt(buf[shard], e_ref[0])
-        y_ref[0, mine] = (nn(buf[shard], wv[...]) + nn(low.astype(bf16), a_ref[...])).astype(bf16)
-        final = nn(lo_ref[mine].astype(f32).T.astype(bf16), buf[shard])
-        leave = nn(low.T.astype(bf16), d_ref[mine])
-        final_ref[...] = final if slot == 0 else final_ref[...] + final
-        exit_ref[...] = leave if slot == 0 else exit_ref[...] + leave
-    gather.drain()
-    summed.drain(LINE - 1)
-
-
-def branch_back(branch, weight, finals, exits, parts, attended, low_out):
-    rows, features = branch.shape
-    rank, width = exits.shape
-    return pl.pallas_call(
-        branch_body,
-        in_specs=[IN_VMEM, IN_HBM, IN_VMEM, IN_VMEM, IN_HBM, IN_VMEM, IN_VMEM],
-        out_specs=[IN_VMEM] * 6,
-        out_shape=[jax.ShapeDtypeStruct((1, LINE * rows, width), bf16)]
-        + [jax.ShapeDtypeStruct((rows, features), bf16)] * 3
-        + [
-            jax.ShapeDtypeStruct((rank, features), f32),
-            jax.ShapeDtypeStruct((rank, width), f32),
-        ],
-        scratch_shapes=[
-            pltpu.VMEM((LINE, rows, features), bf16),
-            pltpu.VMEM((LINE, rows, features), bf16),
-            pltpu.VMEM((2, LINE - 1, rows, features), bf16),
-            pltpu.VMEM((features, width), bf16),
-            pltpu.SemaphoreType.DMA((2,)),
-        ]
-        + line_sems(1)
-        + line_sems(1),
-        compiler_params=comm_params(2),
-    )(branch, weight, finals, exits, parts, attended, low_out)
-
-
 def tokens_body(
     chunks, d_ref, w_ref, a_ref, e_ref, x_ref, gain_ref, mid_ref, n_ref, lone_ref, final_ref, exit_ref,
     middle_ref, own_ref, left_ref, right_ref,
@@ -566,7 +492,7 @@
             (n_ref, nv),
             (mid_ref, midv),
             (middle_ref, acc),
-            (own_ref, terms.at[0]),
+            (own_ref.at[place], terms.at[0]),
             (left_ref, terms.at[1]),
             (right_ref, terms.at[2]),
         ],
@@ -911,18 +837,20 @@
 
 def feed_body(
     rank, tile, chunks,
-    n_ref, c_ref, far_ref, wg_ref, wu_ref, wd_ref, mid_ref,
-    pick_ref, xu_in, xd_in, e_in, f_in, gain_ref,
-    grad_ref, low_grad_ref, res_ref, unit_out, model_out,
-    unit_ref, model_ref, x_ref, e_ref, f_ref, midv, nbuf, cbuf, wbuf, low, low_t, half_t, acc_res, acc_back, acc_low,
-    part, held, resv, nsem, csem, wsem, rsem, msem, send, recv,
+    n_ref, c_ref, far_ref, wg_ref, wu_ref, wd_ref, mid_ref, wo_ref,
+    pick_ref, xu_in, xd_in, e_in, f_in, gain_ref, oe_ref, att_ref, lo_ref,
+    grad_ref, res_ref, right_ref, left_ref, b_ref, held_ref, unit_out, model_out, y_ref, final_ref, exit_ref,
+    unit_ref, model_ref, x_ref, e_ref, f_ref, midv, nbuf, cbuf, wbuf, low, low_t, acc_res, acc_back, acc_low,
+    part, held, resv, own, extra, wo, nsem, csem, wsem, rsem, msem,
+    send, recv, g_send, g_recv, x_send, x_recv, r_send, r_recv,
 ):
     place = lax.axis_index("tensor")
     units = unit_ref.shape[1]
     tiles = units // tile
     rows = part.shape[1]
-    half = rows // 2
     summed = Sum(place, part, held, send, recv, chunks)
+    gather = Gather(place, b_ref, g_send, g_recv, chunks, own)
+    joint = Gather(place, extra, x_send, x_recv, 1)
 
     def load_rows(order, act):
         into = order % 2
@@ -948,7 +876,8 @@
 
     load_rows(jnp.int32(0), start)
     load_weights(0, 0, start)
-    (load_middle,) = fetch([(mid_ref, midv)], msem)
+    width = wo.shape[1]
+    load_middle, load_out = fetch([(mid_ref, midv), (wo_ref.at[:, 3 * width :], wo)], msem)
     for padded in (x_ref, e_ref, f_ref):
         padded[...] = jnp.zeros_like(padded)
     x_ref[0, :rank] = xu_in[0]
@@ -960,118 +889,77 @@
     model_ref[...] = jnp.zeros_like(model_ref)
     greet(place)
 
-    def one_block(n_rows, c_rows, count, turned, stage0, shard, here):
-        first = nt(n_rows(), e_ref[...]) + nt(c_rows(), f_ref[...])
-        low[:count] = first.astype(bf16)
-        turned[...] = first.T.astype(bf16)
-        acc_res[:count] = jnp.zeros((count, acc_res.shape[1]), f32)
-        acc_back[:count] = jnp.zeros((count, acc_back.shape[1]), f32)
-        acc_low[:count] = jnp.zeros((count, acc_low.shape[1]), f32)
+    def one_shard(order, carry):
+        into = order % 2
+        shard = place ^ (LINE - 1 - order)
+        load_rows(order, wait)
+
+        @pl.when(order < LINE - 1)
+        def _():
+            load_rows(order + 1, start)
+
+        first = nt(nbuf[into], e_ref[...]) + nt(cbuf[into], f_ref[...])
+        low[...] = first.astype(bf16)
+        low_t[...] = first.T.astype(bf16)
+        acc_res[...] = jnp.zeros_like(acc_res)
+        acc_back[...] = jnp.zeros_like(acc_back)
+        acc_low[...] = jnp.zeros_like(acc_low)
 
         def one_tile(index, carry):
-            stage = stage0 + index
+            stage = order * tiles + index
             at = stage % 2
             load_weights(index, at, wait)
 
-            @pl.when(stage < (LINE + 1) * tiles - 1)
+            @pl.when(stage < LINE * tiles - 1)
             def _():
                 load_weights((index + 1) % tiles, 1 - at, start)
 
             columns = pl.ds(pl.multiple_of(index * tile, tile), tile)
             x_gate, x_rise, x_fall = x_ref[0, :, columns], x_ref[1, :, columns], x_ref[2, :, columns]
-            gate = nn(n_rows(), wbuf[at, 0]) + nn(low[:count], x_gate)
-            rise = nn(n_rows(), wbuf[at, 1]) + nn(low[:count], x_rise)
-            grad_hidden = nn(c_rows(), wbuf[at, 2]) + nn(low[:count], x_fall)
+            gate = nn(nbuf[into], wbuf[at, 0]) + nn(low[...], x_gate)
+            rise = nn(nbuf[into], wbuf[at, 1]) + nn(low[...], x_rise)
+            grad_hidden = nn(cbuf[into], wbuf[at, 2]) + nn(low[...], x_fall)
             sigmoid = jax.nn.sigmoid(gate)
             silu = gate * sigmoid
             hidden = (silu * rise).astype(bf16)
             grad_gate = (grad_hidden * rise * sigmoid * (1.0 + gate * (1.0 - sigmoid))).astype(bf16)
             grad_rise = (grad_hidden * silu).astype(bf16)
-            acc_back[:count] += nt(grad_gate, wbuf[at, 0]) + nt(grad_rise, wbuf[at, 1])
-            acc_res[:count] += nt(hidden, wbuf[at, 2])
-            acc_low[:count] += nt(grad_gate, x_gate) + nt(grad_rise, x_rise) + nt(hidden, x_fall)
-            unit_ref[:rank, columns] += nn(turned[:rank], grad_gate)
-            unit_ref[rank : 2 * rank, columns] += nn(turned[rank : 2 * rank], grad_rise)
-            unit_ref[2 * rank :, columns] += nn(turned[2 * rank : 3 * rank], hidden)
+            acc_back[...] += nt(grad_gate, wbuf[at, 0]) + nt(grad_rise, wbuf[at, 1])
+            acc_res[...] += nt(hidden, wbuf[at, 2])
+            acc_low[...] += nt(grad_gate, x_gate) + nt(grad_rise, x_rise) + nt(hidden, x_fall)
+            unit_ref[:rank, columns] += nn(low_t[:rank], grad_gate)
+            unit_ref[rank : 2 * rank, columns] += nn(low_t[rank : 2 * rank], grad_rise)
+            unit_ref[2 * rank :, columns] += nn(low_t[2 * rank : 3 * rank], hidden)
             return carry
 
         lax.fori_loop(0, tiles, one_tile, 0)
-        joined = acc_low[:count].astype(bf16)
-        joined_t = acc_low[:count].T.astype(bf16)
-        part[shard, here] = (acc_back[:count] + nn(joined, e_ref[...])).astype(bf16)
-        return joined, joined_t
-
-    def model_grads(joined_t, n_rows, c_rows):
-        model_ref[: 2 * rank] += nn(joined_t[: 2 * rank], n_rows())
-        model_ref[2 * rank :] += nn(joined_t[2 * rank : 3 * rank], c_rows())
-
-    load_rows(jnp.int32(0), wait)
-    load_rows(jnp.int32(1), start)
-
-    def one_half(number, carry):
-        here = pl.ds(pl.multiple_of(number * half, half), half)
-
-        def n_rows():
-            return nbuf[0, here]
-
-        def c_rows():
-            return cbuf[0, here]
-
-        joined, joined_t = one_block(
-            n_rows, c_rows, half, half_t, number * tiles, place ^ (LINE - 1), here
-        )
-        for which in range(2):
-
-            @pl.when(number == which)
-            def _():
-                for chunk in range(which * chunks // 2, (which + 1) * chunks // 2):
-                    summed.begin(1, chunk)
-
-        resv[here] = (acc_res[:half] + nn(joined, f_ref[...])).astype(bf16)
-        model_grads(joined_t, n_rows, c_rows)
-        return carry
-
-    lax.fori_loop(0, 2, one_half, 0)
-    pltpu.make_async_copy(resv, res_ref.at[place ^ (LINE - 1)], rsem.at[0]).start()
-
-    def one_shard(order, carry):
-        into = order % 2
-        shard = place ^ (LINE - 1 - order)
-        load_rows(order, wait)
-
-        @pl.when(order < LINE - 1)
-        def _():
-            load_rows(order + 1, start)
-
-        def n_rows():
-            return nbuf[into]
-
-        def c_rows():
-            return cbuf[into]
-
-        joined, joined_t = one_block(
-            n_rows, c_rows, rows, low_t, (order + 1) * tiles, shard, slice(0, rows)
-        )
-        for step in (2, 3):
+        joined = acc_low[...].astype(bf16)
+        joined_t = acc_low[...].T.astype(bf16)
+        part[shard] = (acc_back[...] + nn(joined, e_ref[...])).astype(bf16)
+        for step in (1, 2, 3):
 
             @pl.when(order == step - 1)
             def _():
                 for chunk in range(chunks):
                     summed.send(step, chunk)
 
-        pltpu.make_async_copy(resv, res_ref.at[shard], rsem.at[0]).wait()
+        @pl.when(order > 0)
+        def _():
+            pltpu.make_async_copy(resv, res_ref.at[shard], rsem.at[0]).wait()
+
         resv[...] = (acc_res[...] + nn(joined, f_ref[...])).astype(bf16)
         pltpu.make_async_copy(resv, res_ref.at[shard], rsem.at[0]).start()
-        model_grads(joined_t, n_rows, c_rows)
+        model_ref[: 2 * rank] += nn(joined_t[: 2 * rank], nbuf[into])
+        model_ref[2 * rank :] += nn(joined_t[2 * rank : 3 * rank], cbuf[into])
         return carry
 
-    lax.fori_loop(1, LINE, one_shard, 0)
-    unit_out[: 3 * rank] = unit_ref[...].astype(bf16)
-    unit_out[3 * rank :] = jnp.full((rank, units), pick_ref[0, 0], f32).astype(bf16)
-    model_out[...] = model_ref[...].astype(bf16)
+    lax.fori_loop(0, LINE, one_shard, 0)
+    extra[place] = model_ref[...].astype(bf16)
+    joint.send(1, 0)
     size = rows // chunks
     last = (LINE - 1) % 2
     load_middle.wait()
+    stores = []
     for chunk in range(chunks):
         summed.total(chunk, acc_back)
         here = chunk_rows(chunk, size)
@@ -1080,26 +968,164 @@
         scaled = acc_back[here] * gain_ref[...]
         mean = jnp.mean(scaled * middle, axis=1, keepdims=True)
         grad = cbuf[last, here].astype(f32) + rms * (scaled - middle * (rms * rms) * mean)
-        grad_ref[here] = grad
-        low_grad_ref[here] = grad.astype(bf16)
+        own[here] = grad.astype(bf16)
+        gather.send(1, chunk, least=1)
+        midv[here] = grad
+        store = pltpu.make_async_copy(midv.at[here], grad_ref.at[here], nsem.at[chunk % 2])
+        if chunk >= 2:
+            stores[chunk - 2].wait()
+        store.start()
+        stores.append(store)
+    for chunk in range(chunks):
+        gather.send(1, chunk, most=0)
     pltpu.make_async_copy(resv, res_ref.at[place], rsem.at[0]).wait()
+
+    def pass_on(side, step, source, target):
+        index = 0 if side == 1 else 1
+        return pltpu.make_async_remote_copy(
+            src_ref=source,
+            dst_ref=held_ref.at[index, step - 1],
+            send_sem=r_send.at[index, step - 1],
+            recv_sem=r_recv.at[index, step - 1],
+            device_id={"tensor": target},
+            device_id_type=MESH,
+        )
+
+    def at_far(side, number, act):
+        pl.when(far_of(place, side) == number)(act)
+
+    def ready(side, step, shard):
+        index = 0 if side == 1 else 1
+        pass_on(side, step, resv, place - side).wait_recv()
+        copies = [
+            pltpu.make_async_copy(res_ref.at[shard], cbuf.at[0], csem.at[0]),
+            pltpu.make_async_copy(held_ref.at[index, step - 1], cbuf.at[1], csem.at[1]),
+        ]
+        for copy in copies:
+            copy.start()
+        for copy in copies:
+            copy.wait()
+        cbuf[0] = (cbuf[0].astype(f32) + cbuf[1].astype(f32)).astype(bf16)
+
+    for side in SIDES:
+        for step in (1, 2):
+            at_far(
+                side,
+                0,
+                lambda: pass_on(side, step, res_ref.at[place + side * (LINE - step)], place + side).start(),
+            )
+
+    load_out.wait()
+    for store in stores[-2:]:
+        store.wait()
+
+    def through(number, rows_ref, shard):
+        mine = pl.ds(pl.multiple_of(shard * rows, rows), rows)
+        value = rows_ref[...]
+        reduced = nt(value, f_in[0])
+        y_ref[0, mine] = (nn(value, wo[...]) + nn(reduced.astype(bf16), oe_ref[...])).astype(bf16)
+        final = nn(lo_ref[mine].astype(f32).T.astype(bf16), value)
+        leave = nn(reduced.T.astype(bf16), att_ref[mine])
+        final_ref[...] = final if number == 0 else final_ref[...] + final
+        exit_ref[...] = leave if number == 0 else exit_ref[...] + leave
+
+    def take(number, shard):
+        copy = pltpu.make_async_copy(b_ref.at[shard], nbuf.at[number % 2], nsem.at[number % 2])
+        copy.start()
+        copy.wait()
+        through(number, nbuf.at[number % 2], shard)
+
+    def edge_got(step):
+        for side in SIDES:
+
+            @pl.when(far_of(place, side) == LINE - 1)
+            def _():
+                for chunk in range(chunks):
+                    gather.copy(side, step, chunk, place - side * step, place - side).wait_recv()
+
+    inside = ((place + 1) // 2) % 2
+    joint.relay(2, 0)
+    through(0, own, place)
+    unit_out[: 3 * rank] = unit_ref[...].astype(bf16)
+    unit_out[3 * rank :] = jnp.full((rank, units), pick_ref[0, 0], f32).astype(bf16)
+    for chunk in range(chunks):
+        gather.relay(2, chunk)
+    edge_got(1)
+    joint.relay(3, 0)
+    take(1, place ^ (1 + 2 * inside))
+    for chunk in range(chunks):
+        gather.relay(3, chunk)
+    for side in SIDES:
+
+        @pl.when(far_of(place, side) == 1)
+        def _():
+            ready(side, 1, place + side * 2)
+            resv[...] = cbuf[0]
+            pass_on(side, 2, resv, place + side).start()
+
+    edge_got(2)
+    take(2, place ^ (2 - inside))
+    joint.close()
+    model_out[...] = functools.reduce(
+        jnp.add, [extra[shard].astype(f32) for shard in range(LINE)]
+    ).astype(bf16)
+    edge_got(3)
+    take(3, place ^ (3 - inside))
+    for index, side in enumerate(SIDES):
+        target = (right_ref, left_ref)[index]
+
+        @pl.when(far_of(place, side) == 0)
+        def _():
+            copy = pltpu.make_async_copy(res_ref.at[place + side], nbuf.at[index], nsem.at[index])
+            copy.start()
+            copy.wait()
+
+        @pl.when((far_of(place, side) > 0) & (far_of(place, side) < LINE - 1))
+        def _():
+            ready(side, 2, place + side)
+            nbuf[index] = cbuf[0]
+
+        copy = pltpu.make_async_copy(nbuf.at[index], target, nsem.at[index])
+        copy.start()
+        copy.wait()
+    for side in SIDES:
+        for step in (1, 2):
+            at_far(
+                side,
+                0,
+                lambda: pass_on(side, step, res_ref.at[place + side * (LINE - step)], place + side).wait_send(),
+            )
+        at_far(side, 1, lambda: pass_on(side, 2, resv, place + side).wait_send())
     summed.drain()
-
-
-def feed(normed, cots, weights, middle, pick, units_exit, fall_entry, entries, finals, gain, tile=512, chunks=4):
+    gather.drain()
+    joint.drain()
+
+
+def feed(
+    normed, cots, weights, middle, w_heads, pick, units_exit, fall_entry, entries, finals, gain, out_entry,
+    attended, low_out, tile=512, chunks=4,
+):
     _, rows, features = normed.shape
     units = weights[0].shape[1]
-    rank = fall_entry.shape[0]
+    rank, width = out_entry.shape
+    total = LINE * rows
+    one = jax.ShapeDtypeStruct((rows, features), bf16)
     return pl.pallas_call(
         functools.partial(feed_body, rank, tile, chunks),
-        in_specs=[IN_HBM] * 7 + [pl.BlockSpec(memory_space=pltpu.SMEM)] + [IN_VMEM] * 5,
-        out_specs=[IN_VMEM, IN_VMEM, IN_HBM, IN_VMEM, IN_VMEM],
+        in_specs=[IN_HBM] * 8 + [pl.BlockSpec(memory_space=pltpu.SMEM)] + [IN_VMEM] * 8,
+        out_specs=[IN_HBM] * 6 + [IN_VMEM] * 5,
         out_shape=[
             jax.ShapeDtypeStruct((rows, features), f32),
-            jax.ShapeDtypeStruct((rows, features), bf16),
             jax.ShapeDtypeStruct((LINE, rows, features), bf16),
+            one,
+            one,
+            jax.ShapeDtypeStruct((LINE, rows, features), bf16),
+            jax.ShapeDtypeStruct((2, LINE - 2, rows, features), bf16),
             jax.ShapeDtypeStruct((4 * rank, units), bf16),
             jax.ShapeDtypeStruct((3 * rank, features), bf16),
+            jax.ShapeDtypeStruct((1, total, width), bf16),
+            jax.ShapeDtypeStruct((rank, features), f32),
+            jax.ShapeDtypeStruct((rank, width), f32),
         ],
         scratch_shapes=[
             pltpu.VMEM((3 * rank, units), f32),
@@ -1113,22 +1139,30 @@
             pltpu.VMEM((2, 3, features, tile), bf16),
             pltpu.VMEM((rows, 3 * rank), bf16),
             pltpu.VMEM((3 * rank, rows), bf16),
-            pltpu.VMEM((3 * rank, rows // 2), bf16),
             pltpu.VMEM((rows, features), f32),
             pltpu.VMEM((rows, features), f32),
             pltpu.VMEM((rows, 3 * rank), f32),
             pltpu.VMEM((LINE, rows, features), bf16),
             pltpu.VMEM((2, LINE - 1, rows, features), bf16),
             pltpu.VMEM((rows, features), bf16),
+            pltpu.VMEM((rows, features), bf16),
+            pltpu.VMEM((LINE, 3 * rank, features), bf16),
+            pltpu.VMEM((features, width), bf16),
             pltpu.SemaphoreType.DMA((2,)),
             pltpu.SemaphoreType.DMA((2,)),
             pltpu.SemaphoreType.DMA((2, 3)),
             pltpu.SemaphoreType.DMA((1,)),
-            pltpu.SemaphoreType.DMA((1,)),
+            pltpu.SemaphoreType.DMA((2,)),
         ]
-        + line_sems(chunks),
+        + line_sems(chunks)
+        + line_sems(chunks)
+        + line_sems(1)
+        + [pltpu.SemaphoreType.DMA((2, LINE - 2))] * 2,
         compiler_params=comm_params(5),
-    )(normed, *cots, *weights, middle, pick, units_exit, fall_entry, entries, finals, gain[None, :])
+    )(
+        normed, *cots, *weights, middle, w_heads, pick, units_exit, fall_entry, entries, finals, gain[None, :], out_entry,
+        attended, low_out,
+    )
 
 
 def pick_body(pick_ref, *refs):
@@ -1284,24 +1318,21 @@
         most_one, w_heads, cotangent, entries, heads_exit, tables, leaf_parent, out_entry, finals, tokens, gain_two, seg
     )
 
-    grad_middle, branch, res_parts, early, model_low = feed(
-        full_two, (cotangent, full_cot), w_units, middle, adapter_pick.astype(f32)[None, :],
-        units_exit, fall_entry, entries, finals, gain_two,
+    (
+        grad_middle, res_parts, res_right, res_left, _, _, early, model_sum, grad_attended, final_grads, exit_grads,
+    ) = feed(
+        full_two, (cotangent, full_cot), w_units, middle, w_heads, adapter_pick.astype(f32)[None, :],
+        units_exit, fall_entry, entries, finals, gain_two, out_entry, attended, adapt_o,
     )
     early = per_tree(early)
-    model_sum = lax.psum(model_low, "tensor")
-
-    grad_attended, res_own, res_right, res_left, final_grads, exit_grads = branch_back(
-        branch, w_heads, finals, out_entry, res_parts, attended, adapt_o
-    )
+    model_all = per_tree(model_sum)
+
     head_grads, from_left, from_right = attend_back(
         qkv, attended, grad_attended, lse, leaf_parent, tables, seg, res_right, res_left
     )
-    head_grads, model_sum = lax.optimization_barrier((head_grads, model_sum))
-    model_all = per_tree(model_sum)
     grad_tokens, late_model, late_head, result = tokens_back(
         head_grads, w_heads, heads_exit, entries, tokens, gain_one, grad_middle,
-        full_one, low_one, final_grads, exit_grads, middle, res_own, from_left, from_right,
+        full_one, low_one, final_grads, exit_grads, middle, res_parts, from_left, from_right,
     )
 
     picks = early[:, 3 * rank, 0].astype(jnp.int32)

time: 692 us -> 684 us (0.988)
  Pallas kernels: 656 us -> 648 us
    pallas_call x1 -> x0, Pallas kernels: 99.8 us -> none  [branch_back(): pl.pallas_call(branch_body, in_specs=[IN_VMEM, IN_HBM, IN_VMEM, IN_VMEM,...]
    pallas_call x1, Pallas kernels: 116 us -> 212 us  [feed(): pl.pallas_call(functools.partial(feed_body, rank, tile, chunks), in_specs...]
  transfers between devices with their start and end apart: 7 -> 6, of which waited for: 0 -> 0; matrix products, arithmetic and copies ran while one was open for 1% -> 1% of each run, Pallas kernels for 78% -> 63%
where the time goes in v10:
time: 684 us; the launch traced here: 675 us
  Pallas kernels  648 us (95%)
  between operations  15.4 us (2%)
    pallas_call x1, Pallas kernels, front(): pl.pallas_call(functools.partial(front_body, chunks, seg), in_specs=[IN_H...  231 us
    pallas_call x1, Pallas kernels, feed(): pl.pallas_call(functools.partial(feed_body, rank, tile, chunks), in_specs...  212 us
    pallas_call x1, Pallas kernels, tokens_back(): pl.pallas_call(functools.partial(tokens_body, chunks), in_specs=[IN_HBM,...  101 us
    pallas_call x1, Pallas kernels, gather_norm(): pl.pallas_call(gather_norm_body, in_specs=[IN_VMEM, IN_VMEM], out_specs=I...  64.9 us
    pallas_call x1, Pallas kernels, attend_back(): pl.pallas_call(functools.partial(attend_back_body, seg), grid=(pairs,), i...  29.3 us
  transfers between devices with their start and end apart: 6, of which 0 were waited for; matrix products, arithmetic and copies ran while one was open for 1% of the time, Pallas kernels for 63%

profile of v10, /device:TPU:0, one launch (start us, length us, event | category | flops | bytes accessed | tf_op | source)
XLA Modules:
  0.0 675.2 jit_solution(5499348922990215412)
XLA Ops:
  7.2 0.0 all-gather.9.cloned.1.call-start
  7.2 2.3 pad_maximum_fusion
  9.5 0.0 copy-start.4
  9.5 0.0 copy-start.2
  9.5 0.0 copy-start.3
  9.5 0.0 all-gather.9.cloned.1.call-update
  9.5 0.0 all-gather.11.cloned.1.call-start
  9.6 0.7 all-gather.11.cloned.1.call-update
  10.3 0.0 all-gather.13.cloned.1.call-start
  10.3 0.7 all-gather.13.cloned.1.call-update
  11.0 0.0 all-gather.15.cloned.1.call-start
  11.1 0.5 all-gather.15.cloned.1.call-update
  11.6 0.0 all-gather.17.cloned.1.call-start
  12.3 0.0 copy-done.4
  12.3 0.1 add_bitcast_fusion
  12.4 0.1 broadcast_in_dim.29
  12.4 0.7 sub.10.p_ref
  13.1 0.0 copy-done.2
  13.1 0.6 broadcast_in_dim.33
  13.7 0.0 copy-done.3
  13.7 0.6 broadcast_in_dim.34
  14.3 64.9 %shard_map.260.x_ref = bf16[4,320,2048]{2,1,0:T(8,128)(2,1)} custom-call(bf16[320,2048]{1,0:T(8,128)(2,1)} %x_ref.3, f32[1,2048]{1,0:T(1,128)} %bitcast.25), custom_call_target="tpu_custom_call" | custom-call | tf_op jit(solution)/shard_map/pallas_call | solution.py:276
  79.2 2.0 shard_map.261
  81.2 0.0 all-gather.9.cloned.1.call-done.w_ref.wo_ref
  81.2 231.1 %shard_map.262 = (bf16[4,320,2048]{2,1,0:T(8,128)(2,1)}, bf16[3,1280,512]{2,1,0:T(8,128)(2,1)}, f32[320,2048]{1,0:T(8,128)}, bf16[4,320,2048]{2,1,0:T(8,128)(2,1...) custom-call(bf16[4,320,2048]{2,1,0:T(8,128)(2,1)} %shard_map.260.x_r, ...), custom_call_target="tpu_custom_call", output_to_operand_aliasing={{0}: (0, {})} | custom-call | tf_op jit(solution)/shard_map/pallas_call | solution.py:436
  312.4 0.0 all-gather.11.cloned.1.call-done.wg_ref
  312.4 0.0 all-gather.13.cloned.1.call-done.wu_ref
  312.4 0.0 all-gather.15.cloned.1.call-done.wd_ref
  312.5 212.1 %shard_map.263 = (f32[320,2048]{1,0:T(8,128)}, bf16[4,320,2048]{2,1,0:T(8,128)(2,1)}, bf16[320,2048]{1,0:T(8,128)(2,1)}, bf16[320,2048]{1,0:T(8,128)(2,1)}, bf16...) custom-call(bf16[4,320,2048]{2,1,0:T(8,128)(2,1)} %get-tuple-element, ...), custom_call_target="tpu_custom_call" | custom-call | tf_op jit(solution)/shard_map/pallas_call | solution.py:1113
  524.5 0.0 all-gather.17.cloned.1.call-update
  524.6 0.3 all-gather.19.cloned.1.call-start
  524.8 0.3 all-gather.19.cloned.1.call-update
  525.1 29.3 %shard_map.264 = (bf16[3,1280,512]{2,1,0:T(8,128)(2,1)}, bf16[320,2048]{1,0:T(8,128)(2,1)}, bf16[320,2048]{1,0:T(8,128)(2,1)}) custom-call(bf16[3,1280,512]{2,1,0:T(8,128)(2,1)} %get-tuple-element.49.q_ref.k_ref.v_ref, bf16[3,1280,512]{2,1,0:T(8,128)(2,1)} %get-tuple-element.49.q_ref.k_ref.v_ref, bf16[3,1280,512]{2,1,0:T(8,128)(2,1)} %get-tuple-element.49.q_ref.k_ref.v_ref, ...), custom_call_target="tpu_custom_call" | custom-call | tf_op jit(solution)/shard_map/pallas_call | solution.py:807
  554.4 100.5 %shard_map.265 = (bf16[320,2048]{1,0:T(8,128)(2,1)}, bf16[8,64,2048]{2,1,0:T(8,128)(2,1)}, bf16[8,64,512]{2,1,0:T(8,128)(2,1)}, bf16[320,2048]{1,0:T(8,128)(2,1)}) custom-call(bf16[3,1280,512]{2,1,0:T(8,128)(2,1)} %get-tuple-element.61.d_ref, bf16[2048,2048]{1,0:T(8,128)(2,1)} %all-gather.9.cloned.1.call-done.w_ref.wo_ref, ...), custom_call_target="tpu_custom_call" | custom-call | tf_op jit(solution)/shard_map/pallas_call | solution.py:656
  655.0 0.0 all-gather.17.cloned.1.call-done
  655.0 1.5 fusion.pick_ref
  656.5 0.0 all-gather.19.cloned.1.call-done
  656.5 0.0 copy-start.1
  656.5 8.5 %shard_map.266 = (f32[5,8,16,2048]{3,2,1,0:T(8,128)}, f32[2,8,16,2048]{3,2,1,0:T(8,128)}, f32[2,8,16,2048]{3,2,1,0:T(8,128)}, f32[8,16,2048]{2,1,0:T(8,128)}, f3...) custom-call(s32[8]{0:T(128)} %fusion.pick_ref, bf16[8,64,2048]{2,1,0:T(8,128)(2,1)} %bitcast.21, ...), custom_call_target="tpu_custom_call" | custom-call | tf_op jit(solution)/shard_map/pallas_call | solution.py:1235
  665.0 0.0 copy-start
  665.0 0.0 copy-done.1
  665.0 1.1 copy.34
  666.1 0.7 copy-done
  666.8 1.1 copy.35
Async XLA Ops:
  7.2 74.1 %all-gather.9.cloned.1.call-start = ((), (), s32[]{:S(2)}) async-start(), calls=%async_computation | async-start | bytes 9437184 | tf_op jit(solution)/shard_map/all_gather | solution.py:1293
  9.5 2.8 copy-start.4
  9.5 3.6 copy-start.2
  9.5 4.2 copy-start.3
  9.5 302.9 %all-gather.11.cloned.1.call-start = ((), (), s32[]{:S(2)}) async-start(), calls=%async_computation.1 | async-start | bytes 9437184 | tf_op jit(solution)/shard_map/all_gather | solution.py:1301
  10.3 302.2 %all-gather.13.cloned.1.call-start = ((), (), s32[]{:S(2)}) async-start(), calls=%async_computation.2 | async-start | bytes 9437184 | tf_op jit(solution)/shard_map/all_gather | solution.py:1301
  11.0 301.4 %all-gather.15.cloned.1.call-start = ((), (), s32[]{:S(2)}) async-start(), calls=%async_computation.3 | async-start | bytes 9437184 | tf_op jit(solution)/shard_map/all_gather | solution.py:1301
  11.6 643.4 %all-gather.17.cloned.1.call-start = ((), (), s32[]{:S(2)}) async-start(), calls=%async_computation.4 | async-start | bytes 2359296 | tf_op jit(solution)/shard_map/all_gather | solution.py:1191
  524.6 131.9 %all-gather.19.cloned.1.call-start = ((), (), s32[]{:S(2)}) async-start(), calls=%async_computation.5 | async-start | bytes 1769472 | tf_op jit(solution)/shard_map/all_gather | solution.py:1191
  656.5 8.5 %copy-start.1 = (bf16[320,2048]{1,0:T(8,128)(2,1)S(1)}, bf16[320,2048]{1,0:T(8,128)(2,1)}, u32[]{:S(2)}) copy-start(bf16[320,2048]{1,0:T(8,128)(2,1)} %get-tuple-element.90) | copy-start | bytes 3932164
  665.0 1.8 copy-start
Sparse Core Ops, SparseCore 0:
  10.5 57.0 all-gather.8
  69.5 54.3 all-gather.10
  125.8 54.3 all-gather.12
  182.0 54.3 all-gather.14
  524.7 28.0 all-gather.16
  554.6 25.6 all-gather.18

commit v11 on v10

--- a/solution.py
+++ b/solution.py
@@ -255,31 +255,34 @@
     )
 
 
-def gather_norm_body(x_ref, gain_ref, buf, own, sem, send, recv):
+def gather_norm_body(chunks, x_ref, gain_ref, buf, own, sem, send, recv):
     place = lax.axis_index("tensor")
     greet(place)
     rows = x_ref[...].astype(f32)
     rms = lax.rsqrt(jnp.mean(rows * rows, axis=1, keepdims=True) + eps)
-    own[...] = (rows * rms * gain_ref[...]).astype(bf16)
-    gather = Gather(place, buf, send, recv, 1, own)
-    gather.send(1, 0)
+    own[...] = (rows * rms * gain_ref[...].astype(f32)).astype(bf16)
+    gather = Gather(place, buf, send, recv, chunks, own)
+    for chunk in range(chunks):
+        gather.send(1, chunk)
     (kept,) = fetch([(own, buf.at[place])], sem)
-    gather.arrive(1, 0)
-    gather.send(2, 0)
+    for chunk in range(chunks):
+        gather.arrive(1, chunk)
+        gather.send(2, chunk)
     kept.wait()
-    gather.arrive(2, 0)
+    for chunk in range(chunks):
+        gather.arrive(2, chunk)
     gather.drain(stop=LINE - 1)
 
 
-def gather_norm(x, gain):
+def gather_norm(x, gain, chunks=2):
     rows, features = x.shape
     return pl.pallas_call(
-        gather_norm_body,
+        functools.partial(gather_norm_body, chunks),
         in_specs=[IN_VMEM, IN_VMEM],
         out_specs=IN_HBM,
         out_shape=jax.ShapeDtypeStruct((LINE, rows, features), bf16),
         scratch_shapes=[pltpu.VMEM((rows, features), bf16), pltpu.SemaphoreType.DMA((1,))]
-        + line_sems(1),
+        + line_sems(chunks),
         compiler_params=comm_params(0),
     )(x, gain[None, :])
 
@@ -405,7 +408,7 @@
         value = midv[here] + tok_ref[here].astype(f32)
         midv[here] = value
         rms = lax.rsqrt(jnp.mean(value * value, axis=1, keepdims=True) + eps)
-        own[here] = (value * rms * gain_ref[...]).astype(bf16)
+        own[here] = (value * rms * gain_ref[...].astype(f32)).astype(bf16)
         stores.append(pltpu.make_async_copy(own.at[here], n_ref.at[place, here], nsem.at[chunk]))
         stores.append(pltpu.make_async_copy(midv.at[here], mid_ref.at[here], msem.at[chunk]))
         gather.send(1, chunk, least=1)
@@ -473,28 +476,67 @@
     )(x, weight, cot, entries, exits, *tables, leaf_parent, out_entry, finals, tokens, gain[None, :])
 
 
-def tokens_body(
-    chunks, d_ref, w_ref, a_ref, e_ref, x_ref, gain_ref, mid_ref, n_ref, lone_ref, final_ref, exit_ref,
-    middle_ref, own_ref, left_ref, right_ref,
-    out_ref, model_ref, head_ref, res_ref,
-    part, held, acc, dv, wv, midv, nv, terms, low, block, extra, wsem, send, recv, x_send, x_recv, t_send, t_recv, h_send, h_recv,
+class Trees:
+    def __init__(self, tree, ref, send, recv):
+        self.tree, self.ref, self.sems = tree, ref, (send, recv)
+        self.rounds = ref.shape[0].bit_length() - 1
+        self.partners = [self.partner(number) for number in range(self.rounds)]
+
+    def partner(self, number):
+        size = 1 << number
+        return self.tree + size - 2 * size * ((self.tree // size) % 2)
+
+    def copy(self, number, owner):
+        size = 1 << number
+        here = pl.ds((owner // size) * size, size)
+        return pltpu.make_async_remote_copy(
+            src_ref=self.ref.at[here],
+            dst_ref=self.ref.at[here],
+            send_sem=self.sems[0].at[number],
+            recv_sem=self.sems[1].at[number],
+            device_id={"dp": self.partner(number)},
+            device_id_type=MESH,
+        )
+
+    def send(self, number):
+        self.copy(number, self.tree).start()
+
+    def arrive(self, number):
+        self.copy(number, self.partner(number)).wait_recv()
+
+    def advance(self, number):
+        if number < self.rounds:
+            self.arrive(number - 1)
+            self.send(number)
+
+    def drain(self):
+        for number in range(self.rounds):
+            self.copy(number, self.tree).wait_send()
+
+
+def back_body(
+    chunks, seg,
+    q_ref, w_ref, n_ref, mid_ref, middle_ref, res_ref, right_ref, left_ref, x_ref,
+    o_ref, g_ref, lse_ref, p_ref, cos_ref, sin_ref, a_ref, e_ref, gain_ref, lone_ref, final_ref, exit_ref,
+    out_ref, model_ref, head_ref, sum_ref,
+    qv, dv, dq_t, dk_sum, dv_sum, part, held, acc, wv, midv, nv, terms, xv, outv, resv, model, head, low, block, extra,
+    qsem, wsem, osem, e_send, e_recv, send, recv, x_send, x_recv, t_send, t_recv, h_send, h_recv,
 ):
     place = lax.axis_index("tensor")
     tree = lax.axis_index("dp")
     trees = Trees(tree, model_ref, t_send, t_recv)
     heads = Trees(tree, head_ref, h_send, h_recv)
-    groups, total, width = d_ref.shape
+    groups, total, width = q_ref.shape
     rank = a_ref.shape[1]
+    (load_q,) = fetch([(q_ref, qv)], qsem)
     loads = fetch(
         [
-            (d_ref, dv),
             (w_ref.at[:, : groups * width], wv),
             (n_ref, nv),
             (mid_ref, midv),
             (middle_ref, acc),
-            (own_ref.at[place], terms.at[0]),
-            (left_ref, terms.at[1]),
-            (right_ref, terms.at[2]),
+            (res_ref.at[place], terms.at[0]),
+            (x_ref, xv),
         ],
         wsem,
     )
@@ -502,8 +544,32 @@
     for g in range(groups):
         block[g * rank : (g + 1) * rank, g * width : (g + 1) * width] = a_ref[g]
     greet(place, trees.partners)
-    for load in loads[:2]:
-        load.wait()
+
+    def exchange(side, target):
+        index = 0 if side == 1 else 1
+        return pltpu.make_async_remote_copy(
+            src_ref=(right_ref, left_ref)[index],
+            dst_ref=terms.at[index + 1],
+            send_sem=e_send.at[index],
+            recv_sem=e_recv.at[index],
+            device_id={"tensor": target},
+            device_id_type=MESH,
+        )
+
+    for side in SIDES:
+        pl.when(far_of(place, side) < LINE - 1)(exchange(side, place + side).start)
+    load_q.wait()
+    pair = 2 * HEAD_DIM
+
+    def one_pair(j, carry):
+        lanes = pl.ds(pl.multiple_of(j * pair, pair), pair)
+        attend_back_pair(
+            seg, qv, lanes, o_ref, g_ref, lse_ref, j, p_ref[...], cos_ref, sin_ref, dv, dq_t, dk_sum, dv_sum
+        )
+        return carry
+
+    lax.fori_loop(0, width // pair, one_pair, 0)
+    loads[0].wait()
     rows = part.shape[1]
     summed = Sum(place, part, held, send, recv, chunks)
     gather = Gather(place, extra, x_send, x_recv, 1)
@@ -528,7 +594,7 @@
     summed.begin(1, 1)
     for slot in (2, 1, 0):
         lower(slot)
-    for load in loads[2:]:
+    for load in loads[1:]:
         load.wait()
 
     def turned(value):
@@ -552,33 +618,51 @@
     low_one = turned(lone_ref[...])
     for g in range(groups):
         band = slice(g * rank, (g + 1) * rank)
-        head_ref[tree, band] = nn(low_one[band], dv[g]).astype(bf16)
-    head_ref[tree, groups * rank :] = exit_ref[...].astype(bf16)
+        head[band] = nn(low_one[band], dv[g]).astype(bf16)
+    head[groups * rank :] = exit_ref[...].astype(bf16)
+    (store,) = fetch([(head, head_ref.at[tree])], osem)
+    summed.relay(2, 3)
+    store.wait()
     heads.send(0)
-    value = acc[...] + terms[0].astype(f32)
-    for index, side in enumerate(SIDES):
-        value += jnp.where(far_of(place, side) > 0, terms[index + 1].astype(f32), 0.0)
-    res_ref[...] = value.astype(bf16)
-    summed.relay(2, 3)
     gather.arrive(2, 0)
     gather.send(3, 0)
     heads.advance(1)
     summed.relay(3, 0)
     gather.arrive(3, 0)
-    model_ref[tree] = functools.reduce(
+    model[...] = functools.reduce(
         jnp.add, [extra[shard].astype(f32) for shard in range(LINE)]
     ).astype(bf16)
+    (store,) = fetch([(model, model_ref.at[tree])], osem)
+    for side in SIDES:
+        pl.when(far_of(place, side) > 0)(exchange(side, place - side).wait_recv)
+    value = acc[...] + terms[0].astype(f32)
+    for index, side in enumerate(SIDES):
+        value += jnp.where(far_of(place, side) > 0, terms[index + 1].astype(f32), 0.0)
+    resv[...] = value.astype(bf16)
+    store.wait()
     trees.send(0)
+    (store,) = fetch([(resv, sum_ref)], osem)
     heads.advance(2)
     summed.relay(3, 1)
     trees.advance(1)
     summed.relay(3, 2)
     summed.relay(3, 3)
     trees.advance(2)
+    store.wait()
     size = rows // chunks
+    stores = []
 
     def finish(chunk):
-        finish_tokens(summed, chunk, size, acc, x_ref, gain_ref, midv, out_ref)
+        summed.total(chunk, acc)
+        here = chunk_rows(chunk, size)
+        values = xv[here].astype(f32)
+        rms = lax.rsqrt(jnp.mean(values * values, axis=1, keepdims=True) + eps)
+        scaled = acc[here] * gain_ref[...].astype(f32)
+        mean = jnp.mean(scaled * values, axis=1, keepdims=True)
+        outv[here] = (midv[here] + rms * (scaled - values * (rms * rms) * mean)).astype(bf16)
+        copy = pltpu.make_async_copy(outv.at[here], out_ref.at[here], wsem.at[chunk])
+        copy.start()
+        stores.append(copy)
 
     finish(0)
     finish(1)
@@ -590,73 +674,31 @@
     for blocks in (trees, heads):
         blocks.arrive(blocks.rounds - 1)
         blocks.drain()
+    for copy in stores:
+        copy.wait()
+    for side in SIDES:
+        pl.when(far_of(place, side) < LINE - 1)(exchange(side, place + side).wait_send)
     summed.drain()
     gather.drain()
 
 
-class Trees:
-    def __init__(self, tree, ref, send, recv):
-        self.tree, self.ref, self.sems = tree, ref, (send, recv)
-        self.rounds = ref.shape[0].bit_length() - 1
-        self.partners = [self.partner(number) for number in range(self.rounds)]
-
-    def partner(self, number):
-        size = 1 << number
-        return self.tree + size - 2 * size * ((self.tree // size) % 2)
-
-    def copy(self, number, owner):
-        size = 1 << number
-        here = pl.ds((owner // size) * size, size)
-        return pltpu.make_async_remote_copy(
-            src_ref=self.ref.at[here],
-            dst_ref=self.ref.at[here],
-            send_sem=self.sems[0].at[number],
-            recv_sem=self.sems[1].at[number],
-            device_id={"dp": self.partner(number)},
-            device_id_type=MESH,
-        )
-
-    def send(self, number):
-        self.copy(number, self.tree).start()
-
-    def arrive(self, number):
-        self.copy(number, self.partner(number)).wait_recv()
-
-    def advance(self, number):
-        if number < self.rounds:
-            self.arrive(number - 1)
-            self.send(number)
-
-    def drain(self):
-        for number in range(self.rounds):
-            self.copy(number, self.tree).wait_send()
-
-
-def finish_tokens(summed, chunk, size, acc, x_ref, gain_ref, mid_ref, out_ref):
-    summed.total(chunk, acc)
-    here = chunk_rows(chunk, size)
-    rows = x_ref[here].astype(f32)
-    rms = lax.rsqrt(jnp.mean(rows * rows, axis=1, keepdims=True) + eps)
-    scaled = acc[here] * gain_ref[...]
-    mean = jnp.mean(scaled * rows, axis=1, keepdims=True)
-    out_ref[here] = (mid_ref[here] + rms * (scaled - rows * (rms * rms) * mean)).astype(bf16)
-
-
-def tokens_back(
-    head_grads, weight, exits, entries, x, gain, grad_middle, normed, low_one, final_grads, exit_grads,
-    middle, own, from_left, from_right,
+def back(
+    qkv, weight, normed, grad_middle, middle, res_parts, right, left, x, attended, grad, lse, leaf_parent, tables, exits,
+    entries, gain, low_one, final_grads, exit_grads, seg,
 ):
     chunks = LINE
     rows, features = x.shape
-    groups, total, width = head_grads.shape
+    groups, total, width = qkv.shape
     rank = exits.shape[1]
     deep = (groups + 1) * rank
+    pair = 2 * HEAD_DIM
     trees = lax.axis_size("dp")
     sems = pltpu.SemaphoreType.DMA((trees.bit_length() - 1,))
+    two = pltpu.SemaphoreType.DMA((2,))
     return pl.pallas_call(
-        functools.partial(tokens_body, chunks),
-        in_specs=[IN_HBM, IN_HBM] + [IN_VMEM] * 4 + [IN_HBM] * 2 + [IN_VMEM] * 3 + [IN_HBM] * 4,
-        out_specs=[IN_VMEM] * 4,
+        functools.partial(back_body, chunks, seg),
+        in_specs=[IN_HBM] * 9 + [IN_VMEM] * 12,
+        out_specs=[IN_HBM] * 4,
         out_shape=[
             jax.ShapeDtypeStruct((rows, features), bf16),
             jax.ShapeDtypeStruct((trees, deep, features), bf16),
@@ -664,26 +706,39 @@
             jax.ShapeDtypeStruct((rows, features), bf16),
         ],
         scratch_shapes=[
+            pltpu.VMEM((groups, total, width), bf16),
+            pltpu.VMEM((groups, total, width), bf16),
+            pltpu.VMEM((pair, total), f32),
+            pltpu.VMEM((total, pair), f32),
+            pltpu.VMEM((total, pair), f32),
             pltpu.VMEM((LINE, rows, features), bf16),
             pltpu.VMEM((2, LINE - 1, rows, features), bf16),
             pltpu.VMEM((rows, features), f32),
-            pltpu.VMEM((groups, total, width), bf16),
             pltpu.VMEM((features, groups * width), bf16),
             pltpu.VMEM((rows, features), f32),
             pltpu.VMEM((LINE, rows, features), bf16),
             pltpu.VMEM((3, rows, features), bf16),
+            pltpu.VMEM((rows, features), bf16),
+            pltpu.VMEM((rows, features), bf16),
+            pltpu.VMEM((rows, features), bf16),
+            pltpu.VMEM((deep, features), bf16),
+            pltpu.VMEM((deep, width), bf16),
             pltpu.VMEM((total, groups * rank), bf16),
             pltpu.VMEM((groups * rank, groups * width), bf16),
             pltpu.VMEM((LINE, deep, features), bf16),
-            pltpu.SemaphoreType.DMA((8,)),
+            pltpu.SemaphoreType.DMA((1,)),
+            pltpu.SemaphoreType.DMA((6,)),
+            pltpu.SemaphoreType.DMA((1,)),
+            two,
+            two,
         ]
         + line_sems(chunks)
         + line_sems(1)
         + [sems] * 4,
         compiler_params=comm_params(3),
     )(
-        head_grads, weight, exits, entries, x, gain[None, :], grad_middle, normed,
-        low_one, final_grads, exit_grads, middle, own, from_left, from_right,
+        qkv, weight, normed, grad_middle, middle, res_parts, right, left, x, attended, grad[0], lse, leaf_parent, *tables,
+        exits, entries, gain[None, :], low_one, final_grads, exit_grads,
     )
 
 
@@ -737,102 +792,41 @@
         o_ref[start : start + QT, lanes] = jnp.concatenate(outs, axis=0).T.astype(bf16)
 
 
-def attend_back_body(
-    seg, q_ref, k_ref, v_ref, o_ref, g_ref, lse_ref, p_ref, cos_ref, sin_ref, right_ref, left_ref,
-    d_ref, from_left_ref, from_right_ref, dq_t, dk, dv, send, recv,
+def attend_back_pair(
+    seg, qkv_ref, lanes, o_ref, g_ref, lse_ref, pair, parent_row, cos_ref, sin_ref, d_ref, dq_t, dk, dv
 ):
-    place = lax.axis_index("tensor")
-
-    def exchange(side, target):
-        index = 0 if side == 1 else 1
-        return pltpu.make_async_remote_copy(
-            src_ref=(right_ref, left_ref)[index],
-            dst_ref=(from_left_ref, from_right_ref)[index],
-            send_sem=send.at[index],
-            recv_sem=recv.at[index],
-            device_id={"tensor": target},
-            device_id_type=MESH,
-        )
-
-    @pl.when(pl.program_id(0) == 0)
-    def _():
-        greet(place)
-        for side in SIDES:
-            pl.when(far_of(place, side) < LINE - 1)(exchange(side, place + side).start)
-
-    rows = q_ref.shape[1]
+    rows = qkv_ref.shape[1]
     scale = bf16(HEAD_DIM**-0.5)
-    key_t = k_ref[0].T
-    weighed_t = (g_ref[0].astype(f32) * o_ref[...].astype(f32)).T
+    key_t = qkv_ref[1, :, lanes].T
+    weighed_t = (g_ref[:, lanes].astype(f32) * o_ref[:, lanes].astype(f32)).T
     lane = lax.broadcasted_iota(jnp.int32, (QT, 2 * HEAD_DIM), 1)
     dk[...] = jnp.zeros_like(dk)
     dv[...] = jnp.zeros_like(dv)
-    for start, pieces in tree_tiles(seg, rows, p_ref[...]):
-        query = q_ref[0, start : start + QT] * scale
-        grad = g_ref[0, start : start + QT]
+    for start, pieces in tree_tiles(seg, rows, parent_row):
+        query = qkv_ref[0, start : start + QT, lanes] * scale
+        grad = g_ref[start : start + QT, lanes]
         for h in range(2):
             mine = lane // HEAD_DIM == h
             own_query = jnp.where(mine, query, bf16(0))
             own_grad = jnp.where(mine, grad, bf16(0))
             band = slice(h * HEAD_DIM, (h + 1) * HEAD_DIM)
             delta = jnp.sum(weighed_t[band, start : start + QT], axis=0, keepdims=True)
-            lse = lse_ref[0, h : h + 1, start : start + QT]
+            lse = lse_ref[pair, h : h + 1, start : start + QT]
             grad_q = 0.0
             for k0, count, mask in pieces:
-                probs = jnp.exp(nt(k_ref[0, k0 : k0 + count], own_query) - lse)
+                probs = jnp.exp(nt(qkv_ref[1, k0 : k0 + count, lanes], own_query) - lse)
                 if mask is not None:
                     probs = jnp.where(mask, probs, 0.0)
-                grad_probs = nt(v_ref[0, k0 : k0 + count], own_grad)
+                grad_probs = nt(qkv_ref[2, k0 : k0 + count, lanes], own_grad)
                 grad_scores = (probs * (grad_probs - delta)).astype(bf16)
                 dk[k0 : k0 + count] += nn(grad_scores, own_query)
                 dv[k0 : k0 + count] += nn(probs.astype(bf16), own_grad)
                 grad_q += nn(key_t[band, k0 : k0 + count], grad_scores)
             dq_t[band, start : start + QT] = grad_q
     cosine, sine = cos_ref[...], -sin_ref[...]
-    d_ref[0] = turn(dq_t[...].T * HEAD_DIM**-0.5, cosine, sine).astype(bf16)
-    d_ref[1] = turn(dk[...], cosine, sine).astype(bf16)
-    d_ref[2] = dv[...].astype(bf16)
-
-    @pl.when(pl.program_id(0) == pl.num_programs(0) - 1)
-    def _():
-        for side in SIDES:
-            pl.when(far_of(place, side) < LINE - 1)(exchange(side, place + side).wait_send)
-            pl.when(far_of(place, side) > 0)(exchange(side, place - side).wait_recv)
-
-
-def attend_back(qkv, attended, grad, lse, leaf_parent, tables, seg, right, left):
-    _, rows, width = qkv.shape
-    pairs = width // (2 * HEAD_DIM)
-    pair = 2 * HEAD_DIM
-    return pl.pallas_call(
-        functools.partial(attend_back_body, seg),
-        grid=(pairs,),
-        in_specs=[pl.BlockSpec((1, rows, pair), lambda j, g=g: (g, 0, j)) for g in range(3)]
-        + [
-            pl.BlockSpec((rows, pair), lambda j: (0, j)),
-            pl.BlockSpec((1, rows, pair), lambda j: (0, 0, j)),
-            pl.BlockSpec((1, 2, rows), lambda j: (j, 0, 0)),
-            pl.BlockSpec(leaf_parent.shape, lambda j: (0, 0)),
-            pl.BlockSpec((rows, pair), lambda j: (0, 0)),
-            pl.BlockSpec((rows, pair), lambda j: (0, 0)),
-            IN_HBM,
-            IN_HBM,
-        ],
-        out_specs=[pl.BlockSpec((3, rows, pair), lambda j: (0, 0, j)), IN_HBM, IN_HBM],
-        out_shape=[
-            jax.ShapeDtypeStruct((3, rows, width), bf16),
-            jax.ShapeDtypeStruct(right.shape, bf16),
-            jax.ShapeDtypeStruct(left.shape, bf16),
-        ],
-        scratch_shapes=[
-            pltpu.VMEM((pair, rows), f32),
-            pltpu.VMEM((rows, pair), f32),
-            pltpu.VMEM((rows, pair), f32),
-            pltpu.SemaphoreType.DMA((2,)),
-            pltpu.SemaphoreType.DMA((2,)),
-        ],
-        compiler_params=comm_params(4),
-    )(qkv, qkv, qkv, attended, grad, lse, leaf_parent, *tables, right, left)
+    d_ref[0, :, lanes] = turn(dq_t[...].T * HEAD_DIM**-0.5, cosine, sine).astype(bf16)
+    d_ref[1, :, lanes] = turn(dk[...], cosine, sine).astype(bf16)
+    d_ref[2, :, lanes] = dv[...].astype(bf16)
 
 
 def feed_body(
@@ -965,7 +959,7 @@
         here = chunk_rows(chunk, size)
         middle = midv[here]
         rms = lax.rsqrt(jnp.mean(middle * middle, axis=1, keepdims=True) + eps)
-        scaled = acc_back[here] * gain_ref[...]
+        scaled = acc_back[here] * gain_ref[...].astype(f32)
         mean = jnp.mean(scaled * middle, axis=1, keepdims=True)
         grad = cbuf[last, here].astype(f32) + rms * (scaled - middle * (rms * rms) * mean)
         own[here] = grad.astype(bf16)
@@ -1191,7 +1185,12 @@
     return lax.all_gather(block, "dp", axis=0, tiled=False)
 
 
-def combine_body(rank, pick_ref, early, model, late, head, entry_ref, final_ref, unit_ref, down_ref, exit_ref, out_ref):
+def combine_body(
+    rank, pick_ref, early, model, late, head, one, two, entry_ref, final_ref, unit_ref, down_ref, exit_ref, out_ref,
+    one_ref, two_ref,
+):
+    one_ref[...] = one[...]
+    two_ref[...] = two[...]
     for ref in (entry_ref, final_ref, unit_ref, down_ref, exit_ref, out_ref):
         ref[...] = jnp.zeros_like(ref)
 
@@ -1216,7 +1215,7 @@
     lax.fori_loop(0, early.shape[0], one_tree, 0)
 
 
-def combine(picks, early, model, late, head, adapters, steps=4):
+def combine(picks, early, model, late, head, one, two, adapters, steps=4):
     trees, _, features = early.shape
     rank = late.shape[1] // 4
     width = head.shape[2]
@@ -1228,6 +1227,8 @@
     def given(lead, tile):
         shape = lead + (adapters, rank, tile)
         return pl.BlockSpec(shape, lambda i, p: (0,) * (len(shape) - 1) + (i,))
+
+    whole = pl.BlockSpec((one.shape[0] // steps, one.shape[1]), lambda i, p: (i, 0))
 
     def shape(lead, full):
         return jax.ShapeDtypeStruct(lead + (adapters, rank, full), f32)
@@ -1237,7 +1238,7 @@
         grid_spec=pltpu.PrefetchScalarGridSpec(
             num_scalar_prefetch=1,
             grid=(steps,),
-            in_specs=[taken(early, wide), taken(model, wide), taken(late, wide), taken(head, narrow)],
+            in_specs=[taken(early, wide), taken(model, wide), taken(late, wide), taken(head, narrow), whole, whole],
             out_specs=[
                 given((5,), wide),
                 given((2,), wide),
@@ -1245,6 +1246,8 @@
                 given((), wide),
                 given((3,), narrow),
                 given((), narrow),
+                whole,
+                whole,
             ],
         ),
         out_shape=[
@@ -1254,9 +1257,11 @@
             shape((), features),
             shape((3,), width),
             shape((), width),
+            jax.ShapeDtypeStruct(one.shape, bf16),
+            jax.ShapeDtypeStruct(two.shape, bf16),
         ],
         compiler_params=pltpu.CompilerParams(vmem_limit_bytes=VMEM_LIMIT),
-    )(picks, early, model, late, head)
+    )(picks, early, model, late, head, one, two)
 
 
 def local(
@@ -1287,8 +1292,7 @@
     seg = total // blocks
     tables = rope_tables(blocks, seg)
     leaf_parent = (jnp.repeat(parents[0, TRUNK + BRANCHES :], seg) - TRUNK)[None, :]
-    gain_one = attention_gain.astype(f32)
-    gain_two = feed_gain.astype(f32)
+    gain_one, gain_two = attention_gain, feed_gain
 
     w_heads = lax.all_gather(
         jnp.concatenate([query_weight, key_weight, value_weight, output_weight], axis=1),
@@ -1327,17 +1331,14 @@
     early = per_tree(early)
     model_all = per_tree(model_sum)
 
-    head_grads, from_left, from_right = attend_back(
-        qkv, attended, grad_attended, lse, leaf_parent, tables, seg, res_right, res_left
-    )
-    grad_tokens, late_model, late_head, result = tokens_back(
-        head_grads, w_heads, heads_exit, entries, tokens, gain_one, grad_middle,
-        full_one, low_one, final_grads, exit_grads, middle, res_parts, from_left, from_right,
+    grad_tokens, late_model, late_head, result = back(
+        qkv, w_heads, full_one, grad_middle, middle, res_parts, res_right, res_left, tokens, attended, grad_attended, lse,
+        leaf_parent, tables, heads_exit, entries, gain_one, low_one, final_grads, exit_grads, seg,
     )
 
     picks = early[:, 3 * rank, 0].astype(jnp.int32)
-    grad_entries, grad_finals, grad_units, grad_down, grad_heads, grad_output = combine(
-        picks, early, model_all, late_model, late_head, adapters
+    grad_entries, grad_finals, grad_units, grad_down, grad_heads, grad_output, result, grad_tokens = combine(
+        picks, early, model_all, late_model, late_head, result, grad_tokens, adapters
     )
     grad_entries = grad_entries.swapaxes(2, 3)
     grad_output = grad_output.swapaxes(1, 2)

time: 684 us -> 680 us (level)
    pallas_call x3 -> x2, Pallas kernels: 195 us -> 189 us  [the longest x1 126 us: back(): pl.pallas_call(functools.partial(back_body, chunks, seg), in_specs=[IN_HB...]
where the time goes in v11:
time: 680 us; the launch traced here: 669 us
  Pallas kernels  645 us (95%)
  between operations  15.3 us (2%)
    pallas_call x1, Pallas kernels, front(): pl.pallas_call(functools.partial(front_body, chunks, seg), in_specs=[IN_H...  232 us
    pallas_call x1, Pallas kernels, feed(): pl.pallas_call(functools.partial(feed_body, rank, tile, chunks), in_specs...  213 us
    pallas_call x1, Pallas kernels, back(): pl.pallas_call(functools.partial(back_body, chunks, seg), in_specs=[IN_HB...  126 us
    pallas_call x1, Pallas kernels, gather_norm(): pl.pallas_call(functools.partial(gather_norm_body, chunks), in_specs=[IN_...  63.3 us
  transfers between devices with their start and end apart: 6, of which 0 were waited for; matrix products, arithmetic and copies ran while one was open for 1% of the time, Pallas kernels for 63%

profile of v11, /device:TPU:0, one launch (start us, length us, event | category | flops | bytes accessed | tf_op | source)
XLA Modules:
  0.0 669.2 jit_solution(8312696795484238940)
XLA Ops:
  7.2 0.0 all-gather.9.cloned.1.call-start
  7.2 2.3 pad_maximum_fusion
  9.5 0.0 copy-start.2
  9.5 0.0 copy-start
  9.5 0.0 copy-start.1
  9.5 0.0 all-gather.9.cloned.1.call-update
  9.5 0.0 all-gather.11.cloned.1.call-start
  9.6 0.7 all-gather.11.cloned.1.call-update
  10.3 0.0 all-gather.13.cloned.1.call-start
  10.3 0.7 all-gather.13.cloned.1.call-update
  11.0 0.0 all-gather.15.cloned.1.call-start
  11.1 0.5 all-gather.15.cloned.1.call-update
  11.6 0.0 all-gather.17.cloned.1.call-start
  12.3 0.0 copy-done.2
  12.3 0.1 add_bitcast_fusion
  12.4 0.1 broadcast_in_dim.24
  12.4 0.6 sub.10.p_ref
  13.1 0.0 copy-done
  13.1 0.6 broadcast_in_dim.21.gain_ref
  13.7 0.0 copy-done.1
  13.7 0.6 broadcast_in_dim.25.gain_ref
  14.3 63.3 %shard_map.260.x_ref = bf16[4,320,2048]{2,1,0:T(8,128)(2,1)} custom-call(bf16[320,2048]{1,0:T(8,128)(2,1)} %x_ref.3, bf16[1,2048]{1,0:T(2,128)(2,1)} %broadcast_in_dim.21.gain_ref), custom_call_target="tpu_custom_call" | custom-call | tf_op jit(solution)/shard_map/pallas_call | solution.py:279
  77.6 2.0 shard_map.261
  79.6 0.0 all-gather.9.cloned.1.call-done.w_ref.wo_ref
  79.6 231.7 %shard_map.262 = (bf16[4,320,2048]{2,1,0:T(8,128)(2,1)}, bf16[3,1280,512]{2,1,0:T(8,128)(2,1)}, f32[320,2048]{1,0:T(8,128)}, bf16[4,320,2048]{2,1,0:T(8,128)(2,1...) custom-call(bf16[4,320,2048]{2,1,0:T(8,128)(2,1)} %shard_map.260.x_r, ...), custom_call_target="tpu_custom_call", output_to_operand_aliasing={{0}: (0, {})} | custom-call | tf_op jit(solution)/shard_map/pallas_call | solution.py:439
  311.4 0.0 all-gather.11.cloned.1.call-done.wg_ref
  311.4 0.0 all-gather.13.cloned.1.call-done.wu_ref
  311.5 0.0 all-gather.15.cloned.1.call-done.wd_ref
  311.5 213.0 %shard_map.263 = (f32[320,2048]{1,0:T(8,128)}, bf16[4,320,2048]{2,1,0:T(8,128)(2,1)}, bf16[320,2048]{1,0:T(8,128)(2,1)}, bf16[320,2048]{1,0:T(8,128)(2,1)}, bf16...) custom-call(bf16[4,320,2048]{2,1,0:T(8,128)(2,1)} %get-tuple-element, ...), custom_call_target="tpu_custom_call" | custom-call | tf_op jit(solution)/shard_map/pallas_call | solution.py:1107
  524.5 0.0 all-gather.17.cloned.1.call-update
  524.5 0.0 all-gather.19.cloned.1.call-start
  524.5 0.5 all-gather.19.cloned.1.call-update
  525.1 125.5 %shard_map.264 = (bf16[320,2048]{1,0:T(8,128)(2,1)}, bf16[8,64,2048]{2,1,0:T(8,128)(2,1)}, bf16[8,64,512]{2,1,0:T(8,128)(2,1)}, bf16[320,2048]{1,0:T(8,128)(2,1)}) custom-call(bf16[3,1280,512]{2,1,0:T(8,128)(2,1)} %get-tuple-element.57.q_ref, bf16[2048,2048]{1,0:T(8,128)(2,1)} %all-gather.9.cloned.1.call-done.w_ref.wo_ref, ...), custom_call_target="tpu_custom_call" | custom-call | tf_op jit(solution)/shard_map/pallas_call | solution.py:698
  650.6 0.0 all-gather.17.cloned.1.call-done
  650.6 1.5 fusion.pick_ref
  652.2 0.0 all-gather.19.cloned.1.call-done
  652.2 9.8 %shard_map.265 = (f32[5,8,16,2048]{3,2,1,0:T(8,128)}, f32[2,8,16,2048]{3,2,1,0:T(8,128)}, f32[2,8,16,2048]{3,2,1,0:T(8,128)}, f32[8,16,2048]{2,1,0:T(8,128)}, f3...) custom-call(s32[8]{0:T(128)} %fusion.pick_ref, ...), custom_call_target="tpu_custom_call" | custom-call | tf_op jit(solution)/shard_map/pallas_call | solution.py:1236
Async XLA Ops:
  7.2 72.5 %all-gather.9.cloned.1.call-start = ((), (), s32[]{:S(2)}) async-start(), calls=%async_computation | async-start | bytes 9437184 | tf_op jit(solution)/shard_map/all_gather | solution.py:1297
  9.5 2.8 copy-start.2
  9.5 3.6 copy-start
  9.5 4.2 copy-start.1
  9.5 301.9 %all-gather.11.cloned.1.call-start = ((), (), s32[]{:S(2)}) async-start(), calls=%async_computation.1 | async-start | bytes 9437184 | tf_op jit(solution)/shard_map/all_gather | solution.py:1305
  10.3 301.2 %all-gather.13.cloned.1.call-start = ((), (), s32[]{:S(2)}) async-start(), calls=%async_computation.2 | async-start | bytes 9437184 | tf_op jit(solution)/shard_map/all_gather | solution.py:1305
  11.0 300.5 %all-gather.15.cloned.1.call-start = ((), (), s32[]{:S(2)}) async-start(), calls=%async_computation.3 | async-start | bytes 9437184 | tf_op jit(solution)/shard_map/all_gather | solution.py:1305
  11.6 639.0 %all-gather.17.cloned.1.call-start = ((), (), s32[]{:S(2)}) async-start(), calls=%async_computation.4 | async-start | bytes 2359296 | tf_op jit(solution)/shard_map/all_gather | solution.py:1185
  524.5 127.7 %all-gather.19.cloned.1.call-start = ((), (), s32[]{:S(2)}) async-start(), calls=%async_computation.5 | async-start | bytes 1769472 | tf_op jit(solution)/shard_map/all_gather | solution.py:1185
Sparse Core Ops, SparseCore 0:
  10.5 57.0 all-gather.8
  69.5 54.3 all-gather.10
  125.8 54.4 all-gather.12
  182.0 54.3 all-gather.14
  524.6 29.4 all-gather.16
  555.8 25.7 all-gather.18

commit v12 on v11

--- a/solution.py
+++ b/solution.py
@@ -94,10 +94,10 @@
 
 
 class Gather:
-    def __init__(self, place, buf, send, recv, chunks, own=None):
+    def __init__(self, place, buf, send, recv, chunks, own=None, second=None):
         self.place, self.buf, self.sems, self.chunks = place, buf, (send, recv), chunks
         self.rows = buf.shape[1] // chunks
-        self.own = own
+        self.own, self.second = own, second
 
     def copy(self, side, step, chunk, shard, target):
         rows = chunk_rows(chunk, self.rows)
@@ -107,6 +107,8 @@
         source = where
         if step == 1 and self.own is not None:
             source = self.own.at[rows]
+        if step == 2 and self.second is not None:
+            source = self.second.at[shard, rows]
         return pltpu.make_async_remote_copy(
             src_ref=source,
             dst_ref=where,
@@ -136,11 +138,11 @@
                 shard = self.place - side * step
                 self.copy(side, step, chunk, shard, self.place - side).wait_recv()
 
-    def relay(self, step, chunk):
+    def relay(self, step, chunk, least=0, most=LINE):
         for side in SIDES:
             far = far_of(self.place, side)
 
-            @pl.when((far < LINE - 1) & (far >= step - 1))
+            @pl.when((far < LINE - 1) & (far >= step - 1) & (far >= least) & (far <= most))
             def _():
                 before = self.place - side * (step - 1)
                 self.copy(side, step - 1, chunk, before, self.place - side).wait_recv()
@@ -155,6 +157,14 @@
                     for chunk in range(self.chunks):
                         shard = self.place - side * step
                         self.copy(side, step, chunk, shard, self.place - side).wait_recv()
+
+    def end_got(self, step):
+        for side in SIDES:
+
+            @pl.when(far_of(self.place, side) == LINE - 1)
+            def _():
+                for chunk in range(self.chunks):
+                    self.copy(side, step, chunk, self.place - side * step, self.place - side).wait_recv()
 
     def drain(self, stop=LINE, start=1):
         for step in range(start, stop):
@@ -232,6 +242,61 @@
                     @pl.when(far <= step - 1)
                     def _():
                         self.copy(side, step, chunk, shard, self.place + side).wait_send()
+
+
+class Near:
+    def __init__(self, place, part, held, send, recv, chunks):
+        self.place, self.part, self.held = place, part, held
+        self.sems, self.chunks = (send, recv), chunks
+        self.rows = part.shape[1] // chunks
+
+    def copy(self, side, away, chunk, shard, target):
+        rows = chunk_rows(chunk, self.rows)
+        index = 0 if side == 1 else 1
+        spot = (index, away - 1, chunk)
+        return pltpu.make_async_remote_copy(
+            src_ref=self.part.at[shard, rows],
+            dst_ref=self.held.at[index, away - 1, rows],
+            send_sem=self.sems[0].at[spot],
+            recv_sem=self.sems[1].at[spot],
+            device_id={"tensor": target},
+            device_id_type=MESH,
+        )
+
+    def send(self, away, chunk, number):
+        rows = chunk_rows(chunk, self.rows)
+        for index, side in enumerate(SIDES):
+            shard = self.place + side * away
+
+            @pl.when(far_of(self.place, side) == number)
+            def _():
+                if number:
+                    self.copy(side, away + 1, chunk, self.place, self.place - side).wait_recv()
+                    self.part[shard, rows] = (
+                        self.part[shard, rows].astype(f32) + self.held[index, away, rows].astype(f32)
+                    ).astype(bf16)
+                self.copy(side, away, chunk, shard, self.place + side).start()
+
+    def total(self, chunk, out):
+        rows = chunk_rows(chunk, self.rows)
+        out[rows] = self.part[self.place, rows].astype(f32)
+        for index, side in enumerate(SIDES):
+
+            @pl.when(far_of(self.place, side) >= 1)
+            def _():
+                self.copy(side, 1, chunk, self.place, self.place - side).wait_recv()
+                out[rows] += self.held[index, 0, rows].astype(f32)
+
+    def drain(self):
+        for number in range(LINE - 1):
+            for away in range(1, LINE - number):
+                for chunk in range(self.chunks):
+                    for side in SIDES:
+
+                        @pl.when(far_of(self.place, side) == number)
+                        def _():
+                            shard = self.place + side * away
+                            self.copy(side, away, chunk, shard, self.place + side).wait_send()
 
 
 def line_sems(chunks):
@@ -373,12 +438,6 @@
     def one_pair(j, carry):
         lanes = pl.ds(pl.multiple_of(j * pair, pair), pair)
         attend_pair(seg, yv, lanes, p_ref[...], j, att_ref, lse_ref)
-
-        @pl.when(j == 0)
-        def _():
-            for chunk in range(chunks):
-                cots.relay(2, chunk)
-
         return carry
 
     lax.fori_loop(0, width // pair, one_pair, 0)
@@ -402,7 +461,6 @@
     for chunk in range(chunks):
         summed.relay(2, chunk)
         summed.relay(3, chunk)
-        cots.relay(3, chunk)
         summed.total(chunk, midv)
         here = chunk_rows(chunk, size)
         value = midv[here] + tok_ref[here].astype(f32)
@@ -414,12 +472,18 @@
         gather.send(1, chunk, least=1)
         for store in stores[-2:]:
             store.start()
+        if chunk:
+            gather.relay(2, chunk - 1, least=2)
     for chunk in range(chunks):
         gather.send(1, chunk, most=0)
-    for step in (2, 3):
-        for chunk in range(chunks):
-            gather.relay(step, chunk)
-    cots.close()
+    gather.relay(2, chunks - 1, least=2)
+    for chunk in range(chunks):
+        gather.relay(2, chunk, most=1)
+        if chunk:
+            gather.relay(3, chunk - 1)
+    gather.relay(3, chunks - 1)
+    for chunk in range(chunks):
+        cots.arrive(1, chunk)
     gather.close()
     pl.when(edge)(kept.wait)
     for out in outs + stores:
@@ -428,7 +492,7 @@
         pl.when(far_of(place, side) == LINE - 2)(passed(side).wait_send)
     summed.drain()
     gather.drain()
-    cots.drain()
+    cots.drain(stop=2)
 
 
 def front(x, weight, cot, entries, exits, tables, leaf_parent, out_entry, finals, tokens, gain, seg, chunks=4):
@@ -831,31 +895,35 @@
 
 def feed_body(
     rank, tile, chunks,
-    n_ref, c_ref, far_ref, wg_ref, wu_ref, wd_ref, mid_ref, wo_ref,
+    n_ref, c_ref, near_ref, wg_ref, wu_ref, wd_ref, mid_ref, wo_ref,
     pick_ref, xu_in, xd_in, e_in, f_in, gain_ref, oe_ref, att_ref, lo_ref,
-    grad_ref, res_ref, right_ref, left_ref, b_ref, held_ref, unit_out, model_out, y_ref, final_ref, exit_ref,
+    grad_ref, res_ref, right_ref, left_ref, b_ref, held_ref, far_ref, unit_out, model_out, y_ref, final_ref, exit_ref,
     unit_ref, model_ref, x_ref, e_ref, f_ref, midv, nbuf, cbuf, wbuf, low, low_t, acc_res, acc_back, acc_low,
     part, held, resv, own, extra, wo, nsem, csem, wsem, rsem, msem,
-    send, recv, g_send, g_recv, x_send, x_recv, r_send, r_recv,
+    send, recv, g_send, g_recv, x_send, x_recv, c_send, c_recv, r_send, r_recv,
 ):
     place = lax.axis_index("tensor")
     units = unit_ref.shape[1]
     tiles = units // tile
     rows = part.shape[1]
-    summed = Sum(place, part, held, send, recv, chunks)
+    summed = Near(place, part, held, send, recv, chunks)
+    cots = Gather(place, far_ref, c_send, c_recv, 1, second=near_ref)
+    inside = ((place + 1) // 2) % 2
     gather = Gather(place, b_ref, g_send, g_recv, chunks, own)
     joint = Gather(place, extra, x_send, x_recv, 1)
 
     def load_rows(order, act):
         into = order % 2
-        shard = place ^ (LINE - 1 - order)
+        shard = place ^ ((order + 1) % LINE)
         act(pltpu.make_async_copy(n_ref.at[shard], nbuf.at[into], nsem.at[into]))
 
         def take(source):
             act(pltpu.make_async_copy(source, cbuf.at[into], csem.at[into]))
 
+        beside = (order == 0) | ((order == 2) & (inside == 1))
         pl.when(order == LINE - 1)(lambda: take(c_ref))
-        pl.when(order < LINE - 1)(lambda: take(far_ref.at[shard]))
+        pl.when(beside)(lambda: take(near_ref.at[shard]))
+        pl.when(jnp.logical_not(beside) & (order < LINE - 1))(lambda: take(far_ref.at[shard]))
 
     def load_weights(index, into, act):
         columns = pl.ds(pl.multiple_of(index * tile, tile), tile)
@@ -882,16 +950,12 @@
     unit_ref[...] = jnp.zeros_like(unit_ref)
     model_ref[...] = jnp.zeros_like(model_ref)
     greet(place)
+    cots.send(2, 0)
 
     def one_shard(order, carry):
         into = order % 2
-        shard = place ^ (LINE - 1 - order)
+        shard = place ^ ((order + 1) % LINE)
         load_rows(order, wait)
-
-        @pl.when(order < LINE - 1)
-        def _():
-            load_rows(order + 1, start)
-
         first = nt(nbuf[into], e_ref[...]) + nt(cbuf[into], f_ref[...])
         low[...] = first.astype(bf16)
         low_t[...] = first.T.astype(bf16)
@@ -924,18 +988,41 @@
             unit_ref[:rank, columns] += nn(low_t[:rank], grad_gate)
             unit_ref[rank : 2 * rank, columns] += nn(low_t[rank : 2 * rank], grad_rise)
             unit_ref[2 * rank :, columns] += nn(low_t[2 * rank : 3 * rank], hidden)
+            for number, (away, chunk) in enumerate(((1, 2), (1, 3), (2, 0), (2, 1))):
+
+                @pl.when((order == LINE - 1) & (index == number))
+                def _():
+                    summed.send(away, chunk, 1)
+
             return carry
 
         lax.fori_loop(0, tiles, one_tile, 0)
+
+        @pl.when(order == 0)
+        def _():
+            cots.relay(3, 0)
+            cots.end_got(2)
+
+        @pl.when(order == 1)
+        def _():
+            cots.end_got(3)
+
+        @pl.when(order < LINE - 1)
+        def _():
+            load_rows(order + 1, start)
+
         joined = acc_low[...].astype(bf16)
         joined_t = acc_low[...].T.astype(bf16)
         part[shard] = (acc_back[...] + nn(joined, e_ref[...])).astype(bf16)
-        for step in (1, 2, 3):
-
-            @pl.when(order == step - 1)
+        for away in (1, 2, 3):
+
+            @pl.when(order == away - 1)
             def _():
                 for chunk in range(chunks):
-                    summed.send(step, chunk)
+                    summed.send(away, chunk, 0)
+                if away == 3:
+                    summed.send(1, 0, 1)
+                    summed.send(1, 1, 1)
 
         @pl.when(order > 0)
         def _():
@@ -948,32 +1035,6 @@
         return carry
 
     lax.fori_loop(0, LINE, one_shard, 0)
-    extra[place] = model_ref[...].astype(bf16)
-    joint.send(1, 0)
-    size = rows // chunks
-    last = (LINE - 1) % 2
-    load_middle.wait()
-    stores = []
-    for chunk in range(chunks):
-        summed.total(chunk, acc_back)
-        here = chunk_rows(chunk, size)
-        middle = midv[here]
-        rms = lax.rsqrt(jnp.mean(middle * middle, axis=1, keepdims=True) + eps)
-        scaled = acc_back[here] * gain_ref[...].astype(f32)
-        mean = jnp.mean(scaled * middle, axis=1, keepdims=True)
-        grad = cbuf[last, here].astype(f32) + rms * (scaled - middle * (rms * rms) * mean)
-        own[here] = grad.astype(bf16)
-        gather.send(1, chunk, least=1)
-        midv[here] = grad
-        store = pltpu.make_async_copy(midv.at[here], grad_ref.at[here], nsem.at[chunk % 2])
-        if chunk >= 2:
-            stores[chunk - 2].wait()
-        store.start()
-        stores.append(store)
-    for chunk in range(chunks):
-        gather.send(1, chunk, most=0)
-    pltpu.make_async_copy(resv, res_ref.at[place], rsem.at[0]).wait()
-
     def pass_on(side, step, source, target):
         index = 0 if side == 1 else 1
         return pltpu.make_async_remote_copy(
@@ -1001,13 +1062,42 @@
             copy.wait()
         cbuf[0] = (cbuf[0].astype(f32) + cbuf[1].astype(f32)).astype(bf16)
 
-    for side in SIDES:
-        for step in (1, 2):
+    def send_result(step):
+        for side in SIDES:
             at_far(
                 side,
                 0,
                 lambda: pass_on(side, step, res_ref.at[place + side * (LINE - step)], place + side).start(),
             )
+
+    summed.send(2, 2, 1)
+    summed.send(2, 3, 1)
+    extra[place] = model_ref[...].astype(bf16)
+    joint.send(1, 0)
+    send_result(1)
+    size = rows // chunks
+    last = (LINE - 1) % 2
+    load_middle.wait()
+    stores = []
+    for chunk in range(chunks):
+        summed.send(1, chunk, 2)
+        summed.total(chunk, acc_back)
+        here = chunk_rows(chunk, size)
+        middle = midv[here]
+        rms = lax.rsqrt(jnp.mean(middle * middle, axis=1, keepdims=True) + eps)
+        scaled = acc_back[here] * gain_ref[...].astype(f32)
+        mean = jnp.mean(scaled * middle, axis=1, keepdims=True)
+        grad = cbuf[last, here].astype(f32) + rms * (scaled - middle * (rms * rms) * mean)
+        own[here] = grad.astype(bf16)
+        gather.send(1, chunk)
+        midv[here] = grad
+        store = pltpu.make_async_copy(midv.at[here], grad_ref.at[here], nsem.at[chunk % 2])
+        if chunk >= 2:
+            stores[chunk - 2].wait()
+        store.start()
+        stores.append(store)
+    send_result(2)
+    pltpu.make_async_copy(resv, res_ref.at[place], rsem.at[0]).wait()
 
     load_out.wait()
     for store in stores[-2:]:
@@ -1029,22 +1119,13 @@
         copy.wait()
         through(number, nbuf.at[number % 2], shard)
 
-    def edge_got(step):
-        for side in SIDES:
-
-            @pl.when(far_of(place, side) == LINE - 1)
-            def _():
-                for chunk in range(chunks):
-                    gather.copy(side, step, chunk, place - side * step, place - side).wait_recv()
-
-    inside = ((place + 1) // 2) % 2
     joint.relay(2, 0)
     through(0, own, place)
     unit_out[: 3 * rank] = unit_ref[...].astype(bf16)
     unit_out[3 * rank :] = jnp.full((rank, units), pick_ref[0, 0], f32).astype(bf16)
     for chunk in range(chunks):
         gather.relay(2, chunk)
-    edge_got(1)
+    gather.end_got(1)
     joint.relay(3, 0)
     take(1, place ^ (1 + 2 * inside))
     for chunk in range(chunks):
@@ -1057,13 +1138,13 @@
             resv[...] = cbuf[0]
             pass_on(side, 2, resv, place + side).start()
 
-    edge_got(2)
+    gather.end_got(2)
     take(2, place ^ (2 - inside))
     joint.close()
     model_out[...] = functools.reduce(
         jnp.add, [extra[shard].astype(f32) for shard in range(LINE)]
     ).astype(bf16)
-    edge_got(3)
+    gather.end_got(3)
     take(3, place ^ (3 - inside))
     for index, side in enumerate(SIDES):
         target = (right_ref, left_ref)[index]
@@ -1093,6 +1174,7 @@
     summed.drain()
     gather.drain()
     joint.drain()
+    cots.drain(start=2)
 
 
 def feed(
@@ -1107,7 +1189,7 @@
     return pl.pallas_call(
         functools.partial(feed_body, rank, tile, chunks),
         in_specs=[IN_HBM] * 8 + [pl.BlockSpec(memory_space=pltpu.SMEM)] + [IN_VMEM] * 8,
-        out_specs=[IN_HBM] * 6 + [IN_VMEM] * 5,
+        out_specs=[IN_HBM] * 7 + [IN_VMEM] * 5,
         out_shape=[
             jax.ShapeDtypeStruct((rows, features), f32),
             jax.ShapeDtypeStruct((LINE, rows, features), bf16),
@@ -1115,6 +1197,7 @@
             one,
             jax.ShapeDtypeStruct((LINE, rows, features), bf16),
             jax.ShapeDtypeStruct((2, LINE - 2, rows, features), bf16),
+            jax.ShapeDtypeStruct((LINE, rows, features), bf16),
             jax.ShapeDtypeStruct((4 * rank, units), bf16),
             jax.ShapeDtypeStruct((3 * rank, features), bf16),
             jax.ShapeDtypeStruct((1, total, width), bf16),
@@ -1151,6 +1234,7 @@
         + line_sems(chunks)
         + line_sems(chunks)
         + line_sems(1)
+        + line_sems(1)
         + [pltpu.SemaphoreType.DMA((2, LINE - 2))] * 2,
         compiler_params=comm_params(5),
     )(
@@ -1323,7 +1407,7 @@
     )
 
     (
-        grad_middle, res_parts, res_right, res_left, _, _, early, model_sum, grad_attended, final_grads, exit_grads,
+        grad_middle, res_parts, res_right, res_left, _, _, _, early, model_sum, grad_attended, final_grads, exit_grads,
     ) = feed(
         full_two, (cotangent, full_cot), w_units, middle, w_heads, adapter_pick.astype(f32)[None, :],
         units_exit, fall_entry, entries, finals, gain_two, out_entry, attended, adapt_o,

time: 680 us -> 674 us (level)
  Pallas kernels: 645 us -> 637 us
    pallas_call x1, Pallas kernels: 232 us -> 200 us  [front(): pl.pallas_call(functools.partial(front_body, chunks, seg), in_specs=[IN_H...]
    pallas_call x1, Pallas kernels: 213 us -> 237 us  [feed(): pl.pallas_call(functools.partial(feed_body, rank, tile, chunks), in_specs...]
  transfers between devices with their start and end apart: 6 -> 6, of which waited for: 0 -> 0; matrix products, arithmetic and copies ran while one was open for 1% -> 1% of each run, Pallas kernels for 63% -> 59%
where the time goes in v12:
time: 674 us; the launch traced here: 661 us
  Pallas kernels  637 us (95%)
  between operations  15.3 us (2%)
    pallas_call x1, Pallas kernels, feed(): pl.pallas_call(functools.partial(feed_body, rank, tile, chunks), in_specs...  237 us
    pallas_call x1, Pallas kernels, front(): pl.pallas_call(functools.partial(front_body, chunks, seg), in_specs=[IN_H...  200 us
    pallas_call x1, Pallas kernels, back(): pl.pallas_call(functools.partial(back_body, chunks, seg), in_specs=[IN_HB...  125 us
    pallas_call x1, Pallas kernels, gather_norm(): pl.pallas_call(functools.partial(gather_norm_body, chunks), in_specs=[IN_...  63.3 us
  transfers between devices with their start and end apart: 6, of which 0 were waited for; matrix products, arithmetic and copies ran while one was open for 1% of the time, Pallas kernels for 59%

profile of v12, /device:TPU:0, one launch (start us, length us, event | category | flops | bytes accessed | tf_op | source)
XLA Modules:
  0.0 661.0 jit_solution(18317537188843084657)
XLA Ops:
  7.2 0.0 all-gather.9.cloned.1.call-start
  7.2 2.3 pad_maximum_fusion
  9.5 0.0 copy-start.2
  9.5 0.0 copy-start
  9.5 0.0 copy-start.1
  9.5 0.0 all-gather.9.cloned.1.call-update
  9.5 0.0 all-gather.11.cloned.1.call-start
  9.6 0.7 all-gather.11.cloned.1.call-update
  10.3 0.0 all-gather.13.cloned.1.call-start
  10.3 0.7 all-gather.13.cloned.1.call-update
  11.0 0.0 all-gather.15.cloned.1.call-start
  11.1 0.5 all-gather.15.cloned.1.call-update
  11.6 0.0 all-gather.17.cloned.1.call-start
  12.3 0.0 copy-done.2
  12.3 0.1 add_bitcast_fusion
  12.4 0.1 broadcast_in_dim.24
  12.4 0.7 sub.10.p_ref
  13.1 0.0 copy-done
  13.1 0.6 broadcast_in_dim.21.gain_ref
  13.7 0.0 copy-done.1
  13.7 0.6 broadcast_in_dim.25.gain_ref
  14.3 63.3 %shard_map.260.x_ref = bf16[4,320,2048]{2,1,0:T(8,128)(2,1)} custom-call(bf16[320,2048]{1,0:T(8,128)(2,1)} %x_ref.3, bf16[1,2048]{1,0:T(2,128)(2,1)} %broadcast_in_dim.21.gain_ref), custom_call_target="tpu_custom_call" | custom-call | tf_op jit(solution)/shard_map/pallas_call | solution.py:344
  77.6 2.0 shard_map.261
  79.7 0.0 all-gather.9.cloned.1.call-done.w_ref.wo_ref
  79.7 200.5 %shard_map.262 = (bf16[4,320,2048]{2,1,0:T(8,128)(2,1)}, bf16[3,1280,512]{2,1,0:T(8,128)(2,1)}, f32[320,2048]{1,0:T(8,128)}, bf16[4,320,2048]{2,1,0:T(8,128)(2,1...) custom-call(bf16[4,320,2048]{2,1,0:T(8,128)(2,1)} %shard_map.260.x_r, ...), custom_call_target="tpu_custom_call", output_to_operand_aliasing={{0}: (0, {})} | custom-call | tf_op jit(solution)/shard_map/pallas_call | solution.py:503
  280.2 0.0 all-gather.11.cloned.1.call-done.wg_ref
  280.2 0.0 all-gather.13.cloned.1.call-done.wu_ref
  280.2 0.0 all-gather.15.cloned.1.call-done.wd_ref
  280.3 236.6 %shard_map.263 = (f32[320,2048]{1,0:T(8,128)}, bf16[4,320,2048]{2,1,0:T(8,128)(2,1)}, bf16[320,2048]{1,0:T(8,128)(2,1)}, bf16[320,2048]{1,0:T(8,128)(2,1)}, bf16...) custom-call(bf16[4,320,2048]{2,1,0:T(8,128)(2,1)} %get-tuple-element, ...), custom_call_target="tpu_custom_call" | custom-call | tf_op jit(solution)/shard_map/pallas_call | solution.py:1189
  516.9 0.0 all-gather.17.cloned.1.call-update
  516.9 0.0 all-gather.19.cloned.1.call-start
  516.9 0.5 all-gather.19.cloned.1.call-update
  517.5 124.9 %shard_map.264 = (bf16[320,2048]{1,0:T(8,128)(2,1)}, bf16[8,64,2048]{2,1,0:T(8,128)(2,1)}, bf16[8,64,512]{2,1,0:T(8,128)(2,1)}, bf16[320,2048]{1,0:T(8,128)(2,1)}) custom-call(bf16[3,1280,512]{2,1,0:T(8,128)(2,1)} %get-tuple-element.57.q_ref, bf16[2048,2048]{1,0:T(8,128)(2,1)} %all-gather.9.cloned.1.call-done.w_ref.wo_ref, ...), custom_call_target="tpu_custom_call" | custom-call | tf_op jit(solution)/shard_map/pallas_call | solution.py:762
  642.4 0.0 all-gather.17.cloned.1.call-done
  642.4 1.5 fusion.pick_ref
  643.9 0.0 all-gather.19.cloned.1.call-done
  643.9 9.8 %shard_map.265 = (f32[5,8,16,2048]{3,2,1,0:T(8,128)}, f32[2,8,16,2048]{3,2,1,0:T(8,128)}, f32[2,8,16,2048]{3,2,1,0:T(8,128)}, f32[8,16,2048]{2,1,0:T(8,128)}, f3...) custom-call(s32[8]{0:T(128)} %fusion.pick_ref, ...), custom_call_target="tpu_custom_call" | custom-call | tf_op jit(solution)/shard_map/pallas_call | solution.py:1320
Async XLA Ops:
  7.2 72.5 %all-gather.9.cloned.1.call-start = ((), (), s32[]{:S(2)}) async-start(), calls=%async_computation | async-start | bytes 9437184 | tf_op jit(solution)/shard_map/all_gather | solution.py:1381
  9.5 2.8 copy-start.2
  9.5 3.6 copy-start
  9.5 4.2 copy-start.1
  9.5 270.7 %all-gather.11.cloned.1.call-start = ((), (), s32[]{:S(2)}) async-start(), calls=%async_computation.1 | async-start | bytes 9437184 | tf_op jit(solution)/shard_map/all_gather | solution.py:1389
  10.3 269.9 %all-gather.13.cloned.1.call-start = ((), (), s32[]{:S(2)}) async-start(), calls=%async_computation.2 | async-start | bytes 9437184 | tf_op jit(solution)/shard_map/all_gather | solution.py:1389
  11.0 269.2 %all-gather.15.cloned.1.call-start = ((), (), s32[]{:S(2)}) async-start(), calls=%async_computation.3 | async-start | bytes 9437184 | tf_op jit(solution)/shard_map/all_gather | solution.py:1389
  11.6 630.8 %all-gather.17.cloned.1.call-start = ((), (), s32[]{:S(2)}) async-start(), calls=%async_computation.4 | async-start | bytes 2359296 | tf_op jit(solution)/shard_map/all_gather | solution.py:1269
  516.9 127.1 %all-gather.19.cloned.1.call-start = ((), (), s32[]{:S(2)}) async-start(), calls=%async_computation.5 | async-start | bytes 1769472 | tf_op jit(solution)/shard_map/all_gather | solution.py:1269
Sparse Core Ops, SparseCore 0:
  10.5 57.0 all-gather.8
  69.5 54.3 all-gather.10
  125.8 54.4 all-gather.12
  182.0 54.3 all-gather.14
  517.0 30.4 all-gather.16
  549.2 25.6 all-gather.18

commit v13 on v12

--- a/solution.py
+++ b/solution.py
@@ -1070,17 +1070,13 @@
                 lambda: pass_on(side, step, res_ref.at[place + side * (LINE - step)], place + side).start(),
             )
 
-    summed.send(2, 2, 1)
-    summed.send(2, 3, 1)
     extra[place] = model_ref[...].astype(bf16)
-    joint.send(1, 0)
-    send_result(1)
     size = rows // chunks
     last = (LINE - 1) % 2
     load_middle.wait()
-    stores = []
-    for chunk in range(chunks):
-        summed.send(1, chunk, 2)
+    send_result(1)
+
+    def finish(chunk):
         summed.total(chunk, acc_back)
         here = chunk_rows(chunk, size)
         middle = midv[here]
@@ -1089,19 +1085,33 @@
         mean = jnp.mean(scaled * middle, axis=1, keepdims=True)
         grad = cbuf[last, here].astype(f32) + rms * (scaled - middle * (rms * rms) * mean)
         own[here] = grad.astype(bf16)
-        gather.send(1, chunk)
         midv[here] = grad
-        store = pltpu.make_async_copy(midv.at[here], grad_ref.at[here], nsem.at[chunk % 2])
-        if chunk >= 2:
-            stores[chunk - 2].wait()
-        store.start()
-        stores.append(store)
+
+    @pl.when(inside == 1)
+    def _():
+        for chunk in range(chunks):
+            finish(chunk)
+            gather.send(1, chunk, least=2)
+
+    joint.send(1, 0)
+    summed.send(2, 2, 1)
+    summed.send(2, 3, 1)
+    for chunk in range(chunks):
+        summed.send(1, chunk, 2)
+    for chunk in range(chunks):
+        gather.send(1, chunk, least=1, most=1)
+
+    @pl.when(inside == 0)
+    def _():
+        for chunk in range(chunks):
+            finish(chunk)
+            gather.send(1, chunk)
+
     send_result(2)
+    (store,) = fetch([(midv, grad_ref)], msem)
     pltpu.make_async_copy(resv, res_ref.at[place], rsem.at[0]).wait()
 
     load_out.wait()
-    for store in stores[-2:]:
-        store.wait()
 
     def through(number, rows_ref, shard):
         mine = pl.ds(pl.multiple_of(shard * rows, rows), rows)
@@ -1124,12 +1134,15 @@
     unit_out[: 3 * rank] = unit_ref[...].astype(bf16)
     unit_out[3 * rank :] = jnp.full((rank, units), pick_ref[0, 0], f32).astype(bf16)
     for chunk in range(chunks):
-        gather.relay(2, chunk)
+        gather.relay(2, chunk, least=2)
     gather.end_got(1)
     joint.relay(3, 0)
     take(1, place ^ (1 + 2 * inside))
     for chunk in range(chunks):
-        gather.relay(3, chunk)
+        gather.relay(2, chunk, most=1)
+        if chunk:
+            gather.relay(3, chunk - 1)
+    gather.relay(3, chunks - 1)
     for side in SIDES:
 
         @pl.when(far_of(place, side) == 1)
@@ -1175,6 +1188,7 @@
     gather.drain()
     joint.drain()
     cots.drain(start=2)
+    store.wait()
 
 
 def feed(

time: 674 us -> 662 us (0.982)
  Pallas kernels: 637 us -> 625 us
    pallas_call x1, Pallas kernels: 237 us -> 224 us  [feed(): pl.pallas_call(functools.partial(feed_body, rank, tile, chunks), in_specs...]
  transfers between devices with their start and end apart: 6 -> 6, of which waited for: 0 -> 0; matrix products, arithmetic and copies ran while one was open for 1% -> 1% of each run, Pallas kernels for 59% -> 60%
where the time goes in v13:
time: 662 us; the launch traced here: 649 us
  Pallas kernels  625 us (94%)
  between operations  15.3 us (2%)
    pallas_call x1, Pallas kernels, feed(): pl.pallas_call(functools.partial(feed_body, rank, tile, chunks), in_specs...  224 us
    pallas_call x1, Pallas kernels, front(): pl.pallas_call(functools.partial(front_body, chunks, seg), in_specs=[IN_H...  201 us
    pallas_call x1, Pallas kernels, back(): pl.pallas_call(functools.partial(back_body, chunks, seg), in_specs=[IN_HB...  125 us
    pallas_call x1, Pallas kernels, gather_norm(): pl.pallas_call(functools.partial(gather_norm_body, chunks), in_specs=[IN_...  63.3 us
  transfers between devices with their start and end apart: 6, of which 0 were waited for; matrix products, arithmetic and copies ran while one was open for 1% of the time, Pallas kernels for 60%

profile of v13, /device:TPU:0, one launch (start us, length us, event | category | flops | bytes accessed | tf_op | source)
XLA Modules:
  0.0 649.1 jit_solution(14747678993928391095)
XLA Ops:
  7.2 0.0 all-gather.9.cloned.1.call-start
  7.2 2.3 pad_maximum_fusion
  9.5 0.0 copy-start.2
  9.5 0.0 copy-start
  9.5 0.0 copy-start.1
  9.5 0.0 all-gather.9.cloned.1.call-update
  9.5 0.0 all-gather.11.cloned.1.call-start
  9.6 0.7 all-gather.11.cloned.1.call-update
  10.3 0.0 all-gather.13.cloned.1.call-start
  10.3 0.7 all-gather.13.cloned.1.call-update
  11.0 0.0 all-gather.15.cloned.1.call-start
  11.1 0.5 all-gather.15.cloned.1.call-update
  11.6 0.0 all-gather.17.cloned.1.call-start
  12.3 0.0 copy-done.2
  12.3 0.1 add_bitcast_fusion
  12.4 0.1 broadcast_in_dim.24
  12.4 0.7 sub.10.p_ref
  13.1 0.0 copy-done
  13.1 0.6 broadcast_in_dim.21.gain_ref
  13.7 0.0 copy-done.1
  13.7 0.6 broadcast_in_dim.25.gain_ref
  14.3 63.3 %shard_map.260.x_ref = bf16[4,320,2048]{2,1,0:T(8,128)(2,1)} custom-call(bf16[320,2048]{1,0:T(8,128)(2,1)} %x_ref.3, bf16[1,2048]{1,0:T(2,128)(2,1)} %broadcast_in_dim.21.gain_ref), custom_call_target="tpu_custom_call" | custom-call | tf_op jit(solution)/shard_map/pallas_call | solution.py:344
  77.6 2.0 shard_map.261
  79.7 0.0 all-gather.9.cloned.1.call-done.w_ref.wo_ref
  79.7 200.6 %shard_map.262 = (bf16[4,320,2048]{2,1,0:T(8,128)(2,1)}, bf16[3,1280,512]{2,1,0:T(8,128)(2,1)}, f32[320,2048]{1,0:T(8,128)}, bf16[4,320,2048]{2,1,0:T(8,128)(2,1...) custom-call(bf16[4,320,2048]{2,1,0:T(8,128)(2,1)} %shard_map.260.x_r, ...), custom_call_target="tpu_custom_call", output_to_operand_aliasing={{0}: (0, {})} | custom-call | tf_op jit(solution)/shard_map/pallas_call | solution.py:503
  280.3 0.0 all-gather.11.cloned.1.call-done.wg_ref
  280.3 0.0 all-gather.13.cloned.1.call-done.wu_ref
  280.3 0.0 all-gather.15.cloned.1.call-done.wd_ref
  280.4 224.2 %shard_map.263 = (f32[320,2048]{1,0:T(8,128)}, bf16[4,320,2048]{2,1,0:T(8,128)(2,1)}, bf16[320,2048]{1,0:T(8,128)(2,1)}, bf16[320,2048]{1,0:T(8,128)(2,1)}, bf16...) custom-call(bf16[4,320,2048]{2,1,0:T(8,128)(2,1)} %get-tuple-element, ...), custom_call_target="tpu_custom_call" | custom-call | tf_op jit(solution)/shard_map/pallas_call | solution.py:1203
  504.6 0.0 all-gather.17.cloned.1.call-update
  504.6 0.0 all-gather.19.cloned.1.call-start
  504.6 0.5 all-gather.19.cloned.1.call-update
  505.2 125.2 %shard_map.264 = (bf16[320,2048]{1,0:T(8,128)(2,1)}, bf16[8,64,2048]{2,1,0:T(8,128)(2,1)}, bf16[8,64,512]{2,1,0:T(8,128)(2,1)}, bf16[320,2048]{1,0:T(8,128)(2,1)}) custom-call(bf16[3,1280,512]{2,1,0:T(8,128)(2,1)} %get-tuple-element.57.q_ref, bf16[2048,2048]{1,0:T(8,128)(2,1)} %all-gather.9.cloned.1.call-done.w_ref.wo_ref, ...), custom_call_target="tpu_custom_call" | custom-call | tf_op jit(solution)/shard_map/pallas_call | solution.py:762
  630.4 0.0 all-gather.17.cloned.1.call-done
  630.4 1.5 fusion.pick_ref
  631.9 0.0 all-gather.19.cloned.1.call-done
  631.9 9.8 %shard_map.265 = (f32[5,8,16,2048]{3,2,1,0:T(8,128)}, f32[2,8,16,2048]{3,2,1,0:T(8,128)}, f32[2,8,16,2048]{3,2,1,0:T(8,128)}, f32[8,16,2048]{2,1,0:T(8,128)}, f3...) custom-call(s32[8]{0:T(128)} %fusion.pick_ref, ...), custom_call_target="tpu_custom_call" | custom-call | tf_op jit(solution)/shard_map/pallas_call | solution.py:1334
Async XLA Ops:
  7.2 72.5 %all-gather.9.cloned.1.call-start = ((), (), s32[]{:S(2)}) async-start(), calls=%async_computation | async-start | bytes 9437184 | tf_op jit(solution)/shard_map/all_gather | solution.py:1395
  9.5 2.8 copy-start.2
  9.5 3.6 copy-start
  9.5 4.2 copy-start.1
  9.5 270.8 %all-gather.11.cloned.1.call-start = ((), (), s32[]{:S(2)}) async-start(), calls=%async_computation.1 | async-start | bytes 9437184 | tf_op jit(solution)/shard_map/all_gather | solution.py:1403
  10.3 270.1 %all-gather.13.cloned.1.call-start = ((), (), s32[]{:S(2)}) async-start(), calls=%async_computation.2 | async-start | bytes 9437184 | tf_op jit(solution)/shard_map/all_gather | solution.py:1403
  11.0 269.3 %all-gather.15.cloned.1.call-start = ((), (), s32[]{:S(2)}) async-start(), calls=%async_computation.3 | async-start | bytes 9437184 | tf_op jit(solution)/shard_map/all_gather | solution.py:1403
  11.6 618.8 %all-gather.17.cloned.1.call-start = ((), (), s32[]{:S(2)}) async-start(), calls=%async_computation.4 | async-start | bytes 2359296 | tf_op jit(solution)/shard_map/all_gather | solution.py:1283
  504.6 127.3 %all-gather.19.cloned.1.call-start = ((), (), s32[]{:S(2)}) async-start(), calls=%async_computation.5 | async-start | bytes 1769472 | tf_op jit(solution)/shard_map/all_gather | solution.py:1283
Sparse Core Ops, SparseCore 0:
  10.5 57.0 all-gather.8
  69.5 54.4 all-gather.10
  125.8 54.3 all-gather.12
  182.0 54.3 all-gather.14
  504.7 30.5 all-gather.16
  537.1 25.6 all-gather.18

commit v14 on v13

--- a/solution.py
+++ b/solution.py
@@ -495,7 +495,7 @@
     cots.drain(stop=2)
 
 
-def front(x, weight, cot, entries, exits, tables, leaf_parent, out_entry, finals, tokens, gain, seg, chunks=4):
+def front(x, weight, cot, entries, exits, tables, leaf_parent, out_entry, finals, tokens, gain, seg, chunks=5):
     _, rows, features = x.shape
     groups, rank, width = exits.shape
     total = LINE * rows
@@ -936,6 +936,7 @@
     def wait(copy):
         copy.wait()
 
+    during = ((1, (2,)), (1, range(3, chunks)), (2, (0,)), (2, (1,)))
     load_rows(jnp.int32(0), start)
     load_weights(0, 0, start)
     width = wo.shape[1]
@@ -988,11 +989,12 @@
             unit_ref[:rank, columns] += nn(low_t[:rank], grad_gate)
             unit_ref[rank : 2 * rank, columns] += nn(low_t[rank : 2 * rank], grad_rise)
             unit_ref[2 * rank :, columns] += nn(low_t[2 * rank : 3 * rank], hidden)
-            for number, (away, chunk) in enumerate(((1, 2), (1, 3), (2, 0), (2, 1))):
+            for number, (away, part_chunks) in enumerate(during):
 
                 @pl.when((order == LINE - 1) & (index == number))
                 def _():
-                    summed.send(away, chunk, 1)
+                    for chunk in part_chunks:
+                        summed.send(away, chunk, 1)
 
             return carry
 
@@ -1094,8 +1096,8 @@
             gather.send(1, chunk, least=2)
 
     joint.send(1, 0)
-    summed.send(2, 2, 1)
-    summed.send(2, 3, 1)
+    for chunk in range(2, chunks):
+        summed.send(2, chunk, 1)
     for chunk in range(chunks):
         summed.send(1, chunk, 2)
     for chunk in range(chunks):
@@ -1193,7 +1195,7 @@
 
 def feed(
     normed, cots, weights, middle, w_heads, pick, units_exit, fall_entry, entries, finals, gain, out_entry,
-    attended, low_out, tile=512, chunks=4,
+    attended, low_out, tile=512, chunks=5,
 ):
     _, rows, features = normed.shape
     units = weights[0].shape[1]

time: 662 us -> 661 us (level)
  no operation moved by 1% of the time
where the time goes in v14:
time: 661 us; the launch traced here: 651 us
  Pallas kernels  627 us (95%)
  between operations  15.1 us (2%)
    pallas_call x1, Pallas kernels, feed(): pl.pallas_call(functools.partial(feed_body, rank, tile, chunks), in_specs...  224 us
    pallas_call x1, Pallas kernels, front(): pl.pallas_call(functools.partial(front_body, chunks, seg), in_specs=[IN_H...  200 us
    pallas_call x1, Pallas kernels, back(): pl.pallas_call(functools.partial(back_body, chunks, seg), in_specs=[IN_HB...  127 us
    pallas_call x1, Pallas kernels, gather_norm(): pl.pallas_call(functools.partial(gather_norm_body, chunks), in_specs=[IN_...  63.3 us
  transfers between devices with their start and end apart: 6, of which 0 were waited for; matrix products, arithmetic and copies ran while one was open for 1% of the time, Pallas kernels for 60%

profile of v14, /device:TPU:0, one launch (start us, length us, event | category | flops | bytes accessed | tf_op | source)
XLA Modules:
  0.0 650.6 jit_solution(2584345466056647988)
XLA Ops:
  7.2 0.0 all-gather.9.cloned.1.call-start
  7.2 2.3 pad_maximum_fusion
  9.5 0.0 copy-start.2
  9.5 0.0 copy-start
  9.5 0.0 copy-start.1
  9.5 0.0 all-gather.9.cloned.1.call-update
  9.5 0.0 all-gather.11.cloned.1.call-start
  9.6 0.7 all-gather.11.cloned.1.call-update
  10.3 0.0 all-gather.13.cloned.1.call-start
  10.3 0.7 all-gather.13.cloned.1.call-update
  11.0 0.0 all-gather.15.cloned.1.call-start
  11.1 0.5 all-gather.15.cloned.1.call-update
  11.6 0.0 all-gather.17.cloned.1.call-start
  12.3 0.0 copy-done.2
  12.3 0.1 add_bitcast_fusion
  12.4 0.1 broadcast_in_dim.24
  12.4 0.7 sub.10.p_ref
  13.1 0.0 copy-done
  13.1 0.6 broadcast_in_dim.21.gain_ref
  13.7 0.0 copy-done.1
  13.7 0.6 broadcast_in_dim.25.gain_ref
  14.3 63.3 %shard_map.260.x_ref = bf16[4,320,2048]{2,1,0:T(8,128)(2,1)} custom-call(bf16[320,2048]{1,0:T(8,128)(2,1)} %x_ref.3, bf16[1,2048]{1,0:T(2,128)(2,1)} %broadcast_in_dim.21.gain_ref), custom_call_target="tpu_custom_call" | custom-call | tf_op jit(solution)/shard_map/pallas_call | solution.py:344
  77.6 2.0 shard_map.261
  79.7 0.0 all-gather.9.cloned.1.call-done.w_ref.wo_ref
  79.7 200.2 %shard_map.262 = (bf16[4,320,2048]{2,1,0:T(8,128)(2,1)}, bf16[3,1280,512]{2,1,0:T(8,128)(2,1)}, f32[320,2048]{1,0:T(8,128)}, bf16[4,320,2048]{2,1,0:T(8,128)(2,1...) custom-call(bf16[4,320,2048]{2,1,0:T(8,128)(2,1)} %shard_map.260.x_r, ...), custom_call_target="tpu_custom_call", output_to_operand_aliasing={{0}: (0, {})} | custom-call | tf_op jit(solution)/shard_map/pallas_call | solution.py:503
  279.9 0.0 all-gather.11.cloned.1.call-done.wg_ref
  279.9 0.0 all-gather.13.cloned.1.call-done.wu_ref
  279.9 0.0 all-gather.15.cloned.1.call-done.wd_ref
  280.0 224.2 %shard_map.263 = (f32[320,2048]{1,0:T(8,128)}, bf16[4,320,2048]{2,1,0:T(8,128)(2,1)}, bf16[320,2048]{1,0:T(8,128)(2,1)}, bf16[320,2048]{1,0:T(8,128)(2,1)}, bf16...) custom-call(bf16[4,320,2048]{2,1,0:T(8,128)(2,1)} %get-tuple-element, ...), custom_call_target="tpu_custom_call" | custom-call | tf_op jit(solution)/shard_map/pallas_call | solution.py:1205
  504.1 0.0 all-gather.17.cloned.1.call-update
  504.1 0.0 all-gather.19.cloned.1.call-start
  504.2 0.5 all-gather.19.cloned.1.call-update
  504.7 127.4 %shard_map.264 = (bf16[320,2048]{1,0:T(8,128)(2,1)}, bf16[8,64,2048]{2,1,0:T(8,128)(2,1)}, bf16[8,64,512]{2,1,0:T(8,128)(2,1)}, bf16[320,2048]{1,0:T(8,128)(2,1)}) custom-call(bf16[3,1280,512]{2,1,0:T(8,128)(2,1)} %get-tuple-element.57.q_ref, bf16[2048,2048]{1,0:T(8,128)(2,1)} %all-gather.9.cloned.1.call-done.w_ref.wo_ref, ...), custom_call_target="tpu_custom_call" | custom-call | tf_op jit(solution)/shard_map/pallas_call | solution.py:762
  632.1 0.0 all-gather.17.cloned.1.call-done
  632.1 1.5 fusion.pick_ref
  633.7 0.0 all-gather.19.cloned.1.call-done
  633.7 9.8 %shard_map.265 = (f32[5,8,16,2048]{3,2,1,0:T(8,128)}, f32[2,8,16,2048]{3,2,1,0:T(8,128)}, f32[2,8,16,2048]{3,2,1,0:T(8,128)}, f32[8,16,2048]{2,1,0:T(8,128)}, f3...) custom-call(s32[8]{0:T(128)} %fusion.pick_ref, ...), custom_call_target="tpu_custom_call" | custom-call | tf_op jit(solution)/shard_map/pallas_call | solution.py:1336
Async XLA Ops:
  7.2 72.5 %all-gather.9.cloned.1.call-start = ((), (), s32[]{:S(2)}) async-start(), calls=%async_computation | async-start | bytes 9437184 | tf_op jit(solution)/shard_map/all_gather | solution.py:1397
  9.5 2.8 copy-start.2
  9.5 3.6 copy-start
  9.5 4.2 copy-start.1
  9.5 270.4 %all-gather.11.cloned.1.call-start = ((), (), s32[]{:S(2)}) async-start(), calls=%async_computation.1 | async-start | bytes 9437184 | tf_op jit(solution)/shard_map/all_gather | solution.py:1405
  10.3 269.6 %all-gather.13.cloned.1.call-start = ((), (), s32[]{:S(2)}) async-start(), calls=%async_computation.2 | async-start | bytes 9437184 | tf_op jit(solution)/shard_map/all_gather | solution.py:1405
  11.0 268.9 %all-gather.15.cloned.1.call-start = ((), (), s32[]{:S(2)}) async-start(), calls=%async_computation.3 | async-start | bytes 9437184 | tf_op jit(solution)/shard_map/all_gather | solution.py:1405
  11.6 620.5 %all-gather.17.cloned.1.call-start = ((), (), s32[]{:S(2)}) async-start(), calls=%async_computation.4 | async-start | bytes 2359296 | tf_op jit(solution)/shard_map/all_gather | solution.py:1285
  504.1 129.5 %all-gather.19.cloned.1.call-start = ((), (), s32[]{:S(2)}) async-start(), calls=%async_computation.5 | async-start | bytes 1769472 | tf_op jit(solution)/shard_map/all_gather | solution.py:1285
Sparse Core Ops, SparseCore 0:
  10.5 57.0 all-gather.8
  69.5 54.3 all-gather.10
  125.8 54.3 all-gather.12
  182.0 54.3 all-gather.14
  504.3 31.4 all-gather.16
  537.4 25.7 all-gather.18

commit v15 on v14

--- a/solution.py
+++ b/solution.py
@@ -339,7 +339,7 @@
     gather.drain(stop=LINE - 1)
 
 
-def gather_norm(x, gain, chunks=2):
+def gather_norm(x, gain, chunks=5):
     rows, features = x.shape
     return pl.pallas_call(
         functools.partial(gather_norm_body, chunks),

time: 661 us -> 660 us (level)
  no operation moved by 1% of the time
where the time goes in v15:
time: 660 us; the launch traced here: 651 us
  Pallas kernels  627 us (95%)
  between operations  15.1 us (2%)
    pallas_call x1, Pallas kernels, feed(): pl.pallas_call(functools.partial(feed_body, rank, tile, chunks), in_specs...  224 us
    pallas_call x1, Pallas kernels, front(): pl.pallas_call(functools.partial(front_body, chunks, seg), in_specs=[IN_H...  200 us
    pallas_call x1, Pallas kernels, back(): pl.pallas_call(functools.partial(back_body, chunks, seg), in_specs=[IN_HB...  127 us
    pallas_call x1, Pallas kernels, gather_norm(): pl.pallas_call(functools.partial(gather_norm_body, chunks), in_specs=[IN_...  63.7 us
  transfers between devices with their start and end apart: 6, of which 0 were waited for; matrix products, arithmetic and copies ran while one was open for 1% of the time, Pallas kernels for 60%

profile of v15, /device:TPU:0, one launch (start us, length us, event | category | flops | bytes accessed | tf_op | source)
XLA Modules:
  0.0 650.7 jit_solution(11488107952352006749)
XLA Ops:
  7.2 0.0 all-gather.9.cloned.1.call-start
  7.2 2.3 pad_maximum_fusion
  9.5 0.0 copy-start.2
  9.5 0.0 copy-start
  9.5 0.0 copy-start.1
  9.5 0.0 all-gather.9.cloned.1.call-update
  9.5 0.0 all-gather.11.cloned.1.call-start
  9.6 0.7 all-gather.11.cloned.1.call-update
  10.3 0.0 all-gather.13.cloned.1.call-start
  10.3 0.7 all-gather.13.cloned.1.call-update
  11.0 0.0 all-gather.15.cloned.1.call-start
  11.1 0.5 all-gather.15.cloned.1.call-update
  11.6 0.0 all-gather.17.cloned.1.call-start
  12.3 0.0 copy-done.2
  12.3 0.1 add_bitcast_fusion
  12.4 0.1 broadcast_in_dim.24
  12.4 0.7 sub.10.p_ref
  13.1 0.0 copy-done
  13.1 0.6 broadcast_in_dim.21.gain_ref
  13.7 0.0 copy-done.1
  13.7 0.6 broadcast_in_dim.25.gain_ref
  14.3 63.7 %shard_map.260.x_ref = bf16[4,320,2048]{2,1,0:T(8,128)(2,1)} custom-call(bf16[320,2048]{1,0:T(8,128)(2,1)} %x_ref.3, bf16[1,2048]{1,0:T(2,128)(2,1)} %broadcast_in_dim.21.gain_ref), custom_call_target="tpu_custom_call" | custom-call | tf_op jit(solution)/shard_map/pallas_call | solution.py:344
  78.0 2.1 shard_map.261
  80.1 0.0 all-gather.9.cloned.1.call-done.w_ref.wo_ref
  80.1 200.5 %shard_map.262 = (bf16[4,320,2048]{2,1,0:T(8,128)(2,1)}, bf16[3,1280,512]{2,1,0:T(8,128)(2,1)}, f32[320,2048]{1,0:T(8,128)}, bf16[4,320,2048]{2,1,0:T(8,128)(2,1...) custom-call(bf16[4,320,2048]{2,1,0:T(8,128)(2,1)} %shard_map.260.x_r, ...), custom_call_target="tpu_custom_call", output_to_operand_aliasing={{0}: (0, {})} | custom-call | tf_op jit(solution)/shard_map/pallas_call | solution.py:503
  280.6 0.0 all-gather.11.cloned.1.call-done.wg_ref
  280.6 0.0 all-gather.13.cloned.1.call-done.wu_ref
  280.6 0.0 all-gather.15.cloned.1.call-done.wd_ref
  280.6 223.8 %shard_map.263 = (f32[320,2048]{1,0:T(8,128)}, bf16[4,320,2048]{2,1,0:T(8,128)(2,1)}, bf16[320,2048]{1,0:T(8,128)(2,1)}, bf16[320,2048]{1,0:T(8,128)(2,1)}, bf16...) custom-call(bf16[4,320,2048]{2,1,0:T(8,128)(2,1)} %get-tuple-element, ...), custom_call_target="tpu_custom_call" | custom-call | tf_op jit(solution)/shard_map/pallas_call | solution.py:1205
  504.5 0.0 all-gather.17.cloned.1.call-update
  504.5 0.0 all-gather.19.cloned.1.call-start
  504.5 0.5 all-gather.19.cloned.1.call-update
  505.1 127.2 %shard_map.264 = (bf16[320,2048]{1,0:T(8,128)(2,1)}, bf16[8,64,2048]{2,1,0:T(8,128)(2,1)}, bf16[8,64,512]{2,1,0:T(8,128)(2,1)}, bf16[320,2048]{1,0:T(8,128)(2,1)}) custom-call(bf16[3,1280,512]{2,1,0:T(8,128)(2,1)} %get-tuple-element.57.q_ref, bf16[2048,2048]{1,0:T(8,128)(2,1)} %all-gather.9.cloned.1.call-done.w_ref.wo_ref, ...), custom_call_target="tpu_custom_call" | custom-call | tf_op jit(solution)/shard_map/pallas_call | solution.py:762
  632.2 0.0 all-gather.17.cloned.1.call-done
  632.3 1.5 fusion.pick_ref
  633.8 0.0 all-gather.19.cloned.1.call-done
  633.8 9.8 %shard_map.265 = (f32[5,8,16,2048]{3,2,1,0:T(8,128)}, f32[2,8,16,2048]{3,2,1,0:T(8,128)}, f32[2,8,16,2048]{3,2,1,0:T(8,128)}, f32[8,16,2048]{2,1,0:T(8,128)}, f3...) custom-call(s32[8]{0:T(128)} %fusion.pick_ref, ...), custom_call_target="tpu_custom_call" | custom-call | tf_op jit(solution)/shard_map/pallas_call | solution.py:1336
Async XLA Ops:
  7.2 72.9 %all-gather.9.cloned.1.call-start = ((), (), s32[]{:S(2)}) async-start(), calls=%async_computation | async-start | bytes 9437184 | tf_op jit(solution)/shard_map/all_gather | solution.py:1397
  9.5 2.8 copy-start.2
  9.5 3.6 copy-start
  9.5 4.2 copy-start.1
  9.5 271.1 %all-gather.11.cloned.1.call-start = ((), (), s32[]{:S(2)}) async-start(), calls=%async_computation.1 | async-start | bytes 9437184 | tf_op jit(solution)/shard_map/all_gather | solution.py:1405
  10.3 270.3 %all-gather.13.cloned.1.call-start = ((), (), s32[]{:S(2)}) async-start(), calls=%async_computation.2 | async-start | bytes 9437184 | tf_op jit(solution)/shard_map/all_gather | solution.py:1405
  11.0 269.6 %all-gather.15.cloned.1.call-start = ((), (), s32[]{:S(2)}) async-start(), calls=%async_computation.3 | async-start | bytes 9437184 | tf_op jit(solution)/shard_map/all_gather | solution.py:1405
  11.6 620.7 %all-gather.17.cloned.1.call-start = ((), (), s32[]{:S(2)}) async-start(), calls=%async_computation.4 | async-start | bytes 2359296 | tf_op jit(solution)/shard_map/all_gather | solution.py:1285
  504.5 129.3 %all-gather.19.cloned.1.call-start = ((), (), s32[]{:S(2)}) async-start(), calls=%async_computation.5 | async-start | bytes 1769472 | tf_op jit(solution)/shard_map/all_gather | solution.py:1285
Sparse Core Ops, SparseCore 0:
  10.5 57.0 all-gather.8
  69.5 54.5 all-gather.10
  125.9 54.3 all-gather.12
  182.0 54.3 all-gather.14
  504.6 31.3 all-gather.16
  537.7 25.6 all-gather.18
